TPU v7x, 32 devices: a whole 2x2x4 slice. The times are simulated.
32 devices in a mesh: slide: 2 (over y), seq: 16 (over z, x, core), head: 1.
Axes of the slice: x: 2, y: 2, z: 4, core: 2. Of those that a mesh axis runs over, the one named last changes fastest.
Arguments:
- queries: bfloat16 [16384, 768], P(('slide', 'seq'), 'head'), parts along dimension 0, may hold values from -14 to 14
- key_states: bfloat16 [16384, 768], P(('slide', 'seq'), 'head'), parts along dimension 0, may hold values from -4 to 4
- value_states: bfloat16 [16384, 768], P(('slide', 'seq'), 'head'), parts along dimension 0, may hold values from -6 to 6
- offsets_mid: int32 [16], replicated, may hold values from 0 to 3
- offsets_top: int32 [16], replicated, may hold values from 0 to 3
- out_weight: bfloat16 [768, 768], P('head'), may hold values from -0.21875 to 0.21875
Outputs:
- projected: bfloat16 [16384, 768], P(('slide', 'seq', 'head')), parts along dimension 0
There are 2 independent parts, one for each index of `slide`. A program takes and returns all parts, laid end to end along the dimension named above; an argument that names none is the same for every part. Nothing has to cross between parts.
All inputs are finite; a program needn't handle non-finite values.
Results may differ from a plain program's by a relative error of at most 0.0052.
Values may be sent and summed in bfloat16 or wider, within the bound.
No kernel may reach another device: no remote copies, remote signals or barrier semaphores. Data moves between devices by JAX's collectives and lax.ppermute only.
A program may use at most 64 MiB of HBM per device.

v0:
```python
import functools

import jax
import jax.numpy as jnp
from jax import lax
from jax.experimental import pallas as pl
from jax.experimental.pallas import tpu as pltpu
from jax.sharding import PartitionSpec as P

SEG = 2048
LOG2E = 1.4426950408889634
VMEM_LIMIT = 40 * 1024 * 1024
VMEM_MOST = 60 * 1024 * 1024
BF16 = jnp.bfloat16
F32 = jnp.float32


def partner_2(block, axis, apart):
    count = lax.axis_size(axis)
    route = []
    for low in range(count):
        high = low | 1 << apart
        if high != low and high < count:
            route += [(low, high), (high, low)]
    return lax.ppermute(block, axis, route)


def attend_head(triple_in):
    query_rows, key_rows, value_rows = triple_in
    score_scale = query_rows.shape[-1] ** (-0.5)
    scores = jnp.dot(query_rows, key_rows.T, preferred_element_type=jnp.float32) * score_scale
    row_max = jnp.max(scores, axis=1)
    shifted = jnp.exp(scores - row_max[:, None])
    row_total = jnp.sum(shifted, axis=1)
    weights = shifted.astype(jnp.bfloat16)
    numerator = jnp.dot(weights, value_rows, preferred_element_type=jnp.float32)
    return (numerator, row_total, row_max)


def attend_local(query_rows, pair_rows):
    return lax.map(
        attend_head,
        (
            query_rows.transpose(1, 0, 2),
            pair_rows[:, 0].transpose(1, 0, 2),
            pair_rows[:, 1].transpose(1, 0, 2),
        ),
    )


def pick_rows(states, offsets, rate):
    row_count, inner_count, heads_here, head_width = states.shape
    picker = (jnp.arange(rate)[:, None] == offsets[None, :]).astype(jnp.bfloat16)
    folded = states.reshape(row_count // rate, rate, inner_count, heads_here, head_width)
    return jnp.einsum("archd,rh->achd", folded, picker, preferred_element_type=jnp.float32).astype(
        jnp.bfloat16
    )


def spread_back(numerator, row_total, row_max, offsets, rate):
    heads_here, picked_count, head_width = numerator.shape
    chosen = jnp.arange(rate)[:, None] == offsets[None, :]
    full_num = jnp.where(chosen[None, :, :, None], numerator.transpose(1, 0, 2)[:, None], 0.0)
    full_total = jnp.where(chosen[None], row_total.T[:, None], 0.0)
    full_max = jnp.where(chosen[None], row_max.T[:, None], -1e30)
    return (
        full_num.reshape(picked_count * rate, heads_here, head_width),
        full_total.reshape(picked_count * rate, heads_here),
        full_max.reshape(picked_count * rate, heads_here),
    )


def doubling(buffer, steps_count):
    position = lax.axis_index("seq")
    for bit_index in range(steps_count):
        partner = partner_2(buffer, "seq", bit_index)
        is_lower = position >> bit_index & 1 == 0
        buffer = jnp.where(
            is_lower, jnp.concatenate([buffer, partner], 0), jnp.concatenate([partner, buffer], 0)
        )
    return buffer


def shards_general(queries, key_states, value_states, offsets_mid, offsets_top, out_weight):
    tok_rows = queries.shape[0]
    heads_local = offsets_mid.shape[0] // lax.axis_size("head")
    head_size = queries.shape[1] // heads_local
    seq_devices = lax.axis_size("seq")
    seq_total = tok_rows * seq_devices
    width_mid = min(16 * SEG, seq_total)
    rate_mid = width_mid // SEG
    rate_top = seq_total // SEG
    start_head = lax.axis_index("head") * heads_local
    mid_local = lax.dynamic_slice(offsets_mid, (start_head,), (heads_local,))
    top_local = lax.dynamic_slice(offsets_top, (start_head,), (heads_local,))
    query_heads = queries.reshape(tok_rows, 1, heads_local, head_size)
    paired = jnp.stack([key_states, value_states], axis=1).reshape(
        tok_rows, 2, heads_local, head_size
    )
    near_bits = (SEG // tok_rows).bit_length() - 1
    near_rows = doubling(paired.reshape(tok_rows, -1), near_bits).reshape(
        SEG, 2, heads_local, head_size
    )
    near_num, near_total, near_max = attend_local(query_heads[:, 0], near_rows)
    level_near = spread_back(
        near_num, near_total, near_max, jnp.zeros((heads_local,), jnp.int32), 1
    )
    mid_q = pick_rows(query_heads, mid_local, rate_mid)[:, 0]
    mid_kv = pick_rows(paired, mid_local, rate_mid)
    mid_group = width_mid // tok_rows
    mid_bits = mid_group.bit_length() - 1
    mid_rows = doubling(mid_kv.reshape(mid_kv.shape[0], -1), mid_bits).reshape(
        SEG, 2, heads_local, head_size
    )
    mid_num, mid_total, mid_max = attend_local(mid_q, mid_rows)
    level_mid = spread_back(mid_num, mid_total, mid_max, mid_local, rate_mid)
    top_q = pick_rows(query_heads, top_local, rate_top)[:, 0]
    top_kv = pick_rows(paired, top_local, rate_top)
    top_rows = lax.all_gather(
        top_kv.reshape(top_kv.shape[0], -1), "seq", axis=0, tiled=True
    ).reshape(SEG, 2, heads_local, head_size)
    top_num, top_total, top_max = attend_local(top_q, top_rows)
    level_top = spread_back(top_num, top_total, top_max, top_local, rate_top)
    levels = [level_near, level_mid, level_top]
    overall = jnp.maximum(jnp.maximum(level_near[2], level_mid[2]), level_top[2])
    numerator = jnp.zeros((tok_rows, heads_local, head_size), jnp.float32)
    row_total = jnp.zeros((tok_rows, heads_local), jnp.float32)
    for level_num, level_total, level_max in levels:
        factor = jnp.exp(level_max - overall)
        numerator = numerator + factor[..., None] * level_num
        row_total = row_total + factor * level_total
    attention = (
        (numerator / row_total[..., None])
        .astype(jnp.bfloat16)
        .reshape(tok_rows, heads_local * head_size)
    )
    result = lax.psum_scatter(
        jnp.dot(attention, out_weight, preferred_element_type=jnp.float32),
        "head",
        scatter_dimension=0,
        tiled=True,
    )
    return result.astype(jnp.bfloat16)


RATE = 4
GROUP = 4
HG = 4
STEP = 2
DH = 48
BLK = 128
HALF = 2 * BLK
TOK = 512
SAFE = 96.0
DX = 64


def dot(a, b):
    return jnp.dot(a, b, preferred_element_type=F32)


def dot_nt(a, b):
    return lax.dot_general(a, b, (((1,), (1,)), ((), ())), preferred_element_type=F32)


def class_of_slots(off_mid, off_top):
    first = off_mid
    second = jnp.where(off_top == off_mid, lax.rem(off_mid + 1, RATE), off_top)
    free0 = (first != 0) & (second != 0)
    free1 = (first != 1) & (second != 1)
    third = jnp.where(free0, 0, jnp.where(free1, 1, 2))
    return first, second, third, 6 - first - second - third


def head_of(place, j, p):
    return ((place[0] & (GROUP - 1)) ^ j) * HG + ((place[0] // GROUP) ^ p)


def token_picker():
    row = lax.broadcasted_iota(jnp.int32, (TOK, TOK), 0)
    col = lax.broadcasted_iota(jnp.int32, (TOK, TOK), 1)
    return (col == RATE * (row % BLK) + row // BLK).astype(BF16)


def fill_class_major(block, picker, scratch):
    scratch[...] = lax.dot_general(
        block, picker, (((0,), (1,)), ((), ())), preferred_element_type=F32
    ).astype(BF16)


def lane_block(index):
    return pl.ds(pl.multiple_of(index * BLK, BLK), BLK)


def head_rows(head):
    return pl.ds(pl.multiple_of(head * DH, 16), DH)


def pack_kernel(place, mid, top, k_hbm, v_hbm, q_hbm, *refs):
    outs, refs = refs[:6], refs[6:]
    blocks, held, packed, sems_in, sems_out = refs[:3], refs[3:6], refs[6:12], refs[12], refs[13]
    loads = [
        pltpu.make_async_copy(hbm, block, sems_in.at[i])
        for i, (hbm, block) in enumerate(zip((k_hbm, v_hbm, q_hbm), blocks))
    ]
    for load in loads:
        load.start()
    picker = token_picker()
    stores = []
    for n, (load, block, scratch) in enumerate(zip(loads, blocks, held)):
        load.wait()
        fill_class_major(block[...], picker, scratch)
        rows = slice(n * DH, (n + 1) * DH)
        for i, (j, first, count) in enumerate(
            ((0, 0, 4), (1, 0, 4), (2, 0, 2), (3, 0, 2), (2, 2, 2), (3, 2, 2))
        ):
            for p in range(HG):
                head = head_of(place, j, p)
                slots = class_of_slots(mid[head], top[head])
                for s in range(count):
                    packed[i][p, rows, s * BLK : (s + 1) * BLK] = scratch[
                        head_rows(head), lane_block(slots[first + s])
                    ]
            store = pltpu.make_async_copy(
                packed[i].at[:, rows], outs[i].at[:, rows], sems_out.at[i, n]
            )
            store.start()
            stores.append(store)
    for store in stores:
        store.wait()


def regroup_kernel(a_ref, b_ref, *refs):
    for s, out in enumerate(refs[-3:]):
        out[0] = a_ref[s + 1, :, 0:HALF]
        out[1] = b_ref[s + 1, :, 0:HALF]


def split_query(q):
    scaled = q.astype(F32) * (DH**-0.5 * LOG2E)
    high = scaled.astype(BF16)
    low = (scaled - high.astype(F32)).astype(BF16)
    return jnp.concatenate([high, low], axis=0)


def twice_keys(keys_t):
    both = jnp.concatenate([keys_t, keys_t], axis=0).astype(F32)
    return both.T.astype(BF16)


def largest(blocks):
    best = None
    for block in blocks:
        wide = block.astype(F32)
        length = jnp.sum(wide * wide, axis=0, keepdims=True)
        for low in range(0, block.shape[1], HALF):
            part = length[:, low : low + HALF]
            best = part if best is None else jnp.maximum(best, part)
    return jnp.max(best)


def is_small(queries, keys):
    scale = DH**-0.5 * LOG2E
    return largest(queries) * largest(keys) * (scale * scale) < SAFE * SAFE


def column_max(blocks):
    best = jnp.max(blocks[0], axis=0, keepdims=True)
    for block in blocks[1:]:
        best = jnp.maximum(best, jnp.max(block, axis=0, keepdims=True))
    return best


def near_kernel(inputs, units, tasks, carried, place, mid, top, *refs):
    pieces = dict(zip(inputs, refs[: len(inputs)]))
    refs = refs[len(inputs) :]
    old = [refs[2 * i : 2 * i + 2] for i in range(carried)]
    outs = refs[2 * carried : 2 * carried + 2 * len(tasks)]
    k_s, v_s = refs[-2:]
    v_s[:, DH:DX, :] = jnp.ones((STEP, DX - DH, v_s.shape[2]), BF16)
    lane_slot = lax.broadcasted_iota(jnp.int32, (1, HALF), 1) // BLK

    def lookup(j, slot):
        first = 0 if (j, 0) in pieces and pieces[j, 0].shape[2] > HALF else slot // 2 * 2
        return pieces[j, first], (slot - first) * BLK

    chunks = []
    row = 0
    for label, members in units:
        chunks.append((label, slice(row, row + len(members) * BLK)))
        row += len(members) * BLK
    members = [member for _, group in units for member in group]

    def prepare(h):
        for i, (j, slot) in enumerate(members):
            ref, lane = lookup(j, slot)
            rows = slice(i * BLK, (i + 1) * BLK)
            k_s[h, rows, :] = twice_keys(ref[h, 0:DH, lane : lane + BLK])
            v_s[h, 0:DH, rows] = ref[h, DH : 2 * DH, lane : lane + BLK]

    def counted_again(h):
        head = head_of(place, 0, pl.program_id(0) * STEP + h)
        same = mid[head] == top[head]
        return [
            jnp.where(lane_slot == 0, jnp.where(same, 1.584962500721156, 1.0), 0.0),
            jnp.where(lane_slot == 1, jnp.where(same, 0.0, 1.0), 0.0),
        ]

    def run(plain, heads):
        again = [counted_again(h) for h in heads]
        flat = [
            (h, again_h, query, low, merge, out, i)
            for h, again_h in zip(heads, again)
            for out, group in enumerate(tasks)
            for i, (query, low, merge) in enumerate(group)
        ]

        def score(task):
            h, _, (j, half), low = task[:4]
            ref, lane = lookup(j, 2 * half)
            query = split_query(ref[h, 2 * DH :, lane : lane + HALF])
            return [dot(k_s[h, rows, :], query) for _, rows in chunks[low:]]

        scores = score(flat[0])
        for n, (h, again_h, (_, half), low, merge, out, i) in enumerate(flat):
            following = score(flat[n + 1]) if n + 1 < len(flat) else None
            best = jnp.zeros((1, HALF), F32) if plain else column_max(scores)
            if merge is not None:
                acc_in, max_in = old[merge[0]]
                old_max = max_in[h, merge[1], 0:1, :]
                best = best if plain else jnp.maximum(best, old_max)
            acc = None
            for (label, rows), block in zip(chunks[low:], scores):
                if half == 0 and label is not None:
                    block = block - (best - again_h[label])
                elif not plain:
                    block = block - best
                part = dot(v_s[h, :, rows], jnp.exp2(block).astype(BF16))
                acc = part if acc is None else acc + part
            if merge is not None:
                before = acc_in[h, merge[1]]
                acc = acc + (before if plain else before * jnp.exp2(old_max - best))
            acc_ref, max_ref = outs[2 * out : 2 * out + 2]
            acc_ref[h, i] = acc
            max_ref[h, i] = jnp.broadcast_to(best, (8, HALF))
            scores = following

    for h in range(STEP):
        prepare(h)
    plain = is_small(
        [ref[h, 2 * DH :, :] for ref in pieces.values() for h in range(STEP)],
        [ref[h, 0:DH, :] for ref in pieces.values() for h in range(STEP)],
    )
    for _, max_in in old:
        plain = plain & (jnp.max(jnp.abs(max_in[...])) == 0.0)

    @pl.when(plain)
    def _():
        run(True, list(range(STEP)))

    @pl.when(jnp.logical_not(plain))
    def _():
        @pl.loop(0, STEP)
        def _(h):
            run(False, [h])


def far_kernel(place, mid, top, *refs):
    own, beyond = refs[:GROUP], refs[GROUP : GROUP + 6]
    outs = refs[GROUP + 6 : GROUP + 6 + RATE]
    k_s, v_s, q_s, result_s, tail_s = refs[GROUP + 6 + RATE :]
    head = head_of(place, 0, 0)
    same = mid[head] == top[head]
    slots = (0, jnp.where(same, 0, 1))

    def source(s, j):
        return own[j].at[0] if s == 0 else beyond[2 * (s - 1) + j // 2].at[j % 2]

    for s in range(RATE):
        for j in range(GROUP):
            ref = source(s, j)
            for level, slot in enumerate(slots):
                here = slice(j * BLK, (j + 1) * BLK)
                k_s[level, s, here, :] = twice_keys(ref[0:DH, lane_block(slot)])
                v_s[level, s, 0:DH, here] = ref[DH : 2 * DH, lane_block(slot)]
                q_s[level, s, :, here] = split_query(ref[2 * DH : 3 * DH, lane_block(slot)])
    v_s[:, :, DH:DX, :] = jnp.ones((2, RATE, DX - DH, TOK), BF16)
    tail_s[...] = jnp.zeros(tail_s.shape, F32)

    def run(plain):
        tasks = [(level, chip) for level in range(2) for chip in range(2)]

        def segment(s, carry):
            def score(task):
                level, chip = task
                query = q_s[level, s, :, chip * HALF : (chip + 1) * HALF]
                return [dot(k_s[level, s ^ d], query) for d in range(1, RATE)]

            scores = score(tasks[0])
            for n, (level, chip) in enumerate(tasks):
                following = score(tasks[n + 1]) if n + 1 < len(tasks) else None
                best = jnp.zeros((1, HALF), F32) if plain else column_max(scores)
                acc = None
                for d in range(1, RATE):
                    block = scores[d - 1] if plain else scores[d - 1] - best
                    part = dot(v_s[level, s ^ d], jnp.exp2(block).astype(BF16))
                    acc = part if acc is None else acc + part
                total = acc[DH : DH + 1, :]
                result = (acc[0:DH, :] / total).astype(BF16)
                lse = best + jnp.log2(total)
                if level == 0:
                    lse = jnp.where(same, lse + 1.0, lse)
                else:
                    lse = jnp.where(same, -1e30, lse)
                high = lse.astype(BF16).astype(F32)
                middle = (lse - high).astype(BF16).astype(F32)
                low = lse - high - middle
                for i in range(2):
                    n = 2 * (2 * chip + i) + level
                    mine = slice(i * BLK, (i + 1) * BLK)
                    result_s[s, :, n * BLK : (n + 1) * BLK] = result[:, mine]
                    for k, part in enumerate((high, middle, low)):
                        tail_s[s, 3 * n + k : 3 * n + k + 1, :] = part[:, mine]
                scores = following
            return carry

        lax.fori_loop(0, RATE, segment, 0, unroll=2 if plain else 1)

    every = [source(s, j) for s in range(RATE) for j in range(GROUP)]
    plain = is_small(
        [ref[2 * DH : 3 * DH, 0:HALF] for ref in every], [ref[0:DH, 0:HALF] for ref in every]
    )
    pl.when(plain)(lambda: run(True))
    pl.when(jnp.logical_not(plain))(lambda: run(False))
    for s in range(RATE):
        outs[s][:, : GROUP * HALF] = result_s[s]
        outs[s][:, GROUP * HALF :] = tail_s[s].astype(BF16)


def join(acc, best, far, j):
    tail = far[:, GROUP * HALF :].astype(F32)
    lse = jnp.concatenate(
        [
            tail[3 * n : 3 * n + 1] + tail[3 * n + 1 : 3 * n + 2] + tail[3 * n + 2 : 3 * n + 3]
            for n in (2 * j, 2 * j + 1)
        ],
        axis=1,
    )
    overall = jnp.maximum(best, lse)
    near_factor, far_factor = jnp.exp2(best - overall), jnp.exp2(lse - overall)
    total = acc[DH : DH + 1] * near_factor + far_factor
    value = far[:, j * HALF : (j + 1) * HALF].astype(F32) * far_factor
    return ((acc[0:DH] * near_factor + value) / total).astype(BF16)


def combine_kernel(chip, acc_ref, max_ref, *refs):
    far, outs = refs[:HG], refs[HG:]
    for i in range(2):
        for p in range(HG):
            outs[i][p, :, 0:HALF] = join(
                acc_ref[p, 2 * i], max_ref[p, 2 * i, 0:1, :], far[p], 2 * chip + i
            )
            acc = acc_ref[p, 2 * i + 1]
            outs[i][p, :, HALF:] = (acc[0:DH] / acc[DH : DH + 1]).astype(BF16)


def project_kernel(place, mid, top, *refs):
    parts = refs[:GROUP]
    w_ref, out_ref, held = refs[GROUP:]
    for j in range(GROUP):
        for p in range(HG):
            head = head_of(place, j, p)
            slots = class_of_slots(mid[head], top[head])
            for s in range(RATE):
                held[head_rows(head), lane_block(slots[s])] = parts[j][
                    p, :, s * BLK : (s + 1) * BLK
                ]
    row = lax.broadcasted_iota(jnp.int32, (TOK, TOK), 0)
    col = lax.broadcasted_iota(jnp.int32, (TOK, TOK), 1)
    picker = (row == RATE * (col % BLK) + col // BLK).astype(BF16)
    attention = dot_nt(picker, held[...]).astype(BF16)
    out_ref[...] = dot(attention, w_ref[...]).astype(BF16)


def whole(shape):
    return pl.BlockSpec(shape, lambda *_: (0,) * len(shape))


def per_head(shape):
    return pl.BlockSpec(shape, lambda h, *_: (h,) + (0,) * (len(shape) - 1))


def call(
    kernel, scalars, args, grid, in_specs, outs, scratch, scores,
    limit=VMEM_LIMIT, after=(), through=(),
):
    known = len(scalars) + len(args)
    extra = (*after, *through)
    count = len(outs)
    anywhere = pl.BlockSpec(memory_space=pl.ANY)

    def body(*refs):
        results = refs[known + len(extra) :]
        kernel(*refs[:known], *results[:count], *results[count + len(through) :])

    return pl.pallas_call(
        body if extra else kernel,
        grid_spec=pltpu.PrefetchScalarGridSpec(
            num_scalar_prefetch=len(scalars),
            grid=grid,
            in_specs=list(in_specs) + [anywhere] * len(extra),
            out_specs=[spec for spec, _ in outs] + [anywhere] * len(through),
            scratch_shapes=scratch,
        ),
        out_shape=[shape for _, shape in outs]
        + [jax.ShapeDtypeStruct(x.shape, x.dtype) for x in through],
        input_output_aliases={known + len(after) + i: count + i for i in range(len(through))},
        compiler_params=pltpu.CompilerParams(vmem_limit_bytes=limit),
        cost_estimate=pl.CostEstimate(flops=0, bytes_accessed=0, transcendentals=0),
    )(*scalars, *args, *extra)


def within(array, apart):
    count = lax.axis_size("seq")
    return lax.ppermute(array, "seq", [(i, i ^ apart) for i in range(count)])


def across(array, segments):
    return within(array, GROUP * segments)


def shards_four(queries, key_states, value_states, offsets_mid, offsets_top, out_weight):
    width = queries.shape[1]
    place = lax.axis_index("seq").astype(jnp.int32).reshape(1)
    scalars = (place, offsets_mid, offsets_top)
    full = jax.ShapeDtypeStruct((HG, 3 * DH, TOK), BF16)
    piece = jax.ShapeDtypeStruct((HG, 3 * DH, HALF), BF16)
    pair = jax.ShapeDtypeStruct((2, 3 * DH, HALF), BF16)
    anywhere = pl.BlockSpec(memory_space=pl.ANY)
    shapes = [full] * 2 + [piece] * 4
    own0, own1, sel2, sel3, rest2, rest3 = call(
        pack_kernel, scalars, (key_states, value_states, queries), (1,),
        [anywhere] * 3,
        [(anywhere, shape) for shape in shapes],
        [pltpu.VMEM((TOK, width), BF16)] * 3
        + [pltpu.VMEM((width, TOK), BF16)] * 3
        + [pltpu.VMEM(shape.shape, BF16) for shape in shapes]
        + [pltpu.SemaphoreType.DMA((3,)), pltpu.SemaphoreType.DMA((6, 3))],
        1 << 19, VMEM_MOST,
    )
    own1 = within(own1, 1)
    sel2, sel3 = within(sel2, 2), within(sel3, 3)

    def regroup(a, b, **order):
        return call(
            regroup_kernel, (), (a, b), (1,),
            [whole(a.shape), whole(b.shape)], [(whole(pair.shape), pair)] * 3,
            [], 1 << 17, **order,
        )

    def state(count):
        return [
            (per_head((STEP, count, rows, HALF)), jax.ShapeDtypeStruct((HG, count, rows, HALF), F32))
            for rows in (DX, 8)
        ]

    def near(held, units, tasks, old, **order):
        sizes = [len(members) * BLK for _, members in units]
        scores = sum(sum(sizes[low:]) * HALF for group in tasks for _, low, _ in group)
        return call(
            functools.partial(near_kernel, list(held), units, tasks, len(old)), scalars,
            (*held.values(), *[x for one in old for x in one]), (HG // STEP,),
            [per_head((STEP,) + x.shape[1:]) for x in held.values()]
            + [per_head((STEP,) + x.shape[1:]) for one in old for x in one],
            [out for group in tasks for out in state(len(group))],
            [
                pltpu.VMEM((STEP, sum(sizes), 2 * DH), BF16),
                pltpu.VMEM((STEP, DX, sum(sizes)), BF16),
            ],
            HG * scores, **order,
        )

    def units_of(a, b):
        return [(0, [(a, 0), (b, 0)]), (1, [(a, 1), (b, 1)])], [
            (None, [(a, 2), (a, 3), (b, 2), (b, 3)])
        ]

    own_sel, own_rest = units_of(0, 1)
    other_sel, other_rest = units_of(2, 3)
    own = [(0, 0), (0, 1), (1, 0), (1, 1)]

    ours = regroup(own0, own1)
    ours = [across(x, s + 1) for s, x in enumerate(ours)]
    held = {(0, 0): own0, (1, 0): own1}
    state_own = near(held, own_sel + own_rest, [[(q, 0, None) for q in own]], [])
    *theirs, rest2, rest3 = regroup(sel2, sel3, after=state_own[1:], through=(rest2, rest3))
    theirs = [across(x, s + 1) for s, x in enumerate(theirs)]
    rest2, rest3 = within(rest2, 2), within(rest3, 3)
    beyond = [x for both in zip(ours, theirs) for x in both]

    held.update({(2, 0): sel2, (3, 0): sel3})
    out = near(
        held, own_sel + own_rest + other_sel,
        [
            [(q, 3, (0, i)) for i, q in enumerate(own)],
            [((2, 0), 0, None), ((3, 0), 0, None)],
        ],
        [state_own],
        after=ours,
    )
    state_own, state_sel = out[:2], out[2:]

    result = jax.ShapeDtypeStruct((DH, GROUP * HALF + BLK), BF16)
    piece_0 = pl.BlockSpec((1, 3 * DH, HALF), lambda *_: (0, 0, 0))
    results = call(
        far_kernel, scalars, (own0, own1, sel2, sel3, *beyond), (1,),
        [piece_0] * GROUP + [whole(pair.shape)] * 6,
        [(whole(result.shape), result)] * RATE,
        [
            pltpu.VMEM((2, RATE, TOK, 2 * DH), BF16),
            pltpu.VMEM((2, RATE, DX, TOK), BF16),
            pltpu.VMEM((2, RATE, 2 * DH, TOK), BF16),
            pltpu.VMEM((RATE, DH, GROUP * HALF), BF16),
            pltpu.VMEM((RATE, DH, BLK), F32),
        ],
        RATE * 2 * 3 * TOK * TOK, after=(out[1],),
    )
    back = [results[0]] + [across(results[s], s) for s in range(1, RATE)]

    held.update({(2, 2): rest2, (3, 2): rest3})
    units = own_sel + own_rest + other_sel + other_rest
    attended = jax.ShapeDtypeStruct((HG, DH, TOK), BF16)

    def combine(chip, state):
        return call(
            functools.partial(combine_kernel, chip), (), (*state, *back), (1,),
            [whole(x.shape) for x in state] + [whole(result.shape)] * HG,
            [(whole(attended.shape), attended)] * 2,
            [],
            1 << 18,
        )

    state_other = near(
        held, units,
        [
            [
                ((2, 0), 5, (0, 0)), ((2, 1), 0, None),
                ((3, 0), 5, (0, 1)), ((3, 1), 0, None),
            ]
        ],
        [state_sel],
        after=results[:1],
    )
    part2, part3 = combine(1, state_other)
    state_own = near(
        {(2, 2): rest2, (3, 2): rest3, **{q: held[q] for q in ((0, 0), (1, 0))}},
        other_rest,
        [[(q, 0, (0, i)) for i, q in enumerate(own)]],
        [state_own],
        after=(part2,),
    )
    part0, part1 = combine(0, state_own)
    parts = [part0, within(part1, 1), within(part2, 2), within(part3, 3)]
    return call(
        project_kernel, scalars, (*parts, out_weight), (1,),
        [whole(attended.shape)] * GROUP + [whole((width, width))],
        [(whole((TOK, width)), jax.ShapeDtypeStruct((TOK, width), BF16))],
        [pltpu.VMEM((width, TOK), BF16)],
        1 << 18,
    )[0]


def shards(queries, key_states, value_states, offsets_mid, offsets_top, out_weight):
    tokens, width = queries.shape
    heads = offsets_mid.shape[0]
    fits = (
        lax.axis_size("head") == 1
        and lax.axis_size("seq") == GROUP * RATE
        and tokens == TOK
        and heads == GROUP * HG
        and width == heads * DH
    )
    run = shards_four if fits else shards_general
    return run(queries, key_states, value_states, offsets_mid, offsets_top, out_weight)


def solution(mesh):
    in_specs = (
        P(("slide", "seq"), "head"),
        P(("slide", "seq"), "head"),
        P(("slide", "seq"), "head"),
        P(),
        P(),
        P("head", None),
    )
    out_specs = P(("slide", "seq", "head"), None)
    return jax.shard_map(shards, mesh=mesh, in_specs=in_specs, out_specs=out_specs, check_vma=False)
```

profile of v0, /device:TPU:0, one launch (start us, length us, event | category | flops | bytes accessed | tf_op | source)
XLA Modules:
  0.0 82.4 jit_solution(192506686312980037)
XLA Ops:
  0.0 5.3 %shard_map.64 = (bf16[4,144,512]{2,1,0:T(8,128)(2,1)}, bf16[4,144,512]{2,1,0:T(8,128)(2,1)}, bf16[4,144,256]{2,1,0:T(8,128)(2,1)}, bf16[4,144,256]{2,1,0:T(8,128...) custom-call(s32[1]{0:T(128)} %bitcast.place.refs_0_, s32[16]{0:T(128)} %mid.5, s32[16]{0:T(128)} %top.5, ...), custom_call_target="tpu_custom_call" | custom-call | tf_op jit(solution)/shard_map/pallas_call | solution.py:506
  5.3 0.0 copy-start.5
  5.3 0.0 copy-start.6
  5.3 0.5 collective-permute-start.2
  5.8 2.6 %collective-permute-start = (bf16[4,144,256]{2,1,0:T(8,128)(2,1)}, bf16[4,144,256]{2,1,0:T(8,128)(2,1)S(1)}, u32[]{:S(2)}, u32[]{:S(2)}) collective-permute-start(bf16[4,144,256]{2,1,0:T(8,128)(2,1)} %get-tuple-element.37), channel_id=1, source_target_pairs={{0,2},{1,3},{2,0},{3,1},{4,6},{5,7},{6,4},{7,5},{8,10},{9,11},{10,... | collective-permute-start | bytes 884744 | tf_op jit(solution)/shard_map/ppermute | solution.py:525
  8.4 0.1 collective-permute-start.1
  8.5 1.1 %copy-done = bf16[4,144,512]{2,1,0:T(8,128)(2,1)S(1)} copy-done((bf16[4,144,512]{2,1,0:T(8,128)(2,1)S(1)}, bf16[4,144,512]{2,1,0:T(8,128)(2,1)}, u32[]{:S(2)}) %copy-start) | copy-done | bytes 589848
  9.6 2.2 %collective-permute-start.5 = (bf16[2,144,256]{2,1,0:T(8,128)(2,1)S(1)}, bf16[2,144,256]{2,1,0:T(8,128)(2,1)S(1)}, u32[]{:S(2)}, u32[]{:S(2)}) collective-permute-start(bf16[2,144,256]{2,1,0:T(8,128)(2,1)S(1)} %get-tuple-element.47), channel_id=1, source_target_pairs={{0,4},{1,5},{2,6},{3,7},{4,0},{5,1},{6,2},{7,3},{8,12},{9,13},{10,... | collective-permute-start | bytes 442376 | tf_op jit(solution)/shard_map/ppermute | solution.py:525
  11.8 2.6 %collective-permute-start.6 = (bf16[2,144,256]{2,1,0:T(8,128)(2,1)S(1)}, bf16[2,144,256]{2,1,0:T(8,128)(2,1)S(1)}, u32[]{:S(2)}, u32[]{:S(2)}) collective-permute-start(bf16[2,144,256]{2,1,0:T(8,128)(2,1)S(1)} %get-tuple-element.48), channel_id=1, source_target_pairs={{0,8},{1,9},{2,10},{3,11},{4,12},{5,13},{6,14},{7,15},{8,0},{9,1},... | collective-permute-start | bytes 442376 | tf_op jit(solution)/shard_map/ppermute | solution.py:525
  14.4 7.6 %shard_map.65 = (f32[4,4,64,256]{3,2,1,0:T(8,128)S(1)}, f32[4,4,8,256]{3,2,1,0:T(8,128)S(1)}) custom-call(s32[1]{0:T(128)} %bitcast.place.refs_0_, s32[16]{0:T(128)S(1)} %copy-done.5, s32[16]{0:T(128)S(1)} %copy-done.6, bf16[4,144,512]{2,1,0:T(8,128)(2,1)S(1)} %copy-done.1, bf16[4,144,512]{2,1,0:T(8,128)(2,1)S(1)} %collective-permute-done.2.refs_1_.b_ref.refs_4_.refs_6_), custom_call_target="tpu_custom_call" | custom-call | tf_op jit(solution)/shard_map/pallas_call | solution.py:506
  22.0 0.3 collective-permute-done.1.refs_1_.refs_6_
  22.3 1.6 %collective-permute-start.3 = (bf16[4,144,256]{2,1,0:T(8,128)(2,1)S(1)}, bf16[4,144,256]{2,1,0:T(8,128)(2,1)S(1)}, u32[]{:S(2)}, u32[]{:S(2)}) collective-permute-start(bf16[4,144,256]{2,1,0:T(8,128)(2,1)S(1)} %get-tuple-element.44), channel_id=1, source_target_pairs={{0,2},{1,3},{2,0},{3,1},{4,6},{5,7},{6,4},{7,5},{8,10},{9,11},{10,... | collective-permute-start | bytes 884744 | tf_op jit(solution)/shard_map/ppermute | solution.py:525
  23.9 0.3 collective-permute-start.4
  24.2 3.8 %collective-permute-start.10 = (bf16[2,144,256]{2,1,0:T(8,128)(2,1)S(1)}, bf16[2,144,256]{2,1,0:T(8,128)(2,1)S(1)}, u32[]{:S(2)}, u32[]{:S(2)}) collective-permute-start(bf16[2,144,256]{2,1,0:T(8,128)(2,1)S(1)} %get-tuple-element.56), channel_id=1, source_target_pairs={{0,12},{1,13},{2,14},{3,15},{4,8},{5,9},{6,10},{7,11},{8,4},{9,5},... | collective-permute-start | bytes 442376 | tf_op jit(solution)/shard_map/ppermute | solution.py:525
  28.0 1.4 %collective-permute-start.9 = (bf16[2,144,256]{2,1,0:T(8,128)(2,1)S(1)}, bf16[2,144,256]{2,1,0:T(8,128)(2,1)S(1)}, u32[]{:S(2)}, u32[]{:S(2)}) collective-permute-start(bf16[2,144,256]{2,1,0:T(8,128)(2,1)S(1)} %get-tuple-element.55), channel_id=1, source_target_pairs={{0,8},{1,9},{2,10},{3,11},{4,12},{5,13},{6,14},{7,15},{8,0},{9,1},... | collective-permute-start | bytes 442376 | tf_op jit(solution)/shard_map/ppermute | solution.py:525
  29.4 9.4 %shard_map.68 = (f32[4,4,64,256]{3,2,1,0:T(8,128)S(1)}, f32[4,4,8,256]{3,2,1,0:T(8,128)S(1)}, f32[4,2,64,256]{3,2,1,0:T(8,128)S(1)}, f32[4,2,8,256]{3,2,1,0:T(8,128)S(1)}) custom-call(s32[1]{0:T(128)} %bitcast.place.refs_0_, s32[16]{0:T(128)S(1)} %copy-done.5, s32[16]{0:T(128)S(1)} %copy-done.6, bf16[4,144,512]{2,1,0:T(8,128)(2,1)S(1)} %copy-done.1, ...), custom_call_target="tpu_custom_call" | custom-call | tf_op jit(solution)/shard_map/pallas_call | solution.py:506
  38.8 2.0 %collective-permute-done.9.refs_10_ = bf16[2,144,256]{2,1,0:T(8,128)(2,1)S(1)} collective-permute-done((bf16[2,144,256]{2,1,0:T(8,128)(2,1)S(1)}, bf16[2,144,256]{2,1,0:T(8,128)(2,1)S(1)}, u32[]{:S(2)}, u32[]{:S(2)}) %collective-permute-start.9) | collective-permute-done | bytes 147488 | tf_op jit(solution)/shard_map/ppermute | solution.py:525
  40.8 10.2 %shard_map.69 = (bf16[48,1152]{1,0:T(8,128)(2,1)S(1)}, bf16[48,1152]{1,0:T(8,128)(2,1)S(1)}, bf16[48,1152]{1,0:T(8,128)(2,1)S(1)}, bf16[48,1152]{1,0:T(8,128)(2,1)S(1)}) custom-call(s32[1]{0:T(128)} %bitcast.place.refs_0_, s32[16]{0:T(128)S(1)} %copy-done.5, s32[16]{0:T(128)S(1)} %copy-done.6, bf16[4,144,512]{2,1,0:T(8,128)(2,1)S(1)} %copy-done.1, ...), custom_call_target="tpu_custom_call" | custom-call | tf_op jit(solution)/shard_map/pallas_call | solution.py:506
  51.0 0.1 collective-permute-start.11
  51.1 3.0 %collective-permute-start.12 = (bf16[48,1152]{1,0:T(8,128)(2,1)S(1)}, bf16[48,1152]{1,0:T(8,128)(2,1)S(1)}, u32[]{:S(2)}, u32[]{:S(2)}) collective-permute-start(bf16[48,1152]{1,0:T(8,128)(2,1)S(1)} %get-tuple-element.61), channel_id=1, source_target_pairs={{0,8},{1,9},{2,10},{3,11},{4,12},{5,13},{6,14},{7,15},{8,0},{9,1},... | collective-permute-start | bytes 331784 | tf_op jit(solution)/shard_map/ppermute | solution.py:525
  54.1 1.3 %collective-permute-start.13 = (bf16[48,1152]{1,0:T(8,128)(2,1)S(1)}, bf16[48,1152]{1,0:T(8,128)(2,1)S(1)}, u32[]{:S(2)}, u32[]{:S(2)}) collective-permute-start(bf16[48,1152]{1,0:T(8,128)(2,1)S(1)} %get-tuple-element.62), channel_id=1, source_target_pairs={{0,12},{1,13},{2,14},{3,15},{4,8},{5,9},{6,10},{7,11},{8,4},{9,5},... | collective-permute-start | bytes 331784 | tf_op jit(solution)/shard_map/ppermute | solution.py:525
  55.5 9.9 %shard_map.70 = (f32[4,4,64,256]{3,2,1,0:T(8,128)S(1)}, f32[4,4,8,256]{3,2,1,0:T(8,128)S(1)}) custom-call(s32[1]{0:T(128)} %bitcast.place.refs_0_, s32[16]{0:T(128)S(1)} %copy-done.5, s32[16]{0:T(128)S(1)} %copy-done.6, bf16[4,144,512]{2,1,0:T(8,128)(2,1)S(1)} %copy-done.1, bf16[4,144,512]{2,1,0:T(8,128)(2,1)S(1)} %collective-permute-done.2.refs_1_.b_ref.refs_4_.refs_6_, ...), custom_call_target="tpu_custom_call" | custom-call | tf_op jit(solution)/shard_map/pallas_call | solution.py:506
  65.4 0.1 shard_map.71
  65.6 1.6 %collective-permute-start.15 = (bf16[4,48,512]{2,1,0:T(8,128)(2,1)S(1)}, bf16[4,48,512]{2,1,0:T(8,128)(2,1)S(1)}, u32[]{:S(2)}, u32[]{:S(2)}) collective-permute-start(bf16[4,48,512]{2,1,0:T(8,128)(2,1)S(1)} %get-tuple-element.63.refs_9_), channel_id=1, source_target_pairs={{0,2},{1,3},{2,0},{3,1},{4,6},{5,7},{6,4},{7,5},{8,10},{9,11},{10,... | collective-permute-start | bytes 589832 | tf_op jit(solution)/shard_map/ppermute | solution.py:525
  67.2 5.3 %shard_map.72 = (f32[4,4,64,256]{3,2,1,0:T(8,128)S(1)}, f32[4,4,8,256]{3,2,1,0:T(8,128)S(1)}) custom-call(s32[1]{0:T(128)} %bitcast.place.refs_0_, s32[16]{0:T(128)S(1)} %copy-done.5, s32[16]{0:T(128)S(1)} %copy-done.6, bf16[4,144,256]{2,1,0:T(8,128)(2,1)S(1)} %collective-permute-done.3.refs_7_.refs_3_, ...), custom_call_target="tpu_custom_call" | custom-call | tf_op jit(solution)/shard_map/pallas_call | solution.py:506
  72.5 0.0 copy-start.2
  72.5 0.2 shard_map.73
  72.6 0.1 collective-permute-start.14
  72.7 0.7 collective-permute-start.16
  73.4 0.8 collective-permute-done.14.refs_1_
  74.1 5.3 %collective-permute-done.16.refs_3_ = bf16[4,48,512]{2,1,0:T(8,128)(2,1)S(1)} collective-permute-done((bf16[4,48,512]{2,1,0:T(8,128)(2,1)S(1)}, bf16[4,48,512]{2,1,0:T(8,128)(2,1)S(1)}, u32[]{:S(2)}, u32[]{:S(2)}) %collective-permute-start.16) | collective-permute-done | bytes 196640 | tf_op jit(solution)/shard_map/ppermute | solution.py:525
  79.4 3.0 %shard_map.74 = bf16[512,768]{1,0:T(8,128)(2,1)} custom-call(s32[1]{0:T(128)} %bitcast.place.refs_0_, s32[16]{0:T(128)S(1)} %copy-done.5, s32[16]{0:T(128)S(1)} %copy-done.6, bf16[4,48,512]{2,1,0:T(8,128)(2,1)S(1)} %get-tuple-element.66.refs_0_, bf16[4,48,512]{2,1,0:T(8,128)(2,1)S(1)} %collective-permute-done.14.refs_1_, ...), custom_call_target="tpu_custom_call" | custom-call | tf_op jit(solution)/shard_map/pallas_call | solution.py:506
  (27 shorter events, 0.1 us)
Async XLA Ops:
  5.3 9.1 %copy-start.5 = (s32[16]{0:T(128)S(1)}, s32[16]{0:T(128)}, u32[]{:S(2)}) copy-start(s32[16]{0:T(128)} %mid.5) | copy-start | bytes 196
  5.3 9.1 %copy-start.6 = (s32[16]{0:T(128)S(1)}, s32[16]{0:T(128)}, u32[]{:S(2)}) copy-start(s32[16]{0:T(128)} %top.5) | copy-start | bytes 196
  5.3 3.2 %collective-permute-start.2 = (bf16[4,144,512]{2,1,0:T(8,128)(2,1)}, bf16[4,144,512]{2,1,0:T(8,128)(2,1)S(1)}, u32[]{:S(2)}, u32[]{:S(2)}) collective-permute-start(bf16[4,144,512]{2,1,0:T(8,128)(2,1)} %get-tuple-element.40), channel_id=1, source_target_pairs={{0,1},{1,0},{2,3},{3,2},{4,5},{5,4},{6,7},{7,6},{8,9},{9,8},{10,11... | collective-permute-start | bytes 1769480 | tf_op jit(solution)/shard_map/ppermute | solution.py:525
  5.8 16.2 %collective-permute-start = (bf16[4,144,256]{2,1,0:T(8,128)(2,1)}, bf16[4,144,256]{2,1,0:T(8,128)(2,1)S(1)}, u32[]{:S(2)}, u32[]{:S(2)}) collective-permute-start(bf16[4,144,256]{2,1,0:T(8,128)(2,1)} %get-tuple-element.37), channel_id=1, source_target_pairs={{0,2},{1,3},{2,0},{3,1},{4,6},{5,7},{6,4},{7,5},{8,10},{9,11},{10,... | collective-permute-start | bytes 884744 | tf_op jit(solution)/shard_map/ppermute | solution.py:525
  8.4 13.9 %collective-permute-start.1 = (bf16[4,144,256]{2,1,0:T(8,128)(2,1)}, bf16[4,144,256]{2,1,0:T(8,128)(2,1)S(1)}, u32[]{:S(2)}, u32[]{:S(2)}) collective-permute-start(bf16[4,144,256]{2,1,0:T(8,128)(2,1)} %get-tuple-element.38), channel_id=1, source_target_pairs={{0,3},{1,2},{2,1},{3,0},{4,7},{5,6},{6,5},{7,4},{8,11},{9,10},{10,... | collective-permute-start | bytes 884744 | tf_op jit(solution)/shard_map/ppermute | solution.py:525
  8.5 1.1 %copy-start = (bf16[4,144,512]{2,1,0:T(8,128)(2,1)S(1)}, bf16[4,144,512]{2,1,0:T(8,128)(2,1)}, u32[]{:S(2)}) copy-start(bf16[4,144,512]{2,1,0:T(8,128)(2,1)} %get-tuple-element.39.refs_0_.a_ref.refs_3_.refs_5_) | copy-start | bytes 1769476
  9.5 4.9 %copy-start.1 = (bf16[4,144,512]{2,1,0:T(8,128)(2,1)S(1)}, bf16[4,144,512]{2,1,0:T(8,128)(2,1)}, u32[]{:S(2)}) copy-start(bf16[4,144,512]{2,1,0:T(8,128)(2,1)} %get-tuple-element.39.refs_0_.a_ref.refs_3_.refs_5_) | copy-start | bytes 1769476
  9.5 12.7 %copy-start.3 = (bf16[4,144,256]{2,1,0:T(8,128)(2,1)S(1)}, bf16[4,144,256]{2,1,0:T(8,128)(2,1)}, u32[]{:S(2)}) copy-start(bf16[4,144,256]{2,1,0:T(8,128)(2,1)} %get-tuple-element.42.refs_3_) | copy-start | bytes 884740
  9.5 12.7 %copy-start.4 = (bf16[4,144,256]{2,1,0:T(8,128)(2,1)S(1)}, bf16[4,144,256]{2,1,0:T(8,128)(2,1)}, u32[]{:S(2)}) copy-start(bf16[4,144,256]{2,1,0:T(8,128)(2,1)} %get-tuple-element.43.refs_4_) | copy-start | bytes 884740
  9.6 14.6 %collective-permute-start.5 = (bf16[2,144,256]{2,1,0:T(8,128)(2,1)S(1)}, bf16[2,144,256]{2,1,0:T(8,128)(2,1)S(1)}, u32[]{:S(2)}, u32[]{:S(2)}) collective-permute-start(bf16[2,144,256]{2,1,0:T(8,128)(2,1)S(1)} %get-tuple-element.47), channel_id=1, source_target_pairs={{0,4},{1,5},{2,6},{3,7},{4,0},{5,1},{6,2},{7,3},{8,12},{9,13},{10,... | collective-permute-start | bytes 442376 | tf_op jit(solution)/shard_map/ppermute | solution.py:525
  11.8 16.2 %collective-permute-start.6 = (bf16[2,144,256]{2,1,0:T(8,128)(2,1)S(1)}, bf16[2,144,256]{2,1,0:T(8,128)(2,1)S(1)}, u32[]{:S(2)}, u32[]{:S(2)}) collective-permute-start(bf16[2,144,256]{2,1,0:T(8,128)(2,1)S(1)} %get-tuple-element.48), channel_id=1, source_target_pairs={{0,8},{1,9},{2,10},{3,11},{4,12},{5,13},{6,14},{7,15},{8,0},{9,1},... | collective-permute-start | bytes 442376 | tf_op jit(solution)/shard_map/ppermute | solution.py:525
  14.4 13.6 %collective-permute-start.7 = (bf16[2,144,256]{2,1,0:T(8,128)(2,1)S(1)}, bf16[2,144,256]{2,1,0:T(8,128)(2,1)S(1)}, u32[]{:S(2)}, u32[]{:S(2)}) collective-permute-start(bf16[2,144,256]{2,1,0:T(8,128)(2,1)S(1)} %get-tuple-element.49), channel_id=1, source_target_pairs={{0,12},{1,13},{2,14},{3,15},{4,8},{5,9},{6,10},{7,11},{8,4},{9,5},... | collective-permute-start | bytes 442376 | tf_op jit(solution)/shard_map/ppermute | solution.py:525
  22.3 33.2 %collective-permute-start.3 = (bf16[4,144,256]{2,1,0:T(8,128)(2,1)S(1)}, bf16[4,144,256]{2,1,0:T(8,128)(2,1)S(1)}, u32[]{:S(2)}, u32[]{:S(2)}) collective-permute-start(bf16[4,144,256]{2,1,0:T(8,128)(2,1)S(1)} %get-tuple-element.44), channel_id=1, source_target_pairs={{0,2},{1,3},{2,0},{3,1},{4,6},{5,7},{6,4},{7,5},{8,10},{9,11},{10,... | collective-permute-start | bytes 884744 | tf_op jit(solution)/shard_map/ppermute | solution.py:525
  23.9 31.6 %collective-permute-start.4 = (bf16[4,144,256]{2,1,0:T(8,128)(2,1)S(1)}, bf16[4,144,256]{2,1,0:T(8,128)(2,1)S(1)}, u32[]{:S(2)}, u32[]{:S(2)}) collective-permute-start(bf16[4,144,256]{2,1,0:T(8,128)(2,1)S(1)} %get-tuple-element.45), channel_id=1, source_target_pairs={{0,3},{1,2},{2,1},{3,0},{4,7},{5,6},{6,5},{7,4},{8,11},{9,10},{10,... | collective-permute-start | bytes 884744 | tf_op jit(solution)/shard_map/ppermute | solution.py:525
  24.2 14.6 %collective-permute-start.10 = (bf16[2,144,256]{2,1,0:T(8,128)(2,1)S(1)}, bf16[2,144,256]{2,1,0:T(8,128)(2,1)S(1)}, u32[]{:S(2)}, u32[]{:S(2)}) collective-permute-start(bf16[2,144,256]{2,1,0:T(8,128)(2,1)S(1)} %get-tuple-element.56), channel_id=1, source_target_pairs={{0,12},{1,13},{2,14},{3,15},{4,8},{5,9},{6,10},{7,11},{8,4},{9,5},... | collective-permute-start | bytes 442376 | tf_op jit(solution)/shard_map/ppermute | solution.py:525
  28.0 10.9 %collective-permute-start.8 = (bf16[2,144,256]{2,1,0:T(8,128)(2,1)S(1)}, bf16[2,144,256]{2,1,0:T(8,128)(2,1)S(1)}, u32[]{:S(2)}, u32[]{:S(2)}) collective-permute-start(bf16[2,144,256]{2,1,0:T(8,128)(2,1)S(1)} %get-tuple-element.54), channel_id=1, source_target_pairs={{0,4},{1,5},{2,6},{3,7},{4,0},{5,1},{6,2},{7,3},{8,12},{9,13},{10,... | collective-permute-start | bytes 442376 | tf_op jit(solution)/shard_map/ppermute | solution.py:525
  28.0 12.9 %collective-permute-start.9 = (bf16[2,144,256]{2,1,0:T(8,128)(2,1)S(1)}, bf16[2,144,256]{2,1,0:T(8,128)(2,1)S(1)}, u32[]{:S(2)}, u32[]{:S(2)}) collective-permute-start(bf16[2,144,256]{2,1,0:T(8,128)(2,1)S(1)} %get-tuple-element.55), channel_id=1, source_target_pairs={{0,8},{1,9},{2,10},{3,11},{4,12},{5,13},{6,14},{7,15},{8,0},{9,1},... | collective-permute-start | bytes 442376 | tf_op jit(solution)/shard_map/ppermute | solution.py:525
  51.0 14.4 %collective-permute-start.11 = (bf16[48,1152]{1,0:T(8,128)(2,1)S(1)}, bf16[48,1152]{1,0:T(8,128)(2,1)S(1)}, u32[]{:S(2)}, u32[]{:S(2)}) collective-permute-start(bf16[48,1152]{1,0:T(8,128)(2,1)S(1)} %get-tuple-element.60), channel_id=1, source_target_pairs={{0,4},{1,5},{2,6},{3,7},{4,0},{5,1},{6,2},{7,3},{8,12},{9,13},{10,... | collective-permute-start | bytes 331784 | tf_op jit(solution)/shard_map/ppermute | solution.py:525
  51.1 14.3 %collective-permute-start.12 = (bf16[48,1152]{1,0:T(8,128)(2,1)S(1)}, bf16[48,1152]{1,0:T(8,128)(2,1)S(1)}, u32[]{:S(2)}, u32[]{:S(2)}) collective-permute-start(bf16[48,1152]{1,0:T(8,128)(2,1)S(1)} %get-tuple-element.61), channel_id=1, source_target_pairs={{0,8},{1,9},{2,10},{3,11},{4,12},{5,13},{6,14},{7,15},{8,0},{9,1},... | collective-permute-start | bytes 331784 | tf_op jit(solution)/shard_map/ppermute | solution.py:525
  54.1 11.3 %collective-permute-start.13 = (bf16[48,1152]{1,0:T(8,128)(2,1)S(1)}, bf16[48,1152]{1,0:T(8,128)(2,1)S(1)}, u32[]{:S(2)}, u32[]{:S(2)}) collective-permute-start(bf16[48,1152]{1,0:T(8,128)(2,1)S(1)} %get-tuple-element.62), channel_id=1, source_target_pairs={{0,12},{1,13},{2,14},{3,15},{4,8},{5,9},{6,10},{7,11},{8,4},{9,5},... | collective-permute-start | bytes 331784 | tf_op jit(solution)/shard_map/ppermute | solution.py:525
  65.6 8.5 %collective-permute-start.15 = (bf16[4,48,512]{2,1,0:T(8,128)(2,1)S(1)}, bf16[4,48,512]{2,1,0:T(8,128)(2,1)S(1)}, u32[]{:S(2)}, u32[]{:S(2)}) collective-permute-start(bf16[4,48,512]{2,1,0:T(8,128)(2,1)S(1)} %get-tuple-element.63.refs_9_), channel_id=1, source_target_pairs={{0,2},{1,3},{2,0},{3,1},{4,6},{5,7},{6,4},{7,5},{8,10},{9,11},{10,... | collective-permute-start | bytes 589832 | tf_op jit(solution)/shard_map/ppermute | solution.py:525
  72.5 6.9 %copy-start.2 = (bf16[768,768]{1,0:T(8,128)(2,1)S(1)}, bf16[768,768]{1,0:T(8,128)(2,1)}, u32[]{:S(2)}) copy-start(bf16[768,768]{1,0:T(8,128)(2,1)} %refs_4_.1) | copy-start | bytes 3538948
  72.6 1.5 %collective-permute-start.14 = (bf16[4,48,512]{2,1,0:T(8,128)(2,1)S(1)}, bf16[4,48,512]{2,1,0:T(8,128)(2,1)S(1)}, u32[]{:S(2)}, u32[]{:S(2)}) collective-permute-start(bf16[4,48,512]{2,1,0:T(8,128)(2,1)S(1)} %get-tuple-element.67), channel_id=1, source_target_pairs={{0,1},{1,0},{2,3},{3,2},{4,5},{5,4},{6,7},{7,6},{8,9},{9,8},{10,11... | collective-permute-start | bytes 589832 | tf_op jit(solution)/shard_map/ppermute | solution.py:525
  72.7 6.7 %collective-permute-start.16 = (bf16[4,48,512]{2,1,0:T(8,128)(2,1)S(1)}, bf16[4,48,512]{2,1,0:T(8,128)(2,1)S(1)}, u32[]{:S(2)}, u32[]{:S(2)}) collective-permute-start(bf16[4,48,512]{2,1,0:T(8,128)(2,1)S(1)} %get-tuple-element.68), channel_id=1, source_target_pairs={{0,3},{1,2},{2,1},{3,0},{4,7},{5,6},{6,5},{7,4},{8,11},{9,10},{10,... | collective-permute-start | bytes 589832 | tf_op jit(solution)/shard_map/ppermute | solution.py:525
where the time goes:
time: 82.6 us; the launch traced here: 82.4 us
  Pallas kernels  51 us (62%)
  starting transfers between devices  21.8 us (26%)
  waiting for transfers between devices  8.32 us (10%)
  local copies, waits for them, and re-layouts  1.09 us (1%)
    pallas_call x11, Pallas kernels, call(): pl.pallas_call(body if extra else kernel, grid_spec=pltpu.PrefetchScalarG...  51 us
    ppermute x17, starting transfers between devices, within(): return lax.ppermute(array, 'seq', [(i, i ^ apart) for i in range(count)])  21.8 us
    ppermute x17, waiting for transfers between devices, within(): return lax.ppermute(array, 'seq', [(i, i ^ apart) for i in range(count)])  8.32 us
  transfers between devices with their start and end apart: 17, of which 4 were waited for; matrix products, arithmetic and copies ran while one was open for 0% of the time, Pallas kernels for 52%

commit v1 on v0

--- a/solution.py
+++ b/solution.py
@@ -10,7 +10,7 @@
 SEG = 2048
 LOG2E = 1.4426950408889634
 VMEM_LIMIT = 40 * 1024 * 1024
-VMEM_MOST = 60 * 1024 * 1024
+VMEM_MOST = 51 * 1024 * 1024
 BF16 = jnp.bfloat16
 F32 = jnp.float32
 
@@ -152,6 +152,8 @@
 HALF = 2 * BLK
 TOK = 512
 SAFE = 96.0
+FAR_ORDER = (2, 1, 3)
+PART_ORDER = (0, 1, 2, 3)
 DX = 64
 
 
@@ -173,7 +175,12 @@
 
 
 def head_of(place, j, p):
-    return ((place[0] & (GROUP - 1)) ^ j) * HG + ((place[0] // GROUP) ^ p)
+    index = place[2 * GROUP * HG]
+    return ((index & (GROUP - 1)) ^ j) * HG + ((index // GROUP) ^ p)
+
+
+def offsets_of(place, head):
+    return place[head], place[GROUP * HG + head]
 
 
 def token_picker():
@@ -196,9 +203,10 @@
     return pl.ds(pl.multiple_of(head * DH, 16), DH)
 
 
-def pack_kernel(place, mid, top, k_hbm, v_hbm, q_hbm, *refs):
+def pack_kernel(place, k_hbm, v_hbm, q_hbm, *refs):
     outs, refs = refs[:6], refs[6:]
-    blocks, held, packed, sems_in, sems_out = refs[:3], refs[3:6], refs[6:12], refs[12], refs[13]
+    blocks, held, packed = refs[:3], refs[3:6], refs[6:12]
+    sems_in, sems_out = refs[12:]
     loads = [
         pltpu.make_async_copy(hbm, block, sems_in.at[i])
         for i, (hbm, block) in enumerate(zip((k_hbm, v_hbm, q_hbm), blocks))
@@ -216,7 +224,7 @@
         ):
             for p in range(HG):
                 head = head_of(place, j, p)
-                slots = class_of_slots(mid[head], top[head])
+                slots = class_of_slots(*offsets_of(place, head))
                 for s in range(count):
                     packed[i][p, rows, s * BLK : (s + 1) * BLK] = scratch[
                         head_rows(head), lane_block(slots[first + s])
@@ -271,7 +279,7 @@
     return best
 
 
-def near_kernel(inputs, units, tasks, carried, place, mid, top, *refs):
+def near_kernel(inputs, units, tasks, carried, place, *refs):
     pieces = dict(zip(inputs, refs[: len(inputs)]))
     refs = refs[len(inputs) :]
     old = [refs[2 * i : 2 * i + 2] for i in range(carried)]
@@ -299,8 +307,8 @@
             v_s[h, 0:DH, rows] = ref[h, DH : 2 * DH, lane : lane + BLK]
 
     def counted_again(h):
-        head = head_of(place, 0, pl.program_id(0) * STEP + h)
-        same = mid[head] == top[head]
+        off_mid, off_top = offsets_of(place, head_of(place, 0, pl.program_id(0) * STEP + h))
+        same = off_mid == off_top
         return [
             jnp.where(lane_slot == 0, jnp.where(same, 1.584962500721156, 1.0), 0.0),
             jnp.where(lane_slot == 1, jnp.where(same, 0.0, 1.0), 0.0),
@@ -365,16 +373,16 @@
             run(False, [h])
 
 
-def far_kernel(place, mid, top, *refs):
+def far_kernel(place, *refs):
     own, beyond = refs[:GROUP], refs[GROUP : GROUP + 6]
     outs = refs[GROUP + 6 : GROUP + 6 + RATE]
     k_s, v_s, q_s, result_s, tail_s = refs[GROUP + 6 + RATE :]
-    head = head_of(place, 0, 0)
-    same = mid[head] == top[head]
+    off_mid, off_top = offsets_of(place, head_of(place, 0, 0))
+    same = off_mid == off_top
     slots = (0, jnp.where(same, 0, 1))
 
     def source(s, j):
-        return own[j].at[0] if s == 0 else beyond[2 * (s - 1) + j // 2].at[j % 2]
+        return own[j].at[0] if s == 0 else beyond[2 * FAR_ORDER.index(s) + j // 2].at[j % 2]
 
     for s in range(RATE):
         for j in range(GROUP):
@@ -454,7 +462,7 @@
 
 
 def combine_kernel(chip, acc_ref, max_ref, *refs):
-    far, outs = refs[:HG], refs[HG:]
+    far, outs = refs[:HG][::-1], refs[HG:]
     for i in range(2):
         for p in range(HG):
             outs[i][p, :, 0:HALF] = join(
@@ -464,15 +472,15 @@
             outs[i][p, :, HALF:] = (acc[0:DH] / acc[DH : DH + 1]).astype(BF16)
 
 
-def project_kernel(place, mid, top, *refs):
+def project_kernel(place, *refs):
     parts = refs[:GROUP]
     w_ref, out_ref, held = refs[GROUP:]
-    for j in range(GROUP):
+    for n, j in enumerate(PART_ORDER):
         for p in range(HG):
             head = head_of(place, j, p)
-            slots = class_of_slots(mid[head], top[head])
+            slots = class_of_slots(*offsets_of(place, head))
             for s in range(RATE):
-                held[head_rows(head), lane_block(slots[s])] = parts[j][
+                held[head_rows(head), lane_block(slots[s])] = parts[n][
                     p, :, s * BLK : (s + 1) * BLK
                 ]
     row = lax.broadcasted_iota(jnp.int32, (TOK, TOK), 0)
@@ -525,21 +533,22 @@
     return lax.ppermute(array, "seq", [(i, i ^ apart) for i in range(count)])
 
 
-def across(array, segments):
-    return within(array, GROUP * segments)
+def swap_segments(arrays):
+    moved = {s: within(arrays[s - 1], GROUP * s) for s in (3, 2, 1)}
+    return [moved[s] for s in (1, 2, 3)]
 
 
 def shards_four(queries, key_states, value_states, offsets_mid, offsets_top, out_weight):
     width = queries.shape[1]
-    place = lax.axis_index("seq").astype(jnp.int32).reshape(1)
-    scalars = (place, offsets_mid, offsets_top)
+    index = lax.axis_index("seq").astype(jnp.int32).reshape(1)
+    place = jnp.concatenate([offsets_mid, offsets_top, index])
     full = jax.ShapeDtypeStruct((HG, 3 * DH, TOK), BF16)
     piece = jax.ShapeDtypeStruct((HG, 3 * DH, HALF), BF16)
     pair = jax.ShapeDtypeStruct((2, 3 * DH, HALF), BF16)
     anywhere = pl.BlockSpec(memory_space=pl.ANY)
     shapes = [full] * 2 + [piece] * 4
     own0, own1, sel2, sel3, rest2, rest3 = call(
-        pack_kernel, scalars, (key_states, value_states, queries), (1,),
+        pack_kernel, (place,), (key_states, value_states, queries), (1,),
         [anywhere] * 3,
         [(anywhere, shape) for shape in shapes],
         [pltpu.VMEM((TOK, width), BF16)] * 3
@@ -568,7 +577,7 @@
         sizes = [len(members) * BLK for _, members in units]
         scores = sum(sum(sizes[low:]) * HALF for group in tasks for _, low, _ in group)
         return call(
-            functools.partial(near_kernel, list(held), units, tasks, len(old)), scalars,
+            functools.partial(near_kernel, list(held), units, tasks, len(old)), (place,),
             (*held.values(), *[x for one in old for x in one]), (HG // STEP,),
             [per_head((STEP,) + x.shape[1:]) for x in held.values()]
             + [per_head((STEP,) + x.shape[1:]) for one in old for x in one],
@@ -590,13 +599,13 @@
     own = [(0, 0), (0, 1), (1, 0), (1, 1)]
 
     ours = regroup(own0, own1)
-    ours = [across(x, s + 1) for s, x in enumerate(ours)]
+    ours = swap_segments(ours)
     held = {(0, 0): own0, (1, 0): own1}
     state_own = near(held, own_sel + own_rest, [[(q, 0, None) for q in own]], [])
     *theirs, rest2, rest3 = regroup(sel2, sel3, after=state_own[1:], through=(rest2, rest3))
-    theirs = [across(x, s + 1) for s, x in enumerate(theirs)]
+    theirs = swap_segments(theirs)
     rest2, rest3 = within(rest2, 2), within(rest3, 3)
-    beyond = [x for both in zip(ours, theirs) for x in both]
+    beyond = [x for s in FAR_ORDER for x in (ours[s - 1], theirs[s - 1])]
 
     held.update({(2, 0): sel2, (3, 0): sel3})
     out = near(
@@ -606,14 +615,14 @@
             [((2, 0), 0, None), ((3, 0), 0, None)],
         ],
         [state_own],
-        after=ours,
+        after=ours[::-1],
     )
     state_own, state_sel = out[:2], out[2:]
 
     result = jax.ShapeDtypeStruct((DH, GROUP * HALF + BLK), BF16)
     piece_0 = pl.BlockSpec((1, 3 * DH, HALF), lambda *_: (0, 0, 0))
     results = call(
-        far_kernel, scalars, (own0, own1, sel2, sel3, *beyond), (1,),
+        far_kernel, (place,), (own0, own1, sel2, sel3, *beyond), (1,),
         [piece_0] * GROUP + [whole(pair.shape)] * 6,
         [(whole(result.shape), result)] * RATE,
         [
@@ -625,7 +634,7 @@
         ],
         RATE * 2 * 3 * TOK * TOK, after=(out[1],),
     )
-    back = [results[0]] + [across(results[s], s) for s in range(1, RATE)]
+    back = [results[0]] + swap_segments(results[1:])
 
     held.update({(2, 2): rest2, (3, 2): rest3})
     units = own_sel + own_rest + other_sel + other_rest
@@ -633,7 +642,7 @@
 
     def combine(chip, state):
         return call(
-            functools.partial(combine_kernel, chip), (), (*state, *back), (1,),
+            functools.partial(combine_kernel, chip), (), (*state, *back[::-1]), (1,),
             [whole(x.shape) for x in state] + [whole(result.shape)] * HG,
             [(whole(attended.shape), attended)] * 2,
             [],
@@ -660,9 +669,9 @@
         after=(part2,),
     )
     part0, part1 = combine(0, state_own)
-    parts = [part0, within(part1, 1), within(part2, 2), within(part3, 3)]
+    parts = {0: part0, 1: within(part1, 1), 2: within(part2, 2), 3: within(part3, 3)}
     return call(
-        project_kernel, scalars, (*parts, out_weight), (1,),
+        project_kernel, (place,), (*[parts[j] for j in PART_ORDER], out_weight), (1,),
         [whole(attended.shape)] * GROUP + [whole((width, width))],
         [(whole((TOK, width)), jax.ShapeDtypeStruct((TOK, width), BF16))],
         [pltpu.VMEM((width, TOK), BF16)],

time: 82.6 us -> 83.5 us (1.011)
  waiting for transfers between devices: 8.32 us -> 10.1 us
  local copies, waits for them, and re-layouts: 1.09 us -> 0.01 us
  starting transfers between devices: 21.8 us -> 20.9 us
    ppermute x17, waiting for transfers between devices: 8.32 us -> 10.1 us  [within(): return lax.ppermute(array, 'seq', [(i, i ^ apart) for i in range(count)])]
    unnamed x14 -> x2, local copies, waits for them, and re-layouts: 1.09 us -> 0.01 us
    ppermute x17, starting transfers between devices: 21.8 us -> 20.9 us  [within(): return lax.ppermute(array, 'seq', [(i, i ^ apart) for i in range(count)])]
  transfers between devices with their start and end apart: 17 -> 17, of which waited for: 4 -> 4; matrix products, arithmetic and copies ran while one was open for 0% -> 0% of each run, Pallas kernels for 52% -> 51%
where the time goes in v1:
time: 83.5 us; the launch traced here: 83.4 us
  Pallas kernels  51.5 us (62%)
  starting transfers between devices  20.9 us (25%)
  waiting for transfers between devices  10.1 us (12%)
    pallas_call x11, Pallas kernels, call(): pl.pallas_call(body if extra else kernel, grid_spec=pltpu.PrefetchScalarG...  51.5 us
    ppermute x17, starting transfers between devices, within(): return lax.ppermute(array, 'seq', [(i, i ^ apart) for i in range(count)])  20.9 us
    ppermute x17, waiting for transfers between devices, within(): return lax.ppermute(array, 'seq', [(i, i ^ apart) for i in range(count)])  10.1 us
  transfers between devices with their start and end apart: 17, of which 4 were waited for; matrix products, arithmetic and copies ran while one was open for 0% of the time, Pallas kernels for 51%

profile of v1, /device:TPU:0, one launch (start us, length us, event | category | flops | bytes accessed | tf_op | source)
XLA Modules:
  0.0 83.4 jit_solution(14730846885104511659)
XLA Ops:
  0.0 0.7 pad_add_fusion.place.refs_0_
  0.7 5.7 %shard_map.64 = (bf16[4,144,512]{2,1,0:T(8,128)(2,1)S(1)}, bf16[4,144,512]{2,1,0:T(8,128)(2,1)S(1)}, bf16[4,144,256]{2,1,0:T(8,128)(2,1)S(1)}, bf16[4,144,256]{2...) custom-call(s32[33]{0:T(128)S(1)} %pad_add_fusion.place.refs_0_, ...), custom_call_target="tpu_custom_call" | custom-call | tf_op jit(solution)/shard_map/pallas_call | solution.py:514
  6.5 0.5 collective-permute-start.2
  7.0 2.6 %collective-permute-start = (bf16[4,144,256]{2,1,0:T(8,128)(2,1)S(1)}, bf16[4,144,256]{2,1,0:T(8,128)(2,1)S(1)}, u32[]{:S(2)}, u32[]{:S(2)}) collective-permute-start(bf16[4,144,256]{2,1,0:T(8,128)(2,1)S(1)} %get-tuple-element.37), channel_id=1, source_target_pairs={{0,2},{1,3},{2,0},{3,1},{4,6},{5,7},{6,4},{7,5},{8,10},{9,11},{10,... | collective-permute-start | bytes 884744 | tf_op jit(solution)/shard_map/ppermute | solution.py:533
  9.5 0.1 collective-permute-start.1
  9.6 0.0 collective-permute-done.2.refs_1_.b_ref.refs_2_.refs_4_
  9.7 4.0 %collective-permute-start.5 = (bf16[2,144,256]{2,1,0:T(8,128)(2,1)S(1)}, bf16[2,144,256]{2,1,0:T(8,128)(2,1)S(1)}, u32[]{:S(2)}, u32[]{:S(2)}) collective-permute-start(bf16[2,144,256]{2,1,0:T(8,128)(2,1)S(1)} %get-tuple-element.47), channel_id=1, source_target_pairs={{0,12},{1,13},{2,14},{3,15},{4,8},{5,9},{6,10},{7,11},{8,4},{9,5},... | collective-permute-start | bytes 442376 | tf_op jit(solution)/shard_map/ppermute | solution.py:533
  13.7 0.0 collective-permute-start.6
  13.7 0.6 collective-permute-start.7
  14.3 7.6 %shard_map.65 = (f32[4,4,64,256]{3,2,1,0:T(8,128)S(1)}, f32[4,4,8,256]{3,2,1,0:T(8,128)S(1)}) custom-call(s32[33]{0:T(128)S(1)} %pad_add_fusion.place.refs_0_, bf16[4,144,512]{2,1,0:T(8,128)(2,1)S(1)} %get-tuple-element.39.refs_0_.a_ref.refs_1_.refs_3_, bf16[4,144,512]{2,1,0:T(8,128)(2,1)S(1)} %collective-permute-done.2.refs_1_.b_ref.refs_2_.refs_4_), custom_call_target="tpu_custom_call" | custom-call | tf_op jit(solution)/shard_map/pallas_call | solution.py:514
  22.0 1.2 %collective-permute-done.1.refs_1_.refs_4_ = bf16[4,144,256]{2,1,0:T(8,128)(2,1)S(1)} collective-permute-done((bf16[4,144,256]{2,1,0:T(8,128)(2,1)S(1)}, bf16[4,144,256]{2,1,0:T(8,128)(2,1)S(1)}, u32[]{:S(2)}, u32[]{:S(2)}) %collective-permute-start.1) | collective-permute-done | bytes 294944 | tf_op jit(solution)/shard_map/ppermute | solution.py:533
  23.2 1.6 %collective-permute-start.3 = (bf16[4,144,256]{2,1,0:T(8,128)(2,1)S(1)}, bf16[4,144,256]{2,1,0:T(8,128)(2,1)S(1)}, u32[]{:S(2)}, u32[]{:S(2)}) collective-permute-start(bf16[4,144,256]{2,1,0:T(8,128)(2,1)S(1)} %get-tuple-element.44), channel_id=1, source_target_pairs={{0,2},{1,3},{2,0},{3,1},{4,6},{5,7},{6,4},{7,5},{8,10},{9,11},{10,... | collective-permute-start | bytes 884744 | tf_op jit(solution)/shard_map/ppermute | solution.py:533
  24.9 0.0 collective-permute-done.5.refs_7_.refs_9_
  24.9 4.0 %collective-permute-start.10 = (bf16[2,144,256]{2,1,0:T(8,128)(2,1)S(1)}, bf16[2,144,256]{2,1,0:T(8,128)(2,1)S(1)}, u32[]{:S(2)}, u32[]{:S(2)}) collective-permute-start(bf16[2,144,256]{2,1,0:T(8,128)(2,1)S(1)} %get-tuple-element.56), channel_id=1, source_target_pairs={{0,12},{1,13},{2,14},{3,15},{4,8},{5,9},{6,10},{7,11},{8,4},{9,5},... | collective-permute-start | bytes 442376 | tf_op jit(solution)/shard_map/ppermute | solution.py:533
  28.9 0.7 collective-permute-start.9
  29.6 9.4 %shard_map.68 = (f32[4,4,64,256]{3,2,1,0:T(8,128)S(1)}, f32[4,4,8,256]{3,2,1,0:T(8,128)S(1)}, f32[4,2,64,256]{3,2,1,0:T(8,128)S(1)}, f32[4,2,8,256]{3,2,1,0:T(8,128)S(1)}) custom-call(s32[33]{0:T(128)S(1)} %pad_add_fusion.place.refs_0_, bf16[4,144,512]{2,1,0:T(8,128)(2,1)S(1)} %get-tuple-element.39.refs_0_.a_ref.refs_1_.refs_3_, ...), custom_call_target="tpu_custom_call" | custom-call | tf_op jit(solution)/shard_map/pallas_call | solution.py:514
  39.0 2.8 %collective-permute-done.8.refs_6_ = bf16[2,144,256]{2,1,0:T(8,128)(2,1)S(1)} collective-permute-done((bf16[2,144,256]{2,1,0:T(8,128)(2,1)S(1)}, bf16[2,144,256]{2,1,0:T(8,128)(2,1)S(1)}, u32[]{:S(2)}, u32[]{:S(2)}) %collective-permute-start.8) | collective-permute-done | bytes 147488 | tf_op jit(solution)/shard_map/ppermute | solution.py:533
  41.8 10.2 %shard_map.69 = (bf16[48,1152]{1,0:T(8,128)(2,1)S(1)}, bf16[48,1152]{1,0:T(8,128)(2,1)S(1)}, bf16[48,1152]{1,0:T(8,128)(2,1)S(1)}, bf16[48,1152]{1,0:T(8,128)(2,1)S(1)}) custom-call(s32[33]{0:T(128)S(1)} %pad_add_fusion.place.refs_0_, bf16[4,144,512]{2,1,0:T(8,128)(2,1)S(1)} %get-tuple-element.39.refs_0_.a_ref.refs_1_.refs_3_, ...), custom_call_target="tpu_custom_call" | custom-call | tf_op jit(solution)/shard_map/pallas_call | solution.py:514
  52.0 2.5 %collective-permute-start.11 = (bf16[48,1152]{1,0:T(8,128)(2,1)S(1)}, bf16[48,1152]{1,0:T(8,128)(2,1)S(1)}, u32[]{:S(2)}, u32[]{:S(2)}) collective-permute-start(bf16[48,1152]{1,0:T(8,128)(2,1)S(1)} %get-tuple-element.60), channel_id=1, source_target_pairs={{0,12},{1,13},{2,14},{3,15},{4,8},{5,9},{6,10},{7,11},{8,4},{9,5},... | collective-permute-start | bytes 331784 | tf_op jit(solution)/shard_map/ppermute | solution.py:533
  54.5 0.0 collective-permute-start.12
  54.5 1.9 %collective-permute-start.13 = (bf16[48,1152]{1,0:T(8,128)(2,1)S(1)}, bf16[48,1152]{1,0:T(8,128)(2,1)S(1)}, u32[]{:S(2)}, u32[]{:S(2)}) collective-permute-start(bf16[48,1152]{1,0:T(8,128)(2,1)S(1)} %get-tuple-element.62), channel_id=1, source_target_pairs={{0,4},{1,5},{2,6},{3,7},{4,0},{5,1},{6,2},{7,3},{8,12},{9,13},{10,... | collective-permute-start | bytes 331784 | tf_op jit(solution)/shard_map/ppermute | solution.py:533
  56.4 9.9 %shard_map.70 = (f32[4,4,64,256]{3,2,1,0:T(8,128)S(1)}, f32[4,4,8,256]{3,2,1,0:T(8,128)S(1)}) custom-call(s32[33]{0:T(128)S(1)} %pad_add_fusion.place.refs_0_, bf16[4,144,512]{2,1,0:T(8,128)(2,1)S(1)} %get-tuple-element.39.refs_0_.a_ref.refs_1_.refs_3_, bf16[4,144,512]{2,1,0:T(8,128)(2,1)S(1)} %collective-permute-done.2.refs_1_.b_ref.refs_2_.refs_4_, ...), custom_call_target="tpu_custom_call" | custom-call | tf_op jit(solution)/shard_map/pallas_call | solution.py:514
  66.4 0.1 shard_map.71
  66.5 1.6 %collective-permute-start.15 = (bf16[4,48,512]{2,1,0:T(8,128)(2,1)S(1)}, bf16[4,48,512]{2,1,0:T(8,128)(2,1)S(1)}, u32[]{:S(2)}, u32[]{:S(2)}) collective-permute-start(bf16[4,48,512]{2,1,0:T(8,128)(2,1)S(1)} %get-tuple-element.63.refs_7_), channel_id=1, source_target_pairs={{0,2},{1,3},{2,0},{3,1},{4,6},{5,7},{6,4},{7,5},{8,10},{9,11},{10,... | collective-permute-start | bytes 589832 | tf_op jit(solution)/shard_map/ppermute | solution.py:533
  68.1 5.3 %shard_map.72 = (f32[4,4,64,256]{3,2,1,0:T(8,128)S(1)}, f32[4,4,8,256]{3,2,1,0:T(8,128)S(1)}) custom-call(s32[33]{0:T(128)S(1)} %pad_add_fusion.place.refs_0_, bf16[4,144,256]{2,1,0:T(8,128)(2,1)S(1)} %collective-permute-done.3.refs_5_.refs_1_, bf16[4,144,256]{2,1,0:T(8,128)(2,1)S(1)} %collective-permute-done.4.refs_6_.refs_2_, ...), custom_call_target="tpu_custom_call" | custom-call | tf_op jit(solution)/shard_map/pallas_call | solution.py:514
  73.4 0.0 copy-start
  73.4 0.1 shard_map.73
  73.6 0.1 collective-permute-start.14
  73.7 0.6 collective-permute-start.16
  74.3 0.8 collective-permute-done.14.refs_1_
  75.1 5.3 %collective-permute-done.16.refs_3_ = bf16[4,48,512]{2,1,0:T(8,128)(2,1)S(1)} collective-permute-done((bf16[4,48,512]{2,1,0:T(8,128)(2,1)S(1)}, bf16[4,48,512]{2,1,0:T(8,128)(2,1)S(1)}, u32[]{:S(2)}, u32[]{:S(2)}) %collective-permute-start.16) | collective-permute-done | bytes 196640 | tf_op jit(solution)/shard_map/ppermute | solution.py:533
  80.4 3.0 %shard_map.74 = bf16[512,768]{1,0:T(8,128)(2,1)} custom-call(s32[33]{0:T(128)S(1)} %pad_add_fusion.place.refs_0_, bf16[4,48,512]{2,1,0:T(8,128)(2,1)S(1)} %get-tuple-element.66.refs_0_, bf16[4,48,512]{2,1,0:T(8,128)(2,1)S(1)} %collective-permute-done.14.refs_1_, bf16[4,48,512]{2,1,0:T(8,128)(2,1)S(1)} %collective-permute-done.15.refs_2_, ...), custom_call_target="tpu_custom_call" | custom-call | tf_op jit(solution)/shard_map/pallas_call | solution.py:514
  (16 shorter events, 0.1 us)
Async XLA Ops:
  6.5 3.1 %collective-permute-start.2 = (bf16[4,144,512]{2,1,0:T(8,128)(2,1)S(1)}, bf16[4,144,512]{2,1,0:T(8,128)(2,1)S(1)}, u32[]{:S(2)}, u32[]{:S(2)}) collective-permute-start(bf16[4,144,512]{2,1,0:T(8,128)(2,1)S(1)} %get-tuple-element.40), channel_id=1, source_target_pairs={{0,1},{1,0},{2,3},{3,2},{4,5},{5,4},{6,7},{7,6},{8,9},{9,8},{10,11... | collective-permute-start | bytes 1769480 | tf_op jit(solution)/shard_map/ppermute | solution.py:533
  7.0 15.0 %collective-permute-start = (bf16[4,144,256]{2,1,0:T(8,128)(2,1)S(1)}, bf16[4,144,256]{2,1,0:T(8,128)(2,1)S(1)}, u32[]{:S(2)}, u32[]{:S(2)}) collective-permute-start(bf16[4,144,256]{2,1,0:T(8,128)(2,1)S(1)} %get-tuple-element.37), channel_id=1, source_target_pairs={{0,2},{1,3},{2,0},{3,1},{4,6},{5,7},{6,4},{7,5},{8,10},{9,11},{10,... | collective-permute-start | bytes 884744 | tf_op jit(solution)/shard_map/ppermute | solution.py:533
  9.5 13.7 %collective-permute-start.1 = (bf16[4,144,256]{2,1,0:T(8,128)(2,1)S(1)}, bf16[4,144,256]{2,1,0:T(8,128)(2,1)S(1)}, u32[]{:S(2)}, u32[]{:S(2)}) collective-permute-start(bf16[4,144,256]{2,1,0:T(8,128)(2,1)S(1)} %get-tuple-element.38), channel_id=1, source_target_pairs={{0,3},{1,2},{2,1},{3,0},{4,7},{5,6},{6,5},{7,4},{8,11},{9,10},{10,... | collective-permute-start | bytes 884744 | tf_op jit(solution)/shard_map/ppermute | solution.py:533
  9.7 15.2 %collective-permute-start.5 = (bf16[2,144,256]{2,1,0:T(8,128)(2,1)S(1)}, bf16[2,144,256]{2,1,0:T(8,128)(2,1)S(1)}, u32[]{:S(2)}, u32[]{:S(2)}) collective-permute-start(bf16[2,144,256]{2,1,0:T(8,128)(2,1)S(1)} %get-tuple-element.47), channel_id=1, source_target_pairs={{0,12},{1,13},{2,14},{3,15},{4,8},{5,9},{6,10},{7,11},{8,4},{9,5},... | collective-permute-start | bytes 442376 | tf_op jit(solution)/shard_map/ppermute | solution.py:533
  13.7 15.2 %collective-permute-start.6 = (bf16[2,144,256]{2,1,0:T(8,128)(2,1)S(1)}, bf16[2,144,256]{2,1,0:T(8,128)(2,1)S(1)}, u32[]{:S(2)}, u32[]{:S(2)}) collective-permute-start(bf16[2,144,256]{2,1,0:T(8,128)(2,1)S(1)} %get-tuple-element.48), channel_id=1, source_target_pairs={{0,8},{1,9},{2,10},{3,11},{4,12},{5,13},{6,14},{7,15},{8,0},{9,1},... | collective-permute-start | bytes 442376 | tf_op jit(solution)/shard_map/ppermute | solution.py:533
  13.7 15.2 %collective-permute-start.7 = (bf16[2,144,256]{2,1,0:T(8,128)(2,1)S(1)}, bf16[2,144,256]{2,1,0:T(8,128)(2,1)S(1)}, u32[]{:S(2)}, u32[]{:S(2)}) collective-permute-start(bf16[2,144,256]{2,1,0:T(8,128)(2,1)S(1)} %get-tuple-element.49), channel_id=1, source_target_pairs={{0,4},{1,5},{2,6},{3,7},{4,0},{5,1},{6,2},{7,3},{8,12},{9,13},{10,... | collective-permute-start | bytes 442376 | tf_op jit(solution)/shard_map/ppermute | solution.py:533
  23.2 33.2 %collective-permute-start.3 = (bf16[4,144,256]{2,1,0:T(8,128)(2,1)S(1)}, bf16[4,144,256]{2,1,0:T(8,128)(2,1)S(1)}, u32[]{:S(2)}, u32[]{:S(2)}) collective-permute-start(bf16[4,144,256]{2,1,0:T(8,128)(2,1)S(1)} %get-tuple-element.44), channel_id=1, source_target_pairs={{0,2},{1,3},{2,0},{3,1},{4,6},{5,7},{6,4},{7,5},{8,10},{9,11},{10,... | collective-permute-start | bytes 884744 | tf_op jit(solution)/shard_map/ppermute | solution.py:533
  24.9 31.6 %collective-permute-start.4 = (bf16[4,144,256]{2,1,0:T(8,128)(2,1)S(1)}, bf16[4,144,256]{2,1,0:T(8,128)(2,1)S(1)}, u32[]{:S(2)}, u32[]{:S(2)}) collective-permute-start(bf16[4,144,256]{2,1,0:T(8,128)(2,1)S(1)} %get-tuple-element.45), channel_id=1, source_target_pairs={{0,3},{1,2},{2,1},{3,0},{4,7},{5,6},{6,5},{7,4},{8,11},{9,10},{10,... | collective-permute-start | bytes 884744 | tf_op jit(solution)/shard_map/ppermute | solution.py:533
  24.9 14.1 %collective-permute-start.10 = (bf16[2,144,256]{2,1,0:T(8,128)(2,1)S(1)}, bf16[2,144,256]{2,1,0:T(8,128)(2,1)S(1)}, u32[]{:S(2)}, u32[]{:S(2)}) collective-permute-start(bf16[2,144,256]{2,1,0:T(8,128)(2,1)S(1)} %get-tuple-element.56), channel_id=1, source_target_pairs={{0,12},{1,13},{2,14},{3,15},{4,8},{5,9},{6,10},{7,11},{8,4},{9,5},... | collective-permute-start | bytes 442376 | tf_op jit(solution)/shard_map/ppermute | solution.py:533
  28.9 12.9 %collective-permute-start.8 = (bf16[2,144,256]{2,1,0:T(8,128)(2,1)S(1)}, bf16[2,144,256]{2,1,0:T(8,128)(2,1)S(1)}, u32[]{:S(2)}, u32[]{:S(2)}) collective-permute-start(bf16[2,144,256]{2,1,0:T(8,128)(2,1)S(1)} %get-tuple-element.54), channel_id=1, source_target_pairs={{0,8},{1,9},{2,10},{3,11},{4,12},{5,13},{6,14},{7,15},{8,0},{9,1},... | collective-permute-start | bytes 442376 | tf_op jit(solution)/shard_map/ppermute | solution.py:533
  28.9 12.9 %collective-permute-start.9 = (bf16[2,144,256]{2,1,0:T(8,128)(2,1)S(1)}, bf16[2,144,256]{2,1,0:T(8,128)(2,1)S(1)}, u32[]{:S(2)}, u32[]{:S(2)}) collective-permute-start(bf16[2,144,256]{2,1,0:T(8,128)(2,1)S(1)} %get-tuple-element.55), channel_id=1, source_target_pairs={{0,4},{1,5},{2,6},{3,7},{4,0},{5,1},{6,2},{7,3},{8,12},{9,13},{10,... | collective-permute-start | bytes 442376 | tf_op jit(solution)/shard_map/ppermute | solution.py:533
  52.0 14.4 %collective-permute-start.11 = (bf16[48,1152]{1,0:T(8,128)(2,1)S(1)}, bf16[48,1152]{1,0:T(8,128)(2,1)S(1)}, u32[]{:S(2)}, u32[]{:S(2)}) collective-permute-start(bf16[48,1152]{1,0:T(8,128)(2,1)S(1)} %get-tuple-element.60), channel_id=1, source_target_pairs={{0,12},{1,13},{2,14},{3,15},{4,8},{5,9},{6,10},{7,11},{8,4},{9,5},... | collective-permute-start | bytes 331784 | tf_op jit(solution)/shard_map/ppermute | solution.py:533
  54.5 11.9 %collective-permute-start.12 = (bf16[48,1152]{1,0:T(8,128)(2,1)S(1)}, bf16[48,1152]{1,0:T(8,128)(2,1)S(1)}, u32[]{:S(2)}, u32[]{:S(2)}) collective-permute-start(bf16[48,1152]{1,0:T(8,128)(2,1)S(1)} %get-tuple-element.61), channel_id=1, source_target_pairs={{0,8},{1,9},{2,10},{3,11},{4,12},{5,13},{6,14},{7,15},{8,0},{9,1},... | collective-permute-start | bytes 331784 | tf_op jit(solution)/shard_map/ppermute | solution.py:533
  54.5 11.9 %collective-permute-start.13 = (bf16[48,1152]{1,0:T(8,128)(2,1)S(1)}, bf16[48,1152]{1,0:T(8,128)(2,1)S(1)}, u32[]{:S(2)}, u32[]{:S(2)}) collective-permute-start(bf16[48,1152]{1,0:T(8,128)(2,1)S(1)} %get-tuple-element.62), channel_id=1, source_target_pairs={{0,4},{1,5},{2,6},{3,7},{4,0},{5,1},{6,2},{7,3},{8,12},{9,13},{10,... | collective-permute-start | bytes 331784 | tf_op jit(solution)/shard_map/ppermute | solution.py:533
  66.5 8.6 %collective-permute-start.15 = (bf16[4,48,512]{2,1,0:T(8,128)(2,1)S(1)}, bf16[4,48,512]{2,1,0:T(8,128)(2,1)S(1)}, u32[]{:S(2)}, u32[]{:S(2)}) collective-permute-start(bf16[4,48,512]{2,1,0:T(8,128)(2,1)S(1)} %get-tuple-element.63.refs_7_), channel_id=1, source_target_pairs={{0,2},{1,3},{2,0},{3,1},{4,6},{5,7},{6,4},{7,5},{8,10},{9,11},{10,... | collective-permute-start | bytes 589832 | tf_op jit(solution)/shard_map/ppermute | solution.py:533
  73.4 6.9 %copy-start = (bf16[768,768]{1,0:T(8,128)(2,1)S(1)}, bf16[768,768]{1,0:T(8,128)(2,1)}, u32[]{:S(2)}) copy-start(bf16[768,768]{1,0:T(8,128)(2,1)} %refs_4_.1) | copy-start | bytes 3538948
  73.6 1.5 %collective-permute-start.14 = (bf16[4,48,512]{2,1,0:T(8,128)(2,1)S(1)}, bf16[4,48,512]{2,1,0:T(8,128)(2,1)S(1)}, u32[]{:S(2)}, u32[]{:S(2)}) collective-permute-start(bf16[4,48,512]{2,1,0:T(8,128)(2,1)S(1)} %get-tuple-element.67), channel_id=1, source_target_pairs={{0,1},{1,0},{2,3},{3,2},{4,5},{5,4},{6,7},{7,6},{8,9},{9,8},{10,11... | collective-permute-start | bytes 589832 | tf_op jit(solution)/shard_map/ppermute | solution.py:533
  73.7 6.7 %collective-permute-start.16 = (bf16[4,48,512]{2,1,0:T(8,128)(2,1)S(1)}, bf16[4,48,512]{2,1,0:T(8,128)(2,1)S(1)}, u32[]{:S(2)}, u32[]{:S(2)}) collective-permute-start(bf16[4,48,512]{2,1,0:T(8,128)(2,1)S(1)} %get-tuple-element.68), channel_id=1, source_target_pairs={{0,3},{1,2},{2,1},{3,0},{4,7},{5,6},{6,5},{7,4},{8,11},{9,10},{10,... | collective-permute-start | bytes 589832 | tf_op jit(solution)/shard_map/ppermute | solution.py:533

commit v2 on v1

--- a/solution.py
+++ b/solution.py
@@ -10,7 +10,7 @@
 SEG = 2048
 LOG2E = 1.4426950408889634
 VMEM_LIMIT = 40 * 1024 * 1024
-VMEM_MOST = 51 * 1024 * 1024
+VMEM_MOST = 60 * 1024 * 1024
 BF16 = jnp.bfloat16
 F32 = jnp.float32
 
@@ -146,14 +146,13 @@
 RATE = 4
 GROUP = 4
 HG = 4
-STEP = 2
 DH = 48
 BLK = 128
 HALF = 2 * BLK
 TOK = 512
 SAFE = 96.0
 FAR_ORDER = (2, 1, 3)
-PART_ORDER = (0, 1, 2, 3)
+CHUNKS = ((0, 4),)
 DX = 64
 
 
@@ -175,12 +174,12 @@
 
 
 def head_of(place, j, p):
-    index = place[2 * GROUP * HG]
+    index = place[0][0]
     return ((index & (GROUP - 1)) ^ j) * HG + ((index // GROUP) ^ p)
 
 
 def offsets_of(place, head):
-    return place[head], place[GROUP * HG + head]
+    return place[1][head], place[2][head]
 
 
 def token_picker():
@@ -203,7 +202,8 @@
     return pl.ds(pl.multiple_of(head * DH, 16), DH)
 
 
-def pack_kernel(place, k_hbm, v_hbm, q_hbm, *refs):
+def pack_kernel(index, mid, top, k_hbm, v_hbm, q_hbm, *refs):
+    place = (index, mid, top)
     outs, refs = refs[:6], refs[6:]
     blocks, held, packed = refs[:3], refs[3:6], refs[6:12]
     sems_in, sems_out = refs[12:]
@@ -279,13 +279,14 @@
     return best
 
 
-def near_kernel(inputs, units, tasks, carried, place, *refs):
+def near_kernel(inputs, units, tasks, carried, first, step, index, mid, top, *refs):
+    place = (index, mid, top)
     pieces = dict(zip(inputs, refs[: len(inputs)]))
     refs = refs[len(inputs) :]
     old = [refs[2 * i : 2 * i + 2] for i in range(carried)]
     outs = refs[2 * carried : 2 * carried + 2 * len(tasks)]
     k_s, v_s = refs[-2:]
-    v_s[:, DH:DX, :] = jnp.ones((STEP, DX - DH, v_s.shape[2]), BF16)
+    v_s[:, DH:DX, :] = jnp.ones((step, DX - DH, v_s.shape[2]), BF16)
     lane_slot = lax.broadcasted_iota(jnp.int32, (1, HALF), 1) // BLK
 
     def lookup(j, slot):
@@ -307,7 +308,7 @@
             v_s[h, 0:DH, rows] = ref[h, DH : 2 * DH, lane : lane + BLK]
 
     def counted_again(h):
-        off_mid, off_top = offsets_of(place, head_of(place, 0, pl.program_id(0) * STEP + h))
+        off_mid, off_top = offsets_of(place, head_of(place, 0, first + pl.program_id(0) * step + h))
         same = off_mid == off_top
         return [
             jnp.where(lane_slot == 0, jnp.where(same, 1.584962500721156, 1.0), 0.0),
@@ -353,27 +354,28 @@
             max_ref[h, i] = jnp.broadcast_to(best, (8, HALF))
             scores = following
 
-    for h in range(STEP):
+    for h in range(step):
         prepare(h)
     plain = is_small(
-        [ref[h, 2 * DH :, :] for ref in pieces.values() for h in range(STEP)],
-        [ref[h, 0:DH, :] for ref in pieces.values() for h in range(STEP)],
+        [ref[h, 2 * DH :, :] for ref in pieces.values() for h in range(step)],
+        [ref[h, 0:DH, :] for ref in pieces.values() for h in range(step)],
     )
     for _, max_in in old:
         plain = plain & (jnp.max(jnp.abs(max_in[...])) == 0.0)
 
     @pl.when(plain)
     def _():
-        run(True, list(range(STEP)))
+        run(True, list(range(step)))
 
     @pl.when(jnp.logical_not(plain))
     def _():
-        @pl.loop(0, STEP)
+        @pl.loop(0, step)
         def _(h):
             run(False, [h])
 
 
-def far_kernel(place, *refs):
+def far_kernel(index, mid, top, *refs):
+    place = (index, mid, top)
     own, beyond = refs[:GROUP], refs[GROUP : GROUP + 6]
     outs = refs[GROUP + 6 : GROUP + 6 + RATE]
     k_s, v_s, q_s, result_s, tail_s = refs[GROUP + 6 + RATE :]
@@ -462,25 +464,25 @@
 
 
 def combine_kernel(chip, acc_ref, max_ref, *refs):
-    far, outs = refs[:HG][::-1], refs[HG:]
+    far, outs = refs[:-2][::-1], refs[-2:]
     for i in range(2):
-        for p in range(HG):
+        for p, results in enumerate(far):
             outs[i][p, :, 0:HALF] = join(
-                acc_ref[p, 2 * i], max_ref[p, 2 * i, 0:1, :], far[p], 2 * chip + i
+                acc_ref[p, 2 * i], max_ref[p, 2 * i, 0:1, :], results, 2 * chip + i
             )
             acc = acc_ref[p, 2 * i + 1]
             outs[i][p, :, HALF:] = (acc[0:DH] / acc[DH : DH + 1]).astype(BF16)
 
 
-def project_kernel(place, *refs):
-    parts = refs[:GROUP]
-    w_ref, out_ref, held = refs[GROUP:]
-    for n, j in enumerate(PART_ORDER):
-        for p in range(HG):
-            head = head_of(place, j, p)
+def project_kernel(sources, index, mid, top, *refs):
+    place = (index, mid, top)
+    parts, (w_ref, out_ref, held) = refs[:-3], refs[-3:]
+    for (j, first), part in zip(sources, parts):
+        for p in range(part.shape[0]):
+            head = head_of(place, j, first + p)
             slots = class_of_slots(*offsets_of(place, head))
             for s in range(RATE):
-                held[head_rows(head), lane_block(slots[s])] = parts[n][
+                held[head_rows(head), lane_block(slots[s])] = part[
                     p, :, s * BLK : (s + 1) * BLK
                 ]
     row = lax.broadcasted_iota(jnp.int32, (TOK, TOK), 0)
@@ -494,8 +496,8 @@
     return pl.BlockSpec(shape, lambda *_: (0,) * len(shape))
 
 
-def per_head(shape):
-    return pl.BlockSpec(shape, lambda h, *_: (h,) + (0,) * (len(shape) - 1))
+def per_head(shape, skip=0):
+    return pl.BlockSpec(shape, lambda h, *_: (h + skip,) + (0,) * (len(shape) - 1))
 
 
 def call(
@@ -528,6 +530,10 @@
     )(*scalars, *args, *extra)
 
 
+def handed_on(arrays):
+    return call(lambda: None, (), (), (1,), [], [], [], 0, through=tuple(arrays))
+
+
 def within(array, apart):
     count = lax.axis_size("seq")
     return lax.ppermute(array, "seq", [(i, i ^ apart) for i in range(count)])
@@ -540,15 +546,14 @@
 
 def shards_four(queries, key_states, value_states, offsets_mid, offsets_top, out_weight):
     width = queries.shape[1]
-    index = lax.axis_index("seq").astype(jnp.int32).reshape(1)
-    place = jnp.concatenate([offsets_mid, offsets_top, index])
+    place = (lax.axis_index("seq").astype(jnp.int32).reshape(1), offsets_mid, offsets_top)
     full = jax.ShapeDtypeStruct((HG, 3 * DH, TOK), BF16)
     piece = jax.ShapeDtypeStruct((HG, 3 * DH, HALF), BF16)
     pair = jax.ShapeDtypeStruct((2, 3 * DH, HALF), BF16)
     anywhere = pl.BlockSpec(memory_space=pl.ANY)
     shapes = [full] * 2 + [piece] * 4
     own0, own1, sel2, sel3, rest2, rest3 = call(
-        pack_kernel, (place,), (key_states, value_states, queries), (1,),
+        pack_kernel, place, (key_states, value_states, queries), (1,),
         [anywhere] * 3,
         [(anywhere, shape) for shape in shapes],
         [pltpu.VMEM((TOK, width), BF16)] * 3
@@ -567,26 +572,25 @@
             [], 1 << 17, **order,
         )
 
-    def state(count):
-        return [
-            (per_head((STEP, count, rows, HALF)), jax.ShapeDtypeStruct((HG, count, rows, HALF), F32))
+    def near(held, units, tasks, old, first=0, heads=HG, step=2, **order):
+        sizes = [len(members) * BLK for _, members in units]
+        scores = sum(sum(sizes[low:]) * HALF for group in tasks for _, low, _ in group)
+        arrays = [*held.values(), *[x for one in old for x in one]]
+        shapes = [
+            jax.ShapeDtypeStruct((heads, len(group), rows, HALF), F32)
+            for group in tasks
             for rows in (DX, 8)
         ]
-
-    def near(held, units, tasks, old, **order):
-        sizes = [len(members) * BLK for _, members in units]
-        scores = sum(sum(sizes[low:]) * HALF for group in tasks for _, low, _ in group)
         return call(
-            functools.partial(near_kernel, list(held), units, tasks, len(old)), (place,),
-            (*held.values(), *[x for one in old for x in one]), (HG // STEP,),
-            [per_head((STEP,) + x.shape[1:]) for x in held.values()]
-            + [per_head((STEP,) + x.shape[1:]) for one in old for x in one],
-            [out for group in tasks for out in state(len(group))],
+            functools.partial(near_kernel, list(held), units, tasks, len(old), first, step),
+            place, arrays, (heads // step,),
+            [per_head((step,) + x.shape[1:], first // step) for x in arrays],
+            [(per_head((step,) + x.shape[1:]), x) for x in shapes],
             [
-                pltpu.VMEM((STEP, sum(sizes), 2 * DH), BF16),
-                pltpu.VMEM((STEP, DX, sum(sizes)), BF16),
+                pltpu.VMEM((step, sum(sizes), 2 * DH), BF16),
+                pltpu.VMEM((step, DX, sum(sizes)), BF16),
             ],
-            HG * scores, **order,
+            heads * scores, **order,
         )
 
     def units_of(a, b):
@@ -622,7 +626,7 @@
     result = jax.ShapeDtypeStruct((DH, GROUP * HALF + BLK), BF16)
     piece_0 = pl.BlockSpec((1, 3 * DH, HALF), lambda *_: (0, 0, 0))
     results = call(
-        far_kernel, (place,), (own0, own1, sel2, sel3, *beyond), (1,),
+        far_kernel, place, (own0, own1, sel2, sel3, *beyond), (1,),
         [piece_0] * GROUP + [whole(pair.shape)] * 6,
         [(whole(result.shape), result)] * RATE,
         [
@@ -632,47 +636,55 @@
             pltpu.VMEM((RATE, DH, GROUP * HALF), BF16),
             pltpu.VMEM((RATE, DH, BLK), F32),
         ],
-        RATE * 2 * 3 * TOK * TOK, after=(out[1],),
+        RATE * 2 * 3 * TOK * TOK, after=(state_sel[1],),
     )
     back = [results[0]] + swap_segments(results[1:])
 
     held.update({(2, 2): rest2, (3, 2): rest3})
     units = own_sel + own_rest + other_sel + other_rest
-    attended = jax.ShapeDtypeStruct((HG, DH, TOK), BF16)
-
-    def combine(chip, state):
+
+    def combine(chip, state, far, **order):
+        heads = state[0].shape[0]
+        attended = jax.ShapeDtypeStruct((heads, DH, TOK), BF16)
         return call(
-            functools.partial(combine_kernel, chip), (), (*state, *back[::-1]), (1,),
-            [whole(x.shape) for x in state] + [whole(result.shape)] * HG,
+            functools.partial(combine_kernel, chip), (), (*state, *far[::-1]), (1,),
+            [whole(x.shape) for x in state] + [whole(result.shape)] * heads,
             [(whole(attended.shape), attended)] * 2,
             [],
-            1 << 18,
+            1 << 18, **order,
         )
 
-    state_other = near(
-        held, units,
-        [
+    parts = {}
+    last = results[0]
+    for first, heads in CHUNKS:
+        state_other = near(
+            held, units,
             [
-                ((2, 0), 5, (0, 0)), ((2, 1), 0, None),
-                ((3, 0), 5, (0, 1)), ((3, 1), 0, None),
-            ]
-        ],
-        [state_sel],
-        after=results[:1],
-    )
-    part2, part3 = combine(1, state_other)
+                [
+                    ((2, 0), 5, (0, 0)), ((2, 1), 0, None),
+                    ((3, 0), 5, (0, 1)), ((3, 1), 0, None),
+                ]
+            ],
+            [state_sel],
+            first, heads, 2, after=(last,),
+        )
+        part2, part3 = combine(1, state_other, back[first : first + heads])
+        parts[2, first], parts[3, first] = within(part2, 2), within(part3, 3)
+        last = part3
     state_own = near(
         {(2, 2): rest2, (3, 2): rest3, **{q: held[q] for q in ((0, 0), (1, 0))}},
         other_rest,
         [[(q, 0, (0, i)) for i, q in enumerate(own)]],
         [state_own],
-        after=(part2,),
-    )
-    part0, part1 = combine(0, state_own)
-    parts = {0: part0, 1: within(part1, 1), 2: within(part2, 2), 3: within(part3, 3)}
+        after=(last,),
+    )
+    early = [parts[j, first] for first, _ in CHUNKS[:-1] for j in (2, 3)]
+    part0, part1 = combine(0, state_own, back, after=early)
+    parts = dict(zip(parts, handed_on(parts.values())))
+    parts[0, 0], parts[1, 0] = part0, within(part1, 1)
     return call(
-        project_kernel, (place,), (*[parts[j] for j in PART_ORDER], out_weight), (1,),
-        [whole(attended.shape)] * GROUP + [whole((width, width))],
+        functools.partial(project_kernel, list(parts)), place, (*parts.values(), out_weight), (1,),
+        [whole(x.shape) for x in parts.values()] + [whole((width, width))],
         [(whole((TOK, width)), jax.ShapeDtypeStruct((TOK, width), BF16))],
         [pltpu.VMEM((width, TOK), BF16)],
         1 << 18,

time: 83.5 us -> 78 us (0.934)
  waiting for transfers between devices: 10.1 us -> 3.16 us
  starting transfers between devices: 20.9 us -> 22.1 us
  local copies, waits for them, and re-layouts: 0.01 us -> 1.09 us
    ppermute x17, waiting for transfers between devices: 10.1 us -> 3.16 us  [within(): return lax.ppermute(array, 'seq', [(i, i ^ apart) for i in range(count)])]
    ppermute x17, starting transfers between devices: 20.9 us -> 22.1 us  [within(): return lax.ppermute(array, 'seq', [(i, i ^ apart) for i in range(count)])]
    unnamed x2 -> x14, local copies, waits for them, and re-layouts: 0.01 us -> 1.09 us
    pallas_call x11 -> x12, Pallas kernels: 51.5 us -> 51 us  [call(): pl.pallas_call(body if extra else kernel, grid_spec=pltpu.PrefetchScalarG...]
  transfers between devices with their start and end apart: 17 -> 17, of which waited for: 4 -> 3; matrix products, arithmetic and copies ran while one was open for 0% -> 0% of each run, Pallas kernels for 51% -> 55%
where the time goes in v2:
time: 78 us; the launch traced here: 77.5 us
  Pallas kernels  51 us (65%)
  starting transfers between devices  22.1 us (28%)
  waiting for transfers between devices  3.16 us (4%)
  local copies, waits for them, and re-layouts  1.09 us (1%)
    pallas_call x12, Pallas kernels, call(): pl.pallas_call(body if extra else kernel, grid_spec=pltpu.PrefetchScalarG...  51 us
    ppermute x17, starting transfers between devices, within(): return lax.ppermute(array, 'seq', [(i, i ^ apart) for i in range(count)])  22.1 us
    ppermute x17, waiting for transfers between devices, within(): return lax.ppermute(array, 'seq', [(i, i ^ apart) for i in range(count)])  3.16 us
  transfers between devices with their start and end apart: 17, of which 3 were waited for; matrix products, arithmetic and copies ran while one was open for 0% of the time, Pallas kernels for 55%

profile of v2, /device:TPU:0, one launch (start us, length us, event | category | flops | bytes accessed | tf_op | source)
XLA Modules:
  0.0 77.5 jit_solution(16237635101159628116)
XLA Ops:
  0.0 5.2 %shard_map.64 = (bf16[4,144,512]{2,1,0:T(8,128)(2,1)}, bf16[4,144,512]{2,1,0:T(8,128)(2,1)}, bf16[4,144,256]{2,1,0:T(8,128)(2,1)}, bf16[4,144,256]{2,1,0:T(8,128...) custom-call(s32[1]{0:T(128)} %bitcast.index.refs_0_, s32[16]{0:T(128)} %mid.5, s32[16]{0:T(128)} %top.5, ...), custom_call_target="tpu_custom_call" | custom-call | tf_op jit(solution)/shard_map/pallas_call | solution.py:516
  5.2 0.0 copy-start.5
  5.2 0.0 copy-start.6
  5.2 0.5 collective-permute-start
  5.8 2.6 %collective-permute-start.1 = (bf16[4,144,256]{2,1,0:T(8,128)(2,1)}, bf16[4,144,256]{2,1,0:T(8,128)(2,1)S(1)}, u32[]{:S(2)}, u32[]{:S(2)}) collective-permute-start(bf16[4,144,256]{2,1,0:T(8,128)(2,1)} %get-tuple-element.41), channel_id=1, source_target_pairs={{0,2},{1,3},{2,0},{3,1},{4,6},{5,7},{6,4},{7,5},{8,10},{9,11},{10,... | collective-permute-start | bytes 884744 | tf_op jit(solution)/shard_map/ppermute | solution.py:539
  8.3 0.1 collective-permute-start.2
  8.4 0.0 collective-permute-done.refs_1_.b_ref.refs_4_.refs_6_
  8.4 1.1 %copy-done = bf16[4,144,512]{2,1,0:T(8,128)(2,1)S(1)} copy-done((bf16[4,144,512]{2,1,0:T(8,128)(2,1)S(1)}, bf16[4,144,512]{2,1,0:T(8,128)(2,1)}, u32[]{:S(2)}) %copy-start) | copy-done | bytes 589848
  9.5 4.2 %collective-permute-start.5 = (bf16[2,144,256]{2,1,0:T(8,128)(2,1)S(1)}, bf16[2,144,256]{2,1,0:T(8,128)(2,1)S(1)}, u32[]{:S(2)}, u32[]{:S(2)}) collective-permute-start(bf16[2,144,256]{2,1,0:T(8,128)(2,1)S(1)} %get-tuple-element.49), channel_id=1, source_target_pairs={{0,12},{1,13},{2,14},{3,15},{4,8},{5,9},{6,10},{7,11},{8,4},{9,5},... | collective-permute-start | bytes 442376 | tf_op jit(solution)/shard_map/ppermute | solution.py:539
  13.7 0.0 collective-permute-start.6
  13.7 0.6 collective-permute-start.7
  14.4 7.6 %shard_map.65 = (f32[4,4,64,256]{3,2,1,0:T(8,128)S(1)}, f32[4,4,8,256]{3,2,1,0:T(8,128)S(1)}) custom-call(s32[1]{0:T(128)} %bitcast.index.refs_0_, s32[16]{0:T(128)S(1)} %copy-done.5, s32[16]{0:T(128)S(1)} %copy-done.6, bf16[4,144,512]{2,1,0:T(8,128)(2,1)S(1)} %copy-done.1, bf16[4,144,512]{2,1,0:T(8,128)(2,1)S(1)} %collective-permute-done.refs_1_.b_ref.refs_4_.refs_6_), custom_call_target="tpu_custom_call" | custom-call | tf_op jit(solution)/shard_map/pallas_call | solution.py:516
  22.0 0.0 collective-permute-done.1.refs_0_.refs_5_
  22.0 0.2 collective-permute-done.2.refs_1_.refs_6_
  22.2 1.6 %collective-permute-start.3 = (bf16[4,144,256]{2,1,0:T(8,128)(2,1)S(1)}, bf16[4,144,256]{2,1,0:T(8,128)(2,1)S(1)}, u32[]{:S(2)}, u32[]{:S(2)}) collective-permute-start(bf16[4,144,256]{2,1,0:T(8,128)(2,1)S(1)} %get-tuple-element.46), channel_id=1, source_target_pairs={{0,2},{1,3},{2,0},{3,1},{4,6},{5,7},{6,4},{7,5},{8,10},{9,11},{10,... | collective-permute-start | bytes 884744 | tf_op jit(solution)/shard_map/ppermute | solution.py:539
  23.9 0.0 collective-permute-start.4
  23.9 3.7 %collective-permute-start.10 = (bf16[2,144,256]{2,1,0:T(8,128)(2,1)S(1)}, bf16[2,144,256]{2,1,0:T(8,128)(2,1)S(1)}, u32[]{:S(2)}, u32[]{:S(2)}) collective-permute-start(bf16[2,144,256]{2,1,0:T(8,128)(2,1)S(1)} %get-tuple-element.56), channel_id=1, source_target_pairs={{0,12},{1,13},{2,14},{3,15},{4,8},{5,9},{6,10},{7,11},{8,4},{9,5},... | collective-permute-start | bytes 442376 | tf_op jit(solution)/shard_map/ppermute | solution.py:539
  27.6 2.0 %collective-permute-start.9 = (bf16[2,144,256]{2,1,0:T(8,128)(2,1)S(1)}, bf16[2,144,256]{2,1,0:T(8,128)(2,1)S(1)}, u32[]{:S(2)}, u32[]{:S(2)}) collective-permute-start(bf16[2,144,256]{2,1,0:T(8,128)(2,1)S(1)} %get-tuple-element.55), channel_id=1, source_target_pairs={{0,4},{1,5},{2,6},{3,7},{4,0},{5,1},{6,2},{7,3},{8,12},{9,13},{10,... | collective-permute-start | bytes 442376 | tf_op jit(solution)/shard_map/ppermute | solution.py:539
  29.6 9.4 %shard_map.68 = (f32[4,4,64,256]{3,2,1,0:T(8,128)S(1)}, f32[4,4,8,256]{3,2,1,0:T(8,128)S(1)}, f32[4,2,64,256]{3,2,1,0:T(8,128)S(1)}, f32[4,2,8,256]{3,2,1,0:T(8,128)S(1)}) custom-call(s32[1]{0:T(128)} %bitcast.index.refs_0_, s32[16]{0:T(128)S(1)} %copy-done.5, s32[16]{0:T(128)S(1)} %copy-done.6, bf16[4,144,512]{2,1,0:T(8,128)(2,1)S(1)} %copy-done.1, ...), custom_call_target="tpu_custom_call" | custom-call | tf_op jit(solution)/shard_map/pallas_call | solution.py:516
  39.0 1.8 %collective-permute-done.8.refs_8_ = bf16[2,144,256]{2,1,0:T(8,128)(2,1)S(1)} collective-permute-done((bf16[2,144,256]{2,1,0:T(8,128)(2,1)S(1)}, bf16[2,144,256]{2,1,0:T(8,128)(2,1)S(1)}, u32[]{:S(2)}, u32[]{:S(2)}) %collective-permute-start.8) | collective-permute-done | bytes 147488 | tf_op jit(solution)/shard_map/ppermute | solution.py:539
  40.8 10.2 %shard_map.69 = (bf16[48,1152]{1,0:T(8,128)(2,1)S(1)}, bf16[48,1152]{1,0:T(8,128)(2,1)S(1)}, bf16[48,1152]{1,0:T(8,128)(2,1)S(1)}, bf16[48,1152]{1,0:T(8,128)(2,1)S(1)}) custom-call(s32[1]{0:T(128)} %bitcast.index.refs_0_, s32[16]{0:T(128)S(1)} %copy-done.5, s32[16]{0:T(128)S(1)} %copy-done.6, bf16[4,144,512]{2,1,0:T(8,128)(2,1)S(1)} %copy-done.1, ...), custom_call_target="tpu_custom_call" | custom-call | tf_op jit(solution)/shard_map/pallas_call | solution.py:516
  51.0 2.5 %collective-permute-start.11 = (bf16[48,1152]{1,0:T(8,128)(2,1)S(1)}, bf16[48,1152]{1,0:T(8,128)(2,1)S(1)}, u32[]{:S(2)}, u32[]{:S(2)}) collective-permute-start(bf16[48,1152]{1,0:T(8,128)(2,1)S(1)} %get-tuple-element.60), channel_id=1, source_target_pairs={{0,12},{1,13},{2,14},{3,15},{4,8},{5,9},{6,10},{7,11},{8,4},{9,5},... | collective-permute-start | bytes 331784 | tf_op jit(solution)/shard_map/ppermute | solution.py:539
  53.5 1.9 %collective-permute-start.13 = (bf16[48,1152]{1,0:T(8,128)(2,1)S(1)}, bf16[48,1152]{1,0:T(8,128)(2,1)S(1)}, u32[]{:S(2)}, u32[]{:S(2)}) collective-permute-start(bf16[48,1152]{1,0:T(8,128)(2,1)S(1)} %get-tuple-element.62), channel_id=1, source_target_pairs={{0,4},{1,5},{2,6},{3,7},{4,0},{5,1},{6,2},{7,3},{8,12},{9,13},{10,... | collective-permute-start | bytes 331784 | tf_op jit(solution)/shard_map/ppermute | solution.py:539
  55.4 9.9 %shard_map.70 = (f32[4,4,64,256]{3,2,1,0:T(8,128)S(1)}, f32[4,4,8,256]{3,2,1,0:T(8,128)S(1)}) custom-call(s32[1]{0:T(128)} %bitcast.index.refs_0_, s32[16]{0:T(128)S(1)} %copy-done.5, s32[16]{0:T(128)S(1)} %copy-done.6, bf16[4,144,512]{2,1,0:T(8,128)(2,1)S(1)} %copy-done.1, bf16[4,144,512]{2,1,0:T(8,128)(2,1)S(1)} %collective-permute-done.refs_1_.b_ref.refs_4_.refs_6_, ...), custom_call_target="tpu_custom_call" | custom-call | tf_op jit(solution)/shard_map/pallas_call | solution.py:516
  65.4 0.1 shard_map.71
  65.5 1.6 %collective-permute-start.14 = (bf16[4,48,512]{2,1,0:T(8,128)(2,1)S(1)}, bf16[4,48,512]{2,1,0:T(8,128)(2,1)S(1)}, u32[]{:S(2)}, u32[]{:S(2)}) collective-permute-start(bf16[4,48,512]{2,1,0:T(8,128)(2,1)S(1)} %get-tuple-element.63), channel_id=1, source_target_pairs={{0,2},{1,3},{2,0},{3,1},{4,6},{5,7},{6,4},{7,5},{8,10},{9,11},{10,... | collective-permute-start | bytes 589832 | tf_op jit(solution)/shard_map/ppermute | solution.py:539
  67.1 5.3 %shard_map.73 = (f32[4,4,64,256]{3,2,1,0:T(8,128)S(1)}, f32[4,4,8,256]{3,2,1,0:T(8,128)S(1)}) custom-call(s32[1]{0:T(128)} %bitcast.index.refs_0_, s32[16]{0:T(128)S(1)} %copy-done.5, s32[16]{0:T(128)S(1)} %copy-done.6, bf16[4,144,256]{2,1,0:T(8,128)(2,1)S(1)} %collective-permute-done.3.refs_7_.refs_3_, ...), custom_call_target="tpu_custom_call" | custom-call | tf_op jit(solution)/shard_map/pallas_call | solution.py:516
  72.4 0.0 copy-start.2
  72.4 0.2 shard_map.74
  72.6 0.7 collective-permute-start.16
  73.3 1.2 %collective-permute-done.15.refs_1_ = bf16[4,48,512]{2,1,0:T(8,128)(2,1)S(1)} collective-permute-done((bf16[4,48,512]{2,1,0:T(8,128)(2,1)S(1)}, bf16[4,48,512]{2,1,0:T(8,128)(2,1)S(1)}, u32[]{:S(2)}, u32[]{:S(2)}) %collective-permute-start.15) | collective-permute-done | bytes 196640 | tf_op jit(solution)/shard_map/ppermute | solution.py:539
  74.5 3.0 %shard_map.75 = bf16[512,768]{1,0:T(8,128)(2,1)} custom-call(s32[1]{0:T(128)} %bitcast.index.refs_0_, s32[16]{0:T(128)S(1)} %copy-done.5, s32[16]{0:T(128)S(1)} %copy-done.6, bf16[4,48,512]{2,1,0:T(8,128)(2,1)S(1)} %get-tuple-element.65.refs_0_, bf16[4,48,512]{2,1,0:T(8,128)(2,1)S(1)} %get-tuple-element.66.refs_1_, ...), custom_call_target="tpu_custom_call" | custom-call | tf_op jit(solution)/shard_map/pallas_call | solution.py:516
  (28 shorter events, 0.1 us)
Async XLA Ops:
  5.2 9.2 %copy-start.5 = (s32[16]{0:T(128)S(1)}, s32[16]{0:T(128)}, u32[]{:S(2)}) copy-start(s32[16]{0:T(128)} %mid.5) | copy-start | bytes 196
  5.2 9.2 %copy-start.6 = (s32[16]{0:T(128)S(1)}, s32[16]{0:T(128)}, u32[]{:S(2)}) copy-start(s32[16]{0:T(128)} %top.5) | copy-start | bytes 196
  5.2 3.2 %collective-permute-start = (bf16[4,144,512]{2,1,0:T(8,128)(2,1)}, bf16[4,144,512]{2,1,0:T(8,128)(2,1)S(1)}, u32[]{:S(2)}, u32[]{:S(2)}) collective-permute-start(bf16[4,144,512]{2,1,0:T(8,128)(2,1)} %get-tuple-element.40), channel_id=1, source_target_pairs={{0,1},{1,0},{2,3},{3,2},{4,5},{5,4},{6,7},{7,6},{8,9},{9,8},{10,11... | collective-permute-start | bytes 1769480 | tf_op jit(solution)/shard_map/ppermute | solution.py:539
  5.8 16.3 %collective-permute-start.1 = (bf16[4,144,256]{2,1,0:T(8,128)(2,1)}, bf16[4,144,256]{2,1,0:T(8,128)(2,1)S(1)}, u32[]{:S(2)}, u32[]{:S(2)}) collective-permute-start(bf16[4,144,256]{2,1,0:T(8,128)(2,1)} %get-tuple-element.41), channel_id=1, source_target_pairs={{0,2},{1,3},{2,0},{3,1},{4,6},{5,7},{6,4},{7,5},{8,10},{9,11},{10,... | collective-permute-start | bytes 884744 | tf_op jit(solution)/shard_map/ppermute | solution.py:539
  8.3 13.9 %collective-permute-start.2 = (bf16[4,144,256]{2,1,0:T(8,128)(2,1)}, bf16[4,144,256]{2,1,0:T(8,128)(2,1)S(1)}, u32[]{:S(2)}, u32[]{:S(2)}) collective-permute-start(bf16[4,144,256]{2,1,0:T(8,128)(2,1)} %get-tuple-element.42), channel_id=1, source_target_pairs={{0,3},{1,2},{2,1},{3,0},{4,7},{5,6},{6,5},{7,4},{8,11},{9,10},{10,... | collective-permute-start | bytes 884744 | tf_op jit(solution)/shard_map/ppermute | solution.py:539
  8.4 1.1 %copy-start = (bf16[4,144,512]{2,1,0:T(8,128)(2,1)S(1)}, bf16[4,144,512]{2,1,0:T(8,128)(2,1)}, u32[]{:S(2)}) copy-start(bf16[4,144,512]{2,1,0:T(8,128)(2,1)} %get-tuple-element.39.refs_0_.a_ref.refs_3_.refs_5_) | copy-start | bytes 1769476
  9.5 4.9 %copy-start.1 = (bf16[4,144,512]{2,1,0:T(8,128)(2,1)S(1)}, bf16[4,144,512]{2,1,0:T(8,128)(2,1)}, u32[]{:S(2)}) copy-start(bf16[4,144,512]{2,1,0:T(8,128)(2,1)} %get-tuple-element.39.refs_0_.a_ref.refs_3_.refs_5_) | copy-start | bytes 1769476
  9.5 12.7 %copy-start.3 = (bf16[4,144,256]{2,1,0:T(8,128)(2,1)S(1)}, bf16[4,144,256]{2,1,0:T(8,128)(2,1)}, u32[]{:S(2)}) copy-start(bf16[4,144,256]{2,1,0:T(8,128)(2,1)} %get-tuple-element.44.refs_3_) | copy-start | bytes 884740
  9.5 12.7 %copy-start.4 = (bf16[4,144,256]{2,1,0:T(8,128)(2,1)S(1)}, bf16[4,144,256]{2,1,0:T(8,128)(2,1)}, u32[]{:S(2)}) copy-start(bf16[4,144,256]{2,1,0:T(8,128)(2,1)} %get-tuple-element.45.refs_4_) | copy-start | bytes 884740
  9.5 14.4 %collective-permute-start.5 = (bf16[2,144,256]{2,1,0:T(8,128)(2,1)S(1)}, bf16[2,144,256]{2,1,0:T(8,128)(2,1)S(1)}, u32[]{:S(2)}, u32[]{:S(2)}) collective-permute-start(bf16[2,144,256]{2,1,0:T(8,128)(2,1)S(1)} %get-tuple-element.49), channel_id=1, source_target_pairs={{0,12},{1,13},{2,14},{3,15},{4,8},{5,9},{6,10},{7,11},{8,4},{9,5},... | collective-permute-start | bytes 442376 | tf_op jit(solution)/shard_map/ppermute | solution.py:539
  13.7 13.9 %collective-permute-start.6 = (bf16[2,144,256]{2,1,0:T(8,128)(2,1)S(1)}, bf16[2,144,256]{2,1,0:T(8,128)(2,1)S(1)}, u32[]{:S(2)}, u32[]{:S(2)}) collective-permute-start(bf16[2,144,256]{2,1,0:T(8,128)(2,1)S(1)} %get-tuple-element.50), channel_id=1, source_target_pairs={{0,8},{1,9},{2,10},{3,11},{4,12},{5,13},{6,14},{7,15},{8,0},{9,1},... | collective-permute-start | bytes 442376 | tf_op jit(solution)/shard_map/ppermute | solution.py:539
  13.7 13.9 %collective-permute-start.7 = (bf16[2,144,256]{2,1,0:T(8,128)(2,1)S(1)}, bf16[2,144,256]{2,1,0:T(8,128)(2,1)S(1)}, u32[]{:S(2)}, u32[]{:S(2)}) collective-permute-start(bf16[2,144,256]{2,1,0:T(8,128)(2,1)S(1)} %get-tuple-element.51), channel_id=1, source_target_pairs={{0,4},{1,5},{2,6},{3,7},{4,0},{5,1},{6,2},{7,3},{8,12},{9,13},{10,... | collective-permute-start | bytes 442376 | tf_op jit(solution)/shard_map/ppermute | solution.py:539
  22.2 33.2 %collective-permute-start.3 = (bf16[4,144,256]{2,1,0:T(8,128)(2,1)S(1)}, bf16[4,144,256]{2,1,0:T(8,128)(2,1)S(1)}, u32[]{:S(2)}, u32[]{:S(2)}) collective-permute-start(bf16[4,144,256]{2,1,0:T(8,128)(2,1)S(1)} %get-tuple-element.46), channel_id=1, source_target_pairs={{0,2},{1,3},{2,0},{3,1},{4,6},{5,7},{6,4},{7,5},{8,10},{9,11},{10,... | collective-permute-start | bytes 884744 | tf_op jit(solution)/shard_map/ppermute | solution.py:539
  23.9 31.6 %collective-permute-start.4 = (bf16[4,144,256]{2,1,0:T(8,128)(2,1)S(1)}, bf16[4,144,256]{2,1,0:T(8,128)(2,1)S(1)}, u32[]{:S(2)}, u32[]{:S(2)}) collective-permute-start(bf16[4,144,256]{2,1,0:T(8,128)(2,1)S(1)} %get-tuple-element.47), channel_id=1, source_target_pairs={{0,3},{1,2},{2,1},{3,0},{4,7},{5,6},{6,5},{7,4},{8,11},{9,10},{10,... | collective-permute-start | bytes 884744 | tf_op jit(solution)/shard_map/ppermute | solution.py:539
  23.9 15.1 %collective-permute-start.10 = (bf16[2,144,256]{2,1,0:T(8,128)(2,1)S(1)}, bf16[2,144,256]{2,1,0:T(8,128)(2,1)S(1)}, u32[]{:S(2)}, u32[]{:S(2)}) collective-permute-start(bf16[2,144,256]{2,1,0:T(8,128)(2,1)S(1)} %get-tuple-element.56), channel_id=1, source_target_pairs={{0,12},{1,13},{2,14},{3,15},{4,8},{5,9},{6,10},{7,11},{8,4},{9,5},... | collective-permute-start | bytes 442376 | tf_op jit(solution)/shard_map/ppermute | solution.py:539
  27.6 13.2 %collective-permute-start.8 = (bf16[2,144,256]{2,1,0:T(8,128)(2,1)S(1)}, bf16[2,144,256]{2,1,0:T(8,128)(2,1)S(1)}, u32[]{:S(2)}, u32[]{:S(2)}) collective-permute-start(bf16[2,144,256]{2,1,0:T(8,128)(2,1)S(1)} %get-tuple-element.54), channel_id=1, source_target_pairs={{0,8},{1,9},{2,10},{3,11},{4,12},{5,13},{6,14},{7,15},{8,0},{9,1},... | collective-permute-start | bytes 442376 | tf_op jit(solution)/shard_map/ppermute | solution.py:539
  27.6 13.2 %collective-permute-start.9 = (bf16[2,144,256]{2,1,0:T(8,128)(2,1)S(1)}, bf16[2,144,256]{2,1,0:T(8,128)(2,1)S(1)}, u32[]{:S(2)}, u32[]{:S(2)}) collective-permute-start(bf16[2,144,256]{2,1,0:T(8,128)(2,1)S(1)} %get-tuple-element.55), channel_id=1, source_target_pairs={{0,4},{1,5},{2,6},{3,7},{4,0},{5,1},{6,2},{7,3},{8,12},{9,13},{10,... | collective-permute-start | bytes 442376 | tf_op jit(solution)/shard_map/ppermute | solution.py:539
  51.0 14.4 %collective-permute-start.11 = (bf16[48,1152]{1,0:T(8,128)(2,1)S(1)}, bf16[48,1152]{1,0:T(8,128)(2,1)S(1)}, u32[]{:S(2)}, u32[]{:S(2)}) collective-permute-start(bf16[48,1152]{1,0:T(8,128)(2,1)S(1)} %get-tuple-element.60), channel_id=1, source_target_pairs={{0,12},{1,13},{2,14},{3,15},{4,8},{5,9},{6,10},{7,11},{8,4},{9,5},... | collective-permute-start | bytes 331784 | tf_op jit(solution)/shard_map/ppermute | solution.py:539
  53.5 11.9 %collective-permute-start.12 = (bf16[48,1152]{1,0:T(8,128)(2,1)S(1)}, bf16[48,1152]{1,0:T(8,128)(2,1)S(1)}, u32[]{:S(2)}, u32[]{:S(2)}) collective-permute-start(bf16[48,1152]{1,0:T(8,128)(2,1)S(1)} %get-tuple-element.61), channel_id=1, source_target_pairs={{0,8},{1,9},{2,10},{3,11},{4,12},{5,13},{6,14},{7,15},{8,0},{9,1},... | collective-permute-start | bytes 331784 | tf_op jit(solution)/shard_map/ppermute | solution.py:539
  53.5 11.9 %collective-permute-start.13 = (bf16[48,1152]{1,0:T(8,128)(2,1)S(1)}, bf16[48,1152]{1,0:T(8,128)(2,1)S(1)}, u32[]{:S(2)}, u32[]{:S(2)}) collective-permute-start(bf16[48,1152]{1,0:T(8,128)(2,1)S(1)} %get-tuple-element.62), channel_id=1, source_target_pairs={{0,4},{1,5},{2,6},{3,7},{4,0},{5,1},{6,2},{7,3},{8,12},{9,13},{10,... | collective-permute-start | bytes 331784 | tf_op jit(solution)/shard_map/ppermute | solution.py:539
  65.5 7.7 %collective-permute-start.14 = (bf16[4,48,512]{2,1,0:T(8,128)(2,1)S(1)}, bf16[4,48,512]{2,1,0:T(8,128)(2,1)S(1)}, u32[]{:S(2)}, u32[]{:S(2)}) collective-permute-start(bf16[4,48,512]{2,1,0:T(8,128)(2,1)S(1)} %get-tuple-element.63), channel_id=1, source_target_pairs={{0,2},{1,3},{2,0},{3,1},{4,6},{5,7},{6,4},{7,5},{8,10},{9,11},{10,... | collective-permute-start | bytes 589832 | tf_op jit(solution)/shard_map/ppermute | solution.py:539
  67.1 7.4 %collective-permute-start.15 = (bf16[4,48,512]{2,1,0:T(8,128)(2,1)S(1)}, bf16[4,48,512]{2,1,0:T(8,128)(2,1)S(1)}, u32[]{:S(2)}, u32[]{:S(2)}) collective-permute-start(bf16[4,48,512]{2,1,0:T(8,128)(2,1)S(1)} %get-tuple-element.64.refs_9_), channel_id=1, source_target_pairs={{0,3},{1,2},{2,1},{3,0},{4,7},{5,6},{6,5},{7,4},{8,11},{9,10},{10,... | collective-permute-start | bytes 589832 | tf_op jit(solution)/shard_map/ppermute | solution.py:539
  72.4 2.1 %copy-start.2 = (bf16[768,768]{1,0:T(8,128)(2,1)S(1)}, bf16[768,768]{1,0:T(8,128)(2,1)}, u32[]{:S(2)}) copy-start(bf16[768,768]{1,0:T(8,128)(2,1)} %refs_4_.1) | copy-start | bytes 3538948
  72.6 1.9 %collective-permute-start.16 = (bf16[4,48,512]{2,1,0:T(8,128)(2,1)S(1)}, bf16[4,48,512]{2,1,0:T(8,128)(2,1)S(1)}, u32[]{:S(2)}, u32[]{:S(2)}) collective-permute-start(bf16[4,48,512]{2,1,0:T(8,128)(2,1)S(1)} %get-tuple-element.72), channel_id=1, source_target_pairs={{0,1},{1,0},{2,3},{3,2},{4,5},{5,4},{6,7},{7,6},{8,9},{9,8},{10,11... | collective-permute-start | bytes 589832 | tf_op jit(solution)/shard_map/ppermute | solution.py:539

commit v3 on v2

--- a/solution.py
+++ b/solution.py
@@ -151,7 +151,6 @@
 HALF = 2 * BLK
 TOK = 512
 SAFE = 96.0
-FAR_ORDER = (2, 1, 3)
 CHUNKS = ((0, 4),)
 DX = 64
 
@@ -267,9 +266,9 @@
     return jnp.max(best)
 
 
-def is_small(queries, keys):
+def is_small(query_length, key_length):
     scale = DH**-0.5 * LOG2E
-    return largest(queries) * largest(keys) * (scale * scale) < SAFE * SAFE
+    return query_length * key_length * (scale * scale) < SAFE * SAFE
 
 
 def column_max(blocks):
@@ -357,8 +356,8 @@
     for h in range(step):
         prepare(h)
     plain = is_small(
-        [ref[h, 2 * DH :, :] for ref in pieces.values() for h in range(step)],
-        [ref[h, 0:DH, :] for ref in pieces.values() for h in range(step)],
+        largest([ref[h, 2 * DH :, :] for ref in pieces.values() for h in range(step)]),
+        largest([ref[h, 0:DH, :] for ref in pieces.values() for h in range(step)]),
     )
     for _, max_in in old:
         plain = plain & (jnp.max(jnp.abs(max_in[...])) == 0.0)
@@ -374,46 +373,109 @@
             run(False, [h])
 
 
-def far_kernel(index, mid, top, *refs):
-    place = (index, mid, top)
-    own, beyond = refs[:GROUP], refs[GROUP : GROUP + 6]
-    outs = refs[GROUP + 6 : GROUP + 6 + RATE]
-    k_s, v_s, q_s, result_s, tail_s = refs[GROUP + 6 + RATE :]
+def far_slots(place):
     off_mid, off_top = offsets_of(place, head_of(place, 0, 0))
     same = off_mid == off_top
-    slots = (0, jnp.where(same, 0, 1))
-
-    def source(s, j):
-        return own[j].at[0] if s == 0 else beyond[2 * FAR_ORDER.index(s) + j // 2].at[j % 2]
-
-    for s in range(RATE):
-        for j in range(GROUP):
-            ref = source(s, j)
+    return same, (0, jnp.where(same, 0, 1))
+
+
+def far_pieces(place, sources, k_s, v_s, q_s):
+    _, slots = far_slots(place)
+    for s, pair in enumerate(sources):
+        for i, ref in enumerate(pair):
+            here = slice(i * BLK, (i + 1) * BLK)
             for level, slot in enumerate(slots):
-                here = slice(j * BLK, (j + 1) * BLK)
                 k_s[level, s, here, :] = twice_keys(ref[0:DH, lane_block(slot)])
                 v_s[level, s, 0:DH, here] = ref[DH : 2 * DH, lane_block(slot)]
                 q_s[level, s, :, here] = split_query(ref[2 * DH : 3 * DH, lane_block(slot)])
-    v_s[:, :, DH:DX, :] = jnp.ones((2, RATE, DX - DH, TOK), BF16)
+    v_s[:, :, DH:DX, :] = jnp.ones((2, RATE, DX - DH, HALF), BF16)
+
+
+def far_lengths(sources):
+    every = [ref for pair in sources for ref in pair]
+    return (
+        largest([ref[2 * DH : 3 * DH, 0:HALF] for ref in every]),
+        largest([ref[0:DH, 0:HALF] for ref in every]),
+    )
+
+
+def far_own_kernel(index, mid, top, own0, own1, beyond1, beyond2, beyond3, *refs):
+    k_s, v_s, q_s, acc_ref, max_ref, length_ref = refs
+    sources = [(own0.at[0], own1.at[0])] + [
+        (ref.at[0], ref.at[1]) for ref in (beyond1, beyond2, beyond3)
+    ]
+    far_pieces((index, mid, top), sources, k_s, v_s, q_s)
+
+    def run(plain):
+        def segment(s, carry):
+            def score(level):
+                return [dot(k_s[level, s ^ d], q_s[level, s]) for d in range(1, RATE)]
+
+            scores = score(0)
+            for level in range(2):
+                following = score(1) if level == 0 else None
+                best = jnp.zeros((1, HALF), F32) if plain else column_max(scores)
+                acc = None
+                for d in range(1, RATE):
+                    block = scores[d - 1] if plain else scores[d - 1] - best
+                    part = dot(v_s[level, s ^ d], jnp.exp2(block).astype(BF16))
+                    acc = part if acc is None else acc + part
+                acc_ref[level, s] = acc
+                max_ref[level, s] = jnp.broadcast_to(best, (8, HALF))
+                scores = following
+            return carry
+
+        lax.fori_loop(0, RATE, segment, 0, unroll=2 if plain else 1)
+
+    query_length, key_length = far_lengths(sources)
+    length_ref[0] = query_length
+    length_ref[1] = key_length
+    plain = is_small(query_length, key_length)
+    pl.when(plain)(lambda: run(True))
+    pl.when(jnp.logical_not(plain))(lambda: run(False))
+
+
+def far_kernel(index, mid, top, *refs):
+    place = (index, mid, top)
+    sel2, sel3, beyond3, beyond2, beyond1, k_own, v_own, q_own, acc_in, max_in, length_in = refs[
+        :11
+    ]
+    outs = refs[11 : 11 + RATE]
+    k_s, v_s, q_s, result_s, tail_s = refs[11 + RATE :]
+    same, _ = far_slots(place)
+    sources = [(sel2.at[0], sel3.at[0])] + [
+        (ref.at[0], ref.at[1]) for ref in (beyond1, beyond2, beyond3)
+    ]
+    far_pieces(place, sources, k_s, v_s, q_s)
     tail_s[...] = jnp.zeros(tail_s.shape, F32)
 
     def run(plain):
         tasks = [(level, chip) for level in range(2) for chip in range(2)]
+        held = ((k_own, v_own, q_own), (k_s, v_s, q_s))
 
         def segment(s, carry):
+            def blocks(chip):
+                return [(held[c], s ^ d) for d in range(1, RATE) for c in ((1,), (0, 1))[chip]]
+
             def score(task):
                 level, chip = task
-                query = q_s[level, s, :, chip * HALF : (chip + 1) * HALF]
-                return [dot(k_s[level, s ^ d], query) for d in range(1, RATE)]
+                query = held[chip][2][level, s]
+                return [dot(keys[0][level, b], query) for keys, b in blocks(chip)]
 
             scores = score(tasks[0])
             for n, (level, chip) in enumerate(tasks):
                 following = score(tasks[n + 1]) if n + 1 < len(tasks) else None
                 best = jnp.zeros((1, HALF), F32) if plain else column_max(scores)
                 acc = None
-                for d in range(1, RATE):
-                    block = scores[d - 1] if plain else scores[d - 1] - best
-                    part = dot(v_s[level, s ^ d], jnp.exp2(block).astype(BF16))
+                if chip == 0:
+                    acc = acc_in[level, s]
+                    if not plain:
+                        old_max = max_in[level, s, 0:1, :]
+                        best = jnp.maximum(best, old_max)
+                        acc = acc * jnp.exp2(old_max - best)
+                for block, (keys, b) in zip(scores, blocks(chip)):
+                    block = block if plain else block - best
+                    part = dot(keys[1][level, b], jnp.exp2(block).astype(BF16))
                     acc = part if acc is None else acc + part
                 total = acc[DH : DH + 1, :]
                 result = (acc[0:DH, :] / total).astype(BF16)
@@ -436,9 +498,9 @@
 
         lax.fori_loop(0, RATE, segment, 0, unroll=2 if plain else 1)
 
-    every = [source(s, j) for s in range(RATE) for j in range(GROUP)]
+    query_length, key_length = far_lengths(sources)
     plain = is_small(
-        [ref[2 * DH : 3 * DH, 0:HALF] for ref in every], [ref[0:DH, 0:HALF] for ref in every]
+        jnp.maximum(query_length, length_in[0]), jnp.maximum(key_length, length_in[1])
     )
     pl.when(plain)(lambda: run(True))
     pl.when(jnp.logical_not(plain))(lambda: run(False))
@@ -476,7 +538,9 @@
 
 def project_kernel(sources, index, mid, top, *refs):
     place = (index, mid, top)
-    parts, (w_ref, out_ref, held) = refs[:-3], refs[-3:]
+    parts, (w_hbm, out_hbm, held, w_ref, out_ref, sems) = refs[:-6], refs[-6:]
+    load = pltpu.make_async_copy(w_hbm, w_ref, sems.at[0])
+    load.start()
     for (j, first), part in zip(sources, parts):
         for p in range(part.shape[0]):
             head = head_of(place, j, first + p)
@@ -485,11 +549,20 @@
                 held[head_rows(head), lane_block(slots[s])] = part[
                     p, :, s * BLK : (s + 1) * BLK
                 ]
-    row = lax.broadcasted_iota(jnp.int32, (TOK, TOK), 0)
-    col = lax.broadcasted_iota(jnp.int32, (TOK, TOK), 1)
-    picker = (row == RATE * (col % BLK) + col // BLK).astype(BF16)
-    attention = dot_nt(picker, held[...]).astype(BF16)
-    out_ref[...] = dot(attention, w_ref[...]).astype(BF16)
+    row = lax.broadcasted_iota(jnp.int32, (HALF, TOK), 0)
+    col = lax.broadcasted_iota(jnp.int32, (HALF, TOK), 1)
+    stores = []
+    for n in range(2):
+        rows = slice(n * HALF, (n + 1) * HALF)
+        picker = (row + n * HALF == RATE * (col % BLK) + col // BLK).astype(BF16)
+        attention = dot_nt(picker, held[...]).astype(BF16)
+        if n == 0:
+            load.wait()
+        out_ref[rows, :] = dot(attention, w_ref[...]).astype(BF16)
+        stores.append(pltpu.make_async_copy(out_ref.at[rows], out_hbm.at[rows], sems.at[1 + n]))
+        stores[n].start()
+    for store in stores:
+        store.wait()
 
 
 def whole(shape):
@@ -609,7 +682,6 @@
     *theirs, rest2, rest3 = regroup(sel2, sel3, after=state_own[1:], through=(rest2, rest3))
     theirs = swap_segments(theirs)
     rest2, rest3 = within(rest2, 2), within(rest3, 3)
-    beyond = [x for s in FAR_ORDER for x in (ours[s - 1], theirs[s - 1])]
 
     held.update({(2, 0): sel2, (3, 0): sel3})
     out = near(
@@ -625,18 +697,34 @@
 
     result = jax.ShapeDtypeStruct((DH, GROUP * HALF + BLK), BF16)
     piece_0 = pl.BlockSpec((1, 3 * DH, HALF), lambda *_: (0, 0, 0))
+    pieces_shapes = [
+        jax.ShapeDtypeStruct((2, RATE, HALF, 2 * DH), BF16),
+        jax.ShapeDtypeStruct((2, RATE, DX, HALF), BF16),
+        jax.ShapeDtypeStruct((2, RATE, 2 * DH, HALF), BF16),
+    ]
+    sums_shapes = [
+        jax.ShapeDtypeStruct((2, RATE, DX, HALF), F32),
+        jax.ShapeDtypeStruct((2, RATE, 8, HALF), F32),
+    ]
+    in_scalars = pl.BlockSpec(memory_space=pltpu.SMEM)
+    far_own = call(
+        far_own_kernel, place, (own0, own1, *ours), (1,),
+        [piece_0] * 2 + [whole(pair.shape)] * 3,
+        [(whole(x.shape), x) for x in pieces_shapes + sums_shapes]
+        + [(in_scalars, jax.ShapeDtypeStruct((2,), F32))],
+        [], RATE * 2 * 3 * HALF * HALF, after=(state_sel[1],),
+    )
     results = call(
-        far_kernel, place, (own0, own1, sel2, sel3, *beyond), (1,),
-        [piece_0] * GROUP + [whole(pair.shape)] * 6,
+        far_kernel, place, (sel2, sel3, *theirs[::-1], *far_own), (1,),
+        [piece_0] * 2 + [whole(pair.shape)] * 3
+        + [whole(x.shape) for x in far_own[:-1]] + [in_scalars],
         [(whole(result.shape), result)] * RATE,
-        [
-            pltpu.VMEM((2, RATE, TOK, 2 * DH), BF16),
-            pltpu.VMEM((2, RATE, DX, TOK), BF16),
-            pltpu.VMEM((2, RATE, 2 * DH, TOK), BF16),
+        [pltpu.VMEM(x.shape, BF16) for x in pieces_shapes]
+        + [
             pltpu.VMEM((RATE, DH, GROUP * HALF), BF16),
             pltpu.VMEM((RATE, DH, BLK), F32),
         ],
-        RATE * 2 * 3 * TOK * TOK, after=(state_sel[1],),
+        RATE * 2 * 3 * 3 * HALF * HALF,
     )
     back = [results[0]] + swap_segments(results[1:])
 
@@ -684,9 +772,14 @@
     parts[0, 0], parts[1, 0] = part0, within(part1, 1)
     return call(
         functools.partial(project_kernel, list(parts)), place, (*parts.values(), out_weight), (1,),
-        [whole(x.shape) for x in parts.values()] + [whole((width, width))],
-        [(whole((TOK, width)), jax.ShapeDtypeStruct((TOK, width), BF16))],
-        [pltpu.VMEM((width, TOK), BF16)],
+        [whole(x.shape) for x in parts.values()] + [anywhere],
+        [(anywhere, jax.ShapeDtypeStruct((TOK, width), BF16))],
+        [
+            pltpu.VMEM((width, TOK), BF16),
+            pltpu.VMEM((width, width), BF16),
+            pltpu.VMEM((TOK, width), BF16),
+            pltpu.SemaphoreType.DMA((3,)),
+        ],
         1 << 18,
     )[0]
 

time: 78 us -> 80.1 us (1.027)
  Pallas kernels: 51 us -> 54.9 us
  waiting for transfers between devices: 3.16 us -> 1.27 us
    pallas_call x12 -> x13, Pallas kernels: 51 us -> 54.9 us  [call(): pl.pallas_call(body if extra else kernel, grid_spec=pltpu.PrefetchScalarG...]
    ppermute x17, waiting for transfers between devices: 3.16 us -> 1.27 us  [within(): return lax.ppermute(array, 'seq', [(i, i ^ apart) for i in range(count)])]
  transfers between devices with their start and end apart: 17 -> 17, of which waited for: 3 -> 3; matrix products, arithmetic and copies ran while one was open for 0% -> 0% of each run, Pallas kernels for 55% -> 58%
where the time goes in v3:
time: 80.1 us; the launch traced here: 79.7 us
  Pallas kernels  54.9 us (69%)
  starting transfers between devices  22.1 us (28%)
  waiting for transfers between devices  1.27 us (2%)
  local copies, waits for them, and re-layouts  1.09 us (1%)
    pallas_call x13, Pallas kernels, call(): pl.pallas_call(body if extra else kernel, grid_spec=pltpu.PrefetchScalarG...  54.9 us
    ppermute x17, starting transfers between devices, within(): return lax.ppermute(array, 'seq', [(i, i ^ apart) for i in range(count)])  22.1 us
  transfers between devices with their start and end apart: 17, of which 3 were waited for; matrix products, arithmetic and copies ran while one was open for 0% of the time, Pallas kernels for 58%

profile of v3, /device:TPU:0, one launch (start us, length us, event | category | flops | bytes accessed | tf_op | source)
XLA Modules:
  0.0 79.7 jit_solution(16699001393179357821)
XLA Ops:
  0.0 5.2 %shard_map.64 = (bf16[4,144,512]{2,1,0:T(8,128)(2,1)}, bf16[4,144,512]{2,1,0:T(8,128)(2,1)}, bf16[4,144,256]{2,1,0:T(8,128)(2,1)}, bf16[4,144,256]{2,1,0:T(8,128...) custom-call(s32[1]{0:T(128)} %bitcast.index.refs_0_, s32[16]{0:T(128)} %mid.7, s32[16]{0:T(128)} %top.7, ...), custom_call_target="tpu_custom_call" | custom-call | tf_op jit(solution)/shard_map/pallas_call | solution.py:589
  5.2 0.0 copy-start.5
  5.2 0.0 copy-start.6
  5.3 0.5 collective-permute-start
  5.8 2.6 %collective-permute-start.1 = (bf16[4,144,256]{2,1,0:T(8,128)(2,1)}, bf16[4,144,256]{2,1,0:T(8,128)(2,1)S(1)}, u32[]{:S(2)}, u32[]{:S(2)}) collective-permute-start(bf16[4,144,256]{2,1,0:T(8,128)(2,1)} %get-tuple-element.47), channel_id=1, source_target_pairs={{0,2},{1,3},{2,0},{3,1},{4,6},{5,7},{6,4},{7,5},{8,10},{9,11},{10,... | collective-permute-start | bytes 884744 | tf_op jit(solution)/shard_map/ppermute | solution.py:612
  8.3 0.1 collective-permute-start.2
  8.4 1.1 %copy-done = bf16[4,144,512]{2,1,0:T(8,128)(2,1)S(1)} copy-done((bf16[4,144,512]{2,1,0:T(8,128)(2,1)S(1)}, bf16[4,144,512]{2,1,0:T(8,128)(2,1)}, u32[]{:S(2)}) %copy-start) | copy-done | bytes 589848
  9.5 4.2 %collective-permute-start.5 = (bf16[2,144,256]{2,1,0:T(8,128)(2,1)S(1)}, bf16[2,144,256]{2,1,0:T(8,128)(2,1)S(1)}, u32[]{:S(2)}, u32[]{:S(2)}) collective-permute-start(bf16[2,144,256]{2,1,0:T(8,128)(2,1)S(1)} %get-tuple-element.55), channel_id=1, source_target_pairs={{0,12},{1,13},{2,14},{3,15},{4,8},{5,9},{6,10},{7,11},{8,4},{9,5},... | collective-permute-start | bytes 442376 | tf_op jit(solution)/shard_map/ppermute | solution.py:612
  13.8 0.6 collective-permute-start.7
  14.4 7.6 %shard_map.65 = (f32[4,4,64,256]{3,2,1,0:T(8,128)S(1)}, f32[4,4,8,256]{3,2,1,0:T(8,128)S(1)}) custom-call(s32[1]{0:T(128)} %bitcast.index.refs_0_, s32[16]{0:T(128)S(1)} %copy-done.5, s32[16]{0:T(128)S(1)} %copy-done.6, bf16[4,144,512]{2,1,0:T(8,128)(2,1)S(1)} %copy-done.1, bf16[4,144,512]{2,1,0:T(8,128)(2,1)S(1)} %collective-permute-done.refs_1_.b_ref.refs_4_.refs_6_), custom_call_target="tpu_custom_call" | custom-call | tf_op jit(solution)/shard_map/pallas_call | solution.py:589
  22.0 0.0 collective-permute-done.1.refs_0_.refs_5_
  22.0 0.2 collective-permute-done.2.refs_1_.refs_6_
  22.2 1.6 %collective-permute-start.3 = (bf16[4,144,256]{2,1,0:T(8,128)(2,1)S(1)}, bf16[4,144,256]{2,1,0:T(8,128)(2,1)S(1)}, u32[]{:S(2)}, u32[]{:S(2)}) collective-permute-start(bf16[4,144,256]{2,1,0:T(8,128)(2,1)S(1)} %get-tuple-element.52), channel_id=1, source_target_pairs={{0,2},{1,3},{2,0},{3,1},{4,6},{5,7},{6,4},{7,5},{8,10},{9,11},{10,... | collective-permute-start | bytes 884744 | tf_op jit(solution)/shard_map/ppermute | solution.py:612
  23.9 0.0 collective-permute-start.4
  23.9 0.0 collective-permute-done.5.refs_9_.refs_7_
  23.9 3.7 %collective-permute-start.8 = (bf16[2,144,256]{2,1,0:T(8,128)(2,1)S(1)}, bf16[2,144,256]{2,1,0:T(8,128)(2,1)S(1)}, u32[]{:S(2)}, u32[]{:S(2)}) collective-permute-start(bf16[2,144,256]{2,1,0:T(8,128)(2,1)S(1)} %get-tuple-element.60), channel_id=1, source_target_pairs={{0,12},{1,13},{2,14},{3,15},{4,8},{5,9},{6,10},{7,11},{8,4},{9,5},... | collective-permute-start | bytes 442376 | tf_op jit(solution)/shard_map/ppermute | solution.py:612
  27.6 2.0 %collective-permute-start.10 = (bf16[2,144,256]{2,1,0:T(8,128)(2,1)S(1)}, bf16[2,144,256]{2,1,0:T(8,128)(2,1)S(1)}, u32[]{:S(2)}, u32[]{:S(2)}) collective-permute-start(bf16[2,144,256]{2,1,0:T(8,128)(2,1)S(1)} %get-tuple-element.62), channel_id=1, source_target_pairs={{0,4},{1,5},{2,6},{3,7},{4,0},{5,1},{6,2},{7,3},{8,12},{9,13},{10,... | collective-permute-start | bytes 442376 | tf_op jit(solution)/shard_map/ppermute | solution.py:612
  29.6 9.4 %shard_map.68 = (f32[4,4,64,256]{3,2,1,0:T(8,128)S(1)}, f32[4,4,8,256]{3,2,1,0:T(8,128)S(1)}, f32[4,2,64,256]{3,2,1,0:T(8,128)S(1)}, f32[4,2,8,256]{3,2,1,0:T(8,128)S(1)}) custom-call(s32[1]{0:T(128)} %bitcast.index.refs_0_, s32[16]{0:T(128)S(1)} %copy-done.5, s32[16]{0:T(128)S(1)} %copy-done.6, bf16[4,144,512]{2,1,0:T(8,128)(2,1)S(1)} %copy-done.1, ...), custom_call_target="tpu_custom_call" | custom-call | tf_op jit(solution)/shard_map/pallas_call | solution.py:589
  39.0 4.7 %shard_map.69 = (bf16[2,4,256,96]{3,2,1,0:T(8,128)(2,1)S(1)}, bf16[2,4,64,256]{3,2,1,0:T(8,128)(2,1)S(1)}, bf16[2,4,96,256]{3,2,1,0:T(8,128)(2,1)S(1)}, f32[2,4,...) custom-call(s32[1]{0:T(128)} %bitcast.index.refs_0_, s32[16]{0:T(128)S(1)} %copy-done.5, ...), custom_call_target="tpu_custom_call" | custom-call | tf_op jit(solution)/shard_map/pallas_call | solution.py:589
  43.7 9.0 %shard_map.70 = (bf16[48,1152]{1,0:T(8,128)(2,1)S(1)}, bf16[48,1152]{1,0:T(8,128)(2,1)S(1)}, bf16[48,1152]{1,0:T(8,128)(2,1)S(1)}, bf16[48,1152]{1,0:T(8,128)(2,1)S(1)}) custom-call(s32[1]{0:T(128)} %bitcast.index.refs_0_, s32[16]{0:T(128)S(1)} %copy-done.5, s32[16]{0:T(128)S(1)} %copy-done.6, ...), custom_call_target="tpu_custom_call" | custom-call | tf_op jit(solution)/shard_map/pallas_call | solution.py:589
  52.7 2.5 %collective-permute-start.11 = (bf16[48,1152]{1,0:T(8,128)(2,1)S(1)}, bf16[48,1152]{1,0:T(8,128)(2,1)S(1)}, u32[]{:S(2)}, u32[]{:S(2)}) collective-permute-start(bf16[48,1152]{1,0:T(8,128)(2,1)S(1)} %get-tuple-element.72), channel_id=1, source_target_pairs={{0,12},{1,13},{2,14},{3,15},{4,8},{5,9},{6,10},{7,11},{8,4},{9,5},... | collective-permute-start | bytes 331784 | tf_op jit(solution)/shard_map/ppermute | solution.py:612
  55.2 2.0 %collective-permute-start.13 = (bf16[48,1152]{1,0:T(8,128)(2,1)S(1)}, bf16[48,1152]{1,0:T(8,128)(2,1)S(1)}, u32[]{:S(2)}, u32[]{:S(2)}) collective-permute-start(bf16[48,1152]{1,0:T(8,128)(2,1)S(1)} %get-tuple-element.74), channel_id=1, source_target_pairs={{0,4},{1,5},{2,6},{3,7},{4,0},{5,1},{6,2},{7,3},{8,12},{9,13},{10,... | collective-permute-start | bytes 331784 | tf_op jit(solution)/shard_map/ppermute | solution.py:612
  57.2 9.9 %shard_map.71 = (f32[4,4,64,256]{3,2,1,0:T(8,128)S(1)}, f32[4,4,8,256]{3,2,1,0:T(8,128)S(1)}) custom-call(s32[1]{0:T(128)} %bitcast.index.refs_0_, s32[16]{0:T(128)S(1)} %copy-done.5, s32[16]{0:T(128)S(1)} %copy-done.6, bf16[4,144,512]{2,1,0:T(8,128)(2,1)S(1)} %copy-done.1, bf16[4,144,512]{2,1,0:T(8,128)(2,1)S(1)} %collective-permute-done.refs_1_.b_ref.refs_4_.refs_6_, ...), custom_call_target="tpu_custom_call" | custom-call | tf_op jit(solution)/shard_map/pallas_call | solution.py:589
  67.2 0.1 shard_map.72
  67.3 0.5 collective-permute-start.14
  67.8 5.3 %shard_map.74 = (f32[4,4,64,256]{3,2,1,0:T(8,128)S(1)}, f32[4,4,8,256]{3,2,1,0:T(8,128)S(1)}) custom-call(s32[1]{0:T(128)} %bitcast.index.refs_0_, s32[16]{0:T(128)S(1)} %copy-done.5, s32[16]{0:T(128)S(1)} %copy-done.6, bf16[4,144,256]{2,1,0:T(8,128)(2,1)S(1)} %collective-permute-done.3.refs_7_.refs_3_, ...), custom_call_target="tpu_custom_call" | custom-call | tf_op jit(solution)/shard_map/pallas_call | solution.py:589
  73.1 0.0 copy-start.2
  73.1 0.1 shard_map.75
  73.2 1.8 %collective-permute-start.16 = (bf16[4,48,512]{2,1,0:T(8,128)(2,1)S(1)}, bf16[4,48,512]{2,1,0:T(8,128)(2,1)S(1)}, u32[]{:S(2)}, u32[]{:S(2)}) collective-permute-start(bf16[4,48,512]{2,1,0:T(8,128)(2,1)S(1)} %get-tuple-element.84), channel_id=1, source_target_pairs={{0,1},{1,0},{2,3},{3,2},{4,5},{5,4},{6,7},{7,6},{8,9},{9,8},{10,11... | collective-permute-start | bytes 589832 | tf_op jit(solution)/shard_map/ppermute | solution.py:612
  75.0 0.1 collective-permute-done.15.refs_1_
  75.2 0.9 %collective-permute-done.16.refs_3_ = bf16[4,48,512]{2,1,0:T(8,128)(2,1)S(1)} collective-permute-done((bf16[4,48,512]{2,1,0:T(8,128)(2,1)S(1)}, bf16[4,48,512]{2,1,0:T(8,128)(2,1)S(1)}, u32[]{:S(2)}, u32[]{:S(2)}) %collective-permute-start.16) | collective-permute-done | bytes 196640 | tf_op jit(solution)/shard_map/ppermute | solution.py:612
  76.1 3.4 %shard_map.76 = bf16[512,768]{1,0:T(8,128)(2,1)} custom-call(s32[1]{0:T(128)} %bitcast.index.refs_0_, s32[16]{0:T(128)S(1)} %copy-done.5, s32[16]{0:T(128)S(1)} %copy-done.6, bf16[4,48,512]{2,1,0:T(8,128)(2,1)S(1)} %get-tuple-element.77.refs_0_, bf16[4,48,512]{2,1,0:T(8,128)(2,1)S(1)} %get-tuple-element.78.refs_1_, ...), custom_call_target="tpu_custom_call" | custom-call | tf_op jit(solution)/shard_map/pallas_call | solution.py:589
  (29 shorter events, 0.1 us)
Async XLA Ops:
  5.2 9.2 %copy-start.5 = (s32[16]{0:T(128)S(1)}, s32[16]{0:T(128)}, u32[]{:S(2)}) copy-start(s32[16]{0:T(128)} %mid.7) | copy-start | bytes 196
  5.2 9.2 %copy-start.6 = (s32[16]{0:T(128)S(1)}, s32[16]{0:T(128)}, u32[]{:S(2)}) copy-start(s32[16]{0:T(128)} %top.7) | copy-start | bytes 196
  5.3 3.2 %collective-permute-start = (bf16[4,144,512]{2,1,0:T(8,128)(2,1)}, bf16[4,144,512]{2,1,0:T(8,128)(2,1)S(1)}, u32[]{:S(2)}, u32[]{:S(2)}) collective-permute-start(bf16[4,144,512]{2,1,0:T(8,128)(2,1)} %get-tuple-element.46), channel_id=1, source_target_pairs={{0,1},{1,0},{2,3},{3,2},{4,5},{5,4},{6,7},{7,6},{8,9},{9,8},{10,11... | collective-permute-start | bytes 1769480 | tf_op jit(solution)/shard_map/ppermute | solution.py:612
  5.8 16.3 %collective-permute-start.1 = (bf16[4,144,256]{2,1,0:T(8,128)(2,1)}, bf16[4,144,256]{2,1,0:T(8,128)(2,1)S(1)}, u32[]{:S(2)}, u32[]{:S(2)}) collective-permute-start(bf16[4,144,256]{2,1,0:T(8,128)(2,1)} %get-tuple-element.47), channel_id=1, source_target_pairs={{0,2},{1,3},{2,0},{3,1},{4,6},{5,7},{6,4},{7,5},{8,10},{9,11},{10,... | collective-permute-start | bytes 884744 | tf_op jit(solution)/shard_map/ppermute | solution.py:612
  8.3 13.9 %collective-permute-start.2 = (bf16[4,144,256]{2,1,0:T(8,128)(2,1)}, bf16[4,144,256]{2,1,0:T(8,128)(2,1)S(1)}, u32[]{:S(2)}, u32[]{:S(2)}) collective-permute-start(bf16[4,144,256]{2,1,0:T(8,128)(2,1)} %get-tuple-element.48), channel_id=1, source_target_pairs={{0,3},{1,2},{2,1},{3,0},{4,7},{5,6},{6,5},{7,4},{8,11},{9,10},{10,... | collective-permute-start | bytes 884744 | tf_op jit(solution)/shard_map/ppermute | solution.py:612
  8.4 1.1 %copy-start = (bf16[4,144,512]{2,1,0:T(8,128)(2,1)S(1)}, bf16[4,144,512]{2,1,0:T(8,128)(2,1)}, u32[]{:S(2)}) copy-start(bf16[4,144,512]{2,1,0:T(8,128)(2,1)} %get-tuple-element.45.refs_0_.a_ref.refs_3_.refs_5_) | copy-start | bytes 1769476
  9.5 4.9 %copy-start.1 = (bf16[4,144,512]{2,1,0:T(8,128)(2,1)S(1)}, bf16[4,144,512]{2,1,0:T(8,128)(2,1)}, u32[]{:S(2)}) copy-start(bf16[4,144,512]{2,1,0:T(8,128)(2,1)} %get-tuple-element.45.refs_0_.a_ref.refs_3_.refs_5_) | copy-start | bytes 1769476
  9.5 12.7 %copy-start.3 = (bf16[4,144,256]{2,1,0:T(8,128)(2,1)S(1)}, bf16[4,144,256]{2,1,0:T(8,128)(2,1)}, u32[]{:S(2)}) copy-start(bf16[4,144,256]{2,1,0:T(8,128)(2,1)} %get-tuple-element.50.refs_3_) | copy-start | bytes 884740
  9.5 12.7 %copy-start.4 = (bf16[4,144,256]{2,1,0:T(8,128)(2,1)S(1)}, bf16[4,144,256]{2,1,0:T(8,128)(2,1)}, u32[]{:S(2)}) copy-start(bf16[4,144,256]{2,1,0:T(8,128)(2,1)} %get-tuple-element.51.refs_4_) | copy-start | bytes 884740
  9.5 14.4 %collective-permute-start.5 = (bf16[2,144,256]{2,1,0:T(8,128)(2,1)S(1)}, bf16[2,144,256]{2,1,0:T(8,128)(2,1)S(1)}, u32[]{:S(2)}, u32[]{:S(2)}) collective-permute-start(bf16[2,144,256]{2,1,0:T(8,128)(2,1)S(1)} %get-tuple-element.55), channel_id=1, source_target_pairs={{0,12},{1,13},{2,14},{3,15},{4,8},{5,9},{6,10},{7,11},{8,4},{9,5},... | collective-permute-start | bytes 442376 | tf_op jit(solution)/shard_map/ppermute | solution.py:612
  13.8 13.9 %collective-permute-start.6 = (bf16[2,144,256]{2,1,0:T(8,128)(2,1)S(1)}, bf16[2,144,256]{2,1,0:T(8,128)(2,1)S(1)}, u32[]{:S(2)}, u32[]{:S(2)}) collective-permute-start(bf16[2,144,256]{2,1,0:T(8,128)(2,1)S(1)} %get-tuple-element.56), channel_id=1, source_target_pairs={{0,8},{1,9},{2,10},{3,11},{4,12},{5,13},{6,14},{7,15},{8,0},{9,1},... | collective-permute-start | bytes 442376 | tf_op jit(solution)/shard_map/ppermute | solution.py:612
  13.8 13.9 %collective-permute-start.7 = (bf16[2,144,256]{2,1,0:T(8,128)(2,1)S(1)}, bf16[2,144,256]{2,1,0:T(8,128)(2,1)S(1)}, u32[]{:S(2)}, u32[]{:S(2)}) collective-permute-start(bf16[2,144,256]{2,1,0:T(8,128)(2,1)S(1)} %get-tuple-element.57), channel_id=1, source_target_pairs={{0,4},{1,5},{2,6},{3,7},{4,0},{5,1},{6,2},{7,3},{8,12},{9,13},{10,... | collective-permute-start | bytes 442376 | tf_op jit(solution)/shard_map/ppermute | solution.py:612
  22.2 34.9 %collective-permute-start.3 = (bf16[4,144,256]{2,1,0:T(8,128)(2,1)S(1)}, bf16[4,144,256]{2,1,0:T(8,128)(2,1)S(1)}, u32[]{:S(2)}, u32[]{:S(2)}) collective-permute-start(bf16[4,144,256]{2,1,0:T(8,128)(2,1)S(1)} %get-tuple-element.52), channel_id=1, source_target_pairs={{0,2},{1,3},{2,0},{3,1},{4,6},{5,7},{6,4},{7,5},{8,10},{9,11},{10,... | collective-permute-start | bytes 884744 | tf_op jit(solution)/shard_map/ppermute | solution.py:612
  23.9 33.3 %collective-permute-start.4 = (bf16[4,144,256]{2,1,0:T(8,128)(2,1)S(1)}, bf16[4,144,256]{2,1,0:T(8,128)(2,1)S(1)}, u32[]{:S(2)}, u32[]{:S(2)}) collective-permute-start(bf16[4,144,256]{2,1,0:T(8,128)(2,1)S(1)} %get-tuple-element.53), channel_id=1, source_target_pairs={{0,3},{1,2},{2,1},{3,0},{4,7},{5,6},{6,5},{7,4},{8,11},{9,10},{10,... | collective-permute-start | bytes 884744 | tf_op jit(solution)/shard_map/ppermute | solution.py:612
  23.9 19.8 %collective-permute-start.8 = (bf16[2,144,256]{2,1,0:T(8,128)(2,1)S(1)}, bf16[2,144,256]{2,1,0:T(8,128)(2,1)S(1)}, u32[]{:S(2)}, u32[]{:S(2)}) collective-permute-start(bf16[2,144,256]{2,1,0:T(8,128)(2,1)S(1)} %get-tuple-element.60), channel_id=1, source_target_pairs={{0,12},{1,13},{2,14},{3,15},{4,8},{5,9},{6,10},{7,11},{8,4},{9,5},... | collective-permute-start | bytes 442376 | tf_op jit(solution)/shard_map/ppermute | solution.py:612
  27.6 16.0 %collective-permute-start.9 = (bf16[2,144,256]{2,1,0:T(8,128)(2,1)S(1)}, bf16[2,144,256]{2,1,0:T(8,128)(2,1)S(1)}, u32[]{:S(2)}, u32[]{:S(2)}) collective-permute-start(bf16[2,144,256]{2,1,0:T(8,128)(2,1)S(1)} %get-tuple-element.61), channel_id=1, source_target_pairs={{0,8},{1,9},{2,10},{3,11},{4,12},{5,13},{6,14},{7,15},{8,0},{9,1},... | collective-permute-start | bytes 442376 | tf_op jit(solution)/shard_map/ppermute | solution.py:612
  27.6 16.0 %collective-permute-start.10 = (bf16[2,144,256]{2,1,0:T(8,128)(2,1)S(1)}, bf16[2,144,256]{2,1,0:T(8,128)(2,1)S(1)}, u32[]{:S(2)}, u32[]{:S(2)}) collective-permute-start(bf16[2,144,256]{2,1,0:T(8,128)(2,1)S(1)} %get-tuple-element.62), channel_id=1, source_target_pairs={{0,4},{1,5},{2,6},{3,7},{4,0},{5,1},{6,2},{7,3},{8,12},{9,13},{10,... | collective-permute-start | bytes 442376 | tf_op jit(solution)/shard_map/ppermute | solution.py:612
  52.7 14.4 %collective-permute-start.11 = (bf16[48,1152]{1,0:T(8,128)(2,1)S(1)}, bf16[48,1152]{1,0:T(8,128)(2,1)S(1)}, u32[]{:S(2)}, u32[]{:S(2)}) collective-permute-start(bf16[48,1152]{1,0:T(8,128)(2,1)S(1)} %get-tuple-element.72), channel_id=1, source_target_pairs={{0,12},{1,13},{2,14},{3,15},{4,8},{5,9},{6,10},{7,11},{8,4},{9,5},... | collective-permute-start | bytes 331784 | tf_op jit(solution)/shard_map/ppermute | solution.py:612
  55.2 11.9 %collective-permute-start.12 = (bf16[48,1152]{1,0:T(8,128)(2,1)S(1)}, bf16[48,1152]{1,0:T(8,128)(2,1)S(1)}, u32[]{:S(2)}, u32[]{:S(2)}) collective-permute-start(bf16[48,1152]{1,0:T(8,128)(2,1)S(1)} %get-tuple-element.73), channel_id=1, source_target_pairs={{0,8},{1,9},{2,10},{3,11},{4,12},{5,13},{6,14},{7,15},{8,0},{9,1},... | collective-permute-start | bytes 331784 | tf_op jit(solution)/shard_map/ppermute | solution.py:612
  55.2 11.9 %collective-permute-start.13 = (bf16[48,1152]{1,0:T(8,128)(2,1)S(1)}, bf16[48,1152]{1,0:T(8,128)(2,1)S(1)}, u32[]{:S(2)}, u32[]{:S(2)}) collective-permute-start(bf16[48,1152]{1,0:T(8,128)(2,1)S(1)} %get-tuple-element.74), channel_id=1, source_target_pairs={{0,4},{1,5},{2,6},{3,7},{4,0},{5,1},{6,2},{7,3},{8,12},{9,13},{10,... | collective-permute-start | bytes 331784 | tf_op jit(solution)/shard_map/ppermute | solution.py:612
  67.3 7.7 %collective-permute-start.14 = (bf16[4,48,512]{2,1,0:T(8,128)(2,1)S(1)}, bf16[4,48,512]{2,1,0:T(8,128)(2,1)S(1)}, u32[]{:S(2)}, u32[]{:S(2)}) collective-permute-start(bf16[4,48,512]{2,1,0:T(8,128)(2,1)S(1)} %get-tuple-element.75), channel_id=1, source_target_pairs={{0,2},{1,3},{2,0},{3,1},{4,6},{5,7},{6,4},{7,5},{8,10},{9,11},{10,... | collective-permute-start | bytes 589832 | tf_op jit(solution)/shard_map/ppermute | solution.py:612
  67.8 7.4 %collective-permute-start.15 = (bf16[4,48,512]{2,1,0:T(8,128)(2,1)S(1)}, bf16[4,48,512]{2,1,0:T(8,128)(2,1)S(1)}, u32[]{:S(2)}, u32[]{:S(2)}) collective-permute-start(bf16[4,48,512]{2,1,0:T(8,128)(2,1)S(1)} %get-tuple-element.76.refs_9_), channel_id=1, source_target_pairs={{0,3},{1,2},{2,1},{3,0},{4,7},{5,6},{6,5},{7,4},{8,11},{9,10},{10,... | collective-permute-start | bytes 589832 | tf_op jit(solution)/shard_map/ppermute | solution.py:612
  73.1 3.0 %copy-start.2 = (bf16[768,768]{1,0:T(8,128)(2,1)S(1)}, bf16[768,768]{1,0:T(8,128)(2,1)}, u32[]{:S(2)}) copy-start(bf16[768,768]{1,0:T(8,128)(2,1)} %refs_4_.1) | copy-start | bytes 3538948
  73.2 2.9 %collective-permute-start.16 = (bf16[4,48,512]{2,1,0:T(8,128)(2,1)S(1)}, bf16[4,48,512]{2,1,0:T(8,128)(2,1)S(1)}, u32[]{:S(2)}, u32[]{:S(2)}) collective-permute-start(bf16[4,48,512]{2,1,0:T(8,128)(2,1)S(1)} %get-tuple-element.84), channel_id=1, source_target_pairs={{0,1},{1,0},{2,3},{3,2},{4,5},{5,4},{6,7},{7,6},{8,9},{9,8},{10,11... | collective-permute-start | bytes 589832 | tf_op jit(solution)/shard_map/ppermute | solution.py:612

commit v4 on v3

--- a/solution.py
+++ b/solution.py
@@ -150,6 +150,7 @@
 BLK = 128
 HALF = 2 * BLK
 TOK = 512
+SCALE = DH**-0.5 * LOG2E
 SAFE = 96.0
 CHUNKS = ((0, 4),)
 DX = 64
@@ -243,16 +244,8 @@
         out[1] = b_ref[s + 1, :, 0:HALF]
 
 
-def split_query(q):
-    scaled = q.astype(F32) * (DH**-0.5 * LOG2E)
-    high = scaled.astype(BF16)
-    low = (scaled - high.astype(F32)).astype(BF16)
-    return jnp.concatenate([high, low], axis=0)
-
-
-def twice_keys(keys_t):
-    both = jnp.concatenate([keys_t, keys_t], axis=0).astype(F32)
-    return both.T.astype(BF16)
+def upright(keys_t):
+    return keys_t.T
 
 
 def largest(blocks):
@@ -267,15 +260,14 @@
 
 
 def is_small(query_length, key_length):
-    scale = DH**-0.5 * LOG2E
-    return query_length * key_length * (scale * scale) < SAFE * SAFE
+    return query_length * key_length * (SCALE * SCALE) < SAFE * SAFE
 
 
 def column_max(blocks):
     best = jnp.max(blocks[0], axis=0, keepdims=True)
     for block in blocks[1:]:
         best = jnp.maximum(best, jnp.max(block, axis=0, keepdims=True))
-    return best
+    return best * SCALE
 
 
 def near_kernel(inputs, units, tasks, carried, first, step, index, mid, top, *refs):
@@ -303,7 +295,7 @@
         for i, (j, slot) in enumerate(members):
             ref, lane = lookup(j, slot)
             rows = slice(i * BLK, (i + 1) * BLK)
-            k_s[h, rows, :] = twice_keys(ref[h, 0:DH, lane : lane + BLK])
+            k_s[h, rows, :] = upright(ref[h, 0:DH, lane : lane + BLK])
             v_s[h, 0:DH, rows] = ref[h, DH : 2 * DH, lane : lane + BLK]
 
     def counted_again(h):
@@ -326,7 +318,7 @@
         def score(task):
             h, _, (j, half), low = task[:4]
             ref, lane = lookup(j, 2 * half)
-            query = split_query(ref[h, 2 * DH :, lane : lane + HALF])
+            query = ref[h, 2 * DH :, lane : lane + HALF]
             return [dot(k_s[h, rows, :], query) for _, rows in chunks[low:]]
 
         scores = score(flat[0])
@@ -339,6 +331,7 @@
                 best = best if plain else jnp.maximum(best, old_max)
             acc = None
             for (label, rows), block in zip(chunks[low:], scores):
+                block = block * SCALE
                 if half == 0 and label is not None:
                     block = block - (best - again_h[label])
                 elif not plain:
@@ -385,9 +378,9 @@
         for i, ref in enumerate(pair):
             here = slice(i * BLK, (i + 1) * BLK)
             for level, slot in enumerate(slots):
-                k_s[level, s, here, :] = twice_keys(ref[0:DH, lane_block(slot)])
+                k_s[level, s, here, :] = upright(ref[0:DH, lane_block(slot)])
                 v_s[level, s, 0:DH, here] = ref[DH : 2 * DH, lane_block(slot)]
-                q_s[level, s, :, here] = split_query(ref[2 * DH : 3 * DH, lane_block(slot)])
+                q_s[level, s, :, here] = ref[2 * DH : 3 * DH, lane_block(slot)]
     v_s[:, :, DH:DX, :] = jnp.ones((2, RATE, DX - DH, HALF), BF16)
 
 
@@ -417,7 +410,8 @@
                 best = jnp.zeros((1, HALF), F32) if plain else column_max(scores)
                 acc = None
                 for d in range(1, RATE):
-                    block = scores[d - 1] if plain else scores[d - 1] - best
+                    block = scores[d - 1] * SCALE
+                    block = block if plain else block - best
                     part = dot(v_s[level, s ^ d], jnp.exp2(block).astype(BF16))
                     acc = part if acc is None else acc + part
                 acc_ref[level, s] = acc
@@ -474,7 +468,7 @@
                         best = jnp.maximum(best, old_max)
                         acc = acc * jnp.exp2(old_max - best)
                 for block, (keys, b) in zip(scores, blocks(chip)):
-                    block = block if plain else block - best
+                    block = block * SCALE if plain else block * SCALE - best
                     part = dot(keys[1][level, b], jnp.exp2(block).astype(BF16))
                     acc = part if acc is None else acc + part
                 total = acc[DH : DH + 1, :]
@@ -538,9 +532,7 @@
 
 def project_kernel(sources, index, mid, top, *refs):
     place = (index, mid, top)
-    parts, (w_hbm, out_hbm, held, w_ref, out_ref, sems) = refs[:-6], refs[-6:]
-    load = pltpu.make_async_copy(w_hbm, w_ref, sems.at[0])
-    load.start()
+    parts, (w_ref, out_ref, held) = refs[:-3], refs[-3:]
     for (j, first), part in zip(sources, parts):
         for p in range(part.shape[0]):
             head = head_of(place, j, first + p)
@@ -549,20 +541,11 @@
                 held[head_rows(head), lane_block(slots[s])] = part[
                     p, :, s * BLK : (s + 1) * BLK
                 ]
-    row = lax.broadcasted_iota(jnp.int32, (HALF, TOK), 0)
-    col = lax.broadcasted_iota(jnp.int32, (HALF, TOK), 1)
-    stores = []
-    for n in range(2):
-        rows = slice(n * HALF, (n + 1) * HALF)
-        picker = (row + n * HALF == RATE * (col % BLK) + col // BLK).astype(BF16)
-        attention = dot_nt(picker, held[...]).astype(BF16)
-        if n == 0:
-            load.wait()
-        out_ref[rows, :] = dot(attention, w_ref[...]).astype(BF16)
-        stores.append(pltpu.make_async_copy(out_ref.at[rows], out_hbm.at[rows], sems.at[1 + n]))
-        stores[n].start()
-    for store in stores:
-        store.wait()
+    row = lax.broadcasted_iota(jnp.int32, (TOK, TOK), 0)
+    col = lax.broadcasted_iota(jnp.int32, (TOK, TOK), 1)
+    picker = (row == RATE * (col % BLK) + col // BLK).astype(BF16)
+    attention = dot_nt(picker, held[...]).astype(BF16)
+    out_ref[...] = dot(attention, w_ref[...]).astype(BF16)
 
 
 def whole(shape):
@@ -660,7 +643,7 @@
             [per_head((step,) + x.shape[1:], first // step) for x in arrays],
             [(per_head((step,) + x.shape[1:]), x) for x in shapes],
             [
-                pltpu.VMEM((step, sum(sizes), 2 * DH), BF16),
+                pltpu.VMEM((step, sum(sizes), DH), BF16),
                 pltpu.VMEM((step, DX, sum(sizes)), BF16),
             ],
             heads * scores, **order,
@@ -698,9 +681,9 @@
     result = jax.ShapeDtypeStruct((DH, GROUP * HALF + BLK), BF16)
     piece_0 = pl.BlockSpec((1, 3 * DH, HALF), lambda *_: (0, 0, 0))
     pieces_shapes = [
-        jax.ShapeDtypeStruct((2, RATE, HALF, 2 * DH), BF16),
+        jax.ShapeDtypeStruct((2, RATE, HALF, DH), BF16),
         jax.ShapeDtypeStruct((2, RATE, DX, HALF), BF16),
-        jax.ShapeDtypeStruct((2, RATE, 2 * DH, HALF), BF16),
+        jax.ShapeDtypeStruct((2, RATE, DH, HALF), BF16),
     ]
     sums_shapes = [
         jax.ShapeDtypeStruct((2, RATE, DX, HALF), F32),
@@ -772,14 +755,9 @@
     parts[0, 0], parts[1, 0] = part0, within(part1, 1)
     return call(
         functools.partial(project_kernel, list(parts)), place, (*parts.values(), out_weight), (1,),
-        [whole(x.shape) for x in parts.values()] + [anywhere],
-        [(anywhere, jax.ShapeDtypeStruct((TOK, width), BF16))],
-        [
-            pltpu.VMEM((width, TOK), BF16),
-            pltpu.VMEM((width, width), BF16),
-            pltpu.VMEM((TOK, width), BF16),
-            pltpu.SemaphoreType.DMA((3,)),
-        ],
+        [whole(x.shape) for x in parts.values()] + [whole((width, width))],
+        [(whole((TOK, width)), jax.ShapeDtypeStruct((TOK, width), BF16))],
+        [pltpu.VMEM((width, TOK), BF16)],
         1 << 18,
     )[0]
 

time: 80.1 us -> 81.7 us (1.020)
  Pallas kernels: 54.9 us -> 57.9 us
  starting transfers between devices: 22.1 us -> 21.2 us
    pallas_call x13, Pallas kernels: 54.9 us -> 57.9 us  [call(): pl.pallas_call(body if extra else kernel, grid_spec=pltpu.PrefetchScalarG...]
    ppermute x17, starting transfers between devices: 22.1 us -> 21.2 us  [within(): return lax.ppermute(array, 'seq', [(i, i ^ apart) for i in range(count)])]
  transfers between devices with their start and end apart: 17 -> 17, of which waited for: 3 -> 1; matrix products, arithmetic and copies ran while one was open for 0% -> 0% of each run, Pallas kernels for 58% -> 61%
where the time goes in v4:
time: 81.7 us; the launch traced here: 81.5 us
  Pallas kernels  57.9 us (71%)
  starting transfers between devices  21.2 us (26%)
  waiting for transfers between devices  1.11 us (1%)
  local copies, waits for them, and re-layouts  1.09 us (1%)
    pallas_call x13, Pallas kernels, call(): pl.pallas_call(body if extra else kernel, grid_spec=pltpu.PrefetchScalarG...  57.9 us
    ppermute x17, starting transfers between devices, within(): return lax.ppermute(array, 'seq', [(i, i ^ apart) for i in range(count)])  21.2 us
  transfers between devices with their start and end apart: 17, of which 1 were waited for; matrix products, arithmetic and copies ran while one was open for 0% of the time, Pallas kernels for 61%

profile of v4, /device:TPU:0, one launch (start us, length us, event | category | flops | bytes accessed | tf_op | source)
XLA Modules:
  0.0 81.5 jit_solution(17411375612276120254)
XLA Ops:
  0.0 5.2 %shard_map.64 = (bf16[4,144,512]{2,1,0:T(8,128)(2,1)}, bf16[4,144,512]{2,1,0:T(8,128)(2,1)}, bf16[4,144,256]{2,1,0:T(8,128)(2,1)}, bf16[4,144,256]{2,1,0:T(8,128...) custom-call(s32[1]{0:T(128)} %bitcast.index.refs_0_, s32[16]{0:T(128)} %mid.7, s32[16]{0:T(128)} %top.7, ...), custom_call_target="tpu_custom_call" | custom-call | tf_op jit(solution)/shard_map/pallas_call | solution.py:572
  5.2 0.0 copy-start.5
  5.2 0.0 copy-start.6
  5.3 0.5 collective-permute-start
  5.8 2.6 %collective-permute-start.1 = (bf16[4,144,256]{2,1,0:T(8,128)(2,1)}, bf16[4,144,256]{2,1,0:T(8,128)(2,1)S(1)}, u32[]{:S(2)}, u32[]{:S(2)}) collective-permute-start(bf16[4,144,256]{2,1,0:T(8,128)(2,1)} %get-tuple-element.47), channel_id=1, source_target_pairs={{0,2},{1,3},{2,0},{3,1},{4,6},{5,7},{6,4},{7,5},{8,10},{9,11},{10,... | collective-permute-start | bytes 884744 | tf_op jit(solution)/shard_map/ppermute | solution.py:595
  8.3 0.1 collective-permute-start.2
  8.4 0.0 collective-permute-done.refs_1_.b_ref.refs_4_.refs_6_
  8.4 1.1 %copy-done = bf16[4,144,512]{2,1,0:T(8,128)(2,1)S(1)} copy-done((bf16[4,144,512]{2,1,0:T(8,128)(2,1)S(1)}, bf16[4,144,512]{2,1,0:T(8,128)(2,1)}, u32[]{:S(2)}) %copy-start) | copy-done | bytes 589848
  9.5 4.2 %collective-permute-start.5 = (bf16[2,144,256]{2,1,0:T(8,128)(2,1)S(1)}, bf16[2,144,256]{2,1,0:T(8,128)(2,1)S(1)}, u32[]{:S(2)}, u32[]{:S(2)}) collective-permute-start(bf16[2,144,256]{2,1,0:T(8,128)(2,1)S(1)} %get-tuple-element.55), channel_id=1, source_target_pairs={{0,12},{1,13},{2,14},{3,15},{4,8},{5,9},{6,10},{7,11},{8,4},{9,5},... | collective-permute-start | bytes 442376 | tf_op jit(solution)/shard_map/ppermute | solution.py:595
  13.8 0.0 collective-permute-start.6
  13.8 0.6 collective-permute-start.7
  14.4 8.6 %shard_map.65 = (f32[4,4,64,256]{3,2,1,0:T(8,128)S(1)}, f32[4,4,8,256]{3,2,1,0:T(8,128)S(1)}) custom-call(s32[1]{0:T(128)} %bitcast.index.refs_0_, s32[16]{0:T(128)S(1)} %copy-done.5, s32[16]{0:T(128)S(1)} %copy-done.6, bf16[4,144,512]{2,1,0:T(8,128)(2,1)S(1)} %copy-done.1, bf16[4,144,512]{2,1,0:T(8,128)(2,1)S(1)} %collective-permute-done.refs_1_.b_ref.refs_4_.refs_6_), custom_call_target="tpu_custom_call" | custom-call | tf_op jit(solution)/shard_map/pallas_call | solution.py:572
  23.0 0.0 collective-permute-done.1.refs_0_.refs_5_
  23.1 0.8 collective-permute-start.3
  23.9 0.2 collective-permute-start.4
  24.1 3.5 %collective-permute-start.8 = (bf16[2,144,256]{2,1,0:T(8,128)(2,1)S(1)}, bf16[2,144,256]{2,1,0:T(8,128)(2,1)S(1)}, u32[]{:S(2)}, u32[]{:S(2)}) collective-permute-start(bf16[2,144,256]{2,1,0:T(8,128)(2,1)S(1)} %get-tuple-element.60), channel_id=1, source_target_pairs={{0,12},{1,13},{2,14},{3,15},{4,8},{5,9},{6,10},{7,11},{8,4},{9,5},... | collective-permute-start | bytes 442376 | tf_op jit(solution)/shard_map/ppermute | solution.py:595
  27.6 2.0 %collective-permute-start.10 = (bf16[2,144,256]{2,1,0:T(8,128)(2,1)S(1)}, bf16[2,144,256]{2,1,0:T(8,128)(2,1)S(1)}, u32[]{:S(2)}, u32[]{:S(2)}) collective-permute-start(bf16[2,144,256]{2,1,0:T(8,128)(2,1)S(1)} %get-tuple-element.62), channel_id=1, source_target_pairs={{0,4},{1,5},{2,6},{3,7},{4,0},{5,1},{6,2},{7,3},{8,12},{9,13},{10,... | collective-permute-start | bytes 442376 | tf_op jit(solution)/shard_map/ppermute | solution.py:595
  29.6 10.0 %shard_map.68 = (f32[4,4,64,256]{3,2,1,0:T(8,128)S(1)}, f32[4,4,8,256]{3,2,1,0:T(8,128)S(1)}, f32[4,2,64,256]{3,2,1,0:T(8,128)S(1)}, f32[4,2,8,256]{3,2,1,0:T(8,128)S(1)}) custom-call(s32[1]{0:T(128)} %bitcast.index.refs_0_, s32[16]{0:T(128)S(1)} %copy-done.5, s32[16]{0:T(128)S(1)} %copy-done.6, bf16[4,144,512]{2,1,0:T(8,128)(2,1)S(1)} %copy-done.1, ...), custom_call_target="tpu_custom_call" | custom-call | tf_op jit(solution)/shard_map/pallas_call | solution.py:572
  39.6 5.2 %shard_map.69 = (bf16[2,4,256,48]{3,2,1,0:T(8,128)(2,1)S(1)}, bf16[2,4,64,256]{3,2,1,0:T(8,128)(2,1)S(1)}, bf16[2,4,48,256]{3,2,1,0:T(8,128)(2,1)S(1)}, f32[2,4,...) custom-call(s32[1]{0:T(128)} %bitcast.index.refs_0_, s32[16]{0:T(128)S(1)} %copy-done.5, ...), custom_call_target="tpu_custom_call" | custom-call | tf_op jit(solution)/shard_map/pallas_call | solution.py:572
  44.9 9.4 %shard_map.70 = (bf16[48,1152]{1,0:T(8,128)(2,1)S(1)}, bf16[48,1152]{1,0:T(8,128)(2,1)S(1)}, bf16[48,1152]{1,0:T(8,128)(2,1)S(1)}, bf16[48,1152]{1,0:T(8,128)(2,1)S(1)}) custom-call(s32[1]{0:T(128)} %bitcast.index.refs_0_, s32[16]{0:T(128)S(1)} %copy-done.5, s32[16]{0:T(128)S(1)} %copy-done.6, ...), custom_call_target="tpu_custom_call" | custom-call | tf_op jit(solution)/shard_map/pallas_call | solution.py:572
  54.3 2.5 %collective-permute-start.11 = (bf16[48,1152]{1,0:T(8,128)(2,1)S(1)}, bf16[48,1152]{1,0:T(8,128)(2,1)S(1)}, u32[]{:S(2)}, u32[]{:S(2)}) collective-permute-start(bf16[48,1152]{1,0:T(8,128)(2,1)S(1)} %get-tuple-element.72), channel_id=1, source_target_pairs={{0,12},{1,13},{2,14},{3,15},{4,8},{5,9},{6,10},{7,11},{8,4},{9,5},... | collective-permute-start | bytes 331784 | tf_op jit(solution)/shard_map/ppermute | solution.py:595
  56.8 2.0 %collective-permute-start.13 = (bf16[48,1152]{1,0:T(8,128)(2,1)S(1)}, bf16[48,1152]{1,0:T(8,128)(2,1)S(1)}, u32[]{:S(2)}, u32[]{:S(2)}) collective-permute-start(bf16[48,1152]{1,0:T(8,128)(2,1)S(1)} %get-tuple-element.74), channel_id=1, source_target_pairs={{0,4},{1,5},{2,6},{3,7},{4,0},{5,1},{6,2},{7,3},{8,12},{9,13},{10,... | collective-permute-start | bytes 331784 | tf_op jit(solution)/shard_map/ppermute | solution.py:595
  58.8 10.3 %shard_map.71 = (f32[4,4,64,256]{3,2,1,0:T(8,128)S(1)}, f32[4,4,8,256]{3,2,1,0:T(8,128)S(1)}) custom-call(s32[1]{0:T(128)} %bitcast.index.refs_0_, s32[16]{0:T(128)S(1)} %copy-done.5, s32[16]{0:T(128)S(1)} %copy-done.6, bf16[4,144,512]{2,1,0:T(8,128)(2,1)S(1)} %copy-done.1, bf16[4,144,512]{2,1,0:T(8,128)(2,1)S(1)} %collective-permute-done.refs_1_.b_ref.refs_4_.refs_6_, ...), custom_call_target="tpu_custom_call" | custom-call | tf_op jit(solution)/shard_map/pallas_call | solution.py:572
  69.1 0.1 shard_map.72
  69.3 0.1 collective-permute-start.14
  69.3 0.1 collective-permute-start.15
  69.4 5.8 %shard_map.74 = (f32[4,4,64,256]{3,2,1,0:T(8,128)S(1)}, f32[4,4,8,256]{3,2,1,0:T(8,128)S(1)}) custom-call(s32[1]{0:T(128)} %bitcast.index.refs_0_, s32[16]{0:T(128)S(1)} %copy-done.5, s32[16]{0:T(128)S(1)} %copy-done.6, bf16[4,144,256]{2,1,0:T(8,128)(2,1)S(1)} %collective-permute-done.3.refs_7_.refs_3_, ...), custom_call_target="tpu_custom_call" | custom-call | tf_op jit(solution)/shard_map/pallas_call | solution.py:572
  75.2 0.0 copy-start.2
  75.2 0.1 shard_map.75
  75.3 2.1 %collective-permute-start.16 = (bf16[4,48,512]{2,1,0:T(8,128)(2,1)S(1)}, bf16[4,48,512]{2,1,0:T(8,128)(2,1)S(1)}, u32[]{:S(2)}, u32[]{:S(2)}) collective-permute-start(bf16[4,48,512]{2,1,0:T(8,128)(2,1)S(1)} %get-tuple-element.84), channel_id=1, source_target_pairs={{0,1},{1,0},{2,3},{3,2},{4,5},{5,4},{6,7},{7,6},{8,9},{9,8},{10,11... | collective-permute-start | bytes 589832 | tf_op jit(solution)/shard_map/ppermute | solution.py:595
  77.5 1.1 %collective-permute-done.16.refs_3_ = bf16[4,48,512]{2,1,0:T(8,128)(2,1)S(1)} collective-permute-done((bf16[4,48,512]{2,1,0:T(8,128)(2,1)S(1)}, bf16[4,48,512]{2,1,0:T(8,128)(2,1)S(1)}, u32[]{:S(2)}, u32[]{:S(2)}) %collective-permute-start.16) | collective-permute-done | bytes 196640 | tf_op jit(solution)/shard_map/ppermute | solution.py:595
  78.5 3.0 %shard_map.76 = bf16[512,768]{1,0:T(8,128)(2,1)} custom-call(s32[1]{0:T(128)} %bitcast.index.refs_0_, s32[16]{0:T(128)S(1)} %copy-done.5, s32[16]{0:T(128)S(1)} %copy-done.6, bf16[4,48,512]{2,1,0:T(8,128)(2,1)S(1)} %get-tuple-element.77.refs_0_, bf16[4,48,512]{2,1,0:T(8,128)(2,1)S(1)} %get-tuple-element.78.refs_1_, ...), custom_call_target="tpu_custom_call" | custom-call | tf_op jit(solution)/shard_map/pallas_call | solution.py:572
  (29 shorter events, 0.1 us)
Async XLA Ops:
  5.2 9.2 %copy-start.5 = (s32[16]{0:T(128)S(1)}, s32[16]{0:T(128)}, u32[]{:S(2)}) copy-start(s32[16]{0:T(128)} %mid.7) | copy-start | bytes 196
  5.2 9.2 %copy-start.6 = (s32[16]{0:T(128)S(1)}, s32[16]{0:T(128)}, u32[]{:S(2)}) copy-start(s32[16]{0:T(128)} %top.7) | copy-start | bytes 196
  5.3 3.2 %collective-permute-start = (bf16[4,144,512]{2,1,0:T(8,128)(2,1)}, bf16[4,144,512]{2,1,0:T(8,128)(2,1)S(1)}, u32[]{:S(2)}, u32[]{:S(2)}) collective-permute-start(bf16[4,144,512]{2,1,0:T(8,128)(2,1)} %get-tuple-element.46), channel_id=1, source_target_pairs={{0,1},{1,0},{2,3},{3,2},{4,5},{5,4},{6,7},{7,6},{8,9},{9,8},{10,11... | collective-permute-start | bytes 1769480 | tf_op jit(solution)/shard_map/ppermute | solution.py:595
  5.8 17.3 %collective-permute-start.1 = (bf16[4,144,256]{2,1,0:T(8,128)(2,1)}, bf16[4,144,256]{2,1,0:T(8,128)(2,1)S(1)}, u32[]{:S(2)}, u32[]{:S(2)}) collective-permute-start(bf16[4,144,256]{2,1,0:T(8,128)(2,1)} %get-tuple-element.47), channel_id=1, source_target_pairs={{0,2},{1,3},{2,0},{3,1},{4,6},{5,7},{6,4},{7,5},{8,10},{9,11},{10,... | collective-permute-start | bytes 884744 | tf_op jit(solution)/shard_map/ppermute | solution.py:595
  8.3 14.7 %collective-permute-start.2 = (bf16[4,144,256]{2,1,0:T(8,128)(2,1)}, bf16[4,144,256]{2,1,0:T(8,128)(2,1)S(1)}, u32[]{:S(2)}, u32[]{:S(2)}) collective-permute-start(bf16[4,144,256]{2,1,0:T(8,128)(2,1)} %get-tuple-element.48), channel_id=1, source_target_pairs={{0,3},{1,2},{2,1},{3,0},{4,7},{5,6},{6,5},{7,4},{8,11},{9,10},{10,... | collective-permute-start | bytes 884744 | tf_op jit(solution)/shard_map/ppermute | solution.py:595
  8.4 1.1 %copy-start = (bf16[4,144,512]{2,1,0:T(8,128)(2,1)S(1)}, bf16[4,144,512]{2,1,0:T(8,128)(2,1)}, u32[]{:S(2)}) copy-start(bf16[4,144,512]{2,1,0:T(8,128)(2,1)} %get-tuple-element.45.refs_0_.a_ref.refs_3_.refs_5_) | copy-start | bytes 1769476
  9.5 4.9 %copy-start.1 = (bf16[4,144,512]{2,1,0:T(8,128)(2,1)S(1)}, bf16[4,144,512]{2,1,0:T(8,128)(2,1)}, u32[]{:S(2)}) copy-start(bf16[4,144,512]{2,1,0:T(8,128)(2,1)} %get-tuple-element.45.refs_0_.a_ref.refs_3_.refs_5_) | copy-start | bytes 1769476
  9.5 13.6 %copy-start.3 = (bf16[4,144,256]{2,1,0:T(8,128)(2,1)S(1)}, bf16[4,144,256]{2,1,0:T(8,128)(2,1)}, u32[]{:S(2)}) copy-start(bf16[4,144,256]{2,1,0:T(8,128)(2,1)} %get-tuple-element.50.refs_3_) | copy-start | bytes 884740
  9.5 13.6 %copy-start.4 = (bf16[4,144,256]{2,1,0:T(8,128)(2,1)S(1)}, bf16[4,144,256]{2,1,0:T(8,128)(2,1)}, u32[]{:S(2)}) copy-start(bf16[4,144,256]{2,1,0:T(8,128)(2,1)} %get-tuple-element.51.refs_4_) | copy-start | bytes 884740
  9.5 14.6 %collective-permute-start.5 = (bf16[2,144,256]{2,1,0:T(8,128)(2,1)S(1)}, bf16[2,144,256]{2,1,0:T(8,128)(2,1)S(1)}, u32[]{:S(2)}, u32[]{:S(2)}) collective-permute-start(bf16[2,144,256]{2,1,0:T(8,128)(2,1)S(1)} %get-tuple-element.55), channel_id=1, source_target_pairs={{0,12},{1,13},{2,14},{3,15},{4,8},{5,9},{6,10},{7,11},{8,4},{9,5},... | collective-permute-start | bytes 442376 | tf_op jit(solution)/shard_map/ppermute | solution.py:595
  13.8 13.9 %collective-permute-start.6 = (bf16[2,144,256]{2,1,0:T(8,128)(2,1)S(1)}, bf16[2,144,256]{2,1,0:T(8,128)(2,1)S(1)}, u32[]{:S(2)}, u32[]{:S(2)}) collective-permute-start(bf16[2,144,256]{2,1,0:T(8,128)(2,1)S(1)} %get-tuple-element.56), channel_id=1, source_target_pairs={{0,8},{1,9},{2,10},{3,11},{4,12},{5,13},{6,14},{7,15},{8,0},{9,1},... | collective-permute-start | bytes 442376 | tf_op jit(solution)/shard_map/ppermute | solution.py:595
  13.8 13.9 %collective-permute-start.7 = (bf16[2,144,256]{2,1,0:T(8,128)(2,1)S(1)}, bf16[2,144,256]{2,1,0:T(8,128)(2,1)S(1)}, u32[]{:S(2)}, u32[]{:S(2)}) collective-permute-start(bf16[2,144,256]{2,1,0:T(8,128)(2,1)S(1)} %get-tuple-element.57), channel_id=1, source_target_pairs={{0,4},{1,5},{2,6},{3,7},{4,0},{5,1},{6,2},{7,3},{8,12},{9,13},{10,... | collective-permute-start | bytes 442376 | tf_op jit(solution)/shard_map/ppermute | solution.py:595
  23.1 35.7 %collective-permute-start.3 = (bf16[4,144,256]{2,1,0:T(8,128)(2,1)S(1)}, bf16[4,144,256]{2,1,0:T(8,128)(2,1)S(1)}, u32[]{:S(2)}, u32[]{:S(2)}) collective-permute-start(bf16[4,144,256]{2,1,0:T(8,128)(2,1)S(1)} %get-tuple-element.52), channel_id=1, source_target_pairs={{0,2},{1,3},{2,0},{3,1},{4,6},{5,7},{6,4},{7,5},{8,10},{9,11},{10,... | collective-permute-start | bytes 884744 | tf_op jit(solution)/shard_map/ppermute | solution.py:595
  23.9 34.9 %collective-permute-start.4 = (bf16[4,144,256]{2,1,0:T(8,128)(2,1)S(1)}, bf16[4,144,256]{2,1,0:T(8,128)(2,1)S(1)}, u32[]{:S(2)}, u32[]{:S(2)}) collective-permute-start(bf16[4,144,256]{2,1,0:T(8,128)(2,1)S(1)} %get-tuple-element.53), channel_id=1, source_target_pairs={{0,3},{1,2},{2,1},{3,0},{4,7},{5,6},{6,5},{7,4},{8,11},{9,10},{10,... | collective-permute-start | bytes 884744 | tf_op jit(solution)/shard_map/ppermute | solution.py:595
  24.1 20.7 %collective-permute-start.8 = (bf16[2,144,256]{2,1,0:T(8,128)(2,1)S(1)}, bf16[2,144,256]{2,1,0:T(8,128)(2,1)S(1)}, u32[]{:S(2)}, u32[]{:S(2)}) collective-permute-start(bf16[2,144,256]{2,1,0:T(8,128)(2,1)S(1)} %get-tuple-element.60), channel_id=1, source_target_pairs={{0,12},{1,13},{2,14},{3,15},{4,8},{5,9},{6,10},{7,11},{8,4},{9,5},... | collective-permute-start | bytes 442376 | tf_op jit(solution)/shard_map/ppermute | solution.py:595
  27.6 17.2 %collective-permute-start.9 = (bf16[2,144,256]{2,1,0:T(8,128)(2,1)S(1)}, bf16[2,144,256]{2,1,0:T(8,128)(2,1)S(1)}, u32[]{:S(2)}, u32[]{:S(2)}) collective-permute-start(bf16[2,144,256]{2,1,0:T(8,128)(2,1)S(1)} %get-tuple-element.61), channel_id=1, source_target_pairs={{0,8},{1,9},{2,10},{3,11},{4,12},{5,13},{6,14},{7,15},{8,0},{9,1},... | collective-permute-start | bytes 442376 | tf_op jit(solution)/shard_map/ppermute | solution.py:595
  27.6 17.2 %collective-permute-start.10 = (bf16[2,144,256]{2,1,0:T(8,128)(2,1)S(1)}, bf16[2,144,256]{2,1,0:T(8,128)(2,1)S(1)}, u32[]{:S(2)}, u32[]{:S(2)}) collective-permute-start(bf16[2,144,256]{2,1,0:T(8,128)(2,1)S(1)} %get-tuple-element.62), channel_id=1, source_target_pairs={{0,4},{1,5},{2,6},{3,7},{4,0},{5,1},{6,2},{7,3},{8,12},{9,13},{10,... | collective-permute-start | bytes 442376 | tf_op jit(solution)/shard_map/ppermute | solution.py:595
  54.3 14.8 %collective-permute-start.11 = (bf16[48,1152]{1,0:T(8,128)(2,1)S(1)}, bf16[48,1152]{1,0:T(8,128)(2,1)S(1)}, u32[]{:S(2)}, u32[]{:S(2)}) collective-permute-start(bf16[48,1152]{1,0:T(8,128)(2,1)S(1)} %get-tuple-element.72), channel_id=1, source_target_pairs={{0,12},{1,13},{2,14},{3,15},{4,8},{5,9},{6,10},{7,11},{8,4},{9,5},... | collective-permute-start | bytes 331784 | tf_op jit(solution)/shard_map/ppermute | solution.py:595
  56.8 12.3 %collective-permute-start.12 = (bf16[48,1152]{1,0:T(8,128)(2,1)S(1)}, bf16[48,1152]{1,0:T(8,128)(2,1)S(1)}, u32[]{:S(2)}, u32[]{:S(2)}) collective-permute-start(bf16[48,1152]{1,0:T(8,128)(2,1)S(1)} %get-tuple-element.73), channel_id=1, source_target_pairs={{0,8},{1,9},{2,10},{3,11},{4,12},{5,13},{6,14},{7,15},{8,0},{9,1},... | collective-permute-start | bytes 331784 | tf_op jit(solution)/shard_map/ppermute | solution.py:595
  56.8 12.3 %collective-permute-start.13 = (bf16[48,1152]{1,0:T(8,128)(2,1)S(1)}, bf16[48,1152]{1,0:T(8,128)(2,1)S(1)}, u32[]{:S(2)}, u32[]{:S(2)}) collective-permute-start(bf16[48,1152]{1,0:T(8,128)(2,1)S(1)} %get-tuple-element.74), channel_id=1, source_target_pairs={{0,4},{1,5},{2,6},{3,7},{4,0},{5,1},{6,2},{7,3},{8,12},{9,13},{10,... | collective-permute-start | bytes 331784 | tf_op jit(solution)/shard_map/ppermute | solution.py:595
  69.3 8.2 %collective-permute-start.14 = (bf16[4,48,512]{2,1,0:T(8,128)(2,1)S(1)}, bf16[4,48,512]{2,1,0:T(8,128)(2,1)S(1)}, u32[]{:S(2)}, u32[]{:S(2)}) collective-permute-start(bf16[4,48,512]{2,1,0:T(8,128)(2,1)S(1)} %get-tuple-element.75), channel_id=1, source_target_pairs={{0,2},{1,3},{2,0},{3,1},{4,6},{5,7},{6,4},{7,5},{8,10},{9,11},{10,... | collective-permute-start | bytes 589832 | tf_op jit(solution)/shard_map/ppermute | solution.py:595
  69.3 8.1 %collective-permute-start.15 = (bf16[4,48,512]{2,1,0:T(8,128)(2,1)S(1)}, bf16[4,48,512]{2,1,0:T(8,128)(2,1)S(1)}, u32[]{:S(2)}, u32[]{:S(2)}) collective-permute-start(bf16[4,48,512]{2,1,0:T(8,128)(2,1)S(1)} %get-tuple-element.76.refs_9_), channel_id=1, source_target_pairs={{0,3},{1,2},{2,1},{3,0},{4,7},{5,6},{6,5},{7,4},{8,11},{9,10},{10,... | collective-permute-start | bytes 589832 | tf_op jit(solution)/shard_map/ppermute | solution.py:595
  75.2 3.3 %copy-start.2 = (bf16[768,768]{1,0:T(8,128)(2,1)S(1)}, bf16[768,768]{1,0:T(8,128)(2,1)}, u32[]{:S(2)}) copy-start(bf16[768,768]{1,0:T(8,128)(2,1)} %refs_4_.1) | copy-start | bytes 3538948
  75.3 3.2 %collective-permute-start.16 = (bf16[4,48,512]{2,1,0:T(8,128)(2,1)S(1)}, bf16[4,48,512]{2,1,0:T(8,128)(2,1)S(1)}, u32[]{:S(2)}, u32[]{:S(2)}) collective-permute-start(bf16[4,48,512]{2,1,0:T(8,128)(2,1)S(1)} %get-tuple-element.84), channel_id=1, source_target_pairs={{0,1},{1,0},{2,3},{3,2},{4,5},{5,4},{6,7},{7,6},{8,9},{9,8},{10,11... | collective-permute-start | bytes 589832 | tf_op jit(solution)/shard_map/ppermute | solution.py:595

commit v5 on v4

--- a/solution.py
+++ b/solution.py
@@ -306,7 +306,7 @@
             jnp.where(lane_slot == 1, jnp.where(same, 0.0, 1.0), 0.0),
         ]
 
-    def run(plain, heads):
+    def run(heads):
         again = [counted_again(h) for h in heads]
         flat = [
             (h, again_h, query, low, merge, out, i)
@@ -324,27 +324,59 @@
         scores = score(flat[0])
         for n, (h, again_h, (_, half), low, merge, out, i) in enumerate(flat):
             following = score(flat[n + 1]) if n + 1 < len(flat) else None
-            best = jnp.zeros((1, HALF), F32) if plain else column_max(scores)
+            best = column_max(scores)
             if merge is not None:
                 acc_in, max_in = old[merge[0]]
                 old_max = max_in[h, merge[1], 0:1, :]
-                best = best if plain else jnp.maximum(best, old_max)
+                best = jnp.maximum(best, old_max)
             acc = None
             for (label, rows), block in zip(chunks[low:], scores):
                 block = block * SCALE
                 if half == 0 and label is not None:
                     block = block - (best - again_h[label])
-                elif not plain:
+                else:
                     block = block - best
                 part = dot(v_s[h, :, rows], jnp.exp2(block).astype(BF16))
                 acc = part if acc is None else acc + part
             if merge is not None:
-                before = acc_in[h, merge[1]]
-                acc = acc + (before if plain else before * jnp.exp2(old_max - best))
+                acc = acc + acc_in[h, merge[1]] * jnp.exp2(old_max - best)
             acc_ref, max_ref = outs[2 * out : 2 * out + 2]
             acc_ref[h, i] = acc
             max_ref[h, i] = jnp.broadcast_to(best, (8, HALF))
             scores = following
+
+    def run_plain():
+        again = [counted_again(h) for h in range(step)]
+        steps = [
+            (h, query, merge, out, i, c, c == low, c == len(chunks) - 1)
+            for h in range(step)
+            for out, group in enumerate(tasks)
+            for i, (query, low, merge) in enumerate(group)
+            for c in range(low, len(chunks))
+        ]
+
+        def score(item):
+            h, (j, half), c = item[0], item[1], item[5]
+            ref, lane = lookup(j, 2 * half)
+            return dot(k_s[h, chunks[c][1], :], ref[h, 2 * DH :, lane : lane + HALF])
+
+        block = score(steps[0])
+        acc = None
+        for n, (h, (_, half), merge, out, i, c, begins, ends) in enumerate(steps):
+            following = score(steps[n + 1]) if n + 1 < len(steps) else None
+            label, rows = chunks[c]
+            block = block * SCALE
+            if half == 0 and label is not None:
+                block = block + again[h][label]
+            part = dot(v_s[h, :, rows], jnp.exp2(block).astype(BF16))
+            acc = part if begins else acc + part
+            if ends:
+                if merge is not None:
+                    acc = acc + old[merge[0]][0][h, merge[1]]
+                acc_ref, max_ref = outs[2 * out : 2 * out + 2]
+                acc_ref[h, i] = acc
+                max_ref[h, i] = jnp.zeros((8, HALF), F32)
+            block = following
 
     for h in range(step):
         prepare(h)
@@ -357,13 +389,13 @@
 
     @pl.when(plain)
     def _():
-        run(True, list(range(step)))
+        run_plain()
 
     @pl.when(jnp.logical_not(plain))
     def _():
         @pl.loop(0, step)
         def _(h):
-            run(False, [h])
+            run([h])
 
 
 def far_slots(place):
@@ -399,7 +431,29 @@
     ]
     far_pieces((index, mid, top), sources, k_s, v_s, q_s)
 
-    def run(plain):
+    def run_plain():
+        steps = [(level, d) for level in range(2) for d in range(1, RATE)]
+
+        def segment(s, carry):
+            def score(item):
+                level, d = item
+                return dot(k_s[level, s ^ d], q_s[level, s])
+
+            block = score(steps[0])
+            acc = None
+            for n, (level, d) in enumerate(steps):
+                following = score(steps[n + 1]) if n + 1 < len(steps) else None
+                part = dot(v_s[level, s ^ d], jnp.exp2(block * SCALE).astype(BF16))
+                acc = part if d == 1 else acc + part
+                if d == RATE - 1:
+                    acc_ref[level, s] = acc
+                    max_ref[level, s] = jnp.zeros((8, HALF), F32)
+                block = following
+            return carry
+
+        lax.fori_loop(0, RATE, segment, 0, unroll=2)
+
+    def run():
         def segment(s, carry):
             def score(level):
                 return [dot(k_s[level, s ^ d], q_s[level, s]) for d in range(1, RATE)]
@@ -407,11 +461,10 @@
             scores = score(0)
             for level in range(2):
                 following = score(1) if level == 0 else None
-                best = jnp.zeros((1, HALF), F32) if plain else column_max(scores)
+                best = column_max(scores)
                 acc = None
                 for d in range(1, RATE):
-                    block = scores[d - 1] * SCALE
-                    block = block if plain else block - best
+                    block = scores[d - 1] * SCALE - best
                     part = dot(v_s[level, s ^ d], jnp.exp2(block).astype(BF16))
                     acc = part if acc is None else acc + part
                 acc_ref[level, s] = acc
@@ -419,14 +472,14 @@
                 scores = following
             return carry
 
-        lax.fori_loop(0, RATE, segment, 0, unroll=2 if plain else 1)
+        lax.fori_loop(0, RATE, segment, 0)
 
     query_length, key_length = far_lengths(sources)
     length_ref[0] = query_length
     length_ref[1] = key_length
     plain = is_small(query_length, key_length)
-    pl.when(plain)(lambda: run(True))
-    pl.when(jnp.logical_not(plain))(lambda: run(False))
+    pl.when(plain)(run_plain)
+    pl.when(jnp.logical_not(plain))(run)
 
 
 def far_kernel(index, mid, top, *refs):
@@ -443,61 +496,82 @@
     far_pieces(place, sources, k_s, v_s, q_s)
     tail_s[...] = jnp.zeros(tail_s.shape, F32)
 
-    def run(plain):
-        tasks = [(level, chip) for level in range(2) for chip in range(2)]
-        held = ((k_own, v_own, q_own), (k_s, v_s, q_s))
-
+    tasks = [(level, chip) for level in range(2) for chip in range(2)]
+    held = ((k_own, v_own, q_own), (k_s, v_s, q_s))
+
+    def blocks(s, chip):
+        return [(held[c], s ^ d) for d in range(1, RATE) for c in ((1,), (0, 1))[chip]]
+
+    def finish(s, level, chip, acc, best):
+        total = acc[DH : DH + 1, :]
+        result = (acc[0:DH, :] / total).astype(BF16)
+        lse = best + jnp.log2(total)
+        if level == 0:
+            lse = jnp.where(same, lse + 1.0, lse)
+        else:
+            lse = jnp.where(same, -1e30, lse)
+        high = lse.astype(BF16).astype(F32)
+        middle = (lse - high).astype(BF16).astype(F32)
+        low = lse - high - middle
+        for i in range(2):
+            n = 2 * (2 * chip + i) + level
+            mine = slice(i * BLK, (i + 1) * BLK)
+            result_s[s, :, n * BLK : (n + 1) * BLK] = result[:, mine]
+            for k, part in enumerate((high, middle, low)):
+                tail_s[s, 3 * n + k : 3 * n + k + 1, :] = part[:, mine]
+
+    def run_plain():
         def segment(s, carry):
-            def blocks(chip):
-                return [(held[c], s ^ d) for d in range(1, RATE) for c in ((1,), (0, 1))[chip]]
-
-            def score(task):
-                level, chip = task
-                query = held[chip][2][level, s]
-                return [dot(keys[0][level, b], query) for keys, b in blocks(chip)]
-
-            scores = score(tasks[0])
-            for n, (level, chip) in enumerate(tasks):
-                following = score(tasks[n + 1]) if n + 1 < len(tasks) else None
-                best = jnp.zeros((1, HALF), F32) if plain else column_max(scores)
-                acc = None
+            steps = [
+                (level, chip, keys, b, n)
+                for level, chip in tasks
+                for n, (keys, b) in enumerate(blocks(s, chip))
+            ]
+
+            def score(item):
+                level, chip, keys, b, _ = item
+                return dot(keys[0][level, b], held[chip][2][level, s])
+
+            block = score(steps[0])
+            acc = None
+            for m, (level, chip, keys, b, n) in enumerate(steps):
+                following = score(steps[m + 1]) if m + 1 < len(steps) else None
+                part = dot(keys[1][level, b], jnp.exp2(block * SCALE).astype(BF16))
+                acc = acc + part if n else part
+                if n + 1 == len(blocks(s, chip)):
+                    if chip == 0:
+                        acc = acc + acc_in[level, s]
+                    finish(s, level, chip, acc, jnp.zeros((1, HALF), F32))
+                block = following
+            return carry
+
+        lax.fori_loop(0, RATE, segment, 0, unroll=2)
+
+    def run():
+        def segment(s, carry):
+            for level, chip in tasks:
+                scores = [
+                    dot(keys[0][level, b], held[chip][2][level, s]) for keys, b in blocks(s, chip)
+                ]
+                best = column_max(scores)
+                acc = jnp.zeros((DX, HALF), F32)
                 if chip == 0:
-                    acc = acc_in[level, s]
-                    if not plain:
-                        old_max = max_in[level, s, 0:1, :]
-                        best = jnp.maximum(best, old_max)
-                        acc = acc * jnp.exp2(old_max - best)
-                for block, (keys, b) in zip(scores, blocks(chip)):
-                    block = block * SCALE if plain else block * SCALE - best
-                    part = dot(keys[1][level, b], jnp.exp2(block).astype(BF16))
-                    acc = part if acc is None else acc + part
-                total = acc[DH : DH + 1, :]
-                result = (acc[0:DH, :] / total).astype(BF16)
-                lse = best + jnp.log2(total)
-                if level == 0:
-                    lse = jnp.where(same, lse + 1.0, lse)
-                else:
-                    lse = jnp.where(same, -1e30, lse)
-                high = lse.astype(BF16).astype(F32)
-                middle = (lse - high).astype(BF16).astype(F32)
-                low = lse - high - middle
-                for i in range(2):
-                    n = 2 * (2 * chip + i) + level
-                    mine = slice(i * BLK, (i + 1) * BLK)
-                    result_s[s, :, n * BLK : (n + 1) * BLK] = result[:, mine]
-                    for k, part in enumerate((high, middle, low)):
-                        tail_s[s, 3 * n + k : 3 * n + k + 1, :] = part[:, mine]
-                scores = following
+                    old_max = max_in[level, s, 0:1, :]
+                    best = jnp.maximum(best, old_max)
+                    acc = acc_in[level, s] * jnp.exp2(old_max - best)
+                for block, (keys, b) in zip(scores, blocks(s, chip)):
+                    acc += dot(keys[1][level, b], jnp.exp2(block * SCALE - best).astype(BF16))
+                finish(s, level, chip, acc, best)
             return carry
 
-        lax.fori_loop(0, RATE, segment, 0, unroll=2 if plain else 1)
+        lax.fori_loop(0, RATE, segment, 0)
 
     query_length, key_length = far_lengths(sources)
     plain = is_small(
         jnp.maximum(query_length, length_in[0]), jnp.maximum(key_length, length_in[1])
     )
-    pl.when(plain)(lambda: run(True))
-    pl.when(jnp.logical_not(plain))(lambda: run(False))
+    pl.when(plain)(run_plain)
+    pl.when(jnp.logical_not(plain))(run)
     for s in range(RATE):
         outs[s][:, : GROUP * HALF] = result_s[s]
         outs[s][:, GROUP * HALF :] = tail_s[s].astype(BF16)

time: 81.7 us -> 83.6 us (1.023)
  Pallas kernels: 57.9 us -> 59.8 us
    pallas_call x13, Pallas kernels: 57.9 us -> 59.8 us  [call(): pl.pallas_call(body if extra else kernel, grid_spec=pltpu.PrefetchScalarG...]
  transfers between devices with their start and end apart: 17 -> 17, of which waited for: 1 -> 1; matrix products, arithmetic and copies ran while one was open for 0% -> 0% of each run, Pallas kernels for 61% -> 62%
where the time goes in v5:
time: 83.6 us; the launch traced here: 83.3 us
  Pallas kernels  59.8 us (72%)
  starting transfers between devices  21.1 us (25%)
  waiting for transfers between devices  1.11 us (1%)
  local copies, waits for them, and re-layouts  1.09 us (1%)
    pallas_call x13, Pallas kernels, call(): pl.pallas_call(body if extra else kernel, grid_spec=pltpu.PrefetchScalarG...  59.8 us
    ppermute x17, starting transfers between devices, within(): return lax.ppermute(array, 'seq', [(i, i ^ apart) for i in range(count)])  21.1 us
  transfers between devices with their start and end apart: 17, of which 1 were waited for; matrix products, arithmetic and copies ran while one was open for 0% of the time, Pallas kernels for 62%

profile of v5, /device:TPU:0, one launch (start us, length us, event | category | flops | bytes accessed | tf_op | source)
XLA Modules:
  0.0 83.3 jit_solution(11706122884253272089)
XLA Ops:
  0.0 5.2 %shard_map.64 = (bf16[4,144,512]{2,1,0:T(8,128)(2,1)}, bf16[4,144,512]{2,1,0:T(8,128)(2,1)}, bf16[4,144,256]{2,1,0:T(8,128)(2,1)}, bf16[4,144,256]{2,1,0:T(8,128...) custom-call(s32[1]{0:T(128)} %bitcast.index.refs_0_, s32[16]{0:T(128)} %mid.7, s32[16]{0:T(128)} %top.7, ...), custom_call_target="tpu_custom_call" | custom-call | tf_op jit(solution)/shard_map/pallas_call | solution.py:646
  5.2 0.0 copy-start.5
  5.2 0.0 copy-start.6
  5.3 0.5 collective-permute-start
  5.8 2.6 %collective-permute-start.1 = (bf16[4,144,256]{2,1,0:T(8,128)(2,1)}, bf16[4,144,256]{2,1,0:T(8,128)(2,1)S(1)}, u32[]{:S(2)}, u32[]{:S(2)}) collective-permute-start(bf16[4,144,256]{2,1,0:T(8,128)(2,1)} %get-tuple-element.47), channel_id=1, source_target_pairs={{0,2},{1,3},{2,0},{3,1},{4,6},{5,7},{6,4},{7,5},{8,10},{9,11},{10,... | collective-permute-start | bytes 884744 | tf_op jit(solution)/shard_map/ppermute | solution.py:669
  8.3 0.1 collective-permute-start.2
  8.4 0.0 collective-permute-done.refs_1_.b_ref.refs_4_.refs_6_
  8.4 1.1 %copy-done = bf16[4,144,512]{2,1,0:T(8,128)(2,1)S(1)} copy-done((bf16[4,144,512]{2,1,0:T(8,128)(2,1)S(1)}, bf16[4,144,512]{2,1,0:T(8,128)(2,1)}, u32[]{:S(2)}) %copy-start) | copy-done | bytes 589848
  9.5 4.2 %collective-permute-start.5 = (bf16[2,144,256]{2,1,0:T(8,128)(2,1)S(1)}, bf16[2,144,256]{2,1,0:T(8,128)(2,1)S(1)}, u32[]{:S(2)}, u32[]{:S(2)}) collective-permute-start(bf16[2,144,256]{2,1,0:T(8,128)(2,1)S(1)} %get-tuple-element.55), channel_id=1, source_target_pairs={{0,12},{1,13},{2,14},{3,15},{4,8},{5,9},{6,10},{7,11},{8,4},{9,5},... | collective-permute-start | bytes 442376 | tf_op jit(solution)/shard_map/ppermute | solution.py:669
  13.8 0.0 collective-permute-start.6
  13.8 0.6 collective-permute-start.7
  14.4 8.7 %shard_map.65 = (f32[4,4,64,256]{3,2,1,0:T(8,128)S(1)}, f32[4,4,8,256]{3,2,1,0:T(8,128)S(1)}) custom-call(s32[1]{0:T(128)} %bitcast.index.refs_0_, s32[16]{0:T(128)S(1)} %copy-done.5, s32[16]{0:T(128)S(1)} %copy-done.6, bf16[4,144,512]{2,1,0:T(8,128)(2,1)S(1)} %copy-done.1, bf16[4,144,512]{2,1,0:T(8,128)(2,1)S(1)} %collective-permute-done.refs_1_.b_ref.refs_4_.refs_6_), custom_call_target="tpu_custom_call" | custom-call | tf_op jit(solution)/shard_map/pallas_call | solution.py:646
  23.1 0.0 collective-permute-done.1.refs_0_.refs_5_
  23.2 0.7 collective-permute-start.3
  23.9 0.3 collective-permute-start.4
  24.2 3.5 %collective-permute-start.8 = (bf16[2,144,256]{2,1,0:T(8,128)(2,1)S(1)}, bf16[2,144,256]{2,1,0:T(8,128)(2,1)S(1)}, u32[]{:S(2)}, u32[]{:S(2)}) collective-permute-start(bf16[2,144,256]{2,1,0:T(8,128)(2,1)S(1)} %get-tuple-element.60), channel_id=1, source_target_pairs={{0,12},{1,13},{2,14},{3,15},{4,8},{5,9},{6,10},{7,11},{8,4},{9,5},... | collective-permute-start | bytes 442376 | tf_op jit(solution)/shard_map/ppermute | solution.py:669
  27.7 1.9 %collective-permute-start.10 = (bf16[2,144,256]{2,1,0:T(8,128)(2,1)S(1)}, bf16[2,144,256]{2,1,0:T(8,128)(2,1)S(1)}, u32[]{:S(2)}, u32[]{:S(2)}) collective-permute-start(bf16[2,144,256]{2,1,0:T(8,128)(2,1)S(1)} %get-tuple-element.62), channel_id=1, source_target_pairs={{0,4},{1,5},{2,6},{3,7},{4,0},{5,1},{6,2},{7,3},{8,12},{9,13},{10,... | collective-permute-start | bytes 442376 | tf_op jit(solution)/shard_map/ppermute | solution.py:669
  29.6 10.0 %shard_map.68 = (f32[4,4,64,256]{3,2,1,0:T(8,128)S(1)}, f32[4,4,8,256]{3,2,1,0:T(8,128)S(1)}, f32[4,2,64,256]{3,2,1,0:T(8,128)S(1)}, f32[4,2,8,256]{3,2,1,0:T(8,128)S(1)}) custom-call(s32[1]{0:T(128)} %bitcast.index.refs_0_, s32[16]{0:T(128)S(1)} %copy-done.5, s32[16]{0:T(128)S(1)} %copy-done.6, bf16[4,144,512]{2,1,0:T(8,128)(2,1)S(1)} %copy-done.1, ...), custom_call_target="tpu_custom_call" | custom-call | tf_op jit(solution)/shard_map/pallas_call | solution.py:646
  39.6 5.0 %shard_map.69 = (bf16[2,4,256,48]{3,2,1,0:T(8,128)(2,1)S(1)}, bf16[2,4,64,256]{3,2,1,0:T(8,128)(2,1)S(1)}, bf16[2,4,48,256]{3,2,1,0:T(8,128)(2,1)S(1)}, f32[2,4,...) custom-call(s32[1]{0:T(128)} %bitcast.index.refs_0_, s32[16]{0:T(128)S(1)} %copy-done.5, ...), custom_call_target="tpu_custom_call" | custom-call | tf_op jit(solution)/shard_map/pallas_call | solution.py:646
  44.7 11.4 %shard_map.70 = (bf16[48,1152]{1,0:T(8,128)(2,1)S(1)}, bf16[48,1152]{1,0:T(8,128)(2,1)S(1)}, bf16[48,1152]{1,0:T(8,128)(2,1)S(1)}, bf16[48,1152]{1,0:T(8,128)(2,1)S(1)}) custom-call(s32[1]{0:T(128)} %bitcast.index.refs_0_, s32[16]{0:T(128)S(1)} %copy-done.5, s32[16]{0:T(128)S(1)} %copy-done.6, ...), custom_call_target="tpu_custom_call" | custom-call | tf_op jit(solution)/shard_map/pallas_call | solution.py:646
  56.1 2.6 %collective-permute-start.11 = (bf16[48,1152]{1,0:T(8,128)(2,1)S(1)}, bf16[48,1152]{1,0:T(8,128)(2,1)S(1)}, u32[]{:S(2)}, u32[]{:S(2)}) collective-permute-start(bf16[48,1152]{1,0:T(8,128)(2,1)S(1)} %get-tuple-element.72), channel_id=1, source_target_pairs={{0,12},{1,13},{2,14},{3,15},{4,8},{5,9},{6,10},{7,11},{8,4},{9,5},... | collective-permute-start | bytes 331784 | tf_op jit(solution)/shard_map/ppermute | solution.py:669
  58.7 1.9 %collective-permute-start.13 = (bf16[48,1152]{1,0:T(8,128)(2,1)S(1)}, bf16[48,1152]{1,0:T(8,128)(2,1)S(1)}, u32[]{:S(2)}, u32[]{:S(2)}) collective-permute-start(bf16[48,1152]{1,0:T(8,128)(2,1)S(1)} %get-tuple-element.74), channel_id=1, source_target_pairs={{0,4},{1,5},{2,6},{3,7},{4,0},{5,1},{6,2},{7,3},{8,12},{9,13},{10,... | collective-permute-start | bytes 331784 | tf_op jit(solution)/shard_map/ppermute | solution.py:669
  60.6 10.3 %shard_map.71 = (f32[4,4,64,256]{3,2,1,0:T(8,128)S(1)}, f32[4,4,8,256]{3,2,1,0:T(8,128)S(1)}) custom-call(s32[1]{0:T(128)} %bitcast.index.refs_0_, s32[16]{0:T(128)S(1)} %copy-done.5, s32[16]{0:T(128)S(1)} %copy-done.6, bf16[4,144,512]{2,1,0:T(8,128)(2,1)S(1)} %copy-done.1, bf16[4,144,512]{2,1,0:T(8,128)(2,1)S(1)} %collective-permute-done.refs_1_.b_ref.refs_4_.refs_6_, ...), custom_call_target="tpu_custom_call" | custom-call | tf_op jit(solution)/shard_map/pallas_call | solution.py:646
  70.9 0.1 shard_map.72
  71.1 0.1 collective-permute-start.14
  71.1 0.2 collective-permute-start.15
  71.3 5.7 %shard_map.74 = (f32[4,4,64,256]{3,2,1,0:T(8,128)S(1)}, f32[4,4,8,256]{3,2,1,0:T(8,128)S(1)}) custom-call(s32[1]{0:T(128)} %bitcast.index.refs_0_, s32[16]{0:T(128)S(1)} %copy-done.5, s32[16]{0:T(128)S(1)} %copy-done.6, bf16[4,144,256]{2,1,0:T(8,128)(2,1)S(1)} %collective-permute-done.3.refs_7_.refs_3_, ...), custom_call_target="tpu_custom_call" | custom-call | tf_op jit(solution)/shard_map/pallas_call | solution.py:646
  77.1 0.0 copy-start.2
  77.1 0.1 shard_map.75
  77.3 2.0 %collective-permute-start.16 = (bf16[4,48,512]{2,1,0:T(8,128)(2,1)S(1)}, bf16[4,48,512]{2,1,0:T(8,128)(2,1)S(1)}, u32[]{:S(2)}, u32[]{:S(2)}) collective-permute-start(bf16[4,48,512]{2,1,0:T(8,128)(2,1)S(1)} %get-tuple-element.84), channel_id=1, source_target_pairs={{0,1},{1,0},{2,3},{3,2},{4,5},{5,4},{6,7},{7,6},{8,9},{9,8},{10,11... | collective-permute-start | bytes 589832 | tf_op jit(solution)/shard_map/ppermute | solution.py:669
  79.3 1.1 %collective-permute-done.16.refs_3_ = bf16[4,48,512]{2,1,0:T(8,128)(2,1)S(1)} collective-permute-done((bf16[4,48,512]{2,1,0:T(8,128)(2,1)S(1)}, bf16[4,48,512]{2,1,0:T(8,128)(2,1)S(1)}, u32[]{:S(2)}, u32[]{:S(2)}) %collective-permute-start.16) | collective-permute-done | bytes 196640 | tf_op jit(solution)/shard_map/ppermute | solution.py:669
  80.3 3.0 %shard_map.76 = bf16[512,768]{1,0:T(8,128)(2,1)} custom-call(s32[1]{0:T(128)} %bitcast.index.refs_0_, s32[16]{0:T(128)S(1)} %copy-done.5, s32[16]{0:T(128)S(1)} %copy-done.6, bf16[4,48,512]{2,1,0:T(8,128)(2,1)S(1)} %get-tuple-element.77.refs_0_, bf16[4,48,512]{2,1,0:T(8,128)(2,1)S(1)} %get-tuple-element.78.refs_1_, ...), custom_call_target="tpu_custom_call" | custom-call | tf_op jit(solution)/shard_map/pallas_call | solution.py:646
  (29 shorter events, 0.1 us)
Async XLA Ops:
  5.2 9.2 %copy-start.5 = (s32[16]{0:T(128)S(1)}, s32[16]{0:T(128)}, u32[]{:S(2)}) copy-start(s32[16]{0:T(128)} %mid.7) | copy-start | bytes 196
  5.2 9.2 %copy-start.6 = (s32[16]{0:T(128)S(1)}, s32[16]{0:T(128)}, u32[]{:S(2)}) copy-start(s32[16]{0:T(128)} %top.7) | copy-start | bytes 196
  5.3 3.2 %collective-permute-start = (bf16[4,144,512]{2,1,0:T(8,128)(2,1)}, bf16[4,144,512]{2,1,0:T(8,128)(2,1)S(1)}, u32[]{:S(2)}, u32[]{:S(2)}) collective-permute-start(bf16[4,144,512]{2,1,0:T(8,128)(2,1)} %get-tuple-element.46), channel_id=1, source_target_pairs={{0,1},{1,0},{2,3},{3,2},{4,5},{5,4},{6,7},{7,6},{8,9},{9,8},{10,11... | collective-permute-start | bytes 1769480 | tf_op jit(solution)/shard_map/ppermute | solution.py:669
  5.8 17.4 %collective-permute-start.1 = (bf16[4,144,256]{2,1,0:T(8,128)(2,1)}, bf16[4,144,256]{2,1,0:T(8,128)(2,1)S(1)}, u32[]{:S(2)}, u32[]{:S(2)}) collective-permute-start(bf16[4,144,256]{2,1,0:T(8,128)(2,1)} %get-tuple-element.47), channel_id=1, source_target_pairs={{0,2},{1,3},{2,0},{3,1},{4,6},{5,7},{6,4},{7,5},{8,10},{9,11},{10,... | collective-permute-start | bytes 884744 | tf_op jit(solution)/shard_map/ppermute | solution.py:669
  8.3 14.8 %collective-permute-start.2 = (bf16[4,144,256]{2,1,0:T(8,128)(2,1)}, bf16[4,144,256]{2,1,0:T(8,128)(2,1)S(1)}, u32[]{:S(2)}, u32[]{:S(2)}) collective-permute-start(bf16[4,144,256]{2,1,0:T(8,128)(2,1)} %get-tuple-element.48), channel_id=1, source_target_pairs={{0,3},{1,2},{2,1},{3,0},{4,7},{5,6},{6,5},{7,4},{8,11},{9,10},{10,... | collective-permute-start | bytes 884744 | tf_op jit(solution)/shard_map/ppermute | solution.py:669
  8.4 1.1 %copy-start = (bf16[4,144,512]{2,1,0:T(8,128)(2,1)S(1)}, bf16[4,144,512]{2,1,0:T(8,128)(2,1)}, u32[]{:S(2)}) copy-start(bf16[4,144,512]{2,1,0:T(8,128)(2,1)} %get-tuple-element.45.refs_0_.a_ref.refs_3_.refs_5_) | copy-start | bytes 1769476
  9.5 4.9 %copy-start.1 = (bf16[4,144,512]{2,1,0:T(8,128)(2,1)S(1)}, bf16[4,144,512]{2,1,0:T(8,128)(2,1)}, u32[]{:S(2)}) copy-start(bf16[4,144,512]{2,1,0:T(8,128)(2,1)} %get-tuple-element.45.refs_0_.a_ref.refs_3_.refs_5_) | copy-start | bytes 1769476
  9.5 13.7 %copy-start.3 = (bf16[4,144,256]{2,1,0:T(8,128)(2,1)S(1)}, bf16[4,144,256]{2,1,0:T(8,128)(2,1)}, u32[]{:S(2)}) copy-start(bf16[4,144,256]{2,1,0:T(8,128)(2,1)} %get-tuple-element.50.refs_3_) | copy-start | bytes 884740
  9.5 13.7 %copy-start.4 = (bf16[4,144,256]{2,1,0:T(8,128)(2,1)S(1)}, bf16[4,144,256]{2,1,0:T(8,128)(2,1)}, u32[]{:S(2)}) copy-start(bf16[4,144,256]{2,1,0:T(8,128)(2,1)} %get-tuple-element.51.refs_4_) | copy-start | bytes 884740
  9.5 14.7 %collective-permute-start.5 = (bf16[2,144,256]{2,1,0:T(8,128)(2,1)S(1)}, bf16[2,144,256]{2,1,0:T(8,128)(2,1)S(1)}, u32[]{:S(2)}, u32[]{:S(2)}) collective-permute-start(bf16[2,144,256]{2,1,0:T(8,128)(2,1)S(1)} %get-tuple-element.55), channel_id=1, source_target_pairs={{0,12},{1,13},{2,14},{3,15},{4,8},{5,9},{6,10},{7,11},{8,4},{9,5},... | collective-permute-start | bytes 442376 | tf_op jit(solution)/shard_map/ppermute | solution.py:669
  13.8 13.9 %collective-permute-start.6 = (bf16[2,144,256]{2,1,0:T(8,128)(2,1)S(1)}, bf16[2,144,256]{2,1,0:T(8,128)(2,1)S(1)}, u32[]{:S(2)}, u32[]{:S(2)}) collective-permute-start(bf16[2,144,256]{2,1,0:T(8,128)(2,1)S(1)} %get-tuple-element.56), channel_id=1, source_target_pairs={{0,8},{1,9},{2,10},{3,11},{4,12},{5,13},{6,14},{7,15},{8,0},{9,1},... | collective-permute-start | bytes 442376 | tf_op jit(solution)/shard_map/ppermute | solution.py:669
  13.8 13.9 %collective-permute-start.7 = (bf16[2,144,256]{2,1,0:T(8,128)(2,1)S(1)}, bf16[2,144,256]{2,1,0:T(8,128)(2,1)S(1)}, u32[]{:S(2)}, u32[]{:S(2)}) collective-permute-start(bf16[2,144,256]{2,1,0:T(8,128)(2,1)S(1)} %get-tuple-element.57), channel_id=1, source_target_pairs={{0,4},{1,5},{2,6},{3,7},{4,0},{5,1},{6,2},{7,3},{8,12},{9,13},{10,... | collective-permute-start | bytes 442376 | tf_op jit(solution)/shard_map/ppermute | solution.py:669
  23.2 37.4 %collective-permute-start.3 = (bf16[4,144,256]{2,1,0:T(8,128)(2,1)S(1)}, bf16[4,144,256]{2,1,0:T(8,128)(2,1)S(1)}, u32[]{:S(2)}, u32[]{:S(2)}) collective-permute-start(bf16[4,144,256]{2,1,0:T(8,128)(2,1)S(1)} %get-tuple-element.52), channel_id=1, source_target_pairs={{0,2},{1,3},{2,0},{3,1},{4,6},{5,7},{6,4},{7,5},{8,10},{9,11},{10,... | collective-permute-start | bytes 884744 | tf_op jit(solution)/shard_map/ppermute | solution.py:669
  23.9 36.7 %collective-permute-start.4 = (bf16[4,144,256]{2,1,0:T(8,128)(2,1)S(1)}, bf16[4,144,256]{2,1,0:T(8,128)(2,1)S(1)}, u32[]{:S(2)}, u32[]{:S(2)}) collective-permute-start(bf16[4,144,256]{2,1,0:T(8,128)(2,1)S(1)} %get-tuple-element.53), channel_id=1, source_target_pairs={{0,3},{1,2},{2,1},{3,0},{4,7},{5,6},{6,5},{7,4},{8,11},{9,10},{10,... | collective-permute-start | bytes 884744 | tf_op jit(solution)/shard_map/ppermute | solution.py:669
  24.2 20.5 %collective-permute-start.8 = (bf16[2,144,256]{2,1,0:T(8,128)(2,1)S(1)}, bf16[2,144,256]{2,1,0:T(8,128)(2,1)S(1)}, u32[]{:S(2)}, u32[]{:S(2)}) collective-permute-start(bf16[2,144,256]{2,1,0:T(8,128)(2,1)S(1)} %get-tuple-element.60), channel_id=1, source_target_pairs={{0,12},{1,13},{2,14},{3,15},{4,8},{5,9},{6,10},{7,11},{8,4},{9,5},... | collective-permute-start | bytes 442376 | tf_op jit(solution)/shard_map/ppermute | solution.py:669
  27.7 17.0 %collective-permute-start.9 = (bf16[2,144,256]{2,1,0:T(8,128)(2,1)S(1)}, bf16[2,144,256]{2,1,0:T(8,128)(2,1)S(1)}, u32[]{:S(2)}, u32[]{:S(2)}) collective-permute-start(bf16[2,144,256]{2,1,0:T(8,128)(2,1)S(1)} %get-tuple-element.61), channel_id=1, source_target_pairs={{0,8},{1,9},{2,10},{3,11},{4,12},{5,13},{6,14},{7,15},{8,0},{9,1},... | collective-permute-start | bytes 442376 | tf_op jit(solution)/shard_map/ppermute | solution.py:669
  27.7 17.0 %collective-permute-start.10 = (bf16[2,144,256]{2,1,0:T(8,128)(2,1)S(1)}, bf16[2,144,256]{2,1,0:T(8,128)(2,1)S(1)}, u32[]{:S(2)}, u32[]{:S(2)}) collective-permute-start(bf16[2,144,256]{2,1,0:T(8,128)(2,1)S(1)} %get-tuple-element.62), channel_id=1, source_target_pairs={{0,4},{1,5},{2,6},{3,7},{4,0},{5,1},{6,2},{7,3},{8,12},{9,13},{10,... | collective-permute-start | bytes 442376 | tf_op jit(solution)/shard_map/ppermute | solution.py:669
  56.1 14.8 %collective-permute-start.11 = (bf16[48,1152]{1,0:T(8,128)(2,1)S(1)}, bf16[48,1152]{1,0:T(8,128)(2,1)S(1)}, u32[]{:S(2)}, u32[]{:S(2)}) collective-permute-start(bf16[48,1152]{1,0:T(8,128)(2,1)S(1)} %get-tuple-element.72), channel_id=1, source_target_pairs={{0,12},{1,13},{2,14},{3,15},{4,8},{5,9},{6,10},{7,11},{8,4},{9,5},... | collective-permute-start | bytes 331784 | tf_op jit(solution)/shard_map/ppermute | solution.py:669
  58.7 12.2 %collective-permute-start.12 = (bf16[48,1152]{1,0:T(8,128)(2,1)S(1)}, bf16[48,1152]{1,0:T(8,128)(2,1)S(1)}, u32[]{:S(2)}, u32[]{:S(2)}) collective-permute-start(bf16[48,1152]{1,0:T(8,128)(2,1)S(1)} %get-tuple-element.73), channel_id=1, source_target_pairs={{0,8},{1,9},{2,10},{3,11},{4,12},{5,13},{6,14},{7,15},{8,0},{9,1},... | collective-permute-start | bytes 331784 | tf_op jit(solution)/shard_map/ppermute | solution.py:669
  58.7 12.2 %collective-permute-start.13 = (bf16[48,1152]{1,0:T(8,128)(2,1)S(1)}, bf16[48,1152]{1,0:T(8,128)(2,1)S(1)}, u32[]{:S(2)}, u32[]{:S(2)}) collective-permute-start(bf16[48,1152]{1,0:T(8,128)(2,1)S(1)} %get-tuple-element.74), channel_id=1, source_target_pairs={{0,4},{1,5},{2,6},{3,7},{4,0},{5,1},{6,2},{7,3},{8,12},{9,13},{10,... | collective-permute-start | bytes 331784 | tf_op jit(solution)/shard_map/ppermute | solution.py:669
  71.1 8.2 %collective-permute-start.14 = (bf16[4,48,512]{2,1,0:T(8,128)(2,1)S(1)}, bf16[4,48,512]{2,1,0:T(8,128)(2,1)S(1)}, u32[]{:S(2)}, u32[]{:S(2)}) collective-permute-start(bf16[4,48,512]{2,1,0:T(8,128)(2,1)S(1)} %get-tuple-element.75), channel_id=1, source_target_pairs={{0,2},{1,3},{2,0},{3,1},{4,6},{5,7},{6,4},{7,5},{8,10},{9,11},{10,... | collective-permute-start | bytes 589832 | tf_op jit(solution)/shard_map/ppermute | solution.py:669
  71.1 8.1 %collective-permute-start.15 = (bf16[4,48,512]{2,1,0:T(8,128)(2,1)S(1)}, bf16[4,48,512]{2,1,0:T(8,128)(2,1)S(1)}, u32[]{:S(2)}, u32[]{:S(2)}) collective-permute-start(bf16[4,48,512]{2,1,0:T(8,128)(2,1)S(1)} %get-tuple-element.76.refs_9_), channel_id=1, source_target_pairs={{0,3},{1,2},{2,1},{3,0},{4,7},{5,6},{6,5},{7,4},{8,11},{9,10},{10,... | collective-permute-start | bytes 589832 | tf_op jit(solution)/shard_map/ppermute | solution.py:669
  77.1 3.3 %copy-start.2 = (bf16[768,768]{1,0:T(8,128)(2,1)S(1)}, bf16[768,768]{1,0:T(8,128)(2,1)}, u32[]{:S(2)}) copy-start(bf16[768,768]{1,0:T(8,128)(2,1)} %refs_4_.1) | copy-start | bytes 3538948
  77.3 3.1 %collective-permute-start.16 = (bf16[4,48,512]{2,1,0:T(8,128)(2,1)S(1)}, bf16[4,48,512]{2,1,0:T(8,128)(2,1)S(1)}, u32[]{:S(2)}, u32[]{:S(2)}) collective-permute-start(bf16[4,48,512]{2,1,0:T(8,128)(2,1)S(1)} %get-tuple-element.84), channel_id=1, source_target_pairs={{0,1},{1,0},{2,3},{3,2},{4,5},{5,4},{6,7},{7,6},{8,9},{9,8},{10,11... | collective-permute-start | bytes 589832 | tf_op jit(solution)/shard_map/ppermute | solution.py:669

commit v6 on v5

--- a/solution.py
+++ b/solution.py
@@ -151,6 +151,7 @@
 HALF = 2 * BLK
 TOK = 512
 SCALE = DH**-0.5 * LOG2E
+AHEAD = 4
 SAFE = 96.0
 CHUNKS = ((0, 4),)
 DX = 64
@@ -270,6 +271,17 @@
     return best * SCALE
 
 
+def in_stages(items, score, weigh, gather):
+    scores = {n: score(item) for n, item in enumerate(items[:AHEAD])}
+    weights = weigh(items[0], scores.pop(0))
+    for n, item in enumerate(items):
+        if n + AHEAD < len(items):
+            scores[n + AHEAD] = score(items[n + AHEAD])
+        following = weigh(items[n + 1], scores.pop(n + 1)) if n + 1 < len(items) else None
+        gather(item, weights)
+        weights = following
+
+
 def near_kernel(inputs, units, tasks, carried, first, step, index, mid, top, *refs):
     place = (index, mid, top)
     pieces = dict(zip(inputs, refs[: len(inputs)]))
@@ -360,23 +372,29 @@
             ref, lane = lookup(j, 2 * half)
             return dot(k_s[h, chunks[c][1], :], ref[h, 2 * DH :, lane : lane + HALF])
 
-        block = score(steps[0])
-        acc = None
-        for n, (h, (_, half), merge, out, i, c, begins, ends) in enumerate(steps):
-            following = score(steps[n + 1]) if n + 1 < len(steps) else None
-            label, rows = chunks[c]
+        def weigh(item, block):
+            h, (_, half), c = item[0], item[1], item[5]
+            label = chunks[c][0]
             block = block * SCALE
             if half == 0 and label is not None:
                 block = block + again[h][label]
-            part = dot(v_s[h, :, rows], jnp.exp2(block).astype(BF16))
-            acc = part if begins else acc + part
+            return jnp.exp2(block).astype(BF16)
+
+        held = {}
+
+        def gather(item, weights):
+            h, _, merge, out, i, c, begins, ends = item
+            part = dot(v_s[h, :, chunks[c][1]], weights)
+            acc = part if begins else held[0] + part
             if ends:
                 if merge is not None:
                     acc = acc + old[merge[0]][0][h, merge[1]]
                 acc_ref, max_ref = outs[2 * out : 2 * out + 2]
                 acc_ref[h, i] = acc
                 max_ref[h, i] = jnp.zeros((8, HALF), F32)
-            block = following
+            held[0] = acc
+
+        in_stages(steps, score, weigh, gather)
 
     for h in range(step):
         prepare(h)
@@ -439,16 +457,20 @@
                 level, d = item
                 return dot(k_s[level, s ^ d], q_s[level, s])
 
-            block = score(steps[0])
-            acc = None
-            for n, (level, d) in enumerate(steps):
-                following = score(steps[n + 1]) if n + 1 < len(steps) else None
-                part = dot(v_s[level, s ^ d], jnp.exp2(block * SCALE).astype(BF16))
-                acc = part if d == 1 else acc + part
+            def weigh(item, block):
+                return jnp.exp2(block * SCALE).astype(BF16)
+
+            held = {}
+
+            def gather(item, weights):
+                level, d = item
+                part = dot(v_s[level, s ^ d], weights)
+                held[0] = part if d == 1 else held[0] + part
                 if d == RATE - 1:
-                    acc_ref[level, s] = acc
+                    acc_ref[level, s] = held[0]
                     max_ref[level, s] = jnp.zeros((8, HALF), F32)
-                block = following
+
+            in_stages(steps, score, weigh, gather)
             return carry
 
         lax.fori_loop(0, RATE, segment, 0, unroll=2)
@@ -532,17 +554,20 @@
                 level, chip, keys, b, _ = item
                 return dot(keys[0][level, b], held[chip][2][level, s])
 
-            block = score(steps[0])
-            acc = None
-            for m, (level, chip, keys, b, n) in enumerate(steps):
-                following = score(steps[m + 1]) if m + 1 < len(steps) else None
-                part = dot(keys[1][level, b], jnp.exp2(block * SCALE).astype(BF16))
-                acc = acc + part if n else part
+            def weigh(item, block):
+                return jnp.exp2(block * SCALE).astype(BF16)
+
+            sums = {}
+
+            def gather(item, weights):
+                level, chip, keys, b, n = item
+                part = dot(keys[1][level, b], weights)
+                sums[0] = sums[0] + part if n else part
                 if n + 1 == len(blocks(s, chip)):
-                    if chip == 0:
-                        acc = acc + acc_in[level, s]
+                    acc = sums[0] + acc_in[level, s] if chip == 0 else sums[0]
                     finish(s, level, chip, acc, jnp.zeros((1, HALF), F32))
-                block = following
+
+            in_stages(steps, score, weigh, gather)
             return carry
 
         lax.fori_loop(0, RATE, segment, 0, unroll=2)

time: 83.6 us -> 83.5 us (level)
  no operation moved by 1% of the time
where the time goes in v6:
time: 83.5 us; the launch traced here: 83.3 us
  Pallas kernels  59.6 us (71%)
  starting transfers between devices  21.2 us (25%)
  waiting for transfers between devices  1.11 us (1%)
  local copies, waits for them, and re-layouts  1.09 us (1%)
    pallas_call x13, Pallas kernels, call(): pl.pallas_call(body if extra else kernel, grid_spec=pltpu.PrefetchScalarG...  59.6 us
    ppermute x17, starting transfers between devices, within(): return lax.ppermute(array, 'seq', [(i, i ^ apart) for i in range(count)])  21.2 us
  transfers between devices with their start and end apart: 17, of which 1 were waited for; matrix products, arithmetic and copies ran while one was open for 0% of the time, Pallas kernels for 62%

profile of v6, /device:TPU:0, one launch (start us, length us, event | category | flops | bytes accessed | tf_op | source)
XLA Modules:
  0.0 83.3 jit_solution(855746314285035144)
XLA Ops:
  0.0 5.2 %shard_map.64 = (bf16[4,144,512]{2,1,0:T(8,128)(2,1)}, bf16[4,144,512]{2,1,0:T(8,128)(2,1)}, bf16[4,144,256]{2,1,0:T(8,128)(2,1)}, bf16[4,144,256]{2,1,0:T(8,128...) custom-call(s32[1]{0:T(128)} %bitcast.index.refs_0_, s32[16]{0:T(128)} %mid.7, s32[16]{0:T(128)} %top.7, ...), custom_call_target="tpu_custom_call" | custom-call | tf_op jit(solution)/shard_map/pallas_call | solution.py:671
  5.2 0.0 copy-start.5
  5.2 0.0 copy-start.6
  5.3 0.5 collective-permute-start
  5.8 2.6 %collective-permute-start.1 = (bf16[4,144,256]{2,1,0:T(8,128)(2,1)}, bf16[4,144,256]{2,1,0:T(8,128)(2,1)S(1)}, u32[]{:S(2)}, u32[]{:S(2)}) collective-permute-start(bf16[4,144,256]{2,1,0:T(8,128)(2,1)} %get-tuple-element.47), channel_id=1, source_target_pairs={{0,2},{1,3},{2,0},{3,1},{4,6},{5,7},{6,4},{7,5},{8,10},{9,11},{10,... | collective-permute-start | bytes 884744 | tf_op jit(solution)/shard_map/ppermute | solution.py:694
  8.3 0.1 collective-permute-start.2
  8.4 0.0 collective-permute-done.refs_1_.b_ref.refs_4_.refs_6_
  8.4 1.1 %copy-done = bf16[4,144,512]{2,1,0:T(8,128)(2,1)S(1)} copy-done((bf16[4,144,512]{2,1,0:T(8,128)(2,1)S(1)}, bf16[4,144,512]{2,1,0:T(8,128)(2,1)}, u32[]{:S(2)}) %copy-start) | copy-done | bytes 589848
  9.5 4.2 %collective-permute-start.5 = (bf16[2,144,256]{2,1,0:T(8,128)(2,1)S(1)}, bf16[2,144,256]{2,1,0:T(8,128)(2,1)S(1)}, u32[]{:S(2)}, u32[]{:S(2)}) collective-permute-start(bf16[2,144,256]{2,1,0:T(8,128)(2,1)S(1)} %get-tuple-element.55), channel_id=1, source_target_pairs={{0,12},{1,13},{2,14},{3,15},{4,8},{5,9},{6,10},{7,11},{8,4},{9,5},... | collective-permute-start | bytes 442376 | tf_op jit(solution)/shard_map/ppermute | solution.py:694
  13.8 0.0 collective-permute-start.6
  13.8 0.6 collective-permute-start.7
  14.4 8.6 %shard_map.65 = (f32[4,4,64,256]{3,2,1,0:T(8,128)S(1)}, f32[4,4,8,256]{3,2,1,0:T(8,128)S(1)}) custom-call(s32[1]{0:T(128)} %bitcast.index.refs_0_, s32[16]{0:T(128)S(1)} %copy-done.5, s32[16]{0:T(128)S(1)} %copy-done.6, bf16[4,144,512]{2,1,0:T(8,128)(2,1)S(1)} %copy-done.1, bf16[4,144,512]{2,1,0:T(8,128)(2,1)S(1)} %collective-permute-done.refs_1_.b_ref.refs_4_.refs_6_), custom_call_target="tpu_custom_call" | custom-call | tf_op jit(solution)/shard_map/pallas_call | solution.py:671
  23.0 0.0 collective-permute-done.1.refs_0_.refs_5_
  23.1 0.8 collective-permute-start.3
  23.9 0.2 collective-permute-start.4
  24.1 3.6 %collective-permute-start.8 = (bf16[2,144,256]{2,1,0:T(8,128)(2,1)S(1)}, bf16[2,144,256]{2,1,0:T(8,128)(2,1)S(1)}, u32[]{:S(2)}, u32[]{:S(2)}) collective-permute-start(bf16[2,144,256]{2,1,0:T(8,128)(2,1)S(1)} %get-tuple-element.60), channel_id=1, source_target_pairs={{0,12},{1,13},{2,14},{3,15},{4,8},{5,9},{6,10},{7,11},{8,4},{9,5},... | collective-permute-start | bytes 442376 | tf_op jit(solution)/shard_map/ppermute | solution.py:694
  27.6 2.0 %collective-permute-start.10 = (bf16[2,144,256]{2,1,0:T(8,128)(2,1)S(1)}, bf16[2,144,256]{2,1,0:T(8,128)(2,1)S(1)}, u32[]{:S(2)}, u32[]{:S(2)}) collective-permute-start(bf16[2,144,256]{2,1,0:T(8,128)(2,1)S(1)} %get-tuple-element.62), channel_id=1, source_target_pairs={{0,4},{1,5},{2,6},{3,7},{4,0},{5,1},{6,2},{7,3},{8,12},{9,13},{10,... | collective-permute-start | bytes 442376 | tf_op jit(solution)/shard_map/ppermute | solution.py:694
  29.6 10.1 %shard_map.68 = (f32[4,4,64,256]{3,2,1,0:T(8,128)S(1)}, f32[4,4,8,256]{3,2,1,0:T(8,128)S(1)}, f32[4,2,64,256]{3,2,1,0:T(8,128)S(1)}, f32[4,2,8,256]{3,2,1,0:T(8,128)S(1)}) custom-call(s32[1]{0:T(128)} %bitcast.index.refs_0_, s32[16]{0:T(128)S(1)} %copy-done.5, s32[16]{0:T(128)S(1)} %copy-done.6, bf16[4,144,512]{2,1,0:T(8,128)(2,1)S(1)} %copy-done.1, ...), custom_call_target="tpu_custom_call" | custom-call | tf_op jit(solution)/shard_map/pallas_call | solution.py:671
  39.6 5.2 %shard_map.69 = (bf16[2,4,256,48]{3,2,1,0:T(8,128)(2,1)S(1)}, bf16[2,4,64,256]{3,2,1,0:T(8,128)(2,1)S(1)}, bf16[2,4,48,256]{3,2,1,0:T(8,128)(2,1)S(1)}, f32[2,4,...) custom-call(s32[1]{0:T(128)} %bitcast.index.refs_0_, s32[16]{0:T(128)S(1)} %copy-done.5, ...), custom_call_target="tpu_custom_call" | custom-call | tf_op jit(solution)/shard_map/pallas_call | solution.py:671
  44.9 11.2 %shard_map.70 = (bf16[48,1152]{1,0:T(8,128)(2,1)S(1)}, bf16[48,1152]{1,0:T(8,128)(2,1)S(1)}, bf16[48,1152]{1,0:T(8,128)(2,1)S(1)}, bf16[48,1152]{1,0:T(8,128)(2,1)S(1)}) custom-call(s32[1]{0:T(128)} %bitcast.index.refs_0_, s32[16]{0:T(128)S(1)} %copy-done.5, s32[16]{0:T(128)S(1)} %copy-done.6, ...), custom_call_target="tpu_custom_call" | custom-call | tf_op jit(solution)/shard_map/pallas_call | solution.py:671
  56.1 2.5 %collective-permute-start.11 = (bf16[48,1152]{1,0:T(8,128)(2,1)S(1)}, bf16[48,1152]{1,0:T(8,128)(2,1)S(1)}, u32[]{:S(2)}, u32[]{:S(2)}) collective-permute-start(bf16[48,1152]{1,0:T(8,128)(2,1)S(1)} %get-tuple-element.72), channel_id=1, source_target_pairs={{0,12},{1,13},{2,14},{3,15},{4,8},{5,9},{6,10},{7,11},{8,4},{9,5},... | collective-permute-start | bytes 331784 | tf_op jit(solution)/shard_map/ppermute | solution.py:694
  58.6 2.0 %collective-permute-start.13 = (bf16[48,1152]{1,0:T(8,128)(2,1)S(1)}, bf16[48,1152]{1,0:T(8,128)(2,1)S(1)}, u32[]{:S(2)}, u32[]{:S(2)}) collective-permute-start(bf16[48,1152]{1,0:T(8,128)(2,1)S(1)} %get-tuple-element.74), channel_id=1, source_target_pairs={{0,4},{1,5},{2,6},{3,7},{4,0},{5,1},{6,2},{7,3},{8,12},{9,13},{10,... | collective-permute-start | bytes 331784 | tf_op jit(solution)/shard_map/ppermute | solution.py:694
  60.5 10.3 %shard_map.71 = (f32[4,4,64,256]{3,2,1,0:T(8,128)S(1)}, f32[4,4,8,256]{3,2,1,0:T(8,128)S(1)}) custom-call(s32[1]{0:T(128)} %bitcast.index.refs_0_, s32[16]{0:T(128)S(1)} %copy-done.5, s32[16]{0:T(128)S(1)} %copy-done.6, bf16[4,144,512]{2,1,0:T(8,128)(2,1)S(1)} %copy-done.1, bf16[4,144,512]{2,1,0:T(8,128)(2,1)S(1)} %collective-permute-done.refs_1_.b_ref.refs_4_.refs_6_, ...), custom_call_target="tpu_custom_call" | custom-call | tf_op jit(solution)/shard_map/pallas_call | solution.py:671
  70.9 0.1 shard_map.72
  71.0 0.1 collective-permute-start.14
  71.1 0.1 collective-permute-start.15
  71.2 5.8 %shard_map.74 = (f32[4,4,64,256]{3,2,1,0:T(8,128)S(1)}, f32[4,4,8,256]{3,2,1,0:T(8,128)S(1)}) custom-call(s32[1]{0:T(128)} %bitcast.index.refs_0_, s32[16]{0:T(128)S(1)} %copy-done.5, s32[16]{0:T(128)S(1)} %copy-done.6, bf16[4,144,256]{2,1,0:T(8,128)(2,1)S(1)} %collective-permute-done.3.refs_7_.refs_3_, ...), custom_call_target="tpu_custom_call" | custom-call | tf_op jit(solution)/shard_map/pallas_call | solution.py:671
  77.0 0.0 copy-start.2
  77.0 0.1 shard_map.75
  77.1 2.1 %collective-permute-start.16 = (bf16[4,48,512]{2,1,0:T(8,128)(2,1)S(1)}, bf16[4,48,512]{2,1,0:T(8,128)(2,1)S(1)}, u32[]{:S(2)}, u32[]{:S(2)}) collective-permute-start(bf16[4,48,512]{2,1,0:T(8,128)(2,1)S(1)} %get-tuple-element.84), channel_id=1, source_target_pairs={{0,1},{1,0},{2,3},{3,2},{4,5},{5,4},{6,7},{7,6},{8,9},{9,8},{10,11... | collective-permute-start | bytes 589832 | tf_op jit(solution)/shard_map/ppermute | solution.py:694
  79.2 1.1 %collective-permute-done.16.refs_3_ = bf16[4,48,512]{2,1,0:T(8,128)(2,1)S(1)} collective-permute-done((bf16[4,48,512]{2,1,0:T(8,128)(2,1)S(1)}, bf16[4,48,512]{2,1,0:T(8,128)(2,1)S(1)}, u32[]{:S(2)}, u32[]{:S(2)}) %collective-permute-start.16) | collective-permute-done | bytes 196640 | tf_op jit(solution)/shard_map/ppermute | solution.py:694
  80.3 3.0 %shard_map.76 = bf16[512,768]{1,0:T(8,128)(2,1)} custom-call(s32[1]{0:T(128)} %bitcast.index.refs_0_, s32[16]{0:T(128)S(1)} %copy-done.5, s32[16]{0:T(128)S(1)} %copy-done.6, bf16[4,48,512]{2,1,0:T(8,128)(2,1)S(1)} %get-tuple-element.77.refs_0_, bf16[4,48,512]{2,1,0:T(8,128)(2,1)S(1)} %get-tuple-element.78.refs_1_, ...), custom_call_target="tpu_custom_call" | custom-call | tf_op jit(solution)/shard_map/pallas_call | solution.py:671
  (29 shorter events, 0.1 us)
Async XLA Ops:
  5.2 9.2 %copy-start.5 = (s32[16]{0:T(128)S(1)}, s32[16]{0:T(128)}, u32[]{:S(2)}) copy-start(s32[16]{0:T(128)} %mid.7) | copy-start | bytes 196
  5.2 9.2 %copy-start.6 = (s32[16]{0:T(128)S(1)}, s32[16]{0:T(128)}, u32[]{:S(2)}) copy-start(s32[16]{0:T(128)} %top.7) | copy-start | bytes 196
  5.3 3.2 %collective-permute-start = (bf16[4,144,512]{2,1,0:T(8,128)(2,1)}, bf16[4,144,512]{2,1,0:T(8,128)(2,1)S(1)}, u32[]{:S(2)}, u32[]{:S(2)}) collective-permute-start(bf16[4,144,512]{2,1,0:T(8,128)(2,1)} %get-tuple-element.46), channel_id=1, source_target_pairs={{0,1},{1,0},{2,3},{3,2},{4,5},{5,4},{6,7},{7,6},{8,9},{9,8},{10,11... | collective-permute-start | bytes 1769480 | tf_op jit(solution)/shard_map/ppermute | solution.py:694
  5.8 17.2 %collective-permute-start.1 = (bf16[4,144,256]{2,1,0:T(8,128)(2,1)}, bf16[4,144,256]{2,1,0:T(8,128)(2,1)S(1)}, u32[]{:S(2)}, u32[]{:S(2)}) collective-permute-start(bf16[4,144,256]{2,1,0:T(8,128)(2,1)} %get-tuple-element.47), channel_id=1, source_target_pairs={{0,2},{1,3},{2,0},{3,1},{4,6},{5,7},{6,4},{7,5},{8,10},{9,11},{10,... | collective-permute-start | bytes 884744 | tf_op jit(solution)/shard_map/ppermute | solution.py:694
  8.3 14.7 %collective-permute-start.2 = (bf16[4,144,256]{2,1,0:T(8,128)(2,1)}, bf16[4,144,256]{2,1,0:T(8,128)(2,1)S(1)}, u32[]{:S(2)}, u32[]{:S(2)}) collective-permute-start(bf16[4,144,256]{2,1,0:T(8,128)(2,1)} %get-tuple-element.48), channel_id=1, source_target_pairs={{0,3},{1,2},{2,1},{3,0},{4,7},{5,6},{6,5},{7,4},{8,11},{9,10},{10,... | collective-permute-start | bytes 884744 | tf_op jit(solution)/shard_map/ppermute | solution.py:694
  8.4 1.1 %copy-start = (bf16[4,144,512]{2,1,0:T(8,128)(2,1)S(1)}, bf16[4,144,512]{2,1,0:T(8,128)(2,1)}, u32[]{:S(2)}) copy-start(bf16[4,144,512]{2,1,0:T(8,128)(2,1)} %get-tuple-element.45.refs_0_.a_ref.refs_3_.refs_5_) | copy-start | bytes 1769476
  9.5 4.9 %copy-start.1 = (bf16[4,144,512]{2,1,0:T(8,128)(2,1)S(1)}, bf16[4,144,512]{2,1,0:T(8,128)(2,1)}, u32[]{:S(2)}) copy-start(bf16[4,144,512]{2,1,0:T(8,128)(2,1)} %get-tuple-element.45.refs_0_.a_ref.refs_3_.refs_5_) | copy-start | bytes 1769476
  9.5 13.5 %copy-start.3 = (bf16[4,144,256]{2,1,0:T(8,128)(2,1)S(1)}, bf16[4,144,256]{2,1,0:T(8,128)(2,1)}, u32[]{:S(2)}) copy-start(bf16[4,144,256]{2,1,0:T(8,128)(2,1)} %get-tuple-element.50.refs_3_) | copy-start | bytes 884740
  9.5 13.5 %copy-start.4 = (bf16[4,144,256]{2,1,0:T(8,128)(2,1)S(1)}, bf16[4,144,256]{2,1,0:T(8,128)(2,1)}, u32[]{:S(2)}) copy-start(bf16[4,144,256]{2,1,0:T(8,128)(2,1)} %get-tuple-element.51.refs_4_) | copy-start | bytes 884740
  9.5 14.5 %collective-permute-start.5 = (bf16[2,144,256]{2,1,0:T(8,128)(2,1)S(1)}, bf16[2,144,256]{2,1,0:T(8,128)(2,1)S(1)}, u32[]{:S(2)}, u32[]{:S(2)}) collective-permute-start(bf16[2,144,256]{2,1,0:T(8,128)(2,1)S(1)} %get-tuple-element.55), channel_id=1, source_target_pairs={{0,12},{1,13},{2,14},{3,15},{4,8},{5,9},{6,10},{7,11},{8,4},{9,5},... | collective-permute-start | bytes 442376 | tf_op jit(solution)/shard_map/ppermute | solution.py:694
  13.8 13.9 %collective-permute-start.6 = (bf16[2,144,256]{2,1,0:T(8,128)(2,1)S(1)}, bf16[2,144,256]{2,1,0:T(8,128)(2,1)S(1)}, u32[]{:S(2)}, u32[]{:S(2)}) collective-permute-start(bf16[2,144,256]{2,1,0:T(8,128)(2,1)S(1)} %get-tuple-element.56), channel_id=1, source_target_pairs={{0,8},{1,9},{2,10},{3,11},{4,12},{5,13},{6,14},{7,15},{8,0},{9,1},... | collective-permute-start | bytes 442376 | tf_op jit(solution)/shard_map/ppermute | solution.py:694
  13.8 13.9 %collective-permute-start.7 = (bf16[2,144,256]{2,1,0:T(8,128)(2,1)S(1)}, bf16[2,144,256]{2,1,0:T(8,128)(2,1)S(1)}, u32[]{:S(2)}, u32[]{:S(2)}) collective-permute-start(bf16[2,144,256]{2,1,0:T(8,128)(2,1)S(1)} %get-tuple-element.57), channel_id=1, source_target_pairs={{0,4},{1,5},{2,6},{3,7},{4,0},{5,1},{6,2},{7,3},{8,12},{9,13},{10,... | collective-permute-start | bytes 442376 | tf_op jit(solution)/shard_map/ppermute | solution.py:694
  23.1 37.5 %collective-permute-start.3 = (bf16[4,144,256]{2,1,0:T(8,128)(2,1)S(1)}, bf16[4,144,256]{2,1,0:T(8,128)(2,1)S(1)}, u32[]{:S(2)}, u32[]{:S(2)}) collective-permute-start(bf16[4,144,256]{2,1,0:T(8,128)(2,1)S(1)} %get-tuple-element.52), channel_id=1, source_target_pairs={{0,2},{1,3},{2,0},{3,1},{4,6},{5,7},{6,4},{7,5},{8,10},{9,11},{10,... | collective-permute-start | bytes 884744 | tf_op jit(solution)/shard_map/ppermute | solution.py:694
  23.9 36.7 %collective-permute-start.4 = (bf16[4,144,256]{2,1,0:T(8,128)(2,1)S(1)}, bf16[4,144,256]{2,1,0:T(8,128)(2,1)S(1)}, u32[]{:S(2)}, u32[]{:S(2)}) collective-permute-start(bf16[4,144,256]{2,1,0:T(8,128)(2,1)S(1)} %get-tuple-element.53), channel_id=1, source_target_pairs={{0,3},{1,2},{2,1},{3,0},{4,7},{5,6},{6,5},{7,4},{8,11},{9,10},{10,... | collective-permute-start | bytes 884744 | tf_op jit(solution)/shard_map/ppermute | solution.py:694
  24.1 20.8 %collective-permute-start.8 = (bf16[2,144,256]{2,1,0:T(8,128)(2,1)S(1)}, bf16[2,144,256]{2,1,0:T(8,128)(2,1)S(1)}, u32[]{:S(2)}, u32[]{:S(2)}) collective-permute-start(bf16[2,144,256]{2,1,0:T(8,128)(2,1)S(1)} %get-tuple-element.60), channel_id=1, source_target_pairs={{0,12},{1,13},{2,14},{3,15},{4,8},{5,9},{6,10},{7,11},{8,4},{9,5},... | collective-permute-start | bytes 442376 | tf_op jit(solution)/shard_map/ppermute | solution.py:694
  27.6 17.2 %collective-permute-start.9 = (bf16[2,144,256]{2,1,0:T(8,128)(2,1)S(1)}, bf16[2,144,256]{2,1,0:T(8,128)(2,1)S(1)}, u32[]{:S(2)}, u32[]{:S(2)}) collective-permute-start(bf16[2,144,256]{2,1,0:T(8,128)(2,1)S(1)} %get-tuple-element.61), channel_id=1, source_target_pairs={{0,8},{1,9},{2,10},{3,11},{4,12},{5,13},{6,14},{7,15},{8,0},{9,1},... | collective-permute-start | bytes 442376 | tf_op jit(solution)/shard_map/ppermute | solution.py:694
  27.6 17.2 %collective-permute-start.10 = (bf16[2,144,256]{2,1,0:T(8,128)(2,1)S(1)}, bf16[2,144,256]{2,1,0:T(8,128)(2,1)S(1)}, u32[]{:S(2)}, u32[]{:S(2)}) collective-permute-start(bf16[2,144,256]{2,1,0:T(8,128)(2,1)S(1)} %get-tuple-element.62), channel_id=1, source_target_pairs={{0,4},{1,5},{2,6},{3,7},{4,0},{5,1},{6,2},{7,3},{8,12},{9,13},{10,... | collective-permute-start | bytes 442376 | tf_op jit(solution)/shard_map/ppermute | solution.py:694
  56.1 14.8 %collective-permute-start.11 = (bf16[48,1152]{1,0:T(8,128)(2,1)S(1)}, bf16[48,1152]{1,0:T(8,128)(2,1)S(1)}, u32[]{:S(2)}, u32[]{:S(2)}) collective-permute-start(bf16[48,1152]{1,0:T(8,128)(2,1)S(1)} %get-tuple-element.72), channel_id=1, source_target_pairs={{0,12},{1,13},{2,14},{3,15},{4,8},{5,9},{6,10},{7,11},{8,4},{9,5},... | collective-permute-start | bytes 331784 | tf_op jit(solution)/shard_map/ppermute | solution.py:694
  58.6 12.3 %collective-permute-start.12 = (bf16[48,1152]{1,0:T(8,128)(2,1)S(1)}, bf16[48,1152]{1,0:T(8,128)(2,1)S(1)}, u32[]{:S(2)}, u32[]{:S(2)}) collective-permute-start(bf16[48,1152]{1,0:T(8,128)(2,1)S(1)} %get-tuple-element.73), channel_id=1, source_target_pairs={{0,8},{1,9},{2,10},{3,11},{4,12},{5,13},{6,14},{7,15},{8,0},{9,1},... | collective-permute-start | bytes 331784 | tf_op jit(solution)/shard_map/ppermute | solution.py:694
  58.6 12.3 %collective-permute-start.13 = (bf16[48,1152]{1,0:T(8,128)(2,1)S(1)}, bf16[48,1152]{1,0:T(8,128)(2,1)S(1)}, u32[]{:S(2)}, u32[]{:S(2)}) collective-permute-start(bf16[48,1152]{1,0:T(8,128)(2,1)S(1)} %get-tuple-element.74), channel_id=1, source_target_pairs={{0,4},{1,5},{2,6},{3,7},{4,0},{5,1},{6,2},{7,3},{8,12},{9,13},{10,... | collective-permute-start | bytes 331784 | tf_op jit(solution)/shard_map/ppermute | solution.py:694
  71.0 8.2 %collective-permute-start.14 = (bf16[4,48,512]{2,1,0:T(8,128)(2,1)S(1)}, bf16[4,48,512]{2,1,0:T(8,128)(2,1)S(1)}, u32[]{:S(2)}, u32[]{:S(2)}) collective-permute-start(bf16[4,48,512]{2,1,0:T(8,128)(2,1)S(1)} %get-tuple-element.75), channel_id=1, source_target_pairs={{0,2},{1,3},{2,0},{3,1},{4,6},{5,7},{6,4},{7,5},{8,10},{9,11},{10,... | collective-permute-start | bytes 589832 | tf_op jit(solution)/shard_map/ppermute | solution.py:694
  71.1 8.1 %collective-permute-start.15 = (bf16[4,48,512]{2,1,0:T(8,128)(2,1)S(1)}, bf16[4,48,512]{2,1,0:T(8,128)(2,1)S(1)}, u32[]{:S(2)}, u32[]{:S(2)}) collective-permute-start(bf16[4,48,512]{2,1,0:T(8,128)(2,1)S(1)} %get-tuple-element.76.refs_9_), channel_id=1, source_target_pairs={{0,3},{1,2},{2,1},{3,0},{4,7},{5,6},{6,5},{7,4},{8,11},{9,10},{10,... | collective-permute-start | bytes 589832 | tf_op jit(solution)/shard_map/ppermute | solution.py:694
  77.0 3.3 %copy-start.2 = (bf16[768,768]{1,0:T(8,128)(2,1)S(1)}, bf16[768,768]{1,0:T(8,128)(2,1)}, u32[]{:S(2)}) copy-start(bf16[768,768]{1,0:T(8,128)(2,1)} %refs_4_.1) | copy-start | bytes 3538948
  77.1 3.2 %collective-permute-start.16 = (bf16[4,48,512]{2,1,0:T(8,128)(2,1)S(1)}, bf16[4,48,512]{2,1,0:T(8,128)(2,1)S(1)}, u32[]{:S(2)}, u32[]{:S(2)}) collective-permute-start(bf16[4,48,512]{2,1,0:T(8,128)(2,1)S(1)} %get-tuple-element.84), channel_id=1, source_target_pairs={{0,1},{1,0},{2,3},{3,2},{4,5},{5,4},{6,7},{7,6},{8,9},{9,8},{10,11... | collective-permute-start | bytes 589832 | tf_op jit(solution)/shard_map/ppermute | solution.py:694

commit v7 on v6

--- a/solution.py
+++ b/solution.py
@@ -151,6 +151,7 @@
 HALF = 2 * BLK
 TOK = 512
 SCALE = DH**-0.5 * LOG2E
+BUSY = 1 << 33
 AHEAD = 4
 SAFE = 96.0
 CHUNKS = ((0, 4),)
@@ -657,7 +658,7 @@
 
 def call(
     kernel, scalars, args, grid, in_specs, outs, scratch, scores,
-    limit=VMEM_LIMIT, after=(), through=(),
+    limit=VMEM_LIMIT, after=(), through=(), busy=0,
 ):
     known = len(scalars) + len(args)
     extra = (*after, *through)
@@ -681,7 +682,7 @@
         + [jax.ShapeDtypeStruct(x.shape, x.dtype) for x in through],
         input_output_aliases={known + len(after) + i: count + i for i in range(len(through))},
         compiler_params=pltpu.CompilerParams(vmem_limit_bytes=limit),
-        cost_estimate=pl.CostEstimate(flops=0, bytes_accessed=0, transcendentals=0),
+        cost_estimate=pl.CostEstimate(flops=busy, bytes_accessed=0, transcendentals=0),
     )(*scalars, *args, *extra)
 
 
@@ -806,7 +807,7 @@
             pltpu.VMEM((RATE, DH, GROUP * HALF), BF16),
             pltpu.VMEM((RATE, DH, BLK), F32),
         ],
-        RATE * 2 * 3 * 3 * HALF * HALF,
+        RATE * 2 * 3 * 3 * HALF * HALF, busy=BUSY,
     )
     back = [results[0]] + swap_segments(results[1:])
 

time: 83.5 us -> 84.7 us (1.014)
  waiting for transfers between devices: 1.11 us -> 3.58 us
  starting transfers between devices: 21.2 us -> 20 us
    ppermute x17, waiting for transfers between devices: 1.11 us -> 3.58 us  [within(): return lax.ppermute(array, 'seq', [(i, i ^ apart) for i in range(count)])]
    ppermute x17, starting transfers between devices: 21.2 us -> 20 us  [within(): return lax.ppermute(array, 'seq', [(i, i ^ apart) for i in range(count)])]
  transfers between devices with their start and end apart: 17 -> 17, of which waited for: 1 -> 1; matrix products, arithmetic and copies ran while one was open for 0% -> 0% of each run, Pallas kernels for 62% -> 61%
where the time goes in v7:
time: 84.7 us; the launch traced here: 84.5 us
  Pallas kernels  59.6 us (70%)
  starting transfers between devices  20 us (24%)
  waiting for transfers between devices  3.58 us (4%)
  local copies, waits for them, and re-layouts  1.09 us (1%)
    pallas_call x13, Pallas kernels, call(): pl.pallas_call(body if extra else kernel, grid_spec=pltpu.PrefetchScalarG...  59.6 us
    ppermute x17, starting transfers between devices, within(): return lax.ppermute(array, 'seq', [(i, i ^ apart) for i in range(count)])  20 us
    ppermute x17, waiting for transfers between devices, within(): return lax.ppermute(array, 'seq', [(i, i ^ apart) for i in range(count)])  3.58 us
  transfers between devices with their start and end apart: 17, of which 1 were waited for; matrix products, arithmetic and copies ran while one was open for 0% of the time, Pallas kernels for 61%

profile of v7, /device:TPU:0, one launch (start us, length us, event | category | flops | bytes accessed | tf_op | source)
XLA Modules:
  0.0 84.5 jit_solution(12407622331709077552)
XLA Ops:
  0.0 5.2 %shard_map.64 = (bf16[4,144,512]{2,1,0:T(8,128)(2,1)}, bf16[4,144,512]{2,1,0:T(8,128)(2,1)}, bf16[4,144,256]{2,1,0:T(8,128)(2,1)}, bf16[4,144,256]{2,1,0:T(8,128...) custom-call(s32[1]{0:T(128)} %bitcast.index.refs_0_, s32[16]{0:T(128)} %mid.7, s32[16]{0:T(128)} %top.7, ...), custom_call_target="tpu_custom_call" | custom-call | tf_op jit(solution)/shard_map/pallas_call | solution.py:672
  5.2 0.0 copy-start.5
  5.2 0.0 copy-start.6
  5.3 0.5 collective-permute-start
  5.8 2.6 %collective-permute-start.1 = (bf16[4,144,256]{2,1,0:T(8,128)(2,1)}, bf16[4,144,256]{2,1,0:T(8,128)(2,1)S(1)}, u32[]{:S(2)}, u32[]{:S(2)}) collective-permute-start(bf16[4,144,256]{2,1,0:T(8,128)(2,1)} %get-tuple-element.47), channel_id=1, source_target_pairs={{0,2},{1,3},{2,0},{3,1},{4,6},{5,7},{6,4},{7,5},{8,10},{9,11},{10,... | collective-permute-start | bytes 884744 | tf_op jit(solution)/shard_map/ppermute | solution.py:695
  8.3 0.1 collective-permute-start.2
  8.4 1.1 %copy-done = bf16[4,144,512]{2,1,0:T(8,128)(2,1)S(1)} copy-done((bf16[4,144,512]{2,1,0:T(8,128)(2,1)S(1)}, bf16[4,144,512]{2,1,0:T(8,128)(2,1)}, u32[]{:S(2)}) %copy-start) | copy-done | bytes 589848
  9.5 4.2 %collective-permute-start.5 = (bf16[2,144,256]{2,1,0:T(8,128)(2,1)S(1)}, bf16[2,144,256]{2,1,0:T(8,128)(2,1)S(1)}, u32[]{:S(2)}, u32[]{:S(2)}) collective-permute-start(bf16[2,144,256]{2,1,0:T(8,128)(2,1)S(1)} %get-tuple-element.55), channel_id=1, source_target_pairs={{0,12},{1,13},{2,14},{3,15},{4,8},{5,9},{6,10},{7,11},{8,4},{9,5},... | collective-permute-start | bytes 442376 | tf_op jit(solution)/shard_map/ppermute | solution.py:695
  13.8 0.6 collective-permute-start.7
  14.4 8.6 %shard_map.65 = (f32[4,4,64,256]{3,2,1,0:T(8,128)S(1)}, f32[4,4,8,256]{3,2,1,0:T(8,128)S(1)}) custom-call(s32[1]{0:T(128)} %bitcast.index.refs_0_, s32[16]{0:T(128)S(1)} %copy-done.5, s32[16]{0:T(128)S(1)} %copy-done.6, bf16[4,144,512]{2,1,0:T(8,128)(2,1)S(1)} %copy-done.1, bf16[4,144,512]{2,1,0:T(8,128)(2,1)S(1)} %collective-permute-done.refs_1_.b_ref.refs_4_.refs_6_), custom_call_target="tpu_custom_call" | custom-call | tf_op jit(solution)/shard_map/pallas_call | solution.py:672
  23.0 0.0 collective-permute-done.2.refs_1_.refs_6_
  23.1 3.8 %collective-permute-start.8 = (bf16[2,144,256]{2,1,0:T(8,128)(2,1)S(1)}, bf16[2,144,256]{2,1,0:T(8,128)(2,1)S(1)}, u32[]{:S(2)}, u32[]{:S(2)}) collective-permute-start(bf16[2,144,256]{2,1,0:T(8,128)(2,1)S(1)} %get-tuple-element.60), channel_id=1, source_target_pairs={{0,12},{1,13},{2,14},{3,15},{4,8},{5,9},{6,10},{7,11},{8,4},{9,5},... | collective-permute-start | bytes 442376 | tf_op jit(solution)/shard_map/ppermute | solution.py:695
  26.9 0.6 collective-permute-start.10
  27.5 0.0 collective-permute-done.6.refs_10_.refs_6_
  27.5 0.7 collective-permute-start.3
  28.3 0.0 collective-permute-done.7.refs_11_.refs_5_
  28.3 0.0 collective-permute-start.4
  28.3 10.0 %shard_map.68 = (f32[4,4,64,256]{3,2,1,0:T(8,128)S(1)}, f32[4,4,8,256]{3,2,1,0:T(8,128)S(1)}, f32[4,2,64,256]{3,2,1,0:T(8,128)S(1)}, f32[4,2,8,256]{3,2,1,0:T(8,128)S(1)}) custom-call(s32[1]{0:T(128)} %bitcast.index.refs_0_, s32[16]{0:T(128)S(1)} %copy-done.5, s32[16]{0:T(128)S(1)} %copy-done.6, bf16[4,144,512]{2,1,0:T(8,128)(2,1)S(1)} %copy-done.1, ...), custom_call_target="tpu_custom_call" | custom-call | tf_op jit(solution)/shard_map/pallas_call | solution.py:672
  38.3 5.2 %shard_map.69 = (bf16[2,4,256,48]{3,2,1,0:T(8,128)(2,1)S(1)}, bf16[2,4,64,256]{3,2,1,0:T(8,128)(2,1)S(1)}, bf16[2,4,48,256]{3,2,1,0:T(8,128)(2,1)S(1)}, f32[2,4,...) custom-call(s32[1]{0:T(128)} %bitcast.index.refs_0_, s32[16]{0:T(128)S(1)} %copy-done.5, ...), custom_call_target="tpu_custom_call" | custom-call | tf_op jit(solution)/shard_map/pallas_call | solution.py:672
  43.6 11.2 %shard_map.70 = (bf16[48,1152]{1,0:T(8,128)(2,1)S(1)}, bf16[48,1152]{1,0:T(8,128)(2,1)S(1)}, bf16[48,1152]{1,0:T(8,128)(2,1)S(1)}, bf16[48,1152]{1,0:T(8,128)(2,1)S(1)}) custom-call(s32[1]{0:T(128)} %bitcast.index.refs_0_, s32[16]{0:T(128)S(1)} %copy-done.5, s32[16]{0:T(128)S(1)} %copy-done.6, ...), custom_call_target="tpu_custom_call" | custom-call | flops 8589934592 | tf_op jit(solution)/shard_map/pallas_call | solution.py:672
  54.8 3.7 %collective-permute-start.11 = (bf16[48,1152]{1,0:T(8,128)(2,1)S(1)}, bf16[48,1152]{1,0:T(8,128)(2,1)S(1)}, u32[]{:S(2)}, u32[]{:S(2)}) collective-permute-start(bf16[48,1152]{1,0:T(8,128)(2,1)S(1)} %get-tuple-element.72), channel_id=1, source_target_pairs={{0,12},{1,13},{2,14},{3,15},{4,8},{5,9},{6,10},{7,11},{8,4},{9,5},... | collective-permute-start | bytes 331784 | tf_op jit(solution)/shard_map/ppermute | solution.py:695
  58.5 0.8 collective-permute-start.13
  59.2 10.3 %shard_map.71 = (f32[4,4,64,256]{3,2,1,0:T(8,128)S(1)}, f32[4,4,8,256]{3,2,1,0:T(8,128)S(1)}) custom-call(s32[1]{0:T(128)} %bitcast.index.refs_0_, s32[16]{0:T(128)S(1)} %copy-done.5, s32[16]{0:T(128)S(1)} %copy-done.6, bf16[4,144,512]{2,1,0:T(8,128)(2,1)S(1)} %copy-done.1, bf16[4,144,512]{2,1,0:T(8,128)(2,1)S(1)} %collective-permute-done.refs_1_.b_ref.refs_4_.refs_6_, ...), custom_call_target="tpu_custom_call" | custom-call | tf_op jit(solution)/shard_map/pallas_call | solution.py:672
  69.6 0.1 shard_map.72
  69.7 0.1 collective-permute-start.14
  69.8 2.2 %collective-permute-start.15 = (bf16[4,48,512]{2,1,0:T(8,128)(2,1)S(1)}, bf16[4,48,512]{2,1,0:T(8,128)(2,1)S(1)}, u32[]{:S(2)}, u32[]{:S(2)}) collective-permute-start(bf16[4,48,512]{2,1,0:T(8,128)(2,1)S(1)} %get-tuple-element.76.refs_9_), channel_id=1, source_target_pairs={{0,3},{1,2},{2,1},{3,0},{4,7},{5,6},{6,5},{7,4},{8,11},{9,10},{10,... | collective-permute-start | bytes 589832 | tf_op jit(solution)/shard_map/ppermute | solution.py:695
  72.0 5.8 %shard_map.74 = (f32[4,4,64,256]{3,2,1,0:T(8,128)S(1)}, f32[4,4,8,256]{3,2,1,0:T(8,128)S(1)}) custom-call(s32[1]{0:T(128)} %bitcast.index.refs_0_, s32[16]{0:T(128)S(1)} %copy-done.5, s32[16]{0:T(128)S(1)} %copy-done.6, bf16[4,144,256]{2,1,0:T(8,128)(2,1)S(1)} %collective-permute-done.3.refs_7_.refs_3_, ...), custom_call_target="tpu_custom_call" | custom-call | tf_op jit(solution)/shard_map/pallas_call | solution.py:672
  77.8 0.0 copy-start.2
  77.8 0.1 shard_map.75
  77.9 0.1 collective-permute-start.16
  78.0 3.5 %collective-permute-done.15.refs_1_ = bf16[4,48,512]{2,1,0:T(8,128)(2,1)S(1)} collective-permute-done((bf16[4,48,512]{2,1,0:T(8,128)(2,1)S(1)}, bf16[4,48,512]{2,1,0:T(8,128)(2,1)S(1)}, u32[]{:S(2)}, u32[]{:S(2)}) %collective-permute-start.15) | collective-permute-done | bytes 196640 | tf_op jit(solution)/shard_map/ppermute | solution.py:695
  81.6 3.0 %shard_map.76 = bf16[512,768]{1,0:T(8,128)(2,1)} custom-call(s32[1]{0:T(128)} %bitcast.index.refs_0_, s32[16]{0:T(128)S(1)} %copy-done.5, s32[16]{0:T(128)S(1)} %copy-done.6, bf16[4,48,512]{2,1,0:T(8,128)(2,1)S(1)} %get-tuple-element.77.refs_0_, bf16[4,48,512]{2,1,0:T(8,128)(2,1)S(1)} %get-tuple-element.78.refs_1_, ...), custom_call_target="tpu_custom_call" | custom-call | tf_op jit(solution)/shard_map/pallas_call | solution.py:672
  (29 shorter events, 0.1 us)
Async XLA Ops:
  5.2 9.2 %copy-start.5 = (s32[16]{0:T(128)S(1)}, s32[16]{0:T(128)}, u32[]{:S(2)}) copy-start(s32[16]{0:T(128)} %mid.7) | copy-start | bytes 196
  5.2 9.2 %copy-start.6 = (s32[16]{0:T(128)S(1)}, s32[16]{0:T(128)}, u32[]{:S(2)}) copy-start(s32[16]{0:T(128)} %top.7) | copy-start | bytes 196
  5.3 3.2 %collective-permute-start = (bf16[4,144,512]{2,1,0:T(8,128)(2,1)}, bf16[4,144,512]{2,1,0:T(8,128)(2,1)S(1)}, u32[]{:S(2)}, u32[]{:S(2)}) collective-permute-start(bf16[4,144,512]{2,1,0:T(8,128)(2,1)} %get-tuple-element.46), channel_id=1, source_target_pairs={{0,1},{1,0},{2,3},{3,2},{4,5},{5,4},{6,7},{7,6},{8,9},{9,8},{10,11... | collective-permute-start | bytes 1769480 | tf_op jit(solution)/shard_map/ppermute | solution.py:695
  5.8 17.2 %collective-permute-start.1 = (bf16[4,144,256]{2,1,0:T(8,128)(2,1)}, bf16[4,144,256]{2,1,0:T(8,128)(2,1)S(1)}, u32[]{:S(2)}, u32[]{:S(2)}) collective-permute-start(bf16[4,144,256]{2,1,0:T(8,128)(2,1)} %get-tuple-element.47), channel_id=1, source_target_pairs={{0,2},{1,3},{2,0},{3,1},{4,6},{5,7},{6,4},{7,5},{8,10},{9,11},{10,... | collective-permute-start | bytes 884744 | tf_op jit(solution)/shard_map/ppermute | solution.py:695
  8.3 14.7 %collective-permute-start.2 = (bf16[4,144,256]{2,1,0:T(8,128)(2,1)}, bf16[4,144,256]{2,1,0:T(8,128)(2,1)S(1)}, u32[]{:S(2)}, u32[]{:S(2)}) collective-permute-start(bf16[4,144,256]{2,1,0:T(8,128)(2,1)} %get-tuple-element.48), channel_id=1, source_target_pairs={{0,3},{1,2},{2,1},{3,0},{4,7},{5,6},{6,5},{7,4},{8,11},{9,10},{10,... | collective-permute-start | bytes 884744 | tf_op jit(solution)/shard_map/ppermute | solution.py:695
  8.4 1.1 %copy-start = (bf16[4,144,512]{2,1,0:T(8,128)(2,1)S(1)}, bf16[4,144,512]{2,1,0:T(8,128)(2,1)}, u32[]{:S(2)}) copy-start(bf16[4,144,512]{2,1,0:T(8,128)(2,1)} %get-tuple-element.45.refs_0_.a_ref.refs_3_.refs_5_) | copy-start | bytes 1769476
  9.5 4.9 %copy-start.1 = (bf16[4,144,512]{2,1,0:T(8,128)(2,1)S(1)}, bf16[4,144,512]{2,1,0:T(8,128)(2,1)}, u32[]{:S(2)}) copy-start(bf16[4,144,512]{2,1,0:T(8,128)(2,1)} %get-tuple-element.45.refs_0_.a_ref.refs_3_.refs_5_) | copy-start | bytes 1769476
  9.5 13.5 %copy-start.3 = (bf16[4,144,256]{2,1,0:T(8,128)(2,1)S(1)}, bf16[4,144,256]{2,1,0:T(8,128)(2,1)}, u32[]{:S(2)}) copy-start(bf16[4,144,256]{2,1,0:T(8,128)(2,1)} %get-tuple-element.50.refs_3_) | copy-start | bytes 884740
  9.5 13.5 %copy-start.4 = (bf16[4,144,256]{2,1,0:T(8,128)(2,1)S(1)}, bf16[4,144,256]{2,1,0:T(8,128)(2,1)}, u32[]{:S(2)}) copy-start(bf16[4,144,256]{2,1,0:T(8,128)(2,1)} %get-tuple-element.51.refs_4_) | copy-start | bytes 884740
  9.5 17.4 %collective-permute-start.5 = (bf16[2,144,256]{2,1,0:T(8,128)(2,1)S(1)}, bf16[2,144,256]{2,1,0:T(8,128)(2,1)S(1)}, u32[]{:S(2)}, u32[]{:S(2)}) collective-permute-start(bf16[2,144,256]{2,1,0:T(8,128)(2,1)S(1)} %get-tuple-element.55), channel_id=1, source_target_pairs={{0,12},{1,13},{2,14},{3,15},{4,8},{5,9},{6,10},{7,11},{8,4},{9,5},... | collective-permute-start | bytes 442376 | tf_op jit(solution)/shard_map/ppermute | solution.py:695
  13.8 13.8 %collective-permute-start.6 = (bf16[2,144,256]{2,1,0:T(8,128)(2,1)S(1)}, bf16[2,144,256]{2,1,0:T(8,128)(2,1)S(1)}, u32[]{:S(2)}, u32[]{:S(2)}) collective-permute-start(bf16[2,144,256]{2,1,0:T(8,128)(2,1)S(1)} %get-tuple-element.56), channel_id=1, source_target_pairs={{0,8},{1,9},{2,10},{3,11},{4,12},{5,13},{6,14},{7,15},{8,0},{9,1},... | collective-permute-start | bytes 442376 | tf_op jit(solution)/shard_map/ppermute | solution.py:695
  13.8 14.5 %collective-permute-start.7 = (bf16[2,144,256]{2,1,0:T(8,128)(2,1)S(1)}, bf16[2,144,256]{2,1,0:T(8,128)(2,1)S(1)}, u32[]{:S(2)}, u32[]{:S(2)}) collective-permute-start(bf16[2,144,256]{2,1,0:T(8,128)(2,1)S(1)} %get-tuple-element.57), channel_id=1, source_target_pairs={{0,4},{1,5},{2,6},{3,7},{4,0},{5,1},{6,2},{7,3},{8,12},{9,13},{10,... | collective-permute-start | bytes 442376 | tf_op jit(solution)/shard_map/ppermute | solution.py:695
  23.1 20.5 %collective-permute-start.8 = (bf16[2,144,256]{2,1,0:T(8,128)(2,1)S(1)}, bf16[2,144,256]{2,1,0:T(8,128)(2,1)S(1)}, u32[]{:S(2)}, u32[]{:S(2)}) collective-permute-start(bf16[2,144,256]{2,1,0:T(8,128)(2,1)S(1)} %get-tuple-element.60), channel_id=1, source_target_pairs={{0,12},{1,13},{2,14},{3,15},{4,8},{5,9},{6,10},{7,11},{8,4},{9,5},... | collective-permute-start | bytes 442376 | tf_op jit(solution)/shard_map/ppermute | solution.py:695
  26.9 16.7 %collective-permute-start.9 = (bf16[2,144,256]{2,1,0:T(8,128)(2,1)S(1)}, bf16[2,144,256]{2,1,0:T(8,128)(2,1)S(1)}, u32[]{:S(2)}, u32[]{:S(2)}) collective-permute-start(bf16[2,144,256]{2,1,0:T(8,128)(2,1)S(1)} %get-tuple-element.61), channel_id=1, source_target_pairs={{0,8},{1,9},{2,10},{3,11},{4,12},{5,13},{6,14},{7,15},{8,0},{9,1},... | collective-permute-start | bytes 442376 | tf_op jit(solution)/shard_map/ppermute | solution.py:695
  26.9 16.7 %collective-permute-start.10 = (bf16[2,144,256]{2,1,0:T(8,128)(2,1)S(1)}, bf16[2,144,256]{2,1,0:T(8,128)(2,1)S(1)}, u32[]{:S(2)}, u32[]{:S(2)}) collective-permute-start(bf16[2,144,256]{2,1,0:T(8,128)(2,1)S(1)} %get-tuple-element.62), channel_id=1, source_target_pairs={{0,4},{1,5},{2,6},{3,7},{4,0},{5,1},{6,2},{7,3},{8,12},{9,13},{10,... | collective-permute-start | bytes 442376 | tf_op jit(solution)/shard_map/ppermute | solution.py:695
  27.5 31.7 %collective-permute-start.3 = (bf16[4,144,256]{2,1,0:T(8,128)(2,1)S(1)}, bf16[4,144,256]{2,1,0:T(8,128)(2,1)S(1)}, u32[]{:S(2)}, u32[]{:S(2)}) collective-permute-start(bf16[4,144,256]{2,1,0:T(8,128)(2,1)S(1)} %get-tuple-element.52), channel_id=1, source_target_pairs={{0,2},{1,3},{2,0},{3,1},{4,6},{5,7},{6,4},{7,5},{8,10},{9,11},{10,... | collective-permute-start | bytes 884744 | tf_op jit(solution)/shard_map/ppermute | solution.py:695
  28.3 31.0 %collective-permute-start.4 = (bf16[4,144,256]{2,1,0:T(8,128)(2,1)S(1)}, bf16[4,144,256]{2,1,0:T(8,128)(2,1)S(1)}, u32[]{:S(2)}, u32[]{:S(2)}) collective-permute-start(bf16[4,144,256]{2,1,0:T(8,128)(2,1)S(1)} %get-tuple-element.53), channel_id=1, source_target_pairs={{0,3},{1,2},{2,1},{3,0},{4,7},{5,6},{6,5},{7,4},{8,11},{9,10},{10,... | collective-permute-start | bytes 884744 | tf_op jit(solution)/shard_map/ppermute | solution.py:695
  54.8 14.8 %collective-permute-start.11 = (bf16[48,1152]{1,0:T(8,128)(2,1)S(1)}, bf16[48,1152]{1,0:T(8,128)(2,1)S(1)}, u32[]{:S(2)}, u32[]{:S(2)}) collective-permute-start(bf16[48,1152]{1,0:T(8,128)(2,1)S(1)} %get-tuple-element.72), channel_id=1, source_target_pairs={{0,12},{1,13},{2,14},{3,15},{4,8},{5,9},{6,10},{7,11},{8,4},{9,5},... | collective-permute-start | bytes 331784 | tf_op jit(solution)/shard_map/ppermute | solution.py:695
  58.4 11.1 %collective-permute-start.12 = (bf16[48,1152]{1,0:T(8,128)(2,1)S(1)}, bf16[48,1152]{1,0:T(8,128)(2,1)S(1)}, u32[]{:S(2)}, u32[]{:S(2)}) collective-permute-start(bf16[48,1152]{1,0:T(8,128)(2,1)S(1)} %get-tuple-element.73), channel_id=1, source_target_pairs={{0,8},{1,9},{2,10},{3,11},{4,12},{5,13},{6,14},{7,15},{8,0},{9,1},... | collective-permute-start | bytes 331784 | tf_op jit(solution)/shard_map/ppermute | solution.py:695
  58.5 11.1 %collective-permute-start.13 = (bf16[48,1152]{1,0:T(8,128)(2,1)S(1)}, bf16[48,1152]{1,0:T(8,128)(2,1)S(1)}, u32[]{:S(2)}, u32[]{:S(2)}) collective-permute-start(bf16[48,1152]{1,0:T(8,128)(2,1)S(1)} %get-tuple-element.74), channel_id=1, source_target_pairs={{0,4},{1,5},{2,6},{3,7},{4,0},{5,1},{6,2},{7,3},{8,12},{9,13},{10,... | collective-permute-start | bytes 331784 | tf_op jit(solution)/shard_map/ppermute | solution.py:695
  69.7 8.3 %collective-permute-start.14 = (bf16[4,48,512]{2,1,0:T(8,128)(2,1)S(1)}, bf16[4,48,512]{2,1,0:T(8,128)(2,1)S(1)}, u32[]{:S(2)}, u32[]{:S(2)}) collective-permute-start(bf16[4,48,512]{2,1,0:T(8,128)(2,1)S(1)} %get-tuple-element.75), channel_id=1, source_target_pairs={{0,2},{1,3},{2,0},{3,1},{4,6},{5,7},{6,4},{7,5},{8,10},{9,11},{10,... | collective-permute-start | bytes 589832 | tf_op jit(solution)/shard_map/ppermute | solution.py:695
  69.8 11.7 %collective-permute-start.15 = (bf16[4,48,512]{2,1,0:T(8,128)(2,1)S(1)}, bf16[4,48,512]{2,1,0:T(8,128)(2,1)S(1)}, u32[]{:S(2)}, u32[]{:S(2)}) collective-permute-start(bf16[4,48,512]{2,1,0:T(8,128)(2,1)S(1)} %get-tuple-element.76.refs_9_), channel_id=1, source_target_pairs={{0,3},{1,2},{2,1},{3,0},{4,7},{5,6},{6,5},{7,4},{8,11},{9,10},{10,... | collective-permute-start | bytes 589832 | tf_op jit(solution)/shard_map/ppermute | solution.py:695
  77.8 3.8 %copy-start.2 = (bf16[768,768]{1,0:T(8,128)(2,1)S(1)}, bf16[768,768]{1,0:T(8,128)(2,1)}, u32[]{:S(2)}) copy-start(bf16[768,768]{1,0:T(8,128)(2,1)} %refs_4_.1) | copy-start | bytes 3538948
  77.9 3.6 %collective-permute-start.16 = (bf16[4,48,512]{2,1,0:T(8,128)(2,1)S(1)}, bf16[4,48,512]{2,1,0:T(8,128)(2,1)S(1)}, u32[]{:S(2)}, u32[]{:S(2)}) collective-permute-start(bf16[4,48,512]{2,1,0:T(8,128)(2,1)S(1)} %get-tuple-element.84), channel_id=1, source_target_pairs={{0,1},{1,0},{2,3},{3,2},{4,5},{5,4},{6,7},{7,6},{8,9},{9,8},{10,11... | collective-permute-start | bytes 589832 | tf_op jit(solution)/shard_map/ppermute | solution.py:695

commit v8 on v7

--- a/solution.py
+++ b/solution.py
@@ -154,7 +154,7 @@
 BUSY = 1 << 33
 AHEAD = 4
 SAFE = 96.0
-CHUNKS = ((0, 4),)
+CHUNKS = ((0, 2), (2, 2))
 DX = 64
 
 
@@ -686,8 +686,8 @@
     )(*scalars, *args, *extra)
 
 
-def handed_on(arrays):
-    return call(lambda: None, (), (), (1,), [], [], [], 0, through=tuple(arrays))
+def handed_on(arrays, **order):
+    return call(lambda: None, (), (), (1,), [], [], [], 0, through=tuple(arrays), **order)
 
 
 def within(array, apart):
@@ -825,8 +825,7 @@
             1 << 18, **order,
         )
 
-    parts = {}
-    last = results[0]
+    parts, last = {}, results[0]
     for first, heads in CHUNKS:
         state_other = near(
             held, units,
@@ -839,7 +838,11 @@
             [state_sel],
             first, heads, 2, after=(last,),
         )
-        part2, part3 = combine(1, state_other, back[first : first + heads])
+        if first:
+            back[1:] = handed_on(back[1:], after=state_other[1:])
+        part2, part3 = combine(
+            1, state_other, back[first : first + heads], after=tuple(parts.values())
+        )
         parts[2, first], parts[3, first] = within(part2, 2), within(part3, 3)
         last = part3
     state_own = near(
@@ -849,9 +852,8 @@
         [state_own],
         after=(last,),
     )
-    early = [parts[j, first] for first, _ in CHUNKS[:-1] for j in (2, 3)]
-    part0, part1 = combine(0, state_own, back, after=early)
-    parts = dict(zip(parts, handed_on(parts.values())))
+    part0, part1 = combine(0, state_own, back)
+    parts = dict(zip(parts, handed_on(parts.values(), busy=BUSY)))
     parts[0, 0], parts[1, 0] = part0, within(part1, 1)
     return call(
         functools.partial(project_kernel, list(parts)), place, (*parts.values(), out_weight), (1,),

time: 84.7 us -> 85.2 us (level)
  waiting for transfers between devices: 3.58 us -> 1.11 us
  starting transfers between devices: 20 us -> 22.1 us
    ppermute x17 -> x19, waiting for transfers between devices: 3.58 us -> 1.11 us  [within(): return lax.ppermute(array, 'seq', [(i, i ^ apart) for i in range(count)])]
    ppermute x17 -> x19, starting transfers between devices: 20 us -> 22.1 us  [within(): return lax.ppermute(array, 'seq', [(i, i ^ apart) for i in range(count)])]
    pallas_call x13 -> x16, Pallas kernels: 59.6 us -> 60.4 us  [call(): pl.pallas_call(body if extra else kernel, grid_spec=pltpu.PrefetchScalarG...]
  transfers between devices with their start and end apart: 17 -> 19, of which waited for: 1 -> 1; matrix products, arithmetic and copies ran while one was open for 0% -> 0% of each run, Pallas kernels for 61% -> 61%
where the time goes in v8:
time: 85.2 us; the launch traced here: 85 us
  Pallas kernels  60.4 us (71%)
  starting transfers between devices  22.1 us (26%)
  waiting for transfers between devices  1.11 us (1%)
  local copies, waits for them, and re-layouts  1.09 us (1%)
    pallas_call x16, Pallas kernels, call(): pl.pallas_call(body if extra else kernel, grid_spec=pltpu.PrefetchScalarG...  60.4 us
    ppermute x19, starting transfers between devices, within(): return lax.ppermute(array, 'seq', [(i, i ^ apart) for i in range(count)])  22.1 us
  transfers between devices with their start and end apart: 19, of which 1 were waited for; matrix products, arithmetic and copies ran while one was open for 0% of the time, Pallas kernels for 61%

profile of v8, /device:TPU:0, one launch (start us, length us, event | category | flops | bytes accessed | tf_op | source)
XLA Modules:
  0.0 85.0 jit_solution(16210753338368930655)
XLA Ops:
  0.0 5.3 %shard_map.64 = (bf16[4,144,512]{2,1,0:T(8,128)(2,1)}, bf16[4,144,512]{2,1,0:T(8,128)(2,1)}, bf16[4,144,256]{2,1,0:T(8,128)(2,1)}, bf16[4,144,256]{2,1,0:T(8,128...) custom-call(s32[1]{0:T(128)} %bitcast.index.refs_0_, s32[16]{0:T(128)} %mid.7, s32[16]{0:T(128)} %top.7, ...), custom_call_target="tpu_custom_call" | custom-call | tf_op jit(solution)/shard_map/pallas_call | solution.py:672
  5.3 0.0 copy-start.6
  5.3 0.5 collective-permute-start
  5.8 2.6 %collective-permute-start.1 = (bf16[4,144,256]{2,1,0:T(8,128)(2,1)}, bf16[4,144,256]{2,1,0:T(8,128)(2,1)S(1)}, u32[]{:S(2)}, u32[]{:S(2)}) collective-permute-start(bf16[4,144,256]{2,1,0:T(8,128)(2,1)} %get-tuple-element.56), channel_id=1, source_target_pairs={{0,2},{1,3},{2,0},{3,1},{4,6},{5,7},{6,4},{7,5},{8,10},{9,11},{10,... | collective-permute-start | bytes 884744 | tf_op jit(solution)/shard_map/ppermute | solution.py:695
  8.4 0.1 collective-permute-start.2
  8.4 1.1 %copy-done = bf16[4,144,512]{2,1,0:T(8,128)(2,1)S(1)} copy-done((bf16[4,144,512]{2,1,0:T(8,128)(2,1)S(1)}, bf16[4,144,512]{2,1,0:T(8,128)(2,1)}, u32[]{:S(2)}) %copy-start) | copy-done | bytes 589848
  9.5 4.2 %collective-permute-start.5 = (bf16[2,144,256]{2,1,0:T(8,128)(2,1)S(1)}, bf16[2,144,256]{2,1,0:T(8,128)(2,1)S(1)}, u32[]{:S(2)}, u32[]{:S(2)}) collective-permute-start(bf16[2,144,256]{2,1,0:T(8,128)(2,1)S(1)} %get-tuple-element.64), channel_id=1, source_target_pairs={{0,12},{1,13},{2,14},{3,15},{4,8},{5,9},{6,10},{7,11},{8,4},{9,5},... | collective-permute-start | bytes 442376 | tf_op jit(solution)/shard_map/ppermute | solution.py:695
  13.8 0.6 collective-permute-start.7
  14.4 8.6 %shard_map.65 = (f32[4,4,64,256]{3,2,1,0:T(8,128)S(1)}, f32[4,4,8,256]{3,2,1,0:T(8,128)S(1)}) custom-call(s32[1]{0:T(128)} %bitcast.index.refs_0_, s32[16]{0:T(128)S(1)} %copy-done.5, s32[16]{0:T(128)S(1)} %copy-done.6, bf16[4,144,512]{2,1,0:T(8,128)(2,1)S(1)} %copy-done.1, bf16[4,144,512]{2,1,0:T(8,128)(2,1)S(1)} %collective-permute-done.refs_1_.b_ref.refs_4_.refs_6_), custom_call_target="tpu_custom_call" | custom-call | tf_op jit(solution)/shard_map/pallas_call | solution.py:672
  23.1 3.8 %collective-permute-start.8 = (bf16[2,144,256]{2,1,0:T(8,128)(2,1)S(1)}, bf16[2,144,256]{2,1,0:T(8,128)(2,1)S(1)}, u32[]{:S(2)}, u32[]{:S(2)}) collective-permute-start(bf16[2,144,256]{2,1,0:T(8,128)(2,1)S(1)} %get-tuple-element.69), channel_id=1, source_target_pairs={{0,12},{1,13},{2,14},{3,15},{4,8},{5,9},{6,10},{7,11},{8,4},{9,5},... | collective-permute-start | bytes 442376 | tf_op jit(solution)/shard_map/ppermute | solution.py:695
  26.9 0.6 collective-permute-start.10
  27.6 0.8 collective-permute-start.3
  28.3 10.1 %shard_map.68 = (f32[4,4,64,256]{3,2,1,0:T(8,128)S(1)}, f32[4,4,8,256]{3,2,1,0:T(8,128)S(1)}, f32[4,2,64,256]{3,2,1,0:T(8,128)S(1)}, f32[4,2,8,256]{3,2,1,0:T(8,128)S(1)}) custom-call(s32[1]{0:T(128)} %bitcast.index.refs_0_, s32[16]{0:T(128)S(1)} %copy-done.5, s32[16]{0:T(128)S(1)} %copy-done.6, bf16[4,144,512]{2,1,0:T(8,128)(2,1)S(1)} %copy-done.1, ...), custom_call_target="tpu_custom_call" | custom-call | tf_op jit(solution)/shard_map/pallas_call | solution.py:672
  38.4 5.2 %shard_map.69 = (bf16[2,4,256,48]{3,2,1,0:T(8,128)(2,1)S(1)}, bf16[2,4,64,256]{3,2,1,0:T(8,128)(2,1)S(1)}, bf16[2,4,48,256]{3,2,1,0:T(8,128)(2,1)S(1)}, f32[2,4,...) custom-call(s32[1]{0:T(128)} %bitcast.index.refs_0_, s32[16]{0:T(128)S(1)} %copy-done.5, ...), custom_call_target="tpu_custom_call" | custom-call | tf_op jit(solution)/shard_map/pallas_call | solution.py:672
  43.6 11.2 %shard_map.70 = (bf16[48,1152]{1,0:T(8,128)(2,1)S(1)}, bf16[48,1152]{1,0:T(8,128)(2,1)S(1)}, bf16[48,1152]{1,0:T(8,128)(2,1)S(1)}, bf16[48,1152]{1,0:T(8,128)(2,1)S(1)}) custom-call(s32[1]{0:T(128)} %bitcast.index.refs_0_, s32[16]{0:T(128)S(1)} %copy-done.5, s32[16]{0:T(128)S(1)} %copy-done.6, ...), custom_call_target="tpu_custom_call" | custom-call | flops 8589934592 | tf_op jit(solution)/shard_map/pallas_call | solution.py:672
  54.8 1.3 %collective-permute-start.11 = (bf16[48,1152]{1,0:T(8,128)(2,1)S(1)}, bf16[48,1152]{1,0:T(8,128)(2,1)S(1)}, u32[]{:S(2)}, u32[]{:S(2)}) collective-permute-start(bf16[48,1152]{1,0:T(8,128)(2,1)S(1)} %get-tuple-element.81), channel_id=1, source_target_pairs={{0,4},{1,5},{2,6},{3,7},{4,0},{5,1},{6,2},{7,3},{8,12},{9,13},{10,... | collective-permute-start | bytes 331784 | tf_op jit(solution)/shard_map/ppermute | solution.py:695
  56.1 2.9 %collective-permute-start.14 = (bf16[48,1152]{1,0:T(8,128)(2,1)S(1)}, bf16[48,1152]{1,0:T(8,128)(2,1)S(1)}, u32[]{:S(2)}, u32[]{:S(2)}) collective-permute-start(bf16[48,1152]{1,0:T(8,128)(2,1)S(1)} %get-tuple-element.86), channel_id=1, source_target_pairs={{0,8},{1,9},{2,10},{3,11},{4,12},{5,13},{6,14},{7,15},{8,0},{9,1},... | collective-permute-start | bytes 331784 | tf_op jit(solution)/shard_map/ppermute | solution.py:695
  59.1 0.2 collective-permute-start.15
  59.3 5.4 %shard_map.71 = (f32[2,4,64,256]{3,2,1,0:T(8,128)S(1)}, f32[2,4,8,256]{3,2,1,0:T(8,128)S(1)}) custom-call(s32[1]{0:T(128)} %bitcast.index.refs_0_, s32[16]{0:T(128)S(1)} %copy-done.5, s32[16]{0:T(128)S(1)} %copy-done.6, bf16[4,144,512]{2,1,0:T(8,128)(2,1)S(1)} %copy-done.1, bf16[4,144,512]{2,1,0:T(8,128)(2,1)S(1)} %collective-permute-done.refs_1_.b_ref.refs_4_.refs_6_, ...), custom_call_target="tpu_custom_call" | custom-call | tf_op jit(solution)/shard_map/pallas_call | solution.py:672
  64.7 0.1 shard_map.72
  64.8 0.1 collective-permute-start.12
  64.9 2.1 %collective-permute-start.13 = (bf16[2,48,512]{2,1,0:T(8,128)(2,1)S(1)}, bf16[2,48,512]{2,1,0:T(8,128)(2,1)S(1)}, u32[]{:S(2)}, u32[]{:S(2)}) collective-permute-start(bf16[2,48,512]{2,1,0:T(8,128)(2,1)S(1)} %get-tuple-element.83.refs_11_), channel_id=1, source_target_pairs={{0,3},{1,2},{2,1},{3,0},{4,7},{5,6},{6,5},{7,4},{8,11},{9,10},{10,... | collective-permute-start | bytes 294920 | tf_op jit(solution)/shard_map/ppermute | solution.py:695
  67.0 5.6 %shard_map.73 = (f32[2,4,64,256]{3,2,1,0:T(8,128)S(1)}, f32[2,4,8,256]{3,2,1,0:T(8,128)S(1)}) custom-call(s32[1]{0:T(128)} %bitcast.index.refs_0_, s32[16]{0:T(128)S(1)} %copy-done.5, s32[16]{0:T(128)S(1)} %copy-done.6, bf16[4,144,512]{2,1,0:T(8,128)(2,1)S(1)} %copy-done.1, bf16[4,144,512]{2,1,0:T(8,128)(2,1)S(1)} %collective-permute-done.refs_1_.b_ref.refs_4_.refs_6_, ...), custom_call_target="tpu_custom_call" | custom-call | tf_op jit(solution)/shard_map/pallas_call | solution.py:672
  72.6 0.1 shard_map.75
  72.7 0.4 collective-permute-start.16
  73.2 1.0 %collective-permute-start.17 = (bf16[2,48,512]{2,1,0:T(8,128)(2,1)S(1)}, bf16[2,48,512]{2,1,0:T(8,128)(2,1)S(1)}, u32[]{:S(2)}, u32[]{:S(2)}) collective-permute-start(bf16[2,48,512]{2,1,0:T(8,128)(2,1)S(1)} %get-tuple-element.91.refs_9_), channel_id=1, source_target_pairs={{0,3},{1,2},{2,1},{3,0},{4,7},{5,6},{6,5},{7,4},{8,11},{9,10},{10,... | collective-permute-start | bytes 294920 | tf_op jit(solution)/shard_map/ppermute | solution.py:695
  74.2 5.8 %shard_map.77 = (f32[4,4,64,256]{3,2,1,0:T(8,128)S(1)}, f32[4,4,8,256]{3,2,1,0:T(8,128)S(1)}) custom-call(s32[1]{0:T(128)} %bitcast.index.refs_0_, s32[16]{0:T(128)S(1)} %copy-done.5, s32[16]{0:T(128)S(1)} %copy-done.6, bf16[4,144,256]{2,1,0:T(8,128)(2,1)S(1)} %collective-permute-done.3.refs_7_.refs_3_, ...), custom_call_target="tpu_custom_call" | custom-call | tf_op jit(solution)/shard_map/pallas_call | solution.py:672
  80.0 0.1 shard_map.78
  80.1 0.0 copy-start.2
  80.1 0.8 collective-permute-start.18
  80.9 1.1 %collective-permute-done.18.refs_5_ = bf16[4,48,512]{2,1,0:T(8,128)(2,1)S(1)} collective-permute-done((bf16[4,48,512]{2,1,0:T(8,128)(2,1)S(1)}, bf16[4,48,512]{2,1,0:T(8,128)(2,1)S(1)}, u32[]{:S(2)}, u32[]{:S(2)}) %collective-permute-start.18) | collective-permute-done | bytes 196640 | tf_op jit(solution)/shard_map/ppermute | solution.py:695
  82.0 3.0 %shard_map.79 = bf16[512,768]{1,0:T(8,128)(2,1)} custom-call(s32[1]{0:T(128)} %bitcast.index.refs_0_, s32[16]{0:T(128)S(1)} %copy-done.5, s32[16]{0:T(128)S(1)} %copy-done.6, bf16[2,48,512]{2,1,0:T(8,128)(2,1)S(1)} %get-tuple-element.92.refs_0_, bf16[2,48,512]{2,1,0:T(8,128)(2,1)S(1)} %get-tuple-element.93.refs_1_, ...), custom_call_target="tpu_custom_call" | custom-call | tf_op jit(solution)/shard_map/pallas_call | solution.py:672
  (36 shorter events, 0.1 us)
Async XLA Ops:
  5.3 9.2 %copy-start.5 = (s32[16]{0:T(128)S(1)}, s32[16]{0:T(128)}, u32[]{:S(2)}) copy-start(s32[16]{0:T(128)} %mid.7) | copy-start | bytes 196
  5.3 9.2 %copy-start.6 = (s32[16]{0:T(128)S(1)}, s32[16]{0:T(128)}, u32[]{:S(2)}) copy-start(s32[16]{0:T(128)} %top.7) | copy-start | bytes 196
  5.3 3.2 %collective-permute-start = (bf16[4,144,512]{2,1,0:T(8,128)(2,1)}, bf16[4,144,512]{2,1,0:T(8,128)(2,1)S(1)}, u32[]{:S(2)}, u32[]{:S(2)}) collective-permute-start(bf16[4,144,512]{2,1,0:T(8,128)(2,1)} %get-tuple-element.55), channel_id=1, source_target_pairs={{0,1},{1,0},{2,3},{3,2},{4,5},{5,4},{6,7},{7,6},{8,9},{9,8},{10,11... | collective-permute-start | bytes 1769480 | tf_op jit(solution)/shard_map/ppermute | solution.py:695
  5.8 17.2 %collective-permute-start.1 = (bf16[4,144,256]{2,1,0:T(8,128)(2,1)}, bf16[4,144,256]{2,1,0:T(8,128)(2,1)S(1)}, u32[]{:S(2)}, u32[]{:S(2)}) collective-permute-start(bf16[4,144,256]{2,1,0:T(8,128)(2,1)} %get-tuple-element.56), channel_id=1, source_target_pairs={{0,2},{1,3},{2,0},{3,1},{4,6},{5,7},{6,4},{7,5},{8,10},{9,11},{10,... | collective-permute-start | bytes 884744 | tf_op jit(solution)/shard_map/ppermute | solution.py:695
  8.4 14.7 %collective-permute-start.2 = (bf16[4,144,256]{2,1,0:T(8,128)(2,1)}, bf16[4,144,256]{2,1,0:T(8,128)(2,1)S(1)}, u32[]{:S(2)}, u32[]{:S(2)}) collective-permute-start(bf16[4,144,256]{2,1,0:T(8,128)(2,1)} %get-tuple-element.57), channel_id=1, source_target_pairs={{0,3},{1,2},{2,1},{3,0},{4,7},{5,6},{6,5},{7,4},{8,11},{9,10},{10,... | collective-permute-start | bytes 884744 | tf_op jit(solution)/shard_map/ppermute | solution.py:695
  8.4 1.1 %copy-start = (bf16[4,144,512]{2,1,0:T(8,128)(2,1)S(1)}, bf16[4,144,512]{2,1,0:T(8,128)(2,1)}, u32[]{:S(2)}) copy-start(bf16[4,144,512]{2,1,0:T(8,128)(2,1)} %get-tuple-element.54.refs_0_.a_ref.refs_3_.refs_5_) | copy-start | bytes 1769476
  9.5 4.9 %copy-start.1 = (bf16[4,144,512]{2,1,0:T(8,128)(2,1)S(1)}, bf16[4,144,512]{2,1,0:T(8,128)(2,1)}, u32[]{:S(2)}) copy-start(bf16[4,144,512]{2,1,0:T(8,128)(2,1)} %get-tuple-element.54.refs_0_.a_ref.refs_3_.refs_5_) | copy-start | bytes 1769476
  9.5 13.5 %copy-start.3 = (bf16[4,144,256]{2,1,0:T(8,128)(2,1)S(1)}, bf16[4,144,256]{2,1,0:T(8,128)(2,1)}, u32[]{:S(2)}) copy-start(bf16[4,144,256]{2,1,0:T(8,128)(2,1)} %get-tuple-element.59.refs_3_) | copy-start | bytes 884740
  9.5 13.5 %copy-start.4 = (bf16[4,144,256]{2,1,0:T(8,128)(2,1)S(1)}, bf16[4,144,256]{2,1,0:T(8,128)(2,1)}, u32[]{:S(2)}) copy-start(bf16[4,144,256]{2,1,0:T(8,128)(2,1)} %get-tuple-element.60.refs_4_) | copy-start | bytes 884740
  9.5 17.4 %collective-permute-start.5 = (bf16[2,144,256]{2,1,0:T(8,128)(2,1)S(1)}, bf16[2,144,256]{2,1,0:T(8,128)(2,1)S(1)}, u32[]{:S(2)}, u32[]{:S(2)}) collective-permute-start(bf16[2,144,256]{2,1,0:T(8,128)(2,1)S(1)} %get-tuple-element.64), channel_id=1, source_target_pairs={{0,12},{1,13},{2,14},{3,15},{4,8},{5,9},{6,10},{7,11},{8,4},{9,5},... | collective-permute-start | bytes 442376 | tf_op jit(solution)/shard_map/ppermute | solution.py:695
  13.8 13.8 %collective-permute-start.6 = (bf16[2,144,256]{2,1,0:T(8,128)(2,1)S(1)}, bf16[2,144,256]{2,1,0:T(8,128)(2,1)S(1)}, u32[]{:S(2)}, u32[]{:S(2)}) collective-permute-start(bf16[2,144,256]{2,1,0:T(8,128)(2,1)S(1)} %get-tuple-element.65), channel_id=1, source_target_pairs={{0,8},{1,9},{2,10},{3,11},{4,12},{5,13},{6,14},{7,15},{8,0},{9,1},... | collective-permute-start | bytes 442376 | tf_op jit(solution)/shard_map/ppermute | solution.py:695
  13.8 14.5 %collective-permute-start.7 = (bf16[2,144,256]{2,1,0:T(8,128)(2,1)S(1)}, bf16[2,144,256]{2,1,0:T(8,128)(2,1)S(1)}, u32[]{:S(2)}, u32[]{:S(2)}) collective-permute-start(bf16[2,144,256]{2,1,0:T(8,128)(2,1)S(1)} %get-tuple-element.66), channel_id=1, source_target_pairs={{0,4},{1,5},{2,6},{3,7},{4,0},{5,1},{6,2},{7,3},{8,12},{9,13},{10,... | collective-permute-start | bytes 442376 | tf_op jit(solution)/shard_map/ppermute | solution.py:695
  23.1 20.5 %collective-permute-start.8 = (bf16[2,144,256]{2,1,0:T(8,128)(2,1)S(1)}, bf16[2,144,256]{2,1,0:T(8,128)(2,1)S(1)}, u32[]{:S(2)}, u32[]{:S(2)}) collective-permute-start(bf16[2,144,256]{2,1,0:T(8,128)(2,1)S(1)} %get-tuple-element.69), channel_id=1, source_target_pairs={{0,12},{1,13},{2,14},{3,15},{4,8},{5,9},{6,10},{7,11},{8,4},{9,5},... | collective-permute-start | bytes 442376 | tf_op jit(solution)/shard_map/ppermute | solution.py:695
  26.9 16.7 %collective-permute-start.9 = (bf16[2,144,256]{2,1,0:T(8,128)(2,1)S(1)}, bf16[2,144,256]{2,1,0:T(8,128)(2,1)S(1)}, u32[]{:S(2)}, u32[]{:S(2)}) collective-permute-start(bf16[2,144,256]{2,1,0:T(8,128)(2,1)S(1)} %get-tuple-element.70), channel_id=1, source_target_pairs={{0,8},{1,9},{2,10},{3,11},{4,12},{5,13},{6,14},{7,15},{8,0},{9,1},... | collective-permute-start | bytes 442376 | tf_op jit(solution)/shard_map/ppermute | solution.py:695
  26.9 16.7 %collective-permute-start.10 = (bf16[2,144,256]{2,1,0:T(8,128)(2,1)S(1)}, bf16[2,144,256]{2,1,0:T(8,128)(2,1)S(1)}, u32[]{:S(2)}, u32[]{:S(2)}) collective-permute-start(bf16[2,144,256]{2,1,0:T(8,128)(2,1)S(1)} %get-tuple-element.71), channel_id=1, source_target_pairs={{0,4},{1,5},{2,6},{3,7},{4,0},{5,1},{6,2},{7,3},{8,12},{9,13},{10,... | collective-permute-start | bytes 442376 | tf_op jit(solution)/shard_map/ppermute | solution.py:695
  27.6 31.7 %collective-permute-start.3 = (bf16[4,144,256]{2,1,0:T(8,128)(2,1)S(1)}, bf16[4,144,256]{2,1,0:T(8,128)(2,1)S(1)}, u32[]{:S(2)}, u32[]{:S(2)}) collective-permute-start(bf16[4,144,256]{2,1,0:T(8,128)(2,1)S(1)} %get-tuple-element.61), channel_id=1, source_target_pairs={{0,2},{1,3},{2,0},{3,1},{4,6},{5,7},{6,4},{7,5},{8,10},{9,11},{10,... | collective-permute-start | bytes 884744 | tf_op jit(solution)/shard_map/ppermute | solution.py:695
  28.3 31.0 %collective-permute-start.4 = (bf16[4,144,256]{2,1,0:T(8,128)(2,1)S(1)}, bf16[4,144,256]{2,1,0:T(8,128)(2,1)S(1)}, u32[]{:S(2)}, u32[]{:S(2)}) collective-permute-start(bf16[4,144,256]{2,1,0:T(8,128)(2,1)S(1)} %get-tuple-element.62), channel_id=1, source_target_pairs={{0,3},{1,2},{2,1},{3,0},{4,7},{5,6},{6,5},{7,4},{8,11},{9,10},{10,... | collective-permute-start | bytes 884744 | tf_op jit(solution)/shard_map/ppermute | solution.py:695
  54.8 9.9 %collective-permute-start.11 = (bf16[48,1152]{1,0:T(8,128)(2,1)S(1)}, bf16[48,1152]{1,0:T(8,128)(2,1)S(1)}, u32[]{:S(2)}, u32[]{:S(2)}) collective-permute-start(bf16[48,1152]{1,0:T(8,128)(2,1)S(1)} %get-tuple-element.81), channel_id=1, source_target_pairs={{0,4},{1,5},{2,6},{3,7},{4,0},{5,1},{6,2},{7,3},{8,12},{9,13},{10,... | collective-permute-start | bytes 331784 | tf_op jit(solution)/shard_map/ppermute | solution.py:695
  56.1 16.5 %collective-permute-start.14 = (bf16[48,1152]{1,0:T(8,128)(2,1)S(1)}, bf16[48,1152]{1,0:T(8,128)(2,1)S(1)}, u32[]{:S(2)}, u32[]{:S(2)}) collective-permute-start(bf16[48,1152]{1,0:T(8,128)(2,1)S(1)} %get-tuple-element.86), channel_id=1, source_target_pairs={{0,8},{1,9},{2,10},{3,11},{4,12},{5,13},{6,14},{7,15},{8,0},{9,1},... | collective-permute-start | bytes 331784 | tf_op jit(solution)/shard_map/ppermute | solution.py:695
  59.1 13.5 %collective-permute-start.15 = (bf16[48,1152]{1,0:T(8,128)(2,1)S(1)}, bf16[48,1152]{1,0:T(8,128)(2,1)S(1)}, u32[]{:S(2)}, u32[]{:S(2)}) collective-permute-start(bf16[48,1152]{1,0:T(8,128)(2,1)S(1)} %get-tuple-element.87), channel_id=1, source_target_pairs={{0,12},{1,13},{2,14},{3,15},{4,8},{5,9},{6,10},{7,11},{8,4},{9,5},... | collective-permute-start | bytes 331784 | tf_op jit(solution)/shard_map/ppermute | solution.py:695
  64.8 7.8 %collective-permute-start.12 = (bf16[2,48,512]{2,1,0:T(8,128)(2,1)S(1)}, bf16[2,48,512]{2,1,0:T(8,128)(2,1)S(1)}, u32[]{:S(2)}, u32[]{:S(2)}) collective-permute-start(bf16[2,48,512]{2,1,0:T(8,128)(2,1)S(1)} %get-tuple-element.82), channel_id=1, source_target_pairs={{0,2},{1,3},{2,0},{3,1},{4,6},{5,7},{6,4},{7,5},{8,10},{9,11},{10,... | collective-permute-start | bytes 294920 | tf_op jit(solution)/shard_map/ppermute | solution.py:695
  64.9 7.8 %collective-permute-start.13 = (bf16[2,48,512]{2,1,0:T(8,128)(2,1)S(1)}, bf16[2,48,512]{2,1,0:T(8,128)(2,1)S(1)}, u32[]{:S(2)}, u32[]{:S(2)}) collective-permute-start(bf16[2,48,512]{2,1,0:T(8,128)(2,1)S(1)} %get-tuple-element.83.refs_11_), channel_id=1, source_target_pairs={{0,3},{1,2},{2,1},{3,0},{4,7},{5,6},{6,5},{7,4},{8,11},{9,10},{10,... | collective-permute-start | bytes 294920 | tf_op jit(solution)/shard_map/ppermute | solution.py:695
  72.7 8.2 %collective-permute-start.16 = (bf16[2,48,512]{2,1,0:T(8,128)(2,1)S(1)}, bf16[2,48,512]{2,1,0:T(8,128)(2,1)S(1)}, u32[]{:S(2)}, u32[]{:S(2)}) collective-permute-start(bf16[2,48,512]{2,1,0:T(8,128)(2,1)S(1)} %get-tuple-element.90), channel_id=1, source_target_pairs={{0,2},{1,3},{2,0},{3,1},{4,6},{5,7},{6,4},{7,5},{8,10},{9,11},{10,... | collective-permute-start | bytes 294920 | tf_op jit(solution)/shard_map/ppermute | solution.py:695
  73.2 7.8 %collective-permute-start.17 = (bf16[2,48,512]{2,1,0:T(8,128)(2,1)S(1)}, bf16[2,48,512]{2,1,0:T(8,128)(2,1)S(1)}, u32[]{:S(2)}, u32[]{:S(2)}) collective-permute-start(bf16[2,48,512]{2,1,0:T(8,128)(2,1)S(1)} %get-tuple-element.91.refs_9_), channel_id=1, source_target_pairs={{0,3},{1,2},{2,1},{3,0},{4,7},{5,6},{6,5},{7,4},{8,11},{9,10},{10,... | collective-permute-start | bytes 294920 | tf_op jit(solution)/shard_map/ppermute | solution.py:695
  80.1 1.9 %copy-start.2 = (bf16[768,768]{1,0:T(8,128)(2,1)S(1)}, bf16[768,768]{1,0:T(8,128)(2,1)}, u32[]{:S(2)}) copy-start(bf16[768,768]{1,0:T(8,128)(2,1)} %refs_6_.1) | copy-start | bytes 3538948
  80.1 1.9 %collective-permute-start.18 = (bf16[4,48,512]{2,1,0:T(8,128)(2,1)S(1)}, bf16[4,48,512]{2,1,0:T(8,128)(2,1)S(1)}, u32[]{:S(2)}, u32[]{:S(2)}) collective-permute-start(bf16[4,48,512]{2,1,0:T(8,128)(2,1)S(1)} %get-tuple-element.102), channel_id=1, source_target_pairs={{0,1},{1,0},{2,3},{3,2},{4,5},{5,4},{6,7},{7,6},{8,9},{9,8},{10,11... | collective-permute-start | bytes 589832 | tf_op jit(solution)/shard_map/ppermute | solution.py:695

commit v9 on v8

--- a/solution.py
+++ b/solution.py
@@ -217,6 +217,8 @@
         load.start()
     picker = token_picker()
     stores = []
+    heads = {(j, p): head_of(place, j, p) for j in range(GROUP) for p in range(HG)}
+    classes = {at: class_of_slots(*offsets_of(place, head)) for at, head in heads.items()}
     for n, (load, block, scratch) in enumerate(zip(loads, blocks, held)):
         load.wait()
         fill_class_major(block[...], picker, scratch)
@@ -225,11 +227,9 @@
             ((0, 0, 4), (1, 0, 4), (2, 0, 2), (3, 0, 2), (2, 2, 2), (3, 2, 2))
         ):
             for p in range(HG):
-                head = head_of(place, j, p)
-                slots = class_of_slots(*offsets_of(place, head))
                 for s in range(count):
                     packed[i][p, rows, s * BLK : (s + 1) * BLK] = scratch[
-                        head_rows(head), lane_block(slots[first + s])
+                        head_rows(heads[j, p]), lane_block(classes[j, p][first + s])
                     ]
             store = pltpu.make_async_copy(
                 packed[i].at[:, rows], outs[i].at[:, rows], sems_out.at[i, n]
@@ -630,6 +630,16 @@
             outs[i][p, :, HALF:] = (acc[0:DH] / acc[DH : DH + 1]).astype(BF16)
 
 
+def last_own_kernel(inputs, units, tasks, index, mid, top, *refs):
+    count = len(inputs) + 2
+    near_refs, far, outs, scratch = refs[:count], refs[count:-6], refs[-6:-4], refs[-4:]
+    acc_s, max_s, k_s, v_s = scratch
+    near_kernel(
+        inputs, units, tasks, 1, 0, HG, index, mid, top, *near_refs, acc_s, max_s, k_s, v_s
+    )
+    combine_kernel(0, acc_s, max_s, *far, *outs)
+
+
 def project_kernel(sources, index, mid, top, *refs):
     place = (index, mid, top)
     parts, (w_ref, out_ref, held) = refs[:-3], refs[-3:]
@@ -845,14 +855,20 @@
         )
         parts[2, first], parts[3, first] = within(part2, 2), within(part3, 3)
         last = part3
-    state_own = near(
-        {(2, 2): rest2, (3, 2): rest3, **{q: held[q] for q in ((0, 0), (1, 0))}},
-        other_rest,
-        [[(q, 0, (0, i)) for i, q in enumerate(own)]],
-        [state_own],
-        after=(last,),
-    )
-    part0, part1 = combine(0, state_own, back)
+    pieces = {(2, 2): rest2, (3, 2): rest3, **{q: held[q] for q in ((0, 0), (1, 0))}}
+    arrays = [*pieces.values(), *state_own, *back[::-1]]
+    attended = jax.ShapeDtypeStruct((HG, DH, TOK), BF16)
+    part0, part1 = call(
+        functools.partial(
+            last_own_kernel, list(pieces), other_rest, [[(q, 0, (0, i)) for i, q in enumerate(own)]]
+        ),
+        place, arrays, (1,),
+        [whole(x.shape) for x in arrays],
+        [(whole(attended.shape), attended)] * 2,
+        [pltpu.VMEM(x.shape, F32) for x in state_own]
+        + [pltpu.VMEM((HG, TOK, DH), BF16), pltpu.VMEM((HG, DX, TOK), BF16)],
+        HG * TOK * GROUP * HALF, after=(last,),
+    )
     parts = dict(zip(parts, handed_on(parts.values(), busy=BUSY)))
     parts[0, 0], parts[1, 0] = part0, within(part1, 1)
     return call(

time: 85.2 us -> 84.9 us (level)
    pallas_call x16 -> x15, Pallas kernels: 60.4 us -> 60.1 us  [call(): pl.pallas_call(body if extra else kernel, grid_spec=pltpu.PrefetchScalarG...]
where the time goes in v9:
time: 84.9 us; the launch traced here: 84.7 us
  Pallas kernels  60.1 us (71%)
  starting transfers between devices  22.1 us (26%)
  waiting for transfers between devices  1.11 us (1%)
  local copies, waits for them, and re-layouts  1.09 us (1%)
    pallas_call x15, Pallas kernels, call(): pl.pallas_call(body if extra else kernel, grid_spec=pltpu.PrefetchScalarG...  60.1 us
    ppermute x19, starting transfers between devices, within(): return lax.ppermute(array, 'seq', [(i, i ^ apart) for i in range(count)])  22.1 us
  transfers between devices with their start and end apart: 19, of which 1 were waited for; matrix products, arithmetic and copies ran while one was open for 0% of the time, Pallas kernels for 61%

profile of v9, /device:TPU:0, one launch (start us, length us, event | category | flops | bytes accessed | tf_op | source)
XLA Modules:
  0.0 84.7 jit_solution(8704984750549336427)
XLA Ops:
  0.0 5.0 %shard_map.64 = (bf16[4,144,512]{2,1,0:T(8,128)(2,1)}, bf16[4,144,512]{2,1,0:T(8,128)(2,1)}, bf16[4,144,256]{2,1,0:T(8,128)(2,1)}, bf16[4,144,256]{2,1,0:T(8,128...) custom-call(s32[1]{0:T(128)} %bitcast.index.refs_0_, s32[16]{0:T(128)} %mid.7, s32[16]{0:T(128)} %top.7, ...), custom_call_target="tpu_custom_call" | custom-call | tf_op jit(solution)/shard_map/pallas_call | solution.py:682
  5.0 0.0 copy-start.5
  5.1 0.0 copy-start.6
  5.1 0.5 collective-permute-start
  5.6 2.6 %collective-permute-start.1 = (bf16[4,144,256]{2,1,0:T(8,128)(2,1)}, bf16[4,144,256]{2,1,0:T(8,128)(2,1)S(1)}, u32[]{:S(2)}, u32[]{:S(2)}) collective-permute-start(bf16[4,144,256]{2,1,0:T(8,128)(2,1)} %get-tuple-element.54), channel_id=1, source_target_pairs={{0,2},{1,3},{2,0},{3,1},{4,6},{5,7},{6,4},{7,5},{8,10},{9,11},{10,... | collective-permute-start | bytes 884744 | tf_op jit(solution)/shard_map/ppermute | solution.py:705
  8.1 0.1 collective-permute-start.2
  8.2 1.1 %copy-done = bf16[4,144,512]{2,1,0:T(8,128)(2,1)S(1)} copy-done((bf16[4,144,512]{2,1,0:T(8,128)(2,1)S(1)}, bf16[4,144,512]{2,1,0:T(8,128)(2,1)}, u32[]{:S(2)}) %copy-start) | copy-done | bytes 589848
  9.3 4.2 %collective-permute-start.5 = (bf16[2,144,256]{2,1,0:T(8,128)(2,1)S(1)}, bf16[2,144,256]{2,1,0:T(8,128)(2,1)S(1)}, u32[]{:S(2)}, u32[]{:S(2)}) collective-permute-start(bf16[2,144,256]{2,1,0:T(8,128)(2,1)S(1)} %get-tuple-element.62), channel_id=1, source_target_pairs={{0,12},{1,13},{2,14},{3,15},{4,8},{5,9},{6,10},{7,11},{8,4},{9,5},... | collective-permute-start | bytes 442376 | tf_op jit(solution)/shard_map/ppermute | solution.py:705
  13.6 0.6 collective-permute-start.7
  14.2 8.6 %shard_map.65 = (f32[4,4,64,256]{3,2,1,0:T(8,128)S(1)}, f32[4,4,8,256]{3,2,1,0:T(8,128)S(1)}) custom-call(s32[1]{0:T(128)} %bitcast.index.refs_0_, s32[16]{0:T(128)S(1)} %copy-done.5, s32[16]{0:T(128)S(1)} %copy-done.6, bf16[4,144,512]{2,1,0:T(8,128)(2,1)S(1)} %copy-done.1, bf16[4,144,512]{2,1,0:T(8,128)(2,1)S(1)} %collective-permute-done.refs_1_.b_ref.refs_4_.refs_6_), custom_call_target="tpu_custom_call" | custom-call | tf_op jit(solution)/shard_map/pallas_call | solution.py:682
  22.9 3.8 %collective-permute-start.8 = (bf16[2,144,256]{2,1,0:T(8,128)(2,1)S(1)}, bf16[2,144,256]{2,1,0:T(8,128)(2,1)S(1)}, u32[]{:S(2)}, u32[]{:S(2)}) collective-permute-start(bf16[2,144,256]{2,1,0:T(8,128)(2,1)S(1)} %get-tuple-element.67), channel_id=1, source_target_pairs={{0,12},{1,13},{2,14},{3,15},{4,8},{5,9},{6,10},{7,11},{8,4},{9,5},... | collective-permute-start | bytes 442376 | tf_op jit(solution)/shard_map/ppermute | solution.py:705
  26.7 0.7 collective-permute-start.10
  27.4 0.7 collective-permute-start.3
  28.1 10.1 %shard_map.68 = (f32[4,4,64,256]{3,2,1,0:T(8,128)S(1)}, f32[4,4,8,256]{3,2,1,0:T(8,128)S(1)}, f32[4,2,64,256]{3,2,1,0:T(8,128)S(1)}, f32[4,2,8,256]{3,2,1,0:T(8,128)S(1)}) custom-call(s32[1]{0:T(128)} %bitcast.index.refs_0_, s32[16]{0:T(128)S(1)} %copy-done.5, s32[16]{0:T(128)S(1)} %copy-done.6, bf16[4,144,512]{2,1,0:T(8,128)(2,1)S(1)} %copy-done.1, ...), custom_call_target="tpu_custom_call" | custom-call | tf_op jit(solution)/shard_map/pallas_call | solution.py:682
  38.2 5.2 %shard_map.69 = (bf16[2,4,256,48]{3,2,1,0:T(8,128)(2,1)S(1)}, bf16[2,4,64,256]{3,2,1,0:T(8,128)(2,1)S(1)}, bf16[2,4,48,256]{3,2,1,0:T(8,128)(2,1)S(1)}, f32[2,4,...) custom-call(s32[1]{0:T(128)} %bitcast.index.refs_0_, s32[16]{0:T(128)S(1)} %copy-done.5, ...), custom_call_target="tpu_custom_call" | custom-call | tf_op jit(solution)/shard_map/pallas_call | solution.py:682
  43.4 11.2 %shard_map.70 = (bf16[48,1152]{1,0:T(8,128)(2,1)S(1)}, bf16[48,1152]{1,0:T(8,128)(2,1)S(1)}, bf16[48,1152]{1,0:T(8,128)(2,1)S(1)}, bf16[48,1152]{1,0:T(8,128)(2,1)S(1)}) custom-call(s32[1]{0:T(128)} %bitcast.index.refs_0_, s32[16]{0:T(128)S(1)} %copy-done.5, s32[16]{0:T(128)S(1)} %copy-done.6, ...), custom_call_target="tpu_custom_call" | custom-call | flops 8589934592 | tf_op jit(solution)/shard_map/pallas_call | solution.py:682
  54.6 1.3 %collective-permute-start.11 = (bf16[48,1152]{1,0:T(8,128)(2,1)S(1)}, bf16[48,1152]{1,0:T(8,128)(2,1)S(1)}, u32[]{:S(2)}, u32[]{:S(2)}) collective-permute-start(bf16[48,1152]{1,0:T(8,128)(2,1)S(1)} %get-tuple-element.79), channel_id=1, source_target_pairs={{0,4},{1,5},{2,6},{3,7},{4,0},{5,1},{6,2},{7,3},{8,12},{9,13},{10,... | collective-permute-start | bytes 331784 | tf_op jit(solution)/shard_map/ppermute | solution.py:705
  55.9 2.9 %collective-permute-start.14 = (bf16[48,1152]{1,0:T(8,128)(2,1)S(1)}, bf16[48,1152]{1,0:T(8,128)(2,1)S(1)}, u32[]{:S(2)}, u32[]{:S(2)}) collective-permute-start(bf16[48,1152]{1,0:T(8,128)(2,1)S(1)} %get-tuple-element.84), channel_id=1, source_target_pairs={{0,8},{1,9},{2,10},{3,11},{4,12},{5,13},{6,14},{7,15},{8,0},{9,1},... | collective-permute-start | bytes 331784 | tf_op jit(solution)/shard_map/ppermute | solution.py:705
  58.8 0.2 collective-permute-start.15
  59.1 5.4 %shard_map.71 = (f32[2,4,64,256]{3,2,1,0:T(8,128)S(1)}, f32[2,4,8,256]{3,2,1,0:T(8,128)S(1)}) custom-call(s32[1]{0:T(128)} %bitcast.index.refs_0_, s32[16]{0:T(128)S(1)} %copy-done.5, s32[16]{0:T(128)S(1)} %copy-done.6, bf16[4,144,512]{2,1,0:T(8,128)(2,1)S(1)} %copy-done.1, bf16[4,144,512]{2,1,0:T(8,128)(2,1)S(1)} %collective-permute-done.refs_1_.b_ref.refs_4_.refs_6_, ...), custom_call_target="tpu_custom_call" | custom-call | tf_op jit(solution)/shard_map/pallas_call | solution.py:682
  64.5 0.1 shard_map.72
  64.6 0.1 collective-permute-start.12
  64.6 2.1 %collective-permute-start.13 = (bf16[2,48,512]{2,1,0:T(8,128)(2,1)S(1)}, bf16[2,48,512]{2,1,0:T(8,128)(2,1)S(1)}, u32[]{:S(2)}, u32[]{:S(2)}) collective-permute-start(bf16[2,48,512]{2,1,0:T(8,128)(2,1)S(1)} %get-tuple-element.81.refs_11_), channel_id=1, source_target_pairs={{0,3},{1,2},{2,1},{3,0},{4,7},{5,6},{6,5},{7,4},{8,11},{9,10},{10,... | collective-permute-start | bytes 294920 | tf_op jit(solution)/shard_map/ppermute | solution.py:705
  66.7 5.6 %shard_map.73 = (f32[2,4,64,256]{3,2,1,0:T(8,128)S(1)}, f32[2,4,8,256]{3,2,1,0:T(8,128)S(1)}) custom-call(s32[1]{0:T(128)} %bitcast.index.refs_0_, s32[16]{0:T(128)S(1)} %copy-done.5, s32[16]{0:T(128)S(1)} %copy-done.6, bf16[4,144,512]{2,1,0:T(8,128)(2,1)S(1)} %copy-done.1, bf16[4,144,512]{2,1,0:T(8,128)(2,1)S(1)} %collective-permute-done.refs_1_.b_ref.refs_4_.refs_6_, ...), custom_call_target="tpu_custom_call" | custom-call | tf_op jit(solution)/shard_map/pallas_call | solution.py:682
  72.4 0.1 shard_map.75
  72.5 0.4 collective-permute-start.16
  72.9 1.0 %collective-permute-start.17 = (bf16[2,48,512]{2,1,0:T(8,128)(2,1)S(1)}, bf16[2,48,512]{2,1,0:T(8,128)(2,1)S(1)}, u32[]{:S(2)}, u32[]{:S(2)}) collective-permute-start(bf16[2,48,512]{2,1,0:T(8,128)(2,1)S(1)} %get-tuple-element.89.refs_13_), channel_id=1, source_target_pairs={{0,3},{1,2},{2,1},{3,0},{4,7},{5,6},{6,5},{7,4},{8,11},{9,10},{10,... | collective-permute-start | bytes 294920 | tf_op jit(solution)/shard_map/ppermute | solution.py:705
  74.0 5.8 %shard_map.77 = (bf16[4,48,512]{2,1,0:T(8,128)(2,1)S(1)}, bf16[4,48,512]{2,1,0:T(8,128)(2,1)S(1)}) custom-call(s32[1]{0:T(128)} %bitcast.index.refs_0_, s32[16]{0:T(128)S(1)} %copy-done.5, s32[16]{0:T(128)S(1)} %copy-done.6, bf16[4,144,256]{2,1,0:T(8,128)(2,1)S(1)} %collective-permute-done.3.refs_7_.refs_3_, ...), custom_call_target="tpu_custom_call" | custom-call | tf_op jit(solution)/shard_map/pallas_call | solution.py:682
  79.8 0.0 copy-start.2
  79.8 0.8 collective-permute-start.18
  80.6 1.1 %collective-permute-done.18.refs_5_ = bf16[4,48,512]{2,1,0:T(8,128)(2,1)S(1)} collective-permute-done((bf16[4,48,512]{2,1,0:T(8,128)(2,1)S(1)}, bf16[4,48,512]{2,1,0:T(8,128)(2,1)S(1)}, u32[]{:S(2)}, u32[]{:S(2)}) %collective-permute-start.18) | collective-permute-done | bytes 196640 | tf_op jit(solution)/shard_map/ppermute | solution.py:705
  81.7 3.0 %shard_map.78 = bf16[512,768]{1,0:T(8,128)(2,1)} custom-call(s32[1]{0:T(128)} %bitcast.index.refs_0_, s32[16]{0:T(128)S(1)} %copy-done.5, s32[16]{0:T(128)S(1)} %copy-done.6, bf16[2,48,512]{2,1,0:T(8,128)(2,1)S(1)} %get-tuple-element.90.refs_0_, bf16[2,48,512]{2,1,0:T(8,128)(2,1)S(1)} %get-tuple-element.91.refs_1_, ...), custom_call_target="tpu_custom_call" | custom-call | tf_op jit(solution)/shard_map/pallas_call | solution.py:682
  (35 shorter events, 0.1 us)
Async XLA Ops:
  5.0 9.2 %copy-start.5 = (s32[16]{0:T(128)S(1)}, s32[16]{0:T(128)}, u32[]{:S(2)}) copy-start(s32[16]{0:T(128)} %mid.7) | copy-start | bytes 196
  5.1 9.2 %copy-start.6 = (s32[16]{0:T(128)S(1)}, s32[16]{0:T(128)}, u32[]{:S(2)}) copy-start(s32[16]{0:T(128)} %top.7) | copy-start | bytes 196
  5.1 3.2 %collective-permute-start = (bf16[4,144,512]{2,1,0:T(8,128)(2,1)}, bf16[4,144,512]{2,1,0:T(8,128)(2,1)S(1)}, u32[]{:S(2)}, u32[]{:S(2)}) collective-permute-start(bf16[4,144,512]{2,1,0:T(8,128)(2,1)} %get-tuple-element.53), channel_id=1, source_target_pairs={{0,1},{1,0},{2,3},{3,2},{4,5},{5,4},{6,7},{7,6},{8,9},{9,8},{10,11... | collective-permute-start | bytes 1769480 | tf_op jit(solution)/shard_map/ppermute | solution.py:705
  5.6 17.2 %collective-permute-start.1 = (bf16[4,144,256]{2,1,0:T(8,128)(2,1)}, bf16[4,144,256]{2,1,0:T(8,128)(2,1)S(1)}, u32[]{:S(2)}, u32[]{:S(2)}) collective-permute-start(bf16[4,144,256]{2,1,0:T(8,128)(2,1)} %get-tuple-element.54), channel_id=1, source_target_pairs={{0,2},{1,3},{2,0},{3,1},{4,6},{5,7},{6,4},{7,5},{8,10},{9,11},{10,... | collective-permute-start | bytes 884744 | tf_op jit(solution)/shard_map/ppermute | solution.py:705
  8.1 14.7 %collective-permute-start.2 = (bf16[4,144,256]{2,1,0:T(8,128)(2,1)}, bf16[4,144,256]{2,1,0:T(8,128)(2,1)S(1)}, u32[]{:S(2)}, u32[]{:S(2)}) collective-permute-start(bf16[4,144,256]{2,1,0:T(8,128)(2,1)} %get-tuple-element.55), channel_id=1, source_target_pairs={{0,3},{1,2},{2,1},{3,0},{4,7},{5,6},{6,5},{7,4},{8,11},{9,10},{10,... | collective-permute-start | bytes 884744 | tf_op jit(solution)/shard_map/ppermute | solution.py:705
  8.2 1.1 %copy-start = (bf16[4,144,512]{2,1,0:T(8,128)(2,1)S(1)}, bf16[4,144,512]{2,1,0:T(8,128)(2,1)}, u32[]{:S(2)}) copy-start(bf16[4,144,512]{2,1,0:T(8,128)(2,1)} %get-tuple-element.52.refs_0_.a_ref.refs_3_.refs_5_) | copy-start | bytes 1769476
  9.3 4.9 %copy-start.1 = (bf16[4,144,512]{2,1,0:T(8,128)(2,1)S(1)}, bf16[4,144,512]{2,1,0:T(8,128)(2,1)}, u32[]{:S(2)}) copy-start(bf16[4,144,512]{2,1,0:T(8,128)(2,1)} %get-tuple-element.52.refs_0_.a_ref.refs_3_.refs_5_) | copy-start | bytes 1769476
  9.3 13.6 %copy-start.3 = (bf16[4,144,256]{2,1,0:T(8,128)(2,1)S(1)}, bf16[4,144,256]{2,1,0:T(8,128)(2,1)}, u32[]{:S(2)}) copy-start(bf16[4,144,256]{2,1,0:T(8,128)(2,1)} %get-tuple-element.57.refs_3_) | copy-start | bytes 884740
  9.3 13.6 %copy-start.4 = (bf16[4,144,256]{2,1,0:T(8,128)(2,1)S(1)}, bf16[4,144,256]{2,1,0:T(8,128)(2,1)}, u32[]{:S(2)}) copy-start(bf16[4,144,256]{2,1,0:T(8,128)(2,1)} %get-tuple-element.58.refs_4_) | copy-start | bytes 884740
  9.3 17.4 %collective-permute-start.5 = (bf16[2,144,256]{2,1,0:T(8,128)(2,1)S(1)}, bf16[2,144,256]{2,1,0:T(8,128)(2,1)S(1)}, u32[]{:S(2)}, u32[]{:S(2)}) collective-permute-start(bf16[2,144,256]{2,1,0:T(8,128)(2,1)S(1)} %get-tuple-element.62), channel_id=1, source_target_pairs={{0,12},{1,13},{2,14},{3,15},{4,8},{5,9},{6,10},{7,11},{8,4},{9,5},... | collective-permute-start | bytes 442376 | tf_op jit(solution)/shard_map/ppermute | solution.py:705
  13.6 13.8 %collective-permute-start.6 = (bf16[2,144,256]{2,1,0:T(8,128)(2,1)S(1)}, bf16[2,144,256]{2,1,0:T(8,128)(2,1)S(1)}, u32[]{:S(2)}, u32[]{:S(2)}) collective-permute-start(bf16[2,144,256]{2,1,0:T(8,128)(2,1)S(1)} %get-tuple-element.63), channel_id=1, source_target_pairs={{0,8},{1,9},{2,10},{3,11},{4,12},{5,13},{6,14},{7,15},{8,0},{9,1},... | collective-permute-start | bytes 442376 | tf_op jit(solution)/shard_map/ppermute | solution.py:705
  13.6 14.5 %collective-permute-start.7 = (bf16[2,144,256]{2,1,0:T(8,128)(2,1)S(1)}, bf16[2,144,256]{2,1,0:T(8,128)(2,1)S(1)}, u32[]{:S(2)}, u32[]{:S(2)}) collective-permute-start(bf16[2,144,256]{2,1,0:T(8,128)(2,1)S(1)} %get-tuple-element.64), channel_id=1, source_target_pairs={{0,4},{1,5},{2,6},{3,7},{4,0},{5,1},{6,2},{7,3},{8,12},{9,13},{10,... | collective-permute-start | bytes 442376 | tf_op jit(solution)/shard_map/ppermute | solution.py:705
  22.9 20.5 %collective-permute-start.8 = (bf16[2,144,256]{2,1,0:T(8,128)(2,1)S(1)}, bf16[2,144,256]{2,1,0:T(8,128)(2,1)S(1)}, u32[]{:S(2)}, u32[]{:S(2)}) collective-permute-start(bf16[2,144,256]{2,1,0:T(8,128)(2,1)S(1)} %get-tuple-element.67), channel_id=1, source_target_pairs={{0,12},{1,13},{2,14},{3,15},{4,8},{5,9},{6,10},{7,11},{8,4},{9,5},... | collective-permute-start | bytes 442376 | tf_op jit(solution)/shard_map/ppermute | solution.py:705
  26.7 16.7 %collective-permute-start.9 = (bf16[2,144,256]{2,1,0:T(8,128)(2,1)S(1)}, bf16[2,144,256]{2,1,0:T(8,128)(2,1)S(1)}, u32[]{:S(2)}, u32[]{:S(2)}) collective-permute-start(bf16[2,144,256]{2,1,0:T(8,128)(2,1)S(1)} %get-tuple-element.68), channel_id=1, source_target_pairs={{0,8},{1,9},{2,10},{3,11},{4,12},{5,13},{6,14},{7,15},{8,0},{9,1},... | collective-permute-start | bytes 442376 | tf_op jit(solution)/shard_map/ppermute | solution.py:705
  26.7 16.7 %collective-permute-start.10 = (bf16[2,144,256]{2,1,0:T(8,128)(2,1)S(1)}, bf16[2,144,256]{2,1,0:T(8,128)(2,1)S(1)}, u32[]{:S(2)}, u32[]{:S(2)}) collective-permute-start(bf16[2,144,256]{2,1,0:T(8,128)(2,1)S(1)} %get-tuple-element.69), channel_id=1, source_target_pairs={{0,4},{1,5},{2,6},{3,7},{4,0},{5,1},{6,2},{7,3},{8,12},{9,13},{10,... | collective-permute-start | bytes 442376 | tf_op jit(solution)/shard_map/ppermute | solution.py:705
  27.4 31.7 %collective-permute-start.3 = (bf16[4,144,256]{2,1,0:T(8,128)(2,1)S(1)}, bf16[4,144,256]{2,1,0:T(8,128)(2,1)S(1)}, u32[]{:S(2)}, u32[]{:S(2)}) collective-permute-start(bf16[4,144,256]{2,1,0:T(8,128)(2,1)S(1)} %get-tuple-element.59), channel_id=1, source_target_pairs={{0,2},{1,3},{2,0},{3,1},{4,6},{5,7},{6,4},{7,5},{8,10},{9,11},{10,... | collective-permute-start | bytes 884744 | tf_op jit(solution)/shard_map/ppermute | solution.py:705
  28.1 31.0 %collective-permute-start.4 = (bf16[4,144,256]{2,1,0:T(8,128)(2,1)S(1)}, bf16[4,144,256]{2,1,0:T(8,128)(2,1)S(1)}, u32[]{:S(2)}, u32[]{:S(2)}) collective-permute-start(bf16[4,144,256]{2,1,0:T(8,128)(2,1)S(1)} %get-tuple-element.60), channel_id=1, source_target_pairs={{0,3},{1,2},{2,1},{3,0},{4,7},{5,6},{6,5},{7,4},{8,11},{9,10},{10,... | collective-permute-start | bytes 884744 | tf_op jit(solution)/shard_map/ppermute | solution.py:705
  54.6 9.9 %collective-permute-start.11 = (bf16[48,1152]{1,0:T(8,128)(2,1)S(1)}, bf16[48,1152]{1,0:T(8,128)(2,1)S(1)}, u32[]{:S(2)}, u32[]{:S(2)}) collective-permute-start(bf16[48,1152]{1,0:T(8,128)(2,1)S(1)} %get-tuple-element.79), channel_id=1, source_target_pairs={{0,4},{1,5},{2,6},{3,7},{4,0},{5,1},{6,2},{7,3},{8,12},{9,13},{10,... | collective-permute-start | bytes 331784 | tf_op jit(solution)/shard_map/ppermute | solution.py:705
  55.9 16.5 %collective-permute-start.14 = (bf16[48,1152]{1,0:T(8,128)(2,1)S(1)}, bf16[48,1152]{1,0:T(8,128)(2,1)S(1)}, u32[]{:S(2)}, u32[]{:S(2)}) collective-permute-start(bf16[48,1152]{1,0:T(8,128)(2,1)S(1)} %get-tuple-element.84), channel_id=1, source_target_pairs={{0,8},{1,9},{2,10},{3,11},{4,12},{5,13},{6,14},{7,15},{8,0},{9,1},... | collective-permute-start | bytes 331784 | tf_op jit(solution)/shard_map/ppermute | solution.py:705
  58.8 13.5 %collective-permute-start.15 = (bf16[48,1152]{1,0:T(8,128)(2,1)S(1)}, bf16[48,1152]{1,0:T(8,128)(2,1)S(1)}, u32[]{:S(2)}, u32[]{:S(2)}) collective-permute-start(bf16[48,1152]{1,0:T(8,128)(2,1)S(1)} %get-tuple-element.85), channel_id=1, source_target_pairs={{0,12},{1,13},{2,14},{3,15},{4,8},{5,9},{6,10},{7,11},{8,4},{9,5},... | collective-permute-start | bytes 331784 | tf_op jit(solution)/shard_map/ppermute | solution.py:705
  64.6 7.8 %collective-permute-start.12 = (bf16[2,48,512]{2,1,0:T(8,128)(2,1)S(1)}, bf16[2,48,512]{2,1,0:T(8,128)(2,1)S(1)}, u32[]{:S(2)}, u32[]{:S(2)}) collective-permute-start(bf16[2,48,512]{2,1,0:T(8,128)(2,1)S(1)} %get-tuple-element.80), channel_id=1, source_target_pairs={{0,2},{1,3},{2,0},{3,1},{4,6},{5,7},{6,4},{7,5},{8,10},{9,11},{10,... | collective-permute-start | bytes 294920 | tf_op jit(solution)/shard_map/ppermute | solution.py:705
  64.6 7.8 %collective-permute-start.13 = (bf16[2,48,512]{2,1,0:T(8,128)(2,1)S(1)}, bf16[2,48,512]{2,1,0:T(8,128)(2,1)S(1)}, u32[]{:S(2)}, u32[]{:S(2)}) collective-permute-start(bf16[2,48,512]{2,1,0:T(8,128)(2,1)S(1)} %get-tuple-element.81.refs_11_), channel_id=1, source_target_pairs={{0,3},{1,2},{2,1},{3,0},{4,7},{5,6},{6,5},{7,4},{8,11},{9,10},{10,... | collective-permute-start | bytes 294920 | tf_op jit(solution)/shard_map/ppermute | solution.py:705
  72.5 8.1 %collective-permute-start.16 = (bf16[2,48,512]{2,1,0:T(8,128)(2,1)S(1)}, bf16[2,48,512]{2,1,0:T(8,128)(2,1)S(1)}, u32[]{:S(2)}, u32[]{:S(2)}) collective-permute-start(bf16[2,48,512]{2,1,0:T(8,128)(2,1)S(1)} %get-tuple-element.88), channel_id=1, source_target_pairs={{0,2},{1,3},{2,0},{3,1},{4,6},{5,7},{6,4},{7,5},{8,10},{9,11},{10,... | collective-permute-start | bytes 294920 | tf_op jit(solution)/shard_map/ppermute | solution.py:705
  72.9 7.7 %collective-permute-start.17 = (bf16[2,48,512]{2,1,0:T(8,128)(2,1)S(1)}, bf16[2,48,512]{2,1,0:T(8,128)(2,1)S(1)}, u32[]{:S(2)}, u32[]{:S(2)}) collective-permute-start(bf16[2,48,512]{2,1,0:T(8,128)(2,1)S(1)} %get-tuple-element.89.refs_13_), channel_id=1, source_target_pairs={{0,3},{1,2},{2,1},{3,0},{4,7},{5,6},{6,5},{7,4},{8,11},{9,10},{10,... | collective-permute-start | bytes 294920 | tf_op jit(solution)/shard_map/ppermute | solution.py:705
  79.8 1.9 %copy-start.2 = (bf16[768,768]{1,0:T(8,128)(2,1)S(1)}, bf16[768,768]{1,0:T(8,128)(2,1)}, u32[]{:S(2)}) copy-start(bf16[768,768]{1,0:T(8,128)(2,1)} %refs_6_.1) | copy-start | bytes 3538948
  79.8 1.9 %collective-permute-start.18 = (bf16[4,48,512]{2,1,0:T(8,128)(2,1)S(1)}, bf16[4,48,512]{2,1,0:T(8,128)(2,1)S(1)}, u32[]{:S(2)}, u32[]{:S(2)}) collective-permute-start(bf16[4,48,512]{2,1,0:T(8,128)(2,1)S(1)} %get-tuple-element.98), channel_id=1, source_target_pairs={{0,1},{1,0},{2,3},{3,2},{4,5},{5,4},{6,7},{7,6},{8,9},{9,8},{10,11... | collective-permute-start | bytes 589832 | tf_op jit(solution)/shard_map/ppermute | solution.py:705

commit v10 on v9

--- a/solution.py
+++ b/solution.py
@@ -850,9 +850,8 @@
         )
         if first:
             back[1:] = handed_on(back[1:], after=state_other[1:])
-        part2, part3 = combine(
-            1, state_other, back[first : first + heads], after=tuple(parts.values())
-        )
+        part2, part3 = combine(1, state_other, back[first : first + heads])
+        early = tuple(parts.values())
         parts[2, first], parts[3, first] = within(part2, 2), within(part3, 3)
         last = part3
     pieces = {(2, 2): rest2, (3, 2): rest3, **{q: held[q] for q in ((0, 0), (1, 0))}}
@@ -867,7 +866,7 @@
         [(whole(attended.shape), attended)] * 2,
         [pltpu.VMEM(x.shape, F32) for x in state_own]
         + [pltpu.VMEM((HG, TOK, DH), BF16), pltpu.VMEM((HG, DX, TOK), BF16)],
-        HG * TOK * GROUP * HALF, after=(last,),
+        HG * TOK * GROUP * HALF, after=(last, *early),
     )
     parts = dict(zip(parts, handed_on(parts.values(), busy=BUSY)))
     parts[0, 0], parts[1, 0] = part0, within(part1, 1)

time: 84.9 us -> 84.9 us (level)
  transfers between devices with their start and end apart: 19 -> 19, of which waited for: 1 -> 1; matrix products, arithmetic and copies ran while one was open for 0% -> 0% of each run, Pallas kernels for 61% -> 62%
where the time goes in v10:
time: 84.9 us; the launch traced here: 84.7 us
  Pallas kernels  60.1 us (71%)
  starting transfers between devices  22.1 us (26%)
  waiting for transfers between devices  1.11 us (1%)
  local copies, waits for them, and re-layouts  1.09 us (1%)
    pallas_call x15, Pallas kernels, call(): pl.pallas_call(body if extra else kernel, grid_spec=pltpu.PrefetchScalarG...  60.1 us
    ppermute x19, starting transfers between devices, within(): return lax.ppermute(array, 'seq', [(i, i ^ apart) for i in range(count)])  22.1 us
  transfers between devices with their start and end apart: 19, of which 1 were waited for; matrix products, arithmetic and copies ran while one was open for 0% of the time, Pallas kernels for 62%

profile of v10, /device:TPU:0, one launch (start us, length us, event | category | flops | bytes accessed | tf_op | source)
XLA Modules:
  0.0 84.7 jit_solution(15685093372090470048)
XLA Ops:
  0.0 5.0 %shard_map.64 = (bf16[4,144,512]{2,1,0:T(8,128)(2,1)}, bf16[4,144,512]{2,1,0:T(8,128)(2,1)}, bf16[4,144,256]{2,1,0:T(8,128)(2,1)}, bf16[4,144,256]{2,1,0:T(8,128...) custom-call(s32[1]{0:T(128)} %bitcast.index.refs_0_, s32[16]{0:T(128)} %mid.7, s32[16]{0:T(128)} %top.7, ...), custom_call_target="tpu_custom_call" | custom-call | tf_op jit(solution)/shard_map/pallas_call | solution.py:682
  5.0 0.0 copy-start.5
  5.1 0.0 copy-start.6
  5.1 0.5 collective-permute-start
  5.6 2.6 %collective-permute-start.1 = (bf16[4,144,256]{2,1,0:T(8,128)(2,1)}, bf16[4,144,256]{2,1,0:T(8,128)(2,1)S(1)}, u32[]{:S(2)}, u32[]{:S(2)}) collective-permute-start(bf16[4,144,256]{2,1,0:T(8,128)(2,1)} %get-tuple-element.54), channel_id=1, source_target_pairs={{0,2},{1,3},{2,0},{3,1},{4,6},{5,7},{6,4},{7,5},{8,10},{9,11},{10,... | collective-permute-start | bytes 884744 | tf_op jit(solution)/shard_map/ppermute | solution.py:705
  8.1 0.1 collective-permute-start.2
  8.2 1.1 %copy-done = bf16[4,144,512]{2,1,0:T(8,128)(2,1)S(1)} copy-done((bf16[4,144,512]{2,1,0:T(8,128)(2,1)S(1)}, bf16[4,144,512]{2,1,0:T(8,128)(2,1)}, u32[]{:S(2)}) %copy-start) | copy-done | bytes 589848
  9.3 4.2 %collective-permute-start.5 = (bf16[2,144,256]{2,1,0:T(8,128)(2,1)S(1)}, bf16[2,144,256]{2,1,0:T(8,128)(2,1)S(1)}, u32[]{:S(2)}, u32[]{:S(2)}) collective-permute-start(bf16[2,144,256]{2,1,0:T(8,128)(2,1)S(1)} %get-tuple-element.62), channel_id=1, source_target_pairs={{0,12},{1,13},{2,14},{3,15},{4,8},{5,9},{6,10},{7,11},{8,4},{9,5},... | collective-permute-start | bytes 442376 | tf_op jit(solution)/shard_map/ppermute | solution.py:705
  13.6 0.6 collective-permute-start.7
  14.2 8.6 %shard_map.65 = (f32[4,4,64,256]{3,2,1,0:T(8,128)S(1)}, f32[4,4,8,256]{3,2,1,0:T(8,128)S(1)}) custom-call(s32[1]{0:T(128)} %bitcast.index.refs_0_, s32[16]{0:T(128)S(1)} %copy-done.5, s32[16]{0:T(128)S(1)} %copy-done.6, bf16[4,144,512]{2,1,0:T(8,128)(2,1)S(1)} %copy-done.1, bf16[4,144,512]{2,1,0:T(8,128)(2,1)S(1)} %collective-permute-done.refs_1_.b_ref.refs_4_.refs_6_), custom_call_target="tpu_custom_call" | custom-call | tf_op jit(solution)/shard_map/pallas_call | solution.py:682
  22.9 3.8 %collective-permute-start.8 = (bf16[2,144,256]{2,1,0:T(8,128)(2,1)S(1)}, bf16[2,144,256]{2,1,0:T(8,128)(2,1)S(1)}, u32[]{:S(2)}, u32[]{:S(2)}) collective-permute-start(bf16[2,144,256]{2,1,0:T(8,128)(2,1)S(1)} %get-tuple-element.67), channel_id=1, source_target_pairs={{0,12},{1,13},{2,14},{3,15},{4,8},{5,9},{6,10},{7,11},{8,4},{9,5},... | collective-permute-start | bytes 442376 | tf_op jit(solution)/shard_map/ppermute | solution.py:705
  26.7 0.7 collective-permute-start.10
  27.4 0.7 collective-permute-start.3
  28.1 10.1 %shard_map.68 = (f32[4,4,64,256]{3,2,1,0:T(8,128)S(1)}, f32[4,4,8,256]{3,2,1,0:T(8,128)S(1)}, f32[4,2,64,256]{3,2,1,0:T(8,128)S(1)}, f32[4,2,8,256]{3,2,1,0:T(8,128)S(1)}) custom-call(s32[1]{0:T(128)} %bitcast.index.refs_0_, s32[16]{0:T(128)S(1)} %copy-done.5, s32[16]{0:T(128)S(1)} %copy-done.6, bf16[4,144,512]{2,1,0:T(8,128)(2,1)S(1)} %copy-done.1, ...), custom_call_target="tpu_custom_call" | custom-call | tf_op jit(solution)/shard_map/pallas_call | solution.py:682
  38.2 5.2 %shard_map.69 = (bf16[2,4,256,48]{3,2,1,0:T(8,128)(2,1)S(1)}, bf16[2,4,64,256]{3,2,1,0:T(8,128)(2,1)S(1)}, bf16[2,4,48,256]{3,2,1,0:T(8,128)(2,1)S(1)}, f32[2,4,...) custom-call(s32[1]{0:T(128)} %bitcast.index.refs_0_, s32[16]{0:T(128)S(1)} %copy-done.5, ...), custom_call_target="tpu_custom_call" | custom-call | tf_op jit(solution)/shard_map/pallas_call | solution.py:682
  43.4 11.2 %shard_map.70 = (bf16[48,1152]{1,0:T(8,128)(2,1)S(1)}, bf16[48,1152]{1,0:T(8,128)(2,1)S(1)}, bf16[48,1152]{1,0:T(8,128)(2,1)S(1)}, bf16[48,1152]{1,0:T(8,128)(2,1)S(1)}) custom-call(s32[1]{0:T(128)} %bitcast.index.refs_0_, s32[16]{0:T(128)S(1)} %copy-done.5, s32[16]{0:T(128)S(1)} %copy-done.6, ...), custom_call_target="tpu_custom_call" | custom-call | flops 8589934592 | tf_op jit(solution)/shard_map/pallas_call | solution.py:682
  54.6 1.3 %collective-permute-start.11 = (bf16[48,1152]{1,0:T(8,128)(2,1)S(1)}, bf16[48,1152]{1,0:T(8,128)(2,1)S(1)}, u32[]{:S(2)}, u32[]{:S(2)}) collective-permute-start(bf16[48,1152]{1,0:T(8,128)(2,1)S(1)} %get-tuple-element.79), channel_id=1, source_target_pairs={{0,4},{1,5},{2,6},{3,7},{4,0},{5,1},{6,2},{7,3},{8,12},{9,13},{10,... | collective-permute-start | bytes 331784 | tf_op jit(solution)/shard_map/ppermute | solution.py:705
  55.9 2.9 %collective-permute-start.14 = (bf16[48,1152]{1,0:T(8,128)(2,1)S(1)}, bf16[48,1152]{1,0:T(8,128)(2,1)S(1)}, u32[]{:S(2)}, u32[]{:S(2)}) collective-permute-start(bf16[48,1152]{1,0:T(8,128)(2,1)S(1)} %get-tuple-element.84), channel_id=1, source_target_pairs={{0,8},{1,9},{2,10},{3,11},{4,12},{5,13},{6,14},{7,15},{8,0},{9,1},... | collective-permute-start | bytes 331784 | tf_op jit(solution)/shard_map/ppermute | solution.py:705
  58.9 0.2 collective-permute-start.15
  59.1 5.4 %shard_map.71 = (f32[2,4,64,256]{3,2,1,0:T(8,128)S(1)}, f32[2,4,8,256]{3,2,1,0:T(8,128)S(1)}) custom-call(s32[1]{0:T(128)} %bitcast.index.refs_0_, s32[16]{0:T(128)S(1)} %copy-done.5, s32[16]{0:T(128)S(1)} %copy-done.6, bf16[4,144,512]{2,1,0:T(8,128)(2,1)S(1)} %copy-done.1, bf16[4,144,512]{2,1,0:T(8,128)(2,1)S(1)} %collective-permute-done.refs_1_.b_ref.refs_4_.refs_6_, ...), custom_call_target="tpu_custom_call" | custom-call | tf_op jit(solution)/shard_map/pallas_call | solution.py:682
  64.5 0.1 shard_map.72
  64.6 0.1 collective-permute-start.12
  64.7 2.1 %collective-permute-start.13 = (bf16[2,48,512]{2,1,0:T(8,128)(2,1)S(1)}, bf16[2,48,512]{2,1,0:T(8,128)(2,1)S(1)}, u32[]{:S(2)}, u32[]{:S(2)}) collective-permute-start(bf16[2,48,512]{2,1,0:T(8,128)(2,1)S(1)} %get-tuple-element.81.refs_11_), channel_id=1, source_target_pairs={{0,3},{1,2},{2,1},{3,0},{4,7},{5,6},{6,5},{7,4},{8,11},{9,10},{10,... | collective-permute-start | bytes 294920 | tf_op jit(solution)/shard_map/ppermute | solution.py:705
  66.8 5.6 %shard_map.73 = (f32[2,4,64,256]{3,2,1,0:T(8,128)S(1)}, f32[2,4,8,256]{3,2,1,0:T(8,128)S(1)}) custom-call(s32[1]{0:T(128)} %bitcast.index.refs_0_, s32[16]{0:T(128)S(1)} %copy-done.5, s32[16]{0:T(128)S(1)} %copy-done.6, bf16[4,144,512]{2,1,0:T(8,128)(2,1)S(1)} %copy-done.1, bf16[4,144,512]{2,1,0:T(8,128)(2,1)S(1)} %collective-permute-done.refs_1_.b_ref.refs_4_.refs_6_, ...), custom_call_target="tpu_custom_call" | custom-call | tf_op jit(solution)/shard_map/pallas_call | solution.py:682
  72.4 0.1 shard_map.75
  72.5 0.4 collective-permute-start.16
  72.9 1.0 %collective-permute-start.17 = (bf16[2,48,512]{2,1,0:T(8,128)(2,1)S(1)}, bf16[2,48,512]{2,1,0:T(8,128)(2,1)S(1)}, u32[]{:S(2)}, u32[]{:S(2)}) collective-permute-start(bf16[2,48,512]{2,1,0:T(8,128)(2,1)S(1)} %get-tuple-element.89.refs_13_), channel_id=1, source_target_pairs={{0,3},{1,2},{2,1},{3,0},{4,7},{5,6},{6,5},{7,4},{8,11},{9,10},{10,... | collective-permute-start | bytes 294920 | tf_op jit(solution)/shard_map/ppermute | solution.py:705
  73.9 5.8 %shard_map.77 = (bf16[4,48,512]{2,1,0:T(8,128)(2,1)S(1)}, bf16[4,48,512]{2,1,0:T(8,128)(2,1)S(1)}) custom-call(s32[1]{0:T(128)} %bitcast.index.refs_0_, s32[16]{0:T(128)S(1)} %copy-done.5, s32[16]{0:T(128)S(1)} %copy-done.6, bf16[4,144,256]{2,1,0:T(8,128)(2,1)S(1)} %collective-permute-done.3.refs_7_.refs_3_, ...), custom_call_target="tpu_custom_call" | custom-call | tf_op jit(solution)/shard_map/pallas_call | solution.py:682
  79.8 0.0 copy-start.2
  79.8 0.8 collective-permute-start.18
  80.6 1.1 %collective-permute-done.18.refs_5_ = bf16[4,48,512]{2,1,0:T(8,128)(2,1)S(1)} collective-permute-done((bf16[4,48,512]{2,1,0:T(8,128)(2,1)S(1)}, bf16[4,48,512]{2,1,0:T(8,128)(2,1)S(1)}, u32[]{:S(2)}, u32[]{:S(2)}) %collective-permute-start.18) | collective-permute-done | bytes 196640 | tf_op jit(solution)/shard_map/ppermute | solution.py:705
  81.7 3.0 %shard_map.78 = bf16[512,768]{1,0:T(8,128)(2,1)} custom-call(s32[1]{0:T(128)} %bitcast.index.refs_0_, s32[16]{0:T(128)S(1)} %copy-done.5, s32[16]{0:T(128)S(1)} %copy-done.6, bf16[2,48,512]{2,1,0:T(8,128)(2,1)S(1)} %get-tuple-element.90.refs_0_, bf16[2,48,512]{2,1,0:T(8,128)(2,1)S(1)} %get-tuple-element.91.refs_1_, ...), custom_call_target="tpu_custom_call" | custom-call | tf_op jit(solution)/shard_map/pallas_call | solution.py:682
  (35 shorter events, 0.1 us)
Async XLA Ops:
  5.0 9.2 %copy-start.5 = (s32[16]{0:T(128)S(1)}, s32[16]{0:T(128)}, u32[]{:S(2)}) copy-start(s32[16]{0:T(128)} %mid.7) | copy-start | bytes 196
  5.1 9.2 %copy-start.6 = (s32[16]{0:T(128)S(1)}, s32[16]{0:T(128)}, u32[]{:S(2)}) copy-start(s32[16]{0:T(128)} %top.7) | copy-start | bytes 196
  5.1 3.2 %collective-permute-start = (bf16[4,144,512]{2,1,0:T(8,128)(2,1)}, bf16[4,144,512]{2,1,0:T(8,128)(2,1)S(1)}, u32[]{:S(2)}, u32[]{:S(2)}) collective-permute-start(bf16[4,144,512]{2,1,0:T(8,128)(2,1)} %get-tuple-element.53), channel_id=1, source_target_pairs={{0,1},{1,0},{2,3},{3,2},{4,5},{5,4},{6,7},{7,6},{8,9},{9,8},{10,11... | collective-permute-start | bytes 1769480 | tf_op jit(solution)/shard_map/ppermute | solution.py:705
  5.6 17.2 %collective-permute-start.1 = (bf16[4,144,256]{2,1,0:T(8,128)(2,1)}, bf16[4,144,256]{2,1,0:T(8,128)(2,1)S(1)}, u32[]{:S(2)}, u32[]{:S(2)}) collective-permute-start(bf16[4,144,256]{2,1,0:T(8,128)(2,1)} %get-tuple-element.54), channel_id=1, source_target_pairs={{0,2},{1,3},{2,0},{3,1},{4,6},{5,7},{6,4},{7,5},{8,10},{9,11},{10,... | collective-permute-start | bytes 884744 | tf_op jit(solution)/shard_map/ppermute | solution.py:705
  8.1 14.7 %collective-permute-start.2 = (bf16[4,144,256]{2,1,0:T(8,128)(2,1)}, bf16[4,144,256]{2,1,0:T(8,128)(2,1)S(1)}, u32[]{:S(2)}, u32[]{:S(2)}) collective-permute-start(bf16[4,144,256]{2,1,0:T(8,128)(2,1)} %get-tuple-element.55), channel_id=1, source_target_pairs={{0,3},{1,2},{2,1},{3,0},{4,7},{5,6},{6,5},{7,4},{8,11},{9,10},{10,... | collective-permute-start | bytes 884744 | tf_op jit(solution)/shard_map/ppermute | solution.py:705
  8.2 1.1 %copy-start = (bf16[4,144,512]{2,1,0:T(8,128)(2,1)S(1)}, bf16[4,144,512]{2,1,0:T(8,128)(2,1)}, u32[]{:S(2)}) copy-start(bf16[4,144,512]{2,1,0:T(8,128)(2,1)} %get-tuple-element.52.refs_0_.a_ref.refs_3_.refs_5_) | copy-start | bytes 1769476
  9.3 4.9 %copy-start.1 = (bf16[4,144,512]{2,1,0:T(8,128)(2,1)S(1)}, bf16[4,144,512]{2,1,0:T(8,128)(2,1)}, u32[]{:S(2)}) copy-start(bf16[4,144,512]{2,1,0:T(8,128)(2,1)} %get-tuple-element.52.refs_0_.a_ref.refs_3_.refs_5_) | copy-start | bytes 1769476
  9.3 13.6 %copy-start.3 = (bf16[4,144,256]{2,1,0:T(8,128)(2,1)S(1)}, bf16[4,144,256]{2,1,0:T(8,128)(2,1)}, u32[]{:S(2)}) copy-start(bf16[4,144,256]{2,1,0:T(8,128)(2,1)} %get-tuple-element.57.refs_3_) | copy-start | bytes 884740
  9.3 13.6 %copy-start.4 = (bf16[4,144,256]{2,1,0:T(8,128)(2,1)S(1)}, bf16[4,144,256]{2,1,0:T(8,128)(2,1)}, u32[]{:S(2)}) copy-start(bf16[4,144,256]{2,1,0:T(8,128)(2,1)} %get-tuple-element.58.refs_4_) | copy-start | bytes 884740
  9.3 17.4 %collective-permute-start.5 = (bf16[2,144,256]{2,1,0:T(8,128)(2,1)S(1)}, bf16[2,144,256]{2,1,0:T(8,128)(2,1)S(1)}, u32[]{:S(2)}, u32[]{:S(2)}) collective-permute-start(bf16[2,144,256]{2,1,0:T(8,128)(2,1)S(1)} %get-tuple-element.62), channel_id=1, source_target_pairs={{0,12},{1,13},{2,14},{3,15},{4,8},{5,9},{6,10},{7,11},{8,4},{9,5},... | collective-permute-start | bytes 442376 | tf_op jit(solution)/shard_map/ppermute | solution.py:705
  13.6 13.8 %collective-permute-start.6 = (bf16[2,144,256]{2,1,0:T(8,128)(2,1)S(1)}, bf16[2,144,256]{2,1,0:T(8,128)(2,1)S(1)}, u32[]{:S(2)}, u32[]{:S(2)}) collective-permute-start(bf16[2,144,256]{2,1,0:T(8,128)(2,1)S(1)} %get-tuple-element.63), channel_id=1, source_target_pairs={{0,8},{1,9},{2,10},{3,11},{4,12},{5,13},{6,14},{7,15},{8,0},{9,1},... | collective-permute-start | bytes 442376 | tf_op jit(solution)/shard_map/ppermute | solution.py:705
  13.6 14.5 %collective-permute-start.7 = (bf16[2,144,256]{2,1,0:T(8,128)(2,1)S(1)}, bf16[2,144,256]{2,1,0:T(8,128)(2,1)S(1)}, u32[]{:S(2)}, u32[]{:S(2)}) collective-permute-start(bf16[2,144,256]{2,1,0:T(8,128)(2,1)S(1)} %get-tuple-element.64), channel_id=1, source_target_pairs={{0,4},{1,5},{2,6},{3,7},{4,0},{5,1},{6,2},{7,3},{8,12},{9,13},{10,... | collective-permute-start | bytes 442376 | tf_op jit(solution)/shard_map/ppermute | solution.py:705
  22.9 20.5 %collective-permute-start.8 = (bf16[2,144,256]{2,1,0:T(8,128)(2,1)S(1)}, bf16[2,144,256]{2,1,0:T(8,128)(2,1)S(1)}, u32[]{:S(2)}, u32[]{:S(2)}) collective-permute-start(bf16[2,144,256]{2,1,0:T(8,128)(2,1)S(1)} %get-tuple-element.67), channel_id=1, source_target_pairs={{0,12},{1,13},{2,14},{3,15},{4,8},{5,9},{6,10},{7,11},{8,4},{9,5},... | collective-permute-start | bytes 442376 | tf_op jit(solution)/shard_map/ppermute | solution.py:705
  26.7 16.7 %collective-permute-start.9 = (bf16[2,144,256]{2,1,0:T(8,128)(2,1)S(1)}, bf16[2,144,256]{2,1,0:T(8,128)(2,1)S(1)}, u32[]{:S(2)}, u32[]{:S(2)}) collective-permute-start(bf16[2,144,256]{2,1,0:T(8,128)(2,1)S(1)} %get-tuple-element.68), channel_id=1, source_target_pairs={{0,8},{1,9},{2,10},{3,11},{4,12},{5,13},{6,14},{7,15},{8,0},{9,1},... | collective-permute-start | bytes 442376 | tf_op jit(solution)/shard_map/ppermute | solution.py:705
  26.7 16.7 %collective-permute-start.10 = (bf16[2,144,256]{2,1,0:T(8,128)(2,1)S(1)}, bf16[2,144,256]{2,1,0:T(8,128)(2,1)S(1)}, u32[]{:S(2)}, u32[]{:S(2)}) collective-permute-start(bf16[2,144,256]{2,1,0:T(8,128)(2,1)S(1)} %get-tuple-element.69), channel_id=1, source_target_pairs={{0,4},{1,5},{2,6},{3,7},{4,0},{5,1},{6,2},{7,3},{8,12},{9,13},{10,... | collective-permute-start | bytes 442376 | tf_op jit(solution)/shard_map/ppermute | solution.py:705
  27.4 31.7 %collective-permute-start.3 = (bf16[4,144,256]{2,1,0:T(8,128)(2,1)S(1)}, bf16[4,144,256]{2,1,0:T(8,128)(2,1)S(1)}, u32[]{:S(2)}, u32[]{:S(2)}) collective-permute-start(bf16[4,144,256]{2,1,0:T(8,128)(2,1)S(1)} %get-tuple-element.59), channel_id=1, source_target_pairs={{0,2},{1,3},{2,0},{3,1},{4,6},{5,7},{6,4},{7,5},{8,10},{9,11},{10,... | collective-permute-start | bytes 884744 | tf_op jit(solution)/shard_map/ppermute | solution.py:705
  28.1 31.0 %collective-permute-start.4 = (bf16[4,144,256]{2,1,0:T(8,128)(2,1)S(1)}, bf16[4,144,256]{2,1,0:T(8,128)(2,1)S(1)}, u32[]{:S(2)}, u32[]{:S(2)}) collective-permute-start(bf16[4,144,256]{2,1,0:T(8,128)(2,1)S(1)} %get-tuple-element.60), channel_id=1, source_target_pairs={{0,3},{1,2},{2,1},{3,0},{4,7},{5,6},{6,5},{7,4},{8,11},{9,10},{10,... | collective-permute-start | bytes 884744 | tf_op jit(solution)/shard_map/ppermute | solution.py:705
  54.6 9.9 %collective-permute-start.11 = (bf16[48,1152]{1,0:T(8,128)(2,1)S(1)}, bf16[48,1152]{1,0:T(8,128)(2,1)S(1)}, u32[]{:S(2)}, u32[]{:S(2)}) collective-permute-start(bf16[48,1152]{1,0:T(8,128)(2,1)S(1)} %get-tuple-element.79), channel_id=1, source_target_pairs={{0,4},{1,5},{2,6},{3,7},{4,0},{5,1},{6,2},{7,3},{8,12},{9,13},{10,... | collective-permute-start | bytes 331784 | tf_op jit(solution)/shard_map/ppermute | solution.py:705
  55.9 16.5 %collective-permute-start.14 = (bf16[48,1152]{1,0:T(8,128)(2,1)S(1)}, bf16[48,1152]{1,0:T(8,128)(2,1)S(1)}, u32[]{:S(2)}, u32[]{:S(2)}) collective-permute-start(bf16[48,1152]{1,0:T(8,128)(2,1)S(1)} %get-tuple-element.84), channel_id=1, source_target_pairs={{0,8},{1,9},{2,10},{3,11},{4,12},{5,13},{6,14},{7,15},{8,0},{9,1},... | collective-permute-start | bytes 331784 | tf_op jit(solution)/shard_map/ppermute | solution.py:705
  58.9 13.5 %collective-permute-start.15 = (bf16[48,1152]{1,0:T(8,128)(2,1)S(1)}, bf16[48,1152]{1,0:T(8,128)(2,1)S(1)}, u32[]{:S(2)}, u32[]{:S(2)}) collective-permute-start(bf16[48,1152]{1,0:T(8,128)(2,1)S(1)} %get-tuple-element.85), channel_id=1, source_target_pairs={{0,12},{1,13},{2,14},{3,15},{4,8},{5,9},{6,10},{7,11},{8,4},{9,5},... | collective-permute-start | bytes 331784 | tf_op jit(solution)/shard_map/ppermute | solution.py:705
  64.6 9.4 %collective-permute-start.12 = (bf16[2,48,512]{2,1,0:T(8,128)(2,1)S(1)}, bf16[2,48,512]{2,1,0:T(8,128)(2,1)S(1)}, u32[]{:S(2)}, u32[]{:S(2)}) collective-permute-start(bf16[2,48,512]{2,1,0:T(8,128)(2,1)S(1)} %get-tuple-element.80), channel_id=1, source_target_pairs={{0,2},{1,3},{2,0},{3,1},{4,6},{5,7},{6,4},{7,5},{8,10},{9,11},{10,... | collective-permute-start | bytes 294920 | tf_op jit(solution)/shard_map/ppermute | solution.py:705
  64.7 9.3 %collective-permute-start.13 = (bf16[2,48,512]{2,1,0:T(8,128)(2,1)S(1)}, bf16[2,48,512]{2,1,0:T(8,128)(2,1)S(1)}, u32[]{:S(2)}, u32[]{:S(2)}) collective-permute-start(bf16[2,48,512]{2,1,0:T(8,128)(2,1)S(1)} %get-tuple-element.81.refs_11_), channel_id=1, source_target_pairs={{0,3},{1,2},{2,1},{3,0},{4,7},{5,6},{6,5},{7,4},{8,11},{9,10},{10,... | collective-permute-start | bytes 294920 | tf_op jit(solution)/shard_map/ppermute | solution.py:705
  72.5 8.1 %collective-permute-start.16 = (bf16[2,48,512]{2,1,0:T(8,128)(2,1)S(1)}, bf16[2,48,512]{2,1,0:T(8,128)(2,1)S(1)}, u32[]{:S(2)}, u32[]{:S(2)}) collective-permute-start(bf16[2,48,512]{2,1,0:T(8,128)(2,1)S(1)} %get-tuple-element.88), channel_id=1, source_target_pairs={{0,2},{1,3},{2,0},{3,1},{4,6},{5,7},{6,4},{7,5},{8,10},{9,11},{10,... | collective-permute-start | bytes 294920 | tf_op jit(solution)/shard_map/ppermute | solution.py:705
  72.9 7.7 %collective-permute-start.17 = (bf16[2,48,512]{2,1,0:T(8,128)(2,1)S(1)}, bf16[2,48,512]{2,1,0:T(8,128)(2,1)S(1)}, u32[]{:S(2)}, u32[]{:S(2)}) collective-permute-start(bf16[2,48,512]{2,1,0:T(8,128)(2,1)S(1)} %get-tuple-element.89.refs_13_), channel_id=1, source_target_pairs={{0,3},{1,2},{2,1},{3,0},{4,7},{5,6},{6,5},{7,4},{8,11},{9,10},{10,... | collective-permute-start | bytes 294920 | tf_op jit(solution)/shard_map/ppermute | solution.py:705
  79.8 1.9 %copy-start.2 = (bf16[768,768]{1,0:T(8,128)(2,1)S(1)}, bf16[768,768]{1,0:T(8,128)(2,1)}, u32[]{:S(2)}) copy-start(bf16[768,768]{1,0:T(8,128)(2,1)} %refs_6_.1) | copy-start | bytes 3538948
  79.8 1.9 %collective-permute-start.18 = (bf16[4,48,512]{2,1,0:T(8,128)(2,1)S(1)}, bf16[4,48,512]{2,1,0:T(8,128)(2,1)S(1)}, u32[]{:S(2)}, u32[]{:S(2)}) collective-permute-start(bf16[4,48,512]{2,1,0:T(8,128)(2,1)S(1)} %get-tuple-element.98), channel_id=1, source_target_pairs={{0,1},{1,0},{2,3},{3,2},{4,5},{5,4},{6,7},{7,6},{8,9},{9,8},{10,11... | collective-permute-start | bytes 589832 | tf_op jit(solution)/shard_map/ppermute | solution.py:705

commit v11 on v10

--- a/solution.py
+++ b/solution.py
@@ -213,14 +213,15 @@
         pltpu.make_async_copy(hbm, block, sems_in.at[i])
         for i, (hbm, block) in enumerate(zip((k_hbm, v_hbm, q_hbm), blocks))
     ]
-    for load in loads:
-        load.start()
+    loads[0].start()
     picker = token_picker()
     stores = []
     heads = {(j, p): head_of(place, j, p) for j in range(GROUP) for p in range(HG)}
     classes = {at: class_of_slots(*offsets_of(place, head)) for at, head in heads.items()}
     for n, (load, block, scratch) in enumerate(zip(loads, blocks, held)):
         load.wait()
+        for later in loads[1:] if n == 0 else ():
+            later.start()
         fill_class_major(block[...], picker, scratch)
         rows = slice(n * DH, (n + 1) * DH)
         for i, (j, first, count) in enumerate(
@@ -443,7 +444,7 @@
     )
 
 
-def far_own_kernel(index, mid, top, own0, own1, beyond1, beyond2, beyond3, *refs):
+def far_own_kernel(index, mid, top, own0, own1, beyond3, beyond2, beyond1, *refs):
     k_s, v_s, q_s, acc_ref, max_ref, length_ref = refs
     sources = [(own0.at[0], own1.at[0])] + [
         (ref.at[0], ref.at[1]) for ref in (beyond1, beyond2, beyond3)
@@ -505,9 +506,25 @@
     pl.when(jnp.logical_not(plain))(run)
 
 
+def near_and_far_kernel(near_args, steps, index, mid, top, *refs):
+    scalars = (index, mid, top)
+    inputs, tasks, carried = near_args[0], near_args[2], near_args[3]
+    count = len(inputs) + 2 * carried
+    near_in, far_in, refs = refs[:count], refs[count : count + 5], refs[count + 5 :]
+    near_out, far_out, scratch = refs[: 2 * len(tasks)], refs[2 * len(tasks) : -2], refs[-2:]
+
+    @pl.when(pl.program_id(0) < steps)
+    def _():
+        near_kernel(*near_args, *scalars, *near_in, *near_out, *scratch)
+
+    @pl.when(pl.program_id(0) == steps)
+    def _():
+        far_own_kernel(*scalars, *far_in, *far_out)
+
+
 def far_kernel(index, mid, top, *refs):
     place = (index, mid, top)
-    sel2, sel3, beyond3, beyond2, beyond1, k_own, v_own, q_own, acc_in, max_in, length_in = refs[
+    sel2, sel3, beyond2, beyond1, beyond3, k_own, v_own, q_own, acc_in, max_in, length_in = refs[
         :11
     ]
     outs = refs[11 : 11 + RATE]
@@ -662,8 +679,12 @@
     return pl.BlockSpec(shape, lambda *_: (0,) * len(shape))
 
 
-def per_head(shape, skip=0):
-    return pl.BlockSpec(shape, lambda h, *_: (h + skip,) + (0,) * (len(shape) - 1))
+def per_head(shape, skip=0, last=None):
+    def index(h, *_):
+        at = h + skip if last is None else jnp.minimum(h, last)
+        return (at,) + (0,) * (len(shape) - 1)
+
+    return pl.BlockSpec(shape, index)
 
 
 def call(
@@ -777,42 +798,50 @@
     rest2, rest3 = within(rest2, 2), within(rest3, 3)
 
     held.update({(2, 0): sel2, (3, 0): sel3})
-    out = near(
-        held, own_sel + own_rest + other_sel,
-        [
-            [(q, 3, (0, i)) for i, q in enumerate(own)],
-            [((2, 0), 0, None), ((3, 0), 0, None)],
-        ],
-        [state_own],
-        after=ours[::-1],
-    )
-    state_own, state_sel = out[:2], out[2:]
-
-    result = jax.ShapeDtypeStruct((DH, GROUP * HALF + BLK), BF16)
-    piece_0 = pl.BlockSpec((1, 3 * DH, HALF), lambda *_: (0, 0, 0))
-    pieces_shapes = [
+    units = own_sel + own_rest + other_sel
+    tasks = [
+        [(q, 3, (0, i)) for i, q in enumerate(own)],
+        [((2, 0), 0, None), ((3, 0), 0, None)],
+    ]
+    arrays = [*held.values(), *state_own]
+    near_shapes = [
+        jax.ShapeDtypeStruct((HG, len(group), rows, HALF), F32)
+        for group in tasks
+        for rows in (DX, 8)
+    ]
+    far_shapes = [
         jax.ShapeDtypeStruct((2, RATE, HALF, DH), BF16),
         jax.ShapeDtypeStruct((2, RATE, DX, HALF), BF16),
         jax.ShapeDtypeStruct((2, RATE, DH, HALF), BF16),
-    ]
-    sums_shapes = [
         jax.ShapeDtypeStruct((2, RATE, DX, HALF), F32),
         jax.ShapeDtypeStruct((2, RATE, 8, HALF), F32),
     ]
+    piece_0 = pl.BlockSpec((1, 3 * DH, HALF), lambda *_: (0, 0, 0))
     in_scalars = pl.BlockSpec(memory_space=pltpu.SMEM)
-    far_own = call(
-        far_own_kernel, place, (own0, own1, *ours), (1,),
-        [piece_0] * 2 + [whole(pair.shape)] * 3,
-        [(whole(x.shape), x) for x in pieces_shapes + sums_shapes]
+    step, steps = 2, HG // 2
+    keys = sum(len(members) for _, members in units) * BLK
+    out = call(
+        functools.partial(
+            near_and_far_kernel, (list(held), units, tasks, 1, 0, step), steps
+        ),
+        place, (*arrays, own0, own1, *ours[::-1]), (steps + 1,),
+        [per_head((step,) + x.shape[1:], last=steps - 1) for x in arrays]
+        + [piece_0] * 2 + [whole(pair.shape)] * 3,
+        [(per_head((step,) + x.shape[1:], last=steps - 1), x) for x in near_shapes]
+        + [(whole(x.shape), x) for x in far_shapes]
         + [(in_scalars, jax.ShapeDtypeStruct((2,), F32))],
-        [], RATE * 2 * 3 * HALF * HALF, after=(state_sel[1],),
-    )
+        [pltpu.VMEM((step, keys, DH), BF16), pltpu.VMEM((step, DX, keys), BF16)],
+        1 << 18,
+    )
+    state_own, state_sel, far_own = out[:2], out[2:4], out[4:]
+
+    result = jax.ShapeDtypeStruct((DH, GROUP * HALF + BLK), BF16)
     results = call(
-        far_kernel, place, (sel2, sel3, *theirs[::-1], *far_own), (1,),
+        far_kernel, place, (sel2, sel3, theirs[1], theirs[0], theirs[2], *far_own), (1,),
         [piece_0] * 2 + [whole(pair.shape)] * 3
         + [whole(x.shape) for x in far_own[:-1]] + [in_scalars],
         [(whole(result.shape), result)] * RATE,
-        [pltpu.VMEM(x.shape, BF16) for x in pieces_shapes]
+        [pltpu.VMEM(x.shape, BF16) for x in far_shapes[:3]]
         + [
             pltpu.VMEM((RATE, DH, GROUP * HALF), BF16),
             pltpu.VMEM((RATE, DH, BLK), F32),

time: 84.9 us -> 86 us (1.013)
  Pallas kernels: 60.1 us -> 61.2 us
    pallas_call x15 -> x14, Pallas kernels: 60.1 us -> 61.2 us  [call(): pl.pallas_call(body if extra else kernel, grid_spec=pltpu.PrefetchScalarG...]
  transfers between devices with their start and end apart: 19 -> 19, of which waited for: 1 -> 1; matrix products, arithmetic and copies ran while one was open for 0% -> 0% of each run, Pallas kernels for 62% -> 60%
where the time goes in v11:
time: 86 us; the launch traced here: 85.8 us
  Pallas kernels  61.2 us (71%)
  starting transfers between devices  22.1 us (26%)
  waiting for transfers between devices  1.11 us (1%)
  local copies, waits for them, and re-layouts  1.09 us (1%)
    pallas_call x14, Pallas kernels, call(): pl.pallas_call(body if extra else kernel, grid_spec=pltpu.PrefetchScalarG...  61.2 us
    ppermute x19, starting transfers between devices, within(): return lax.ppermute(array, 'seq', [(i, i ^ apart) for i in range(count)])  22.1 us
  transfers between devices with their start and end apart: 19, of which 1 were waited for; matrix products, arithmetic and copies ran while one was open for 0% of the time, Pallas kernels for 60%

profile of v11, /device:TPU:0, one launch (start us, length us, event | category | flops | bytes accessed | tf_op | source)
XLA Modules:
  0.0 85.8 jit_solution(7263602710635192007)
XLA Ops:
  0.0 6.3 %shard_map.64 = (bf16[4,144,512]{2,1,0:T(8,128)(2,1)}, bf16[4,144,512]{2,1,0:T(8,128)(2,1)}, bf16[4,144,256]{2,1,0:T(8,128)(2,1)}, bf16[4,144,256]{2,1,0:T(8,128...) custom-call(s32[1]{0:T(128)} %bitcast.index.refs_0_, s32[16]{0:T(128)} %mid.9, s32[16]{0:T(128)} %top.9, ...), custom_call_target="tpu_custom_call" | custom-call | tf_op jit(solution)/shard_map/pallas_call | solution.py:703
  6.3 0.0 copy-start.5
  6.3 0.0 copy-start.6
  6.4 0.5 collective-permute-start
  6.9 2.6 %collective-permute-start.1 = (bf16[4,144,256]{2,1,0:T(8,128)(2,1)}, bf16[4,144,256]{2,1,0:T(8,128)(2,1)S(1)}, u32[]{:S(2)}, u32[]{:S(2)}) collective-permute-start(bf16[4,144,256]{2,1,0:T(8,128)(2,1)} %get-tuple-element.54), channel_id=1, source_target_pairs={{0,2},{1,3},{2,0},{3,1},{4,6},{5,7},{6,4},{7,5},{8,10},{9,11},{10,... | collective-permute-start | bytes 884744 | tf_op jit(solution)/shard_map/ppermute | solution.py:726
  9.4 0.1 collective-permute-start.2
  9.5 0.0 collective-permute-done.refs_1_.b_ref.refs_7_.refs_4_.refs_6_
  9.5 1.1 %copy-done = bf16[4,144,512]{2,1,0:T(8,128)(2,1)S(1)} copy-done((bf16[4,144,512]{2,1,0:T(8,128)(2,1)S(1)}, bf16[4,144,512]{2,1,0:T(8,128)(2,1)}, u32[]{:S(2)}) %copy-start) | copy-done | bytes 589848
  10.6 4.2 %collective-permute-start.5 = (bf16[2,144,256]{2,1,0:T(8,128)(2,1)S(1)}, bf16[2,144,256]{2,1,0:T(8,128)(2,1)S(1)}, u32[]{:S(2)}, u32[]{:S(2)}) collective-permute-start(bf16[2,144,256]{2,1,0:T(8,128)(2,1)S(1)} %get-tuple-element.62), channel_id=1, source_target_pairs={{0,12},{1,13},{2,14},{3,15},{4,8},{5,9},{6,10},{7,11},{8,4},{9,5},... | collective-permute-start | bytes 442376 | tf_op jit(solution)/shard_map/ppermute | solution.py:726
  14.9 0.6 collective-permute-start.7
  15.5 8.7 %shard_map.65 = (f32[4,4,64,256]{3,2,1,0:T(8,128)S(1)}, f32[4,4,8,256]{3,2,1,0:T(8,128)S(1)}) custom-call(s32[1]{0:T(128)} %bitcast.index.refs_0_, s32[16]{0:T(128)S(1)} %copy-done.5, s32[16]{0:T(128)S(1)} %copy-done.6, bf16[4,144,512]{2,1,0:T(8,128)(2,1)S(1)} %copy-done.1, bf16[4,144,512]{2,1,0:T(8,128)(2,1)S(1)} %collective-permute-done.refs_1_.b_ref.refs_7_.refs_4_.refs_6_), custom_call_target="tpu_custom_call" | custom-call | tf_op jit(solution)/shard_map/pallas_call | solution.py:703
  24.3 3.8 %collective-permute-start.10 = (bf16[2,144,256]{2,1,0:T(8,128)(2,1)S(1)}, bf16[2,144,256]{2,1,0:T(8,128)(2,1)S(1)}, u32[]{:S(2)}, u32[]{:S(2)}) collective-permute-start(bf16[2,144,256]{2,1,0:T(8,128)(2,1)S(1)} %get-tuple-element.69), channel_id=1, source_target_pairs={{0,12},{1,13},{2,14},{3,15},{4,8},{5,9},{6,10},{7,11},{8,4},{9,5},... | collective-permute-start | bytes 442376 | tf_op jit(solution)/shard_map/ppermute | solution.py:726
  28.1 0.6 collective-permute-start.9
  28.8 0.6 collective-permute-start.3
  29.4 14.6 %shard_map.68 = (f32[4,4,64,256]{3,2,1,0:T(8,128)S(1)}, f32[4,4,8,256]{3,2,1,0:T(8,128)S(1)}, f32[4,2,64,256]{3,2,1,0:T(8,128)S(1)}, f32[4,2,8,256]{3,2,1,0:T(8,...) custom-call(s32[1]{0:T(128)} %bitcast.index.refs_0_, ...), custom_call_target="tpu_custom_call" | custom-call | tf_op jit(solution)/shard_map/pallas_call | solution.py:703
  44.1 11.4 %shard_map.69 = (bf16[48,1152]{1,0:T(8,128)(2,1)S(1)}, bf16[48,1152]{1,0:T(8,128)(2,1)S(1)}, bf16[48,1152]{1,0:T(8,128)(2,1)S(1)}, bf16[48,1152]{1,0:T(8,128)(2,1)S(1)}) custom-call(s32[1]{0:T(128)} %bitcast.index.refs_0_, s32[16]{0:T(128)S(1)} %copy-done.5, s32[16]{0:T(128)S(1)} %copy-done.6, ...), custom_call_target="tpu_custom_call" | custom-call | flops 8589934592 | tf_op jit(solution)/shard_map/pallas_call | solution.py:703
  55.5 1.3 %collective-permute-start.11 = (bf16[48,1152]{1,0:T(8,128)(2,1)S(1)}, bf16[48,1152]{1,0:T(8,128)(2,1)S(1)}, u32[]{:S(2)}, u32[]{:S(2)}) collective-permute-start(bf16[48,1152]{1,0:T(8,128)(2,1)S(1)} %get-tuple-element.79), channel_id=1, source_target_pairs={{0,4},{1,5},{2,6},{3,7},{4,0},{5,1},{6,2},{7,3},{8,12},{9,13},{10,... | collective-permute-start | bytes 331784 | tf_op jit(solution)/shard_map/ppermute | solution.py:726
  56.8 2.9 %collective-permute-start.14 = (bf16[48,1152]{1,0:T(8,128)(2,1)S(1)}, bf16[48,1152]{1,0:T(8,128)(2,1)S(1)}, u32[]{:S(2)}, u32[]{:S(2)}) collective-permute-start(bf16[48,1152]{1,0:T(8,128)(2,1)S(1)} %get-tuple-element.84), channel_id=1, source_target_pairs={{0,8},{1,9},{2,10},{3,11},{4,12},{5,13},{6,14},{7,15},{8,0},{9,1},... | collective-permute-start | bytes 331784 | tf_op jit(solution)/shard_map/ppermute | solution.py:726
  59.7 0.2 collective-permute-start.15
  60.0 5.4 %shard_map.70 = (f32[2,4,64,256]{3,2,1,0:T(8,128)S(1)}, f32[2,4,8,256]{3,2,1,0:T(8,128)S(1)}) custom-call(s32[1]{0:T(128)} %bitcast.index.refs_0_, s32[16]{0:T(128)S(1)} %copy-done.5, s32[16]{0:T(128)S(1)} %copy-done.6, bf16[4,144,512]{2,1,0:T(8,128)(2,1)S(1)} %copy-done.1, ...), custom_call_target="tpu_custom_call" | custom-call | tf_op jit(solution)/shard_map/pallas_call | solution.py:703
  65.4 0.1 shard_map.71
  65.5 0.1 collective-permute-start.12
  65.5 2.3 %collective-permute-start.13 = (bf16[2,48,512]{2,1,0:T(8,128)(2,1)S(1)}, bf16[2,48,512]{2,1,0:T(8,128)(2,1)S(1)}, u32[]{:S(2)}, u32[]{:S(2)}) collective-permute-start(bf16[2,48,512]{2,1,0:T(8,128)(2,1)S(1)} %get-tuple-element.81.refs_11_), channel_id=1, source_target_pairs={{0,3},{1,2},{2,1},{3,0},{4,7},{5,6},{6,5},{7,4},{8,11},{9,10},{10,... | collective-permute-start | bytes 294920 | tf_op jit(solution)/shard_map/ppermute | solution.py:726
  67.8 5.7 %shard_map.72 = (f32[2,4,64,256]{3,2,1,0:T(8,128)S(1)}, f32[2,4,8,256]{3,2,1,0:T(8,128)S(1)}) custom-call(s32[1]{0:T(128)} %bitcast.index.refs_0_, s32[16]{0:T(128)S(1)} %copy-done.5, s32[16]{0:T(128)S(1)} %copy-done.6, bf16[4,144,512]{2,1,0:T(8,128)(2,1)S(1)} %copy-done.1, ...), custom_call_target="tpu_custom_call" | custom-call | tf_op jit(solution)/shard_map/pallas_call | solution.py:703
  73.5 0.1 shard_map.74
  73.6 0.4 collective-permute-start.16
  74.0 0.8 collective-permute-start.17
  74.9 5.8 %shard_map.76 = (bf16[4,48,512]{2,1,0:T(8,128)(2,1)S(1)}, bf16[4,48,512]{2,1,0:T(8,128)(2,1)S(1)}) custom-call(s32[1]{0:T(128)} %bitcast.index.refs_0_, s32[16]{0:T(128)S(1)} %copy-done.5, s32[16]{0:T(128)S(1)} %copy-done.6, bf16[4,144,256]{2,1,0:T(8,128)(2,1)S(1)} %collective-permute-done.3.refs_7_.refs_3_, ...), custom_call_target="tpu_custom_call" | custom-call | tf_op jit(solution)/shard_map/pallas_call | solution.py:703
  80.7 0.0 copy-start.2
  80.7 1.0 %collective-permute-start.18 = (bf16[4,48,512]{2,1,0:T(8,128)(2,1)S(1)}, bf16[4,48,512]{2,1,0:T(8,128)(2,1)S(1)}, u32[]{:S(2)}, u32[]{:S(2)}) collective-permute-start(bf16[4,48,512]{2,1,0:T(8,128)(2,1)S(1)} %get-tuple-element.98), channel_id=1, source_target_pairs={{0,1},{1,0},{2,3},{3,2},{4,5},{5,4},{6,7},{7,6},{8,9},{9,8},{10,11... | collective-permute-start | bytes 589832 | tf_op jit(solution)/shard_map/ppermute | solution.py:726
  81.7 1.1 %collective-permute-done.18.refs_5_ = bf16[4,48,512]{2,1,0:T(8,128)(2,1)S(1)} collective-permute-done((bf16[4,48,512]{2,1,0:T(8,128)(2,1)S(1)}, bf16[4,48,512]{2,1,0:T(8,128)(2,1)S(1)}, u32[]{:S(2)}, u32[]{:S(2)}) %collective-permute-start.18) | collective-permute-done | bytes 196640 | tf_op jit(solution)/shard_map/ppermute | solution.py:726
  82.8 3.0 %shard_map.77 = bf16[512,768]{1,0:T(8,128)(2,1)} custom-call(s32[1]{0:T(128)} %bitcast.index.refs_0_, s32[16]{0:T(128)S(1)} %copy-done.5, s32[16]{0:T(128)S(1)} %copy-done.6, bf16[2,48,512]{2,1,0:T(8,128)(2,1)S(1)} %get-tuple-element.90.refs_0_, bf16[2,48,512]{2,1,0:T(8,128)(2,1)S(1)} %get-tuple-element.91.refs_1_, ...), custom_call_target="tpu_custom_call" | custom-call | tf_op jit(solution)/shard_map/pallas_call | solution.py:703
  (34 shorter events, 0.1 us)
Async XLA Ops:
  6.3 9.2 %copy-start.5 = (s32[16]{0:T(128)S(1)}, s32[16]{0:T(128)}, u32[]{:S(2)}) copy-start(s32[16]{0:T(128)} %mid.9) | copy-start | bytes 196
  6.3 9.2 %copy-start.6 = (s32[16]{0:T(128)S(1)}, s32[16]{0:T(128)}, u32[]{:S(2)}) copy-start(s32[16]{0:T(128)} %top.9) | copy-start | bytes 196
  6.4 3.2 %collective-permute-start = (bf16[4,144,512]{2,1,0:T(8,128)(2,1)}, bf16[4,144,512]{2,1,0:T(8,128)(2,1)S(1)}, u32[]{:S(2)}, u32[]{:S(2)}) collective-permute-start(bf16[4,144,512]{2,1,0:T(8,128)(2,1)} %get-tuple-element.53), channel_id=1, source_target_pairs={{0,1},{1,0},{2,3},{3,2},{4,5},{5,4},{6,7},{7,6},{8,9},{9,8},{10,11... | collective-permute-start | bytes 1769480 | tf_op jit(solution)/shard_map/ppermute | solution.py:726
  6.9 17.4 %collective-permute-start.1 = (bf16[4,144,256]{2,1,0:T(8,128)(2,1)}, bf16[4,144,256]{2,1,0:T(8,128)(2,1)S(1)}, u32[]{:S(2)}, u32[]{:S(2)}) collective-permute-start(bf16[4,144,256]{2,1,0:T(8,128)(2,1)} %get-tuple-element.54), channel_id=1, source_target_pairs={{0,2},{1,3},{2,0},{3,1},{4,6},{5,7},{6,4},{7,5},{8,10},{9,11},{10,... | collective-permute-start | bytes 884744 | tf_op jit(solution)/shard_map/ppermute | solution.py:726
  9.4 14.8 %collective-permute-start.2 = (bf16[4,144,256]{2,1,0:T(8,128)(2,1)}, bf16[4,144,256]{2,1,0:T(8,128)(2,1)S(1)}, u32[]{:S(2)}, u32[]{:S(2)}) collective-permute-start(bf16[4,144,256]{2,1,0:T(8,128)(2,1)} %get-tuple-element.55), channel_id=1, source_target_pairs={{0,3},{1,2},{2,1},{3,0},{4,7},{5,6},{6,5},{7,4},{8,11},{9,10},{10,... | collective-permute-start | bytes 884744 | tf_op jit(solution)/shard_map/ppermute | solution.py:726
  9.5 1.1 %copy-start = (bf16[4,144,512]{2,1,0:T(8,128)(2,1)S(1)}, bf16[4,144,512]{2,1,0:T(8,128)(2,1)}, u32[]{:S(2)}) copy-start(bf16[4,144,512]{2,1,0:T(8,128)(2,1)} %get-tuple-element.52.refs_0_.a_ref.refs_6_.refs_3_.refs_5_) | copy-start | bytes 1769476
  10.6 4.9 %copy-start.1 = (bf16[4,144,512]{2,1,0:T(8,128)(2,1)S(1)}, bf16[4,144,512]{2,1,0:T(8,128)(2,1)}, u32[]{:S(2)}) copy-start(bf16[4,144,512]{2,1,0:T(8,128)(2,1)} %get-tuple-element.52.refs_0_.a_ref.refs_6_.refs_3_.refs_5_) | copy-start | bytes 1769476
  10.6 13.7 %copy-start.3 = (bf16[4,144,256]{2,1,0:T(8,128)(2,1)S(1)}, bf16[4,144,256]{2,1,0:T(8,128)(2,1)}, u32[]{:S(2)}) copy-start(bf16[4,144,256]{2,1,0:T(8,128)(2,1)} %get-tuple-element.57.refs_3_) | copy-start | bytes 884740
  10.6 13.7 %copy-start.4 = (bf16[4,144,256]{2,1,0:T(8,128)(2,1)S(1)}, bf16[4,144,256]{2,1,0:T(8,128)(2,1)}, u32[]{:S(2)}) copy-start(bf16[4,144,256]{2,1,0:T(8,128)(2,1)} %get-tuple-element.58.refs_4_) | copy-start | bytes 884740
  10.6 17.5 %collective-permute-start.5 = (bf16[2,144,256]{2,1,0:T(8,128)(2,1)S(1)}, bf16[2,144,256]{2,1,0:T(8,128)(2,1)S(1)}, u32[]{:S(2)}, u32[]{:S(2)}) collective-permute-start(bf16[2,144,256]{2,1,0:T(8,128)(2,1)S(1)} %get-tuple-element.62), channel_id=1, source_target_pairs={{0,12},{1,13},{2,14},{3,15},{4,8},{5,9},{6,10},{7,11},{8,4},{9,5},... | collective-permute-start | bytes 442376 | tf_op jit(solution)/shard_map/ppermute | solution.py:726
  14.9 13.9 %collective-permute-start.6 = (bf16[2,144,256]{2,1,0:T(8,128)(2,1)S(1)}, bf16[2,144,256]{2,1,0:T(8,128)(2,1)S(1)}, u32[]{:S(2)}, u32[]{:S(2)}) collective-permute-start(bf16[2,144,256]{2,1,0:T(8,128)(2,1)S(1)} %get-tuple-element.63), channel_id=1, source_target_pairs={{0,8},{1,9},{2,10},{3,11},{4,12},{5,13},{6,14},{7,15},{8,0},{9,1},... | collective-permute-start | bytes 442376 | tf_op jit(solution)/shard_map/ppermute | solution.py:726
  14.9 14.5 %collective-permute-start.7 = (bf16[2,144,256]{2,1,0:T(8,128)(2,1)S(1)}, bf16[2,144,256]{2,1,0:T(8,128)(2,1)S(1)}, u32[]{:S(2)}, u32[]{:S(2)}) collective-permute-start(bf16[2,144,256]{2,1,0:T(8,128)(2,1)S(1)} %get-tuple-element.64), channel_id=1, source_target_pairs={{0,4},{1,5},{2,6},{3,7},{4,0},{5,1},{6,2},{7,3},{8,12},{9,13},{10,... | collective-permute-start | bytes 442376 | tf_op jit(solution)/shard_map/ppermute | solution.py:726
  24.3 19.7 %collective-permute-start.10 = (bf16[2,144,256]{2,1,0:T(8,128)(2,1)S(1)}, bf16[2,144,256]{2,1,0:T(8,128)(2,1)S(1)}, u32[]{:S(2)}, u32[]{:S(2)}) collective-permute-start(bf16[2,144,256]{2,1,0:T(8,128)(2,1)S(1)} %get-tuple-element.69), channel_id=1, source_target_pairs={{0,12},{1,13},{2,14},{3,15},{4,8},{5,9},{6,10},{7,11},{8,4},{9,5},... | collective-permute-start | bytes 442376 | tf_op jit(solution)/shard_map/ppermute | solution.py:726
  28.1 15.9 %collective-permute-start.8 = (bf16[2,144,256]{2,1,0:T(8,128)(2,1)S(1)}, bf16[2,144,256]{2,1,0:T(8,128)(2,1)S(1)}, u32[]{:S(2)}, u32[]{:S(2)}) collective-permute-start(bf16[2,144,256]{2,1,0:T(8,128)(2,1)S(1)} %get-tuple-element.67), channel_id=1, source_target_pairs={{0,8},{1,9},{2,10},{3,11},{4,12},{5,13},{6,14},{7,15},{8,0},{9,1},... | collective-permute-start | bytes 442376 | tf_op jit(solution)/shard_map/ppermute | solution.py:726
  28.1 15.9 %collective-permute-start.9 = (bf16[2,144,256]{2,1,0:T(8,128)(2,1)S(1)}, bf16[2,144,256]{2,1,0:T(8,128)(2,1)S(1)}, u32[]{:S(2)}, u32[]{:S(2)}) collective-permute-start(bf16[2,144,256]{2,1,0:T(8,128)(2,1)S(1)} %get-tuple-element.68), channel_id=1, source_target_pairs={{0,4},{1,5},{2,6},{3,7},{4,0},{5,1},{6,2},{7,3},{8,12},{9,13},{10,... | collective-permute-start | bytes 442376 | tf_op jit(solution)/shard_map/ppermute | solution.py:726
  28.8 31.2 %collective-permute-start.3 = (bf16[4,144,256]{2,1,0:T(8,128)(2,1)S(1)}, bf16[4,144,256]{2,1,0:T(8,128)(2,1)S(1)}, u32[]{:S(2)}, u32[]{:S(2)}) collective-permute-start(bf16[4,144,256]{2,1,0:T(8,128)(2,1)S(1)} %get-tuple-element.59), channel_id=1, source_target_pairs={{0,2},{1,3},{2,0},{3,1},{4,6},{5,7},{6,4},{7,5},{8,10},{9,11},{10,... | collective-permute-start | bytes 884744 | tf_op jit(solution)/shard_map/ppermute | solution.py:726
  29.4 30.6 %collective-permute-start.4 = (bf16[4,144,256]{2,1,0:T(8,128)(2,1)S(1)}, bf16[4,144,256]{2,1,0:T(8,128)(2,1)S(1)}, u32[]{:S(2)}, u32[]{:S(2)}) collective-permute-start(bf16[4,144,256]{2,1,0:T(8,128)(2,1)S(1)} %get-tuple-element.60), channel_id=1, source_target_pairs={{0,3},{1,2},{2,1},{3,0},{4,7},{5,6},{6,5},{7,4},{8,11},{9,10},{10,... | collective-permute-start | bytes 884744 | tf_op jit(solution)/shard_map/ppermute | solution.py:726
  55.5 9.9 %collective-permute-start.11 = (bf16[48,1152]{1,0:T(8,128)(2,1)S(1)}, bf16[48,1152]{1,0:T(8,128)(2,1)S(1)}, u32[]{:S(2)}, u32[]{:S(2)}) collective-permute-start(bf16[48,1152]{1,0:T(8,128)(2,1)S(1)} %get-tuple-element.79), channel_id=1, source_target_pairs={{0,4},{1,5},{2,6},{3,7},{4,0},{5,1},{6,2},{7,3},{8,12},{9,13},{10,... | collective-permute-start | bytes 331784 | tf_op jit(solution)/shard_map/ppermute | solution.py:726
  56.8 16.7 %collective-permute-start.14 = (bf16[48,1152]{1,0:T(8,128)(2,1)S(1)}, bf16[48,1152]{1,0:T(8,128)(2,1)S(1)}, u32[]{:S(2)}, u32[]{:S(2)}) collective-permute-start(bf16[48,1152]{1,0:T(8,128)(2,1)S(1)} %get-tuple-element.84), channel_id=1, source_target_pairs={{0,8},{1,9},{2,10},{3,11},{4,12},{5,13},{6,14},{7,15},{8,0},{9,1},... | collective-permute-start | bytes 331784 | tf_op jit(solution)/shard_map/ppermute | solution.py:726
  59.7 13.7 %collective-permute-start.15 = (bf16[48,1152]{1,0:T(8,128)(2,1)S(1)}, bf16[48,1152]{1,0:T(8,128)(2,1)S(1)}, u32[]{:S(2)}, u32[]{:S(2)}) collective-permute-start(bf16[48,1152]{1,0:T(8,128)(2,1)S(1)} %get-tuple-element.85), channel_id=1, source_target_pairs={{0,12},{1,13},{2,14},{3,15},{4,8},{5,9},{6,10},{7,11},{8,4},{9,5},... | collective-permute-start | bytes 331784 | tf_op jit(solution)/shard_map/ppermute | solution.py:726
  65.5 9.4 %collective-permute-start.12 = (bf16[2,48,512]{2,1,0:T(8,128)(2,1)S(1)}, bf16[2,48,512]{2,1,0:T(8,128)(2,1)S(1)}, u32[]{:S(2)}, u32[]{:S(2)}) collective-permute-start(bf16[2,48,512]{2,1,0:T(8,128)(2,1)S(1)} %get-tuple-element.80), channel_id=1, source_target_pairs={{0,2},{1,3},{2,0},{3,1},{4,6},{5,7},{6,4},{7,5},{8,10},{9,11},{10,... | collective-permute-start | bytes 294920 | tf_op jit(solution)/shard_map/ppermute | solution.py:726
  65.5 9.3 %collective-permute-start.13 = (bf16[2,48,512]{2,1,0:T(8,128)(2,1)S(1)}, bf16[2,48,512]{2,1,0:T(8,128)(2,1)S(1)}, u32[]{:S(2)}, u32[]{:S(2)}) collective-permute-start(bf16[2,48,512]{2,1,0:T(8,128)(2,1)S(1)} %get-tuple-element.81.refs_11_), channel_id=1, source_target_pairs={{0,3},{1,2},{2,1},{3,0},{4,7},{5,6},{6,5},{7,4},{8,11},{9,10},{10,... | collective-permute-start | bytes 294920 | tf_op jit(solution)/shard_map/ppermute | solution.py:726
  73.6 8.1 %collective-permute-start.16 = (bf16[2,48,512]{2,1,0:T(8,128)(2,1)S(1)}, bf16[2,48,512]{2,1,0:T(8,128)(2,1)S(1)}, u32[]{:S(2)}, u32[]{:S(2)}) collective-permute-start(bf16[2,48,512]{2,1,0:T(8,128)(2,1)S(1)} %get-tuple-element.88), channel_id=1, source_target_pairs={{0,2},{1,3},{2,0},{3,1},{4,6},{5,7},{6,4},{7,5},{8,10},{9,11},{10,... | collective-permute-start | bytes 294920 | tf_op jit(solution)/shard_map/ppermute | solution.py:726
  74.0 7.7 %collective-permute-start.17 = (bf16[2,48,512]{2,1,0:T(8,128)(2,1)S(1)}, bf16[2,48,512]{2,1,0:T(8,128)(2,1)S(1)}, u32[]{:S(2)}, u32[]{:S(2)}) collective-permute-start(bf16[2,48,512]{2,1,0:T(8,128)(2,1)S(1)} %get-tuple-element.89.refs_13_), channel_id=1, source_target_pairs={{0,3},{1,2},{2,1},{3,0},{4,7},{5,6},{6,5},{7,4},{8,11},{9,10},{10,... | collective-permute-start | bytes 294920 | tf_op jit(solution)/shard_map/ppermute | solution.py:726
  80.7 2.1 %copy-start.2 = (bf16[768,768]{1,0:T(8,128)(2,1)S(1)}, bf16[768,768]{1,0:T(8,128)(2,1)}, u32[]{:S(2)}) copy-start(bf16[768,768]{1,0:T(8,128)(2,1)} %refs_6_.1) | copy-start | bytes 3538948
  80.7 2.1 %collective-permute-start.18 = (bf16[4,48,512]{2,1,0:T(8,128)(2,1)S(1)}, bf16[4,48,512]{2,1,0:T(8,128)(2,1)S(1)}, u32[]{:S(2)}, u32[]{:S(2)}) collective-permute-start(bf16[4,48,512]{2,1,0:T(8,128)(2,1)S(1)} %get-tuple-element.98), channel_id=1, source_target_pairs={{0,1},{1,0},{2,3},{3,2},{4,5},{5,4},{6,7},{7,6},{8,9},{9,8},{10,11... | collective-permute-start | bytes 589832 | tf_op jit(solution)/shard_map/ppermute | solution.py:726

commit v12 on v11

--- a/solution.py
+++ b/solution.py
@@ -210,18 +210,22 @@
     blocks, held, packed = refs[:3], refs[3:6], refs[6:12]
     sems_in, sems_out = refs[12:]
     loads = [
-        pltpu.make_async_copy(hbm, block, sems_in.at[i])
+        [
+            pltpu.make_async_copy(hbm.at[rows], block.at[rows], sems_in.at[i, n])
+            for n, rows in enumerate((slice(0, HALF), slice(HALF, TOK)))
+        ]
         for i, (hbm, block) in enumerate(zip((k_hbm, v_hbm, q_hbm), blocks))
     ]
-    loads[0].start()
+    for pair in loads:
+        for load in pair:
+            load.start()
     picker = token_picker()
     stores = []
     heads = {(j, p): head_of(place, j, p) for j in range(GROUP) for p in range(HG)}
     classes = {at: class_of_slots(*offsets_of(place, head)) for at, head in heads.items()}
     for n, (load, block, scratch) in enumerate(zip(loads, blocks, held)):
-        load.wait()
-        for later in loads[1:] if n == 0 else ():
-            later.start()
+        for half in load:
+            half.wait()
         fill_class_major(block[...], picker, scratch)
         rows = slice(n * DH, (n + 1) * DH)
         for i, (j, first, count) in enumerate(
@@ -746,7 +750,7 @@
         [pltpu.VMEM((TOK, width), BF16)] * 3
         + [pltpu.VMEM((width, TOK), BF16)] * 3
         + [pltpu.VMEM(shape.shape, BF16) for shape in shapes]
-        + [pltpu.SemaphoreType.DMA((3,)), pltpu.SemaphoreType.DMA((6, 3))],
+        + [pltpu.SemaphoreType.DMA((3, 2)), pltpu.SemaphoreType.DMA((6, 3))],
         1 << 19, VMEM_MOST,
     )
     own1 = within(own1, 1)

time: 86 us -> 84.7 us (0.985)
  Pallas kernels: 61.2 us -> 59.9 us
    pallas_call x14, Pallas kernels: 61.2 us -> 59.9 us  [call(): pl.pallas_call(body if extra else kernel, grid_spec=pltpu.PrefetchScalarG...]
  transfers between devices with their start and end apart: 19 -> 19, of which waited for: 1 -> 1; matrix products, arithmetic and copies ran while one was open for 0% -> 0% of each run, Pallas kernels for 60% -> 61%
where the time goes in v12:
time: 84.7 us; the launch traced here: 84.5 us
  Pallas kernels  59.9 us (71%)
  starting transfers between devices  22.1 us (26%)
  waiting for transfers between devices  1.11 us (1%)
  local copies, waits for them, and re-layouts  1.09 us (1%)
    pallas_call x14, Pallas kernels, call(): pl.pallas_call(body if extra else kernel, grid_spec=pltpu.PrefetchScalarG...  59.9 us
    ppermute x19, starting transfers between devices, within(): return lax.ppermute(array, 'seq', [(i, i ^ apart) for i in range(count)])  22.1 us
  transfers between devices with their start and end apart: 19, of which 1 were waited for; matrix products, arithmetic and copies ran while one was open for 0% of the time, Pallas kernels for 61%

profile of v12, /device:TPU:0, one launch (start us, length us, event | category | flops | bytes accessed | tf_op | source)
XLA Modules:
  0.0 84.5 jit_solution(6406831010241683848)
XLA Ops:
  0.0 5.0 %shard_map.64 = (bf16[4,144,512]{2,1,0:T(8,128)(2,1)}, bf16[4,144,512]{2,1,0:T(8,128)(2,1)}, bf16[4,144,256]{2,1,0:T(8,128)(2,1)}, bf16[4,144,256]{2,1,0:T(8,128...) custom-call(s32[1]{0:T(128)} %bitcast.index.refs_0_, s32[16]{0:T(128)} %mid.9, s32[16]{0:T(128)} %top.9, ...), custom_call_target="tpu_custom_call" | custom-call | tf_op jit(solution)/shard_map/pallas_call | solution.py:707
  5.0 0.0 copy-start.5
  5.1 0.0 copy-start.6
  5.1 0.5 collective-permute-start
  5.6 2.6 %collective-permute-start.1 = (bf16[4,144,256]{2,1,0:T(8,128)(2,1)}, bf16[4,144,256]{2,1,0:T(8,128)(2,1)S(1)}, u32[]{:S(2)}, u32[]{:S(2)}) collective-permute-start(bf16[4,144,256]{2,1,0:T(8,128)(2,1)} %get-tuple-element.54), channel_id=1, source_target_pairs={{0,2},{1,3},{2,0},{3,1},{4,6},{5,7},{6,4},{7,5},{8,10},{9,11},{10,... | collective-permute-start | bytes 884744 | tf_op jit(solution)/shard_map/ppermute | solution.py:730
  8.2 0.1 collective-permute-start.2
  8.2 1.1 %copy-done = bf16[4,144,512]{2,1,0:T(8,128)(2,1)S(1)} copy-done((bf16[4,144,512]{2,1,0:T(8,128)(2,1)S(1)}, bf16[4,144,512]{2,1,0:T(8,128)(2,1)}, u32[]{:S(2)}) %copy-start) | copy-done | bytes 589848
  9.3 4.2 %collective-permute-start.5 = (bf16[2,144,256]{2,1,0:T(8,128)(2,1)S(1)}, bf16[2,144,256]{2,1,0:T(8,128)(2,1)S(1)}, u32[]{:S(2)}, u32[]{:S(2)}) collective-permute-start(bf16[2,144,256]{2,1,0:T(8,128)(2,1)S(1)} %get-tuple-element.62), channel_id=1, source_target_pairs={{0,12},{1,13},{2,14},{3,15},{4,8},{5,9},{6,10},{7,11},{8,4},{9,5},... | collective-permute-start | bytes 442376 | tf_op jit(solution)/shard_map/ppermute | solution.py:730
  13.6 0.6 collective-permute-start.7
  14.2 8.7 %shard_map.65 = (f32[4,4,64,256]{3,2,1,0:T(8,128)S(1)}, f32[4,4,8,256]{3,2,1,0:T(8,128)S(1)}) custom-call(s32[1]{0:T(128)} %bitcast.index.refs_0_, s32[16]{0:T(128)S(1)} %copy-done.5, s32[16]{0:T(128)S(1)} %copy-done.6, bf16[4,144,512]{2,1,0:T(8,128)(2,1)S(1)} %copy-done.1, bf16[4,144,512]{2,1,0:T(8,128)(2,1)S(1)} %collective-permute-done.refs_1_.b_ref.refs_7_.refs_4_.refs_6_), custom_call_target="tpu_custom_call" | custom-call | tf_op jit(solution)/shard_map/pallas_call | solution.py:707
  23.0 0.0 collective-permute-done.1.refs_0_.refs_2_.refs_5_
  23.1 3.8 %collective-permute-start.10 = (bf16[2,144,256]{2,1,0:T(8,128)(2,1)S(1)}, bf16[2,144,256]{2,1,0:T(8,128)(2,1)S(1)}, u32[]{:S(2)}, u32[]{:S(2)}) collective-permute-start(bf16[2,144,256]{2,1,0:T(8,128)(2,1)S(1)} %get-tuple-element.69), channel_id=1, source_target_pairs={{0,12},{1,13},{2,14},{3,15},{4,8},{5,9},{6,10},{7,11},{8,4},{9,5},... | collective-permute-start | bytes 442376 | tf_op jit(solution)/shard_map/ppermute | solution.py:730
  26.8 0.7 collective-permute-start.9
  27.5 0.6 collective-permute-start.3
  28.1 14.6 %shard_map.68 = (f32[4,4,64,256]{3,2,1,0:T(8,128)S(1)}, f32[4,4,8,256]{3,2,1,0:T(8,128)S(1)}, f32[4,2,64,256]{3,2,1,0:T(8,128)S(1)}, f32[4,2,8,256]{3,2,1,0:T(8,...) custom-call(s32[1]{0:T(128)} %bitcast.index.refs_0_, ...), custom_call_target="tpu_custom_call" | custom-call | tf_op jit(solution)/shard_map/pallas_call | solution.py:707
  42.8 11.4 %shard_map.69 = (bf16[48,1152]{1,0:T(8,128)(2,1)S(1)}, bf16[48,1152]{1,0:T(8,128)(2,1)S(1)}, bf16[48,1152]{1,0:T(8,128)(2,1)S(1)}, bf16[48,1152]{1,0:T(8,128)(2,1)S(1)}) custom-call(s32[1]{0:T(128)} %bitcast.index.refs_0_, s32[16]{0:T(128)S(1)} %copy-done.5, s32[16]{0:T(128)S(1)} %copy-done.6, ...), custom_call_target="tpu_custom_call" | custom-call | flops 8589934592 | tf_op jit(solution)/shard_map/pallas_call | solution.py:707
  54.2 1.3 %collective-permute-start.11 = (bf16[48,1152]{1,0:T(8,128)(2,1)S(1)}, bf16[48,1152]{1,0:T(8,128)(2,1)S(1)}, u32[]{:S(2)}, u32[]{:S(2)}) collective-permute-start(bf16[48,1152]{1,0:T(8,128)(2,1)S(1)} %get-tuple-element.79), channel_id=1, source_target_pairs={{0,4},{1,5},{2,6},{3,7},{4,0},{5,1},{6,2},{7,3},{8,12},{9,13},{10,... | collective-permute-start | bytes 331784 | tf_op jit(solution)/shard_map/ppermute | solution.py:730
  55.5 2.9 %collective-permute-start.14 = (bf16[48,1152]{1,0:T(8,128)(2,1)S(1)}, bf16[48,1152]{1,0:T(8,128)(2,1)S(1)}, u32[]{:S(2)}, u32[]{:S(2)}) collective-permute-start(bf16[48,1152]{1,0:T(8,128)(2,1)S(1)} %get-tuple-element.84), channel_id=1, source_target_pairs={{0,8},{1,9},{2,10},{3,11},{4,12},{5,13},{6,14},{7,15},{8,0},{9,1},... | collective-permute-start | bytes 331784 | tf_op jit(solution)/shard_map/ppermute | solution.py:730
  58.4 0.2 collective-permute-start.15
  58.7 5.4 %shard_map.70 = (f32[2,4,64,256]{3,2,1,0:T(8,128)S(1)}, f32[2,4,8,256]{3,2,1,0:T(8,128)S(1)}) custom-call(s32[1]{0:T(128)} %bitcast.index.refs_0_, s32[16]{0:T(128)S(1)} %copy-done.5, s32[16]{0:T(128)S(1)} %copy-done.6, bf16[4,144,512]{2,1,0:T(8,128)(2,1)S(1)} %copy-done.1, ...), custom_call_target="tpu_custom_call" | custom-call | tf_op jit(solution)/shard_map/pallas_call | solution.py:707
  64.1 0.1 shard_map.71
  64.2 0.1 collective-permute-start.12
  64.2 2.3 %collective-permute-start.13 = (bf16[2,48,512]{2,1,0:T(8,128)(2,1)S(1)}, bf16[2,48,512]{2,1,0:T(8,128)(2,1)S(1)}, u32[]{:S(2)}, u32[]{:S(2)}) collective-permute-start(bf16[2,48,512]{2,1,0:T(8,128)(2,1)S(1)} %get-tuple-element.81.refs_11_), channel_id=1, source_target_pairs={{0,3},{1,2},{2,1},{3,0},{4,7},{5,6},{6,5},{7,4},{8,11},{9,10},{10,... | collective-permute-start | bytes 294920 | tf_op jit(solution)/shard_map/ppermute | solution.py:730
  66.5 5.7 %shard_map.72 = (f32[2,4,64,256]{3,2,1,0:T(8,128)S(1)}, f32[2,4,8,256]{3,2,1,0:T(8,128)S(1)}) custom-call(s32[1]{0:T(128)} %bitcast.index.refs_0_, s32[16]{0:T(128)S(1)} %copy-done.5, s32[16]{0:T(128)S(1)} %copy-done.6, bf16[4,144,512]{2,1,0:T(8,128)(2,1)S(1)} %copy-done.1, ...), custom_call_target="tpu_custom_call" | custom-call | tf_op jit(solution)/shard_map/pallas_call | solution.py:707
  72.2 0.1 shard_map.74
  72.3 0.4 collective-permute-start.16
  72.7 0.9 %collective-permute-start.17 = (bf16[2,48,512]{2,1,0:T(8,128)(2,1)S(1)}, bf16[2,48,512]{2,1,0:T(8,128)(2,1)S(1)}, u32[]{:S(2)}, u32[]{:S(2)}) collective-permute-start(bf16[2,48,512]{2,1,0:T(8,128)(2,1)S(1)} %get-tuple-element.89.refs_13_), channel_id=1, source_target_pairs={{0,3},{1,2},{2,1},{3,0},{4,7},{5,6},{6,5},{7,4},{8,11},{9,10},{10,... | collective-permute-start | bytes 294920 | tf_op jit(solution)/shard_map/ppermute | solution.py:730
  73.6 5.8 %shard_map.76 = (bf16[4,48,512]{2,1,0:T(8,128)(2,1)S(1)}, bf16[4,48,512]{2,1,0:T(8,128)(2,1)S(1)}) custom-call(s32[1]{0:T(128)} %bitcast.index.refs_0_, s32[16]{0:T(128)S(1)} %copy-done.5, s32[16]{0:T(128)S(1)} %copy-done.6, bf16[4,144,256]{2,1,0:T(8,128)(2,1)S(1)} %collective-permute-done.3.refs_7_.refs_3_, ...), custom_call_target="tpu_custom_call" | custom-call | tf_op jit(solution)/shard_map/pallas_call | solution.py:707
  79.4 0.0 copy-start.2
  79.4 1.0 %collective-permute-start.18 = (bf16[4,48,512]{2,1,0:T(8,128)(2,1)S(1)}, bf16[4,48,512]{2,1,0:T(8,128)(2,1)S(1)}, u32[]{:S(2)}, u32[]{:S(2)}) collective-permute-start(bf16[4,48,512]{2,1,0:T(8,128)(2,1)S(1)} %get-tuple-element.98), channel_id=1, source_target_pairs={{0,1},{1,0},{2,3},{3,2},{4,5},{5,4},{6,7},{7,6},{8,9},{9,8},{10,11... | collective-permute-start | bytes 589832 | tf_op jit(solution)/shard_map/ppermute | solution.py:730
  80.4 1.1 %collective-permute-done.18.refs_5_ = bf16[4,48,512]{2,1,0:T(8,128)(2,1)S(1)} collective-permute-done((bf16[4,48,512]{2,1,0:T(8,128)(2,1)S(1)}, bf16[4,48,512]{2,1,0:T(8,128)(2,1)S(1)}, u32[]{:S(2)}, u32[]{:S(2)}) %collective-permute-start.18) | collective-permute-done | bytes 196640 | tf_op jit(solution)/shard_map/ppermute | solution.py:730
  81.5 3.0 %shard_map.77 = bf16[512,768]{1,0:T(8,128)(2,1)} custom-call(s32[1]{0:T(128)} %bitcast.index.refs_0_, s32[16]{0:T(128)S(1)} %copy-done.5, s32[16]{0:T(128)S(1)} %copy-done.6, bf16[2,48,512]{2,1,0:T(8,128)(2,1)S(1)} %get-tuple-element.90.refs_0_, bf16[2,48,512]{2,1,0:T(8,128)(2,1)S(1)} %get-tuple-element.91.refs_1_, ...), custom_call_target="tpu_custom_call" | custom-call | tf_op jit(solution)/shard_map/pallas_call | solution.py:707
  (34 shorter events, 0.1 us)
Async XLA Ops:
  5.0 9.2 %copy-start.5 = (s32[16]{0:T(128)S(1)}, s32[16]{0:T(128)}, u32[]{:S(2)}) copy-start(s32[16]{0:T(128)} %mid.9) | copy-start | bytes 196
  5.1 9.2 %copy-start.6 = (s32[16]{0:T(128)S(1)}, s32[16]{0:T(128)}, u32[]{:S(2)}) copy-start(s32[16]{0:T(128)} %top.9) | copy-start | bytes 196
  5.1 3.2 %collective-permute-start = (bf16[4,144,512]{2,1,0:T(8,128)(2,1)}, bf16[4,144,512]{2,1,0:T(8,128)(2,1)S(1)}, u32[]{:S(2)}, u32[]{:S(2)}) collective-permute-start(bf16[4,144,512]{2,1,0:T(8,128)(2,1)} %get-tuple-element.53), channel_id=1, source_target_pairs={{0,1},{1,0},{2,3},{3,2},{4,5},{5,4},{6,7},{7,6},{8,9},{9,8},{10,11... | collective-permute-start | bytes 1769480 | tf_op jit(solution)/shard_map/ppermute | solution.py:730
  5.6 17.4 %collective-permute-start.1 = (bf16[4,144,256]{2,1,0:T(8,128)(2,1)}, bf16[4,144,256]{2,1,0:T(8,128)(2,1)S(1)}, u32[]{:S(2)}, u32[]{:S(2)}) collective-permute-start(bf16[4,144,256]{2,1,0:T(8,128)(2,1)} %get-tuple-element.54), channel_id=1, source_target_pairs={{0,2},{1,3},{2,0},{3,1},{4,6},{5,7},{6,4},{7,5},{8,10},{9,11},{10,... | collective-permute-start | bytes 884744 | tf_op jit(solution)/shard_map/ppermute | solution.py:730
  8.2 14.8 %collective-permute-start.2 = (bf16[4,144,256]{2,1,0:T(8,128)(2,1)}, bf16[4,144,256]{2,1,0:T(8,128)(2,1)S(1)}, u32[]{:S(2)}, u32[]{:S(2)}) collective-permute-start(bf16[4,144,256]{2,1,0:T(8,128)(2,1)} %get-tuple-element.55), channel_id=1, source_target_pairs={{0,3},{1,2},{2,1},{3,0},{4,7},{5,6},{6,5},{7,4},{8,11},{9,10},{10,... | collective-permute-start | bytes 884744 | tf_op jit(solution)/shard_map/ppermute | solution.py:730
  8.2 1.1 %copy-start = (bf16[4,144,512]{2,1,0:T(8,128)(2,1)S(1)}, bf16[4,144,512]{2,1,0:T(8,128)(2,1)}, u32[]{:S(2)}) copy-start(bf16[4,144,512]{2,1,0:T(8,128)(2,1)} %get-tuple-element.52.refs_0_.a_ref.refs_6_.refs_3_.refs_5_) | copy-start | bytes 1769476
  9.3 4.9 %copy-start.1 = (bf16[4,144,512]{2,1,0:T(8,128)(2,1)S(1)}, bf16[4,144,512]{2,1,0:T(8,128)(2,1)}, u32[]{:S(2)}) copy-start(bf16[4,144,512]{2,1,0:T(8,128)(2,1)} %get-tuple-element.52.refs_0_.a_ref.refs_6_.refs_3_.refs_5_) | copy-start | bytes 1769476
  9.3 13.7 %copy-start.3 = (bf16[4,144,256]{2,1,0:T(8,128)(2,1)S(1)}, bf16[4,144,256]{2,1,0:T(8,128)(2,1)}, u32[]{:S(2)}) copy-start(bf16[4,144,256]{2,1,0:T(8,128)(2,1)} %get-tuple-element.57.refs_3_) | copy-start | bytes 884740
  9.3 13.7 %copy-start.4 = (bf16[4,144,256]{2,1,0:T(8,128)(2,1)S(1)}, bf16[4,144,256]{2,1,0:T(8,128)(2,1)}, u32[]{:S(2)}) copy-start(bf16[4,144,256]{2,1,0:T(8,128)(2,1)} %get-tuple-element.58.refs_4_) | copy-start | bytes 884740
  9.3 17.5 %collective-permute-start.5 = (bf16[2,144,256]{2,1,0:T(8,128)(2,1)S(1)}, bf16[2,144,256]{2,1,0:T(8,128)(2,1)S(1)}, u32[]{:S(2)}, u32[]{:S(2)}) collective-permute-start(bf16[2,144,256]{2,1,0:T(8,128)(2,1)S(1)} %get-tuple-element.62), channel_id=1, source_target_pairs={{0,12},{1,13},{2,14},{3,15},{4,8},{5,9},{6,10},{7,11},{8,4},{9,5},... | collective-permute-start | bytes 442376 | tf_op jit(solution)/shard_map/ppermute | solution.py:730
  13.6 13.9 %collective-permute-start.6 = (bf16[2,144,256]{2,1,0:T(8,128)(2,1)S(1)}, bf16[2,144,256]{2,1,0:T(8,128)(2,1)S(1)}, u32[]{:S(2)}, u32[]{:S(2)}) collective-permute-start(bf16[2,144,256]{2,1,0:T(8,128)(2,1)S(1)} %get-tuple-element.63), channel_id=1, source_target_pairs={{0,8},{1,9},{2,10},{3,11},{4,12},{5,13},{6,14},{7,15},{8,0},{9,1},... | collective-permute-start | bytes 442376 | tf_op jit(solution)/shard_map/ppermute | solution.py:730
  13.6 14.5 %collective-permute-start.7 = (bf16[2,144,256]{2,1,0:T(8,128)(2,1)S(1)}, bf16[2,144,256]{2,1,0:T(8,128)(2,1)S(1)}, u32[]{:S(2)}, u32[]{:S(2)}) collective-permute-start(bf16[2,144,256]{2,1,0:T(8,128)(2,1)S(1)} %get-tuple-element.64), channel_id=1, source_target_pairs={{0,4},{1,5},{2,6},{3,7},{4,0},{5,1},{6,2},{7,3},{8,12},{9,13},{10,... | collective-permute-start | bytes 442376 | tf_op jit(solution)/shard_map/ppermute | solution.py:730
  23.1 19.7 %collective-permute-start.10 = (bf16[2,144,256]{2,1,0:T(8,128)(2,1)S(1)}, bf16[2,144,256]{2,1,0:T(8,128)(2,1)S(1)}, u32[]{:S(2)}, u32[]{:S(2)}) collective-permute-start(bf16[2,144,256]{2,1,0:T(8,128)(2,1)S(1)} %get-tuple-element.69), channel_id=1, source_target_pairs={{0,12},{1,13},{2,14},{3,15},{4,8},{5,9},{6,10},{7,11},{8,4},{9,5},... | collective-permute-start | bytes 442376 | tf_op jit(solution)/shard_map/ppermute | solution.py:730
  26.8 15.9 %collective-permute-start.8 = (bf16[2,144,256]{2,1,0:T(8,128)(2,1)S(1)}, bf16[2,144,256]{2,1,0:T(8,128)(2,1)S(1)}, u32[]{:S(2)}, u32[]{:S(2)}) collective-permute-start(bf16[2,144,256]{2,1,0:T(8,128)(2,1)S(1)} %get-tuple-element.67), channel_id=1, source_target_pairs={{0,8},{1,9},{2,10},{3,11},{4,12},{5,13},{6,14},{7,15},{8,0},{9,1},... | collective-permute-start | bytes 442376 | tf_op jit(solution)/shard_map/ppermute | solution.py:730
  26.8 15.9 %collective-permute-start.9 = (bf16[2,144,256]{2,1,0:T(8,128)(2,1)S(1)}, bf16[2,144,256]{2,1,0:T(8,128)(2,1)S(1)}, u32[]{:S(2)}, u32[]{:S(2)}) collective-permute-start(bf16[2,144,256]{2,1,0:T(8,128)(2,1)S(1)} %get-tuple-element.68), channel_id=1, source_target_pairs={{0,4},{1,5},{2,6},{3,7},{4,0},{5,1},{6,2},{7,3},{8,12},{9,13},{10,... | collective-permute-start | bytes 442376 | tf_op jit(solution)/shard_map/ppermute | solution.py:730
  27.5 31.2 %collective-permute-start.3 = (bf16[4,144,256]{2,1,0:T(8,128)(2,1)S(1)}, bf16[4,144,256]{2,1,0:T(8,128)(2,1)S(1)}, u32[]{:S(2)}, u32[]{:S(2)}) collective-permute-start(bf16[4,144,256]{2,1,0:T(8,128)(2,1)S(1)} %get-tuple-element.59), channel_id=1, source_target_pairs={{0,2},{1,3},{2,0},{3,1},{4,6},{5,7},{6,4},{7,5},{8,10},{9,11},{10,... | collective-permute-start | bytes 884744 | tf_op jit(solution)/shard_map/ppermute | solution.py:730
  28.1 30.6 %collective-permute-start.4 = (bf16[4,144,256]{2,1,0:T(8,128)(2,1)S(1)}, bf16[4,144,256]{2,1,0:T(8,128)(2,1)S(1)}, u32[]{:S(2)}, u32[]{:S(2)}) collective-permute-start(bf16[4,144,256]{2,1,0:T(8,128)(2,1)S(1)} %get-tuple-element.60), channel_id=1, source_target_pairs={{0,3},{1,2},{2,1},{3,0},{4,7},{5,6},{6,5},{7,4},{8,11},{9,10},{10,... | collective-permute-start | bytes 884744 | tf_op jit(solution)/shard_map/ppermute | solution.py:730
  54.2 9.9 %collective-permute-start.11 = (bf16[48,1152]{1,0:T(8,128)(2,1)S(1)}, bf16[48,1152]{1,0:T(8,128)(2,1)S(1)}, u32[]{:S(2)}, u32[]{:S(2)}) collective-permute-start(bf16[48,1152]{1,0:T(8,128)(2,1)S(1)} %get-tuple-element.79), channel_id=1, source_target_pairs={{0,4},{1,5},{2,6},{3,7},{4,0},{5,1},{6,2},{7,3},{8,12},{9,13},{10,... | collective-permute-start | bytes 331784 | tf_op jit(solution)/shard_map/ppermute | solution.py:730
  55.5 16.6 %collective-permute-start.14 = (bf16[48,1152]{1,0:T(8,128)(2,1)S(1)}, bf16[48,1152]{1,0:T(8,128)(2,1)S(1)}, u32[]{:S(2)}, u32[]{:S(2)}) collective-permute-start(bf16[48,1152]{1,0:T(8,128)(2,1)S(1)} %get-tuple-element.84), channel_id=1, source_target_pairs={{0,8},{1,9},{2,10},{3,11},{4,12},{5,13},{6,14},{7,15},{8,0},{9,1},... | collective-permute-start | bytes 331784 | tf_op jit(solution)/shard_map/ppermute | solution.py:730
  58.4 13.7 %collective-permute-start.15 = (bf16[48,1152]{1,0:T(8,128)(2,1)S(1)}, bf16[48,1152]{1,0:T(8,128)(2,1)S(1)}, u32[]{:S(2)}, u32[]{:S(2)}) collective-permute-start(bf16[48,1152]{1,0:T(8,128)(2,1)S(1)} %get-tuple-element.85), channel_id=1, source_target_pairs={{0,12},{1,13},{2,14},{3,15},{4,8},{5,9},{6,10},{7,11},{8,4},{9,5},... | collective-permute-start | bytes 331784 | tf_op jit(solution)/shard_map/ppermute | solution.py:730
  64.2 9.4 %collective-permute-start.12 = (bf16[2,48,512]{2,1,0:T(8,128)(2,1)S(1)}, bf16[2,48,512]{2,1,0:T(8,128)(2,1)S(1)}, u32[]{:S(2)}, u32[]{:S(2)}) collective-permute-start(bf16[2,48,512]{2,1,0:T(8,128)(2,1)S(1)} %get-tuple-element.80), channel_id=1, source_target_pairs={{0,2},{1,3},{2,0},{3,1},{4,6},{5,7},{6,4},{7,5},{8,10},{9,11},{10,... | collective-permute-start | bytes 294920 | tf_op jit(solution)/shard_map/ppermute | solution.py:730
  64.2 9.3 %collective-permute-start.13 = (bf16[2,48,512]{2,1,0:T(8,128)(2,1)S(1)}, bf16[2,48,512]{2,1,0:T(8,128)(2,1)S(1)}, u32[]{:S(2)}, u32[]{:S(2)}) collective-permute-start(bf16[2,48,512]{2,1,0:T(8,128)(2,1)S(1)} %get-tuple-element.81.refs_11_), channel_id=1, source_target_pairs={{0,3},{1,2},{2,1},{3,0},{4,7},{5,6},{6,5},{7,4},{8,11},{9,10},{10,... | collective-permute-start | bytes 294920 | tf_op jit(solution)/shard_map/ppermute | solution.py:730
  72.3 8.1 %collective-permute-start.16 = (bf16[2,48,512]{2,1,0:T(8,128)(2,1)S(1)}, bf16[2,48,512]{2,1,0:T(8,128)(2,1)S(1)}, u32[]{:S(2)}, u32[]{:S(2)}) collective-permute-start(bf16[2,48,512]{2,1,0:T(8,128)(2,1)S(1)} %get-tuple-element.88), channel_id=1, source_target_pairs={{0,2},{1,3},{2,0},{3,1},{4,6},{5,7},{6,4},{7,5},{8,10},{9,11},{10,... | collective-permute-start | bytes 294920 | tf_op jit(solution)/shard_map/ppermute | solution.py:730
  72.7 7.7 %collective-permute-start.17 = (bf16[2,48,512]{2,1,0:T(8,128)(2,1)S(1)}, bf16[2,48,512]{2,1,0:T(8,128)(2,1)S(1)}, u32[]{:S(2)}, u32[]{:S(2)}) collective-permute-start(bf16[2,48,512]{2,1,0:T(8,128)(2,1)S(1)} %get-tuple-element.89.refs_13_), channel_id=1, source_target_pairs={{0,3},{1,2},{2,1},{3,0},{4,7},{5,6},{6,5},{7,4},{8,11},{9,10},{10,... | collective-permute-start | bytes 294920 | tf_op jit(solution)/shard_map/ppermute | solution.py:730
  79.4 2.1 %copy-start.2 = (bf16[768,768]{1,0:T(8,128)(2,1)S(1)}, bf16[768,768]{1,0:T(8,128)(2,1)}, u32[]{:S(2)}) copy-start(bf16[768,768]{1,0:T(8,128)(2,1)} %refs_6_.1) | copy-start | bytes 3538948
  79.4 2.0 %collective-permute-start.18 = (bf16[4,48,512]{2,1,0:T(8,128)(2,1)S(1)}, bf16[4,48,512]{2,1,0:T(8,128)(2,1)S(1)}, u32[]{:S(2)}, u32[]{:S(2)}) collective-permute-start(bf16[4,48,512]{2,1,0:T(8,128)(2,1)S(1)} %get-tuple-element.98), channel_id=1, source_target_pairs={{0,1},{1,0},{2,3},{3,2},{4,5},{5,4},{6,7},{7,6},{8,9},{9,8},{10,11... | collective-permute-start | bytes 589832 | tf_op jit(solution)/shard_map/ppermute | solution.py:730

commit v13 on v12

--- a/solution.py
+++ b/solution.py
@@ -152,7 +152,7 @@
 TOK = 512
 SCALE = DH**-0.5 * LOG2E
 BUSY = 1 << 33
-AHEAD = 4
+AHEAD = 6
 SAFE = 96.0
 CHUNKS = ((0, 2), (2, 2))
 DX = 64
@@ -479,7 +479,7 @@
             in_stages(steps, score, weigh, gather)
             return carry
 
-        lax.fori_loop(0, RATE, segment, 0, unroll=2)
+        lax.fori_loop(0, RATE, segment, 0, unroll=RATE)
 
     def run():
         def segment(s, carry):
@@ -592,7 +592,7 @@
             in_stages(steps, score, weigh, gather)
             return carry
 
-        lax.fori_loop(0, RATE, segment, 0, unroll=2)
+        lax.fori_loop(0, RATE, segment, 0, unroll=RATE)
 
     def run():
         def segment(s, carry):

time: 84.7 us -> 84.7 us (level)
  no operation moved by 1% of the time
where the time goes in v13:
time: 84.7 us; the launch traced here: 84.5 us
  Pallas kernels  60 us (71%)
  starting transfers between devices  22.1 us (26%)
  waiting for transfers between devices  1.11 us (1%)
  local copies, waits for them, and re-layouts  1.09 us (1%)
    pallas_call x14, Pallas kernels, call(): pl.pallas_call(body if extra else kernel, grid_spec=pltpu.PrefetchScalarG...  60 us
    ppermute x19, starting transfers between devices, within(): return lax.ppermute(array, 'seq', [(i, i ^ apart) for i in range(count)])  22.1 us
  transfers between devices with their start and end apart: 19, of which 1 were waited for; matrix products, arithmetic and copies ran while one was open for 0% of the time, Pallas kernels for 61%

profile of v13, /device:TPU:0, one launch (start us, length us, event | category | flops | bytes accessed | tf_op | source)
XLA Modules:
  0.0 84.5 jit_solution(12002485265609605076)
XLA Ops:
  0.0 5.0 %shard_map.64 = (bf16[4,144,512]{2,1,0:T(8,128)(2,1)}, bf16[4,144,512]{2,1,0:T(8,128)(2,1)}, bf16[4,144,256]{2,1,0:T(8,128)(2,1)}, bf16[4,144,256]{2,1,0:T(8,128...) custom-call(s32[1]{0:T(128)} %bitcast.index.refs_0_, s32[16]{0:T(128)} %mid.9, s32[16]{0:T(128)} %top.9, ...), custom_call_target="tpu_custom_call" | custom-call | tf_op jit(solution)/shard_map/pallas_call | solution.py:707
  5.0 0.0 copy-start.5
  5.1 0.0 copy-start.6
  5.1 0.5 collective-permute-start
  5.6 2.6 %collective-permute-start.1 = (bf16[4,144,256]{2,1,0:T(8,128)(2,1)}, bf16[4,144,256]{2,1,0:T(8,128)(2,1)S(1)}, u32[]{:S(2)}, u32[]{:S(2)}) collective-permute-start(bf16[4,144,256]{2,1,0:T(8,128)(2,1)} %get-tuple-element.54), channel_id=1, source_target_pairs={{0,2},{1,3},{2,0},{3,1},{4,6},{5,7},{6,4},{7,5},{8,10},{9,11},{10,... | collective-permute-start | bytes 884744 | tf_op jit(solution)/shard_map/ppermute | solution.py:730
  8.2 0.1 collective-permute-start.2
  8.2 1.1 %copy-done = bf16[4,144,512]{2,1,0:T(8,128)(2,1)S(1)} copy-done((bf16[4,144,512]{2,1,0:T(8,128)(2,1)S(1)}, bf16[4,144,512]{2,1,0:T(8,128)(2,1)}, u32[]{:S(2)}) %copy-start) | copy-done | bytes 589848
  9.3 4.2 %collective-permute-start.5 = (bf16[2,144,256]{2,1,0:T(8,128)(2,1)S(1)}, bf16[2,144,256]{2,1,0:T(8,128)(2,1)S(1)}, u32[]{:S(2)}, u32[]{:S(2)}) collective-permute-start(bf16[2,144,256]{2,1,0:T(8,128)(2,1)S(1)} %get-tuple-element.62), channel_id=1, source_target_pairs={{0,12},{1,13},{2,14},{3,15},{4,8},{5,9},{6,10},{7,11},{8,4},{9,5},... | collective-permute-start | bytes 442376 | tf_op jit(solution)/shard_map/ppermute | solution.py:730
  13.6 0.6 collective-permute-start.7
  14.2 8.7 %shard_map.65 = (f32[4,4,64,256]{3,2,1,0:T(8,128)S(1)}, f32[4,4,8,256]{3,2,1,0:T(8,128)S(1)}) custom-call(s32[1]{0:T(128)} %bitcast.index.refs_0_, s32[16]{0:T(128)S(1)} %copy-done.5, s32[16]{0:T(128)S(1)} %copy-done.6, bf16[4,144,512]{2,1,0:T(8,128)(2,1)S(1)} %copy-done.1, bf16[4,144,512]{2,1,0:T(8,128)(2,1)S(1)} %collective-permute-done.refs_1_.b_ref.refs_7_.refs_4_.refs_6_), custom_call_target="tpu_custom_call" | custom-call | tf_op jit(solution)/shard_map/pallas_call | solution.py:707
  23.0 0.0 collective-permute-done.2.refs_1_.refs_3_.refs_6_
  23.1 3.8 %collective-permute-start.10 = (bf16[2,144,256]{2,1,0:T(8,128)(2,1)S(1)}, bf16[2,144,256]{2,1,0:T(8,128)(2,1)S(1)}, u32[]{:S(2)}, u32[]{:S(2)}) collective-permute-start(bf16[2,144,256]{2,1,0:T(8,128)(2,1)S(1)} %get-tuple-element.69), channel_id=1, source_target_pairs={{0,12},{1,13},{2,14},{3,15},{4,8},{5,9},{6,10},{7,11},{8,4},{9,5},... | collective-permute-start | bytes 442376 | tf_op jit(solution)/shard_map/ppermute | solution.py:730
  26.8 0.7 collective-permute-start.9
  27.5 0.6 collective-permute-start.3
  28.1 14.7 %shard_map.68 = (f32[4,4,64,256]{3,2,1,0:T(8,128)S(1)}, f32[4,4,8,256]{3,2,1,0:T(8,128)S(1)}, f32[4,2,64,256]{3,2,1,0:T(8,128)S(1)}, f32[4,2,8,256]{3,2,1,0:T(8,...) custom-call(s32[1]{0:T(128)} %bitcast.index.refs_0_, ...), custom_call_target="tpu_custom_call" | custom-call | tf_op jit(solution)/shard_map/pallas_call | solution.py:707
  42.8 11.4 %shard_map.69 = (bf16[48,1152]{1,0:T(8,128)(2,1)S(1)}, bf16[48,1152]{1,0:T(8,128)(2,1)S(1)}, bf16[48,1152]{1,0:T(8,128)(2,1)S(1)}, bf16[48,1152]{1,0:T(8,128)(2,1)S(1)}) custom-call(s32[1]{0:T(128)} %bitcast.index.refs_0_, s32[16]{0:T(128)S(1)} %copy-done.5, s32[16]{0:T(128)S(1)} %copy-done.6, ...), custom_call_target="tpu_custom_call" | custom-call | flops 8589934592 | tf_op jit(solution)/shard_map/pallas_call | solution.py:707
  54.2 1.3 %collective-permute-start.11 = (bf16[48,1152]{1,0:T(8,128)(2,1)S(1)}, bf16[48,1152]{1,0:T(8,128)(2,1)S(1)}, u32[]{:S(2)}, u32[]{:S(2)}) collective-permute-start(bf16[48,1152]{1,0:T(8,128)(2,1)S(1)} %get-tuple-element.79), channel_id=1, source_target_pairs={{0,4},{1,5},{2,6},{3,7},{4,0},{5,1},{6,2},{7,3},{8,12},{9,13},{10,... | collective-permute-start | bytes 331784 | tf_op jit(solution)/shard_map/ppermute | solution.py:730
  55.5 3.0 %collective-permute-start.14 = (bf16[48,1152]{1,0:T(8,128)(2,1)S(1)}, bf16[48,1152]{1,0:T(8,128)(2,1)S(1)}, u32[]{:S(2)}, u32[]{:S(2)}) collective-permute-start(bf16[48,1152]{1,0:T(8,128)(2,1)S(1)} %get-tuple-element.84), channel_id=1, source_target_pairs={{0,8},{1,9},{2,10},{3,11},{4,12},{5,13},{6,14},{7,15},{8,0},{9,1},... | collective-permute-start | bytes 331784 | tf_op jit(solution)/shard_map/ppermute | solution.py:730
  58.5 0.2 collective-permute-start.15
  58.7 5.4 %shard_map.70 = (f32[2,4,64,256]{3,2,1,0:T(8,128)S(1)}, f32[2,4,8,256]{3,2,1,0:T(8,128)S(1)}) custom-call(s32[1]{0:T(128)} %bitcast.index.refs_0_, s32[16]{0:T(128)S(1)} %copy-done.5, s32[16]{0:T(128)S(1)} %copy-done.6, bf16[4,144,512]{2,1,0:T(8,128)(2,1)S(1)} %copy-done.1, ...), custom_call_target="tpu_custom_call" | custom-call | tf_op jit(solution)/shard_map/pallas_call | solution.py:707
  64.1 0.1 shard_map.71
  64.2 0.1 collective-permute-start.12
  64.3 2.2 %collective-permute-start.13 = (bf16[2,48,512]{2,1,0:T(8,128)(2,1)S(1)}, bf16[2,48,512]{2,1,0:T(8,128)(2,1)S(1)}, u32[]{:S(2)}, u32[]{:S(2)}) collective-permute-start(bf16[2,48,512]{2,1,0:T(8,128)(2,1)S(1)} %get-tuple-element.81.refs_11_), channel_id=1, source_target_pairs={{0,3},{1,2},{2,1},{3,0},{4,7},{5,6},{6,5},{7,4},{8,11},{9,10},{10,... | collective-permute-start | bytes 294920 | tf_op jit(solution)/shard_map/ppermute | solution.py:730
  66.5 5.4 %shard_map.72 = (f32[2,4,64,256]{3,2,1,0:T(8,128)S(1)}, f32[2,4,8,256]{3,2,1,0:T(8,128)S(1)}) custom-call(s32[1]{0:T(128)} %bitcast.index.refs_0_, s32[16]{0:T(128)S(1)} %copy-done.5, s32[16]{0:T(128)S(1)} %copy-done.6, bf16[4,144,512]{2,1,0:T(8,128)(2,1)S(1)} %copy-done.1, ...), custom_call_target="tpu_custom_call" | custom-call | tf_op jit(solution)/shard_map/pallas_call | solution.py:707
  71.9 0.1 shard_map.74
  72.0 0.4 collective-permute-start.16
  72.4 0.9 %collective-permute-start.17 = (bf16[2,48,512]{2,1,0:T(8,128)(2,1)S(1)}, bf16[2,48,512]{2,1,0:T(8,128)(2,1)S(1)}, u32[]{:S(2)}, u32[]{:S(2)}) collective-permute-start(bf16[2,48,512]{2,1,0:T(8,128)(2,1)S(1)} %get-tuple-element.89.refs_13_), channel_id=1, source_target_pairs={{0,3},{1,2},{2,1},{3,0},{4,7},{5,6},{6,5},{7,4},{8,11},{9,10},{10,... | collective-permute-start | bytes 294920 | tf_op jit(solution)/shard_map/ppermute | solution.py:730
  73.4 6.1 %shard_map.76 = (bf16[4,48,512]{2,1,0:T(8,128)(2,1)S(1)}, bf16[4,48,512]{2,1,0:T(8,128)(2,1)S(1)}) custom-call(s32[1]{0:T(128)} %bitcast.index.refs_0_, s32[16]{0:T(128)S(1)} %copy-done.5, s32[16]{0:T(128)S(1)} %copy-done.6, bf16[4,144,256]{2,1,0:T(8,128)(2,1)S(1)} %collective-permute-done.3.refs_7_.refs_3_, ...), custom_call_target="tpu_custom_call" | custom-call | tf_op jit(solution)/shard_map/pallas_call | solution.py:707
  79.5 0.0 copy-start.2
  79.5 0.9 %collective-permute-start.18 = (bf16[4,48,512]{2,1,0:T(8,128)(2,1)S(1)}, bf16[4,48,512]{2,1,0:T(8,128)(2,1)S(1)}, u32[]{:S(2)}, u32[]{:S(2)}) collective-permute-start(bf16[4,48,512]{2,1,0:T(8,128)(2,1)S(1)} %get-tuple-element.98), channel_id=1, source_target_pairs={{0,1},{1,0},{2,3},{3,2},{4,5},{5,4},{6,7},{7,6},{8,9},{9,8},{10,11... | collective-permute-start | bytes 589832 | tf_op jit(solution)/shard_map/ppermute | solution.py:730
  80.4 1.1 %collective-permute-done.18.refs_5_ = bf16[4,48,512]{2,1,0:T(8,128)(2,1)S(1)} collective-permute-done((bf16[4,48,512]{2,1,0:T(8,128)(2,1)S(1)}, bf16[4,48,512]{2,1,0:T(8,128)(2,1)S(1)}, u32[]{:S(2)}, u32[]{:S(2)}) %collective-permute-start.18) | collective-permute-done | bytes 196640 | tf_op jit(solution)/shard_map/ppermute | solution.py:730
  81.5 3.0 %shard_map.77 = bf16[512,768]{1,0:T(8,128)(2,1)} custom-call(s32[1]{0:T(128)} %bitcast.index.refs_0_, s32[16]{0:T(128)S(1)} %copy-done.5, s32[16]{0:T(128)S(1)} %copy-done.6, bf16[2,48,512]{2,1,0:T(8,128)(2,1)S(1)} %get-tuple-element.90.refs_0_, bf16[2,48,512]{2,1,0:T(8,128)(2,1)S(1)} %get-tuple-element.91.refs_1_, ...), custom_call_target="tpu_custom_call" | custom-call | tf_op jit(solution)/shard_map/pallas_call | solution.py:707
  (34 shorter events, 0.1 us)
Async XLA Ops:
  5.0 9.2 %copy-start.5 = (s32[16]{0:T(128)S(1)}, s32[16]{0:T(128)}, u32[]{:S(2)}) copy-start(s32[16]{0:T(128)} %mid.9) | copy-start | bytes 196
  5.1 9.2 %copy-start.6 = (s32[16]{0:T(128)S(1)}, s32[16]{0:T(128)}, u32[]{:S(2)}) copy-start(s32[16]{0:T(128)} %top.9) | copy-start | bytes 196
  5.1 3.2 %collective-permute-start = (bf16[4,144,512]{2,1,0:T(8,128)(2,1)}, bf16[4,144,512]{2,1,0:T(8,128)(2,1)S(1)}, u32[]{:S(2)}, u32[]{:S(2)}) collective-permute-start(bf16[4,144,512]{2,1,0:T(8,128)(2,1)} %get-tuple-element.53), channel_id=1, source_target_pairs={{0,1},{1,0},{2,3},{3,2},{4,5},{5,4},{6,7},{7,6},{8,9},{9,8},{10,11... | collective-permute-start | bytes 1769480 | tf_op jit(solution)/shard_map/ppermute | solution.py:730
  5.6 17.4 %collective-permute-start.1 = (bf16[4,144,256]{2,1,0:T(8,128)(2,1)}, bf16[4,144,256]{2,1,0:T(8,128)(2,1)S(1)}, u32[]{:S(2)}, u32[]{:S(2)}) collective-permute-start(bf16[4,144,256]{2,1,0:T(8,128)(2,1)} %get-tuple-element.54), channel_id=1, source_target_pairs={{0,2},{1,3},{2,0},{3,1},{4,6},{5,7},{6,4},{7,5},{8,10},{9,11},{10,... | collective-permute-start | bytes 884744 | tf_op jit(solution)/shard_map/ppermute | solution.py:730
  8.2 14.8 %collective-permute-start.2 = (bf16[4,144,256]{2,1,0:T(8,128)(2,1)}, bf16[4,144,256]{2,1,0:T(8,128)(2,1)S(1)}, u32[]{:S(2)}, u32[]{:S(2)}) collective-permute-start(bf16[4,144,256]{2,1,0:T(8,128)(2,1)} %get-tuple-element.55), channel_id=1, source_target_pairs={{0,3},{1,2},{2,1},{3,0},{4,7},{5,6},{6,5},{7,4},{8,11},{9,10},{10,... | collective-permute-start | bytes 884744 | tf_op jit(solution)/shard_map/ppermute | solution.py:730
  8.2 1.1 %copy-start = (bf16[4,144,512]{2,1,0:T(8,128)(2,1)S(1)}, bf16[4,144,512]{2,1,0:T(8,128)(2,1)}, u32[]{:S(2)}) copy-start(bf16[4,144,512]{2,1,0:T(8,128)(2,1)} %get-tuple-element.52.refs_0_.a_ref.refs_6_.refs_3_.refs_5_) | copy-start | bytes 1769476
  9.3 4.9 %copy-start.1 = (bf16[4,144,512]{2,1,0:T(8,128)(2,1)S(1)}, bf16[4,144,512]{2,1,0:T(8,128)(2,1)}, u32[]{:S(2)}) copy-start(bf16[4,144,512]{2,1,0:T(8,128)(2,1)} %get-tuple-element.52.refs_0_.a_ref.refs_6_.refs_3_.refs_5_) | copy-start | bytes 1769476
  9.3 13.7 %copy-start.3 = (bf16[4,144,256]{2,1,0:T(8,128)(2,1)S(1)}, bf16[4,144,256]{2,1,0:T(8,128)(2,1)}, u32[]{:S(2)}) copy-start(bf16[4,144,256]{2,1,0:T(8,128)(2,1)} %get-tuple-element.57.refs_3_) | copy-start | bytes 884740
  9.3 13.7 %copy-start.4 = (bf16[4,144,256]{2,1,0:T(8,128)(2,1)S(1)}, bf16[4,144,256]{2,1,0:T(8,128)(2,1)}, u32[]{:S(2)}) copy-start(bf16[4,144,256]{2,1,0:T(8,128)(2,1)} %get-tuple-element.58.refs_4_) | copy-start | bytes 884740
  9.3 17.5 %collective-permute-start.5 = (bf16[2,144,256]{2,1,0:T(8,128)(2,1)S(1)}, bf16[2,144,256]{2,1,0:T(8,128)(2,1)S(1)}, u32[]{:S(2)}, u32[]{:S(2)}) collective-permute-start(bf16[2,144,256]{2,1,0:T(8,128)(2,1)S(1)} %get-tuple-element.62), channel_id=1, source_target_pairs={{0,12},{1,13},{2,14},{3,15},{4,8},{5,9},{6,10},{7,11},{8,4},{9,5},... | collective-permute-start | bytes 442376 | tf_op jit(solution)/shard_map/ppermute | solution.py:730
  13.6 13.9 %collective-permute-start.6 = (bf16[2,144,256]{2,1,0:T(8,128)(2,1)S(1)}, bf16[2,144,256]{2,1,0:T(8,128)(2,1)S(1)}, u32[]{:S(2)}, u32[]{:S(2)}) collective-permute-start(bf16[2,144,256]{2,1,0:T(8,128)(2,1)S(1)} %get-tuple-element.63), channel_id=1, source_target_pairs={{0,8},{1,9},{2,10},{3,11},{4,12},{5,13},{6,14},{7,15},{8,0},{9,1},... | collective-permute-start | bytes 442376 | tf_op jit(solution)/shard_map/ppermute | solution.py:730
  13.6 14.5 %collective-permute-start.7 = (bf16[2,144,256]{2,1,0:T(8,128)(2,1)S(1)}, bf16[2,144,256]{2,1,0:T(8,128)(2,1)S(1)}, u32[]{:S(2)}, u32[]{:S(2)}) collective-permute-start(bf16[2,144,256]{2,1,0:T(8,128)(2,1)S(1)} %get-tuple-element.64), channel_id=1, source_target_pairs={{0,4},{1,5},{2,6},{3,7},{4,0},{5,1},{6,2},{7,3},{8,12},{9,13},{10,... | collective-permute-start | bytes 442376 | tf_op jit(solution)/shard_map/ppermute | solution.py:730
  23.1 19.7 %collective-permute-start.10 = (bf16[2,144,256]{2,1,0:T(8,128)(2,1)S(1)}, bf16[2,144,256]{2,1,0:T(8,128)(2,1)S(1)}, u32[]{:S(2)}, u32[]{:S(2)}) collective-permute-start(bf16[2,144,256]{2,1,0:T(8,128)(2,1)S(1)} %get-tuple-element.69), channel_id=1, source_target_pairs={{0,12},{1,13},{2,14},{3,15},{4,8},{5,9},{6,10},{7,11},{8,4},{9,5},... | collective-permute-start | bytes 442376 | tf_op jit(solution)/shard_map/ppermute | solution.py:730
  26.8 16.0 %collective-permute-start.8 = (bf16[2,144,256]{2,1,0:T(8,128)(2,1)S(1)}, bf16[2,144,256]{2,1,0:T(8,128)(2,1)S(1)}, u32[]{:S(2)}, u32[]{:S(2)}) collective-permute-start(bf16[2,144,256]{2,1,0:T(8,128)(2,1)S(1)} %get-tuple-element.67), channel_id=1, source_target_pairs={{0,8},{1,9},{2,10},{3,11},{4,12},{5,13},{6,14},{7,15},{8,0},{9,1},... | collective-permute-start | bytes 442376 | tf_op jit(solution)/shard_map/ppermute | solution.py:730
  26.8 16.0 %collective-permute-start.9 = (bf16[2,144,256]{2,1,0:T(8,128)(2,1)S(1)}, bf16[2,144,256]{2,1,0:T(8,128)(2,1)S(1)}, u32[]{:S(2)}, u32[]{:S(2)}) collective-permute-start(bf16[2,144,256]{2,1,0:T(8,128)(2,1)S(1)} %get-tuple-element.68), channel_id=1, source_target_pairs={{0,4},{1,5},{2,6},{3,7},{4,0},{5,1},{6,2},{7,3},{8,12},{9,13},{10,... | collective-permute-start | bytes 442376 | tf_op jit(solution)/shard_map/ppermute | solution.py:730
  27.5 31.2 %collective-permute-start.3 = (bf16[4,144,256]{2,1,0:T(8,128)(2,1)S(1)}, bf16[4,144,256]{2,1,0:T(8,128)(2,1)S(1)}, u32[]{:S(2)}, u32[]{:S(2)}) collective-permute-start(bf16[4,144,256]{2,1,0:T(8,128)(2,1)S(1)} %get-tuple-element.59), channel_id=1, source_target_pairs={{0,2},{1,3},{2,0},{3,1},{4,6},{5,7},{6,4},{7,5},{8,10},{9,11},{10,... | collective-permute-start | bytes 884744 | tf_op jit(solution)/shard_map/ppermute | solution.py:730
  28.1 30.6 %collective-permute-start.4 = (bf16[4,144,256]{2,1,0:T(8,128)(2,1)S(1)}, bf16[4,144,256]{2,1,0:T(8,128)(2,1)S(1)}, u32[]{:S(2)}, u32[]{:S(2)}) collective-permute-start(bf16[4,144,256]{2,1,0:T(8,128)(2,1)S(1)} %get-tuple-element.60), channel_id=1, source_target_pairs={{0,3},{1,2},{2,1},{3,0},{4,7},{5,6},{6,5},{7,4},{8,11},{9,10},{10,... | collective-permute-start | bytes 884744 | tf_op jit(solution)/shard_map/ppermute | solution.py:730
  54.2 9.9 %collective-permute-start.11 = (bf16[48,1152]{1,0:T(8,128)(2,1)S(1)}, bf16[48,1152]{1,0:T(8,128)(2,1)S(1)}, u32[]{:S(2)}, u32[]{:S(2)}) collective-permute-start(bf16[48,1152]{1,0:T(8,128)(2,1)S(1)} %get-tuple-element.79), channel_id=1, source_target_pairs={{0,4},{1,5},{2,6},{3,7},{4,0},{5,1},{6,2},{7,3},{8,12},{9,13},{10,... | collective-permute-start | bytes 331784 | tf_op jit(solution)/shard_map/ppermute | solution.py:730
  55.5 16.4 %collective-permute-start.14 = (bf16[48,1152]{1,0:T(8,128)(2,1)S(1)}, bf16[48,1152]{1,0:T(8,128)(2,1)S(1)}, u32[]{:S(2)}, u32[]{:S(2)}) collective-permute-start(bf16[48,1152]{1,0:T(8,128)(2,1)S(1)} %get-tuple-element.84), channel_id=1, source_target_pairs={{0,8},{1,9},{2,10},{3,11},{4,12},{5,13},{6,14},{7,15},{8,0},{9,1},... | collective-permute-start | bytes 331784 | tf_op jit(solution)/shard_map/ppermute | solution.py:730
  58.5 13.4 %collective-permute-start.15 = (bf16[48,1152]{1,0:T(8,128)(2,1)S(1)}, bf16[48,1152]{1,0:T(8,128)(2,1)S(1)}, u32[]{:S(2)}, u32[]{:S(2)}) collective-permute-start(bf16[48,1152]{1,0:T(8,128)(2,1)S(1)} %get-tuple-element.85), channel_id=1, source_target_pairs={{0,12},{1,13},{2,14},{3,15},{4,8},{5,9},{6,10},{7,11},{8,4},{9,5},... | collective-permute-start | bytes 331784 | tf_op jit(solution)/shard_map/ppermute | solution.py:730
  64.2 9.2 %collective-permute-start.12 = (bf16[2,48,512]{2,1,0:T(8,128)(2,1)S(1)}, bf16[2,48,512]{2,1,0:T(8,128)(2,1)S(1)}, u32[]{:S(2)}, u32[]{:S(2)}) collective-permute-start(bf16[2,48,512]{2,1,0:T(8,128)(2,1)S(1)} %get-tuple-element.80), channel_id=1, source_target_pairs={{0,2},{1,3},{2,0},{3,1},{4,6},{5,7},{6,4},{7,5},{8,10},{9,11},{10,... | collective-permute-start | bytes 294920 | tf_op jit(solution)/shard_map/ppermute | solution.py:730
  64.3 9.1 %collective-permute-start.13 = (bf16[2,48,512]{2,1,0:T(8,128)(2,1)S(1)}, bf16[2,48,512]{2,1,0:T(8,128)(2,1)S(1)}, u32[]{:S(2)}, u32[]{:S(2)}) collective-permute-start(bf16[2,48,512]{2,1,0:T(8,128)(2,1)S(1)} %get-tuple-element.81.refs_11_), channel_id=1, source_target_pairs={{0,3},{1,2},{2,1},{3,0},{4,7},{5,6},{6,5},{7,4},{8,11},{9,10},{10,... | collective-permute-start | bytes 294920 | tf_op jit(solution)/shard_map/ppermute | solution.py:730
  72.0 8.4 %collective-permute-start.16 = (bf16[2,48,512]{2,1,0:T(8,128)(2,1)S(1)}, bf16[2,48,512]{2,1,0:T(8,128)(2,1)S(1)}, u32[]{:S(2)}, u32[]{:S(2)}) collective-permute-start(bf16[2,48,512]{2,1,0:T(8,128)(2,1)S(1)} %get-tuple-element.88), channel_id=1, source_target_pairs={{0,2},{1,3},{2,0},{3,1},{4,6},{5,7},{6,4},{7,5},{8,10},{9,11},{10,... | collective-permute-start | bytes 294920 | tf_op jit(solution)/shard_map/ppermute | solution.py:730
  72.4 8.0 %collective-permute-start.17 = (bf16[2,48,512]{2,1,0:T(8,128)(2,1)S(1)}, bf16[2,48,512]{2,1,0:T(8,128)(2,1)S(1)}, u32[]{:S(2)}, u32[]{:S(2)}) collective-permute-start(bf16[2,48,512]{2,1,0:T(8,128)(2,1)S(1)} %get-tuple-element.89.refs_13_), channel_id=1, source_target_pairs={{0,3},{1,2},{2,1},{3,0},{4,7},{5,6},{6,5},{7,4},{8,11},{9,10},{10,... | collective-permute-start | bytes 294920 | tf_op jit(solution)/shard_map/ppermute | solution.py:730
  79.5 2.0 %copy-start.2 = (bf16[768,768]{1,0:T(8,128)(2,1)S(1)}, bf16[768,768]{1,0:T(8,128)(2,1)}, u32[]{:S(2)}) copy-start(bf16[768,768]{1,0:T(8,128)(2,1)} %refs_6_.1) | copy-start | bytes 3538948
  79.5 2.0 %collective-permute-start.18 = (bf16[4,48,512]{2,1,0:T(8,128)(2,1)S(1)}, bf16[4,48,512]{2,1,0:T(8,128)(2,1)S(1)}, u32[]{:S(2)}, u32[]{:S(2)}) collective-permute-start(bf16[4,48,512]{2,1,0:T(8,128)(2,1)S(1)} %get-tuple-element.98), channel_id=1, source_target_pairs={{0,1},{1,0},{2,3},{3,2},{4,5},{5,4},{6,7},{7,6},{8,9},{9,8},{10,11... | collective-permute-start | bytes 589832 | tf_op jit(solution)/shard_map/ppermute | solution.py:730

commit v14 on v13

--- a/solution.py
+++ b/solution.py
@@ -663,7 +663,7 @@
 
 def project_kernel(sources, index, mid, top, *refs):
     place = (index, mid, top)
-    parts, (w_ref, out_ref, held) = refs[:-3], refs[-3:]
+    parts, (w_ref, out_hbm, held, out_ref, sems) = refs[:-5], refs[-5:]
     for (j, first), part in zip(sources, parts):
         for p in range(part.shape[0]):
             head = head_of(place, j, first + p)
@@ -676,7 +676,13 @@
     col = lax.broadcasted_iota(jnp.int32, (TOK, TOK), 1)
     picker = (row == RATE * (col % BLK) + col // BLK).astype(BF16)
     attention = dot_nt(picker, held[...]).astype(BF16)
-    out_ref[...] = dot(attention, w_ref[...]).astype(BF16)
+    stores = []
+    for n, rows in enumerate((slice(0, HALF), slice(HALF, TOK))):
+        out_ref[rows, :] = dot(attention[rows, :], w_ref[...]).astype(BF16)
+        stores.append(pltpu.make_async_copy(out_ref.at[rows], out_hbm.at[rows], sems.at[n]))
+        stores[n].start()
+    for store in stores:
+        store.wait()
 
 
 def whole(shape):
@@ -906,8 +912,12 @@
     return call(
         functools.partial(project_kernel, list(parts)), place, (*parts.values(), out_weight), (1,),
         [whole(x.shape) for x in parts.values()] + [whole((width, width))],
-        [(whole((TOK, width)), jax.ShapeDtypeStruct((TOK, width), BF16))],
-        [pltpu.VMEM((width, TOK), BF16)],
+        [(anywhere, jax.ShapeDtypeStruct((TOK, width), BF16))],
+        [
+            pltpu.VMEM((width, TOK), BF16),
+            pltpu.VMEM((TOK, width), BF16),
+            pltpu.SemaphoreType.DMA((2,)),
+        ],
         1 << 18,
     )[0]
 

time: 84.7 us -> 84.9 us (level)
  no operation moved by 1% of the time
where the time goes in v14:
time: 84.9 us; the launch traced here: 84.7 us
  Pallas kernels  60 us (71%)
  starting transfers between devices  22.1 us (26%)
  waiting for transfers between devices  1.11 us (1%)
  local copies, waits for them, and re-layouts  1.09 us (1%)
    pallas_call x14, Pallas kernels, call(): pl.pallas_call(body if extra else kernel, grid_spec=pltpu.PrefetchScalarG...  60 us
    ppermute x19, starting transfers between devices, within(): return lax.ppermute(array, 'seq', [(i, i ^ apart) for i in range(count)])  22.1 us
  transfers between devices with their start and end apart: 19, of which 1 were waited for; matrix products, arithmetic and copies ran while one was open for 0% of the time, Pallas kernels for 61%

profile of v14, /device:TPU:0, one launch (start us, length us, event | category | flops | bytes accessed | tf_op | source)
XLA Modules:
  0.0 84.7 jit_solution(3617844006363116367)
XLA Ops:
  0.0 5.0 %shard_map.64 = (bf16[4,144,512]{2,1,0:T(8,128)(2,1)}, bf16[4,144,512]{2,1,0:T(8,128)(2,1)}, bf16[4,144,256]{2,1,0:T(8,128)(2,1)}, bf16[4,144,256]{2,1,0:T(8,128...) custom-call(s32[1]{0:T(128)} %bitcast.index.refs_0_, s32[16]{0:T(128)} %mid.9, s32[16]{0:T(128)} %top.9, ...), custom_call_target="tpu_custom_call" | custom-call | tf_op jit(solution)/shard_map/pallas_call | solution.py:713
  5.0 0.0 copy-start.5
  5.1 0.0 copy-start.6
  5.1 0.5 collective-permute-start
  5.6 2.6 %collective-permute-start.1 = (bf16[4,144,256]{2,1,0:T(8,128)(2,1)}, bf16[4,144,256]{2,1,0:T(8,128)(2,1)S(1)}, u32[]{:S(2)}, u32[]{:S(2)}) collective-permute-start(bf16[4,144,256]{2,1,0:T(8,128)(2,1)} %get-tuple-element.54), channel_id=1, source_target_pairs={{0,2},{1,3},{2,0},{3,1},{4,6},{5,7},{6,4},{7,5},{8,10},{9,11},{10,... | collective-permute-start | bytes 884744 | tf_op jit(solution)/shard_map/ppermute | solution.py:736
  8.2 0.1 collective-permute-start.2
  8.2 0.0 collective-permute-done.refs_1_.b_ref.refs_7_.refs_4_.refs_6_
  8.2 1.1 %copy-done = bf16[4,144,512]{2,1,0:T(8,128)(2,1)S(1)} copy-done((bf16[4,144,512]{2,1,0:T(8,128)(2,1)S(1)}, bf16[4,144,512]{2,1,0:T(8,128)(2,1)}, u32[]{:S(2)}) %copy-start) | copy-done | bytes 589848
  9.3 4.2 %collective-permute-start.5 = (bf16[2,144,256]{2,1,0:T(8,128)(2,1)S(1)}, bf16[2,144,256]{2,1,0:T(8,128)(2,1)S(1)}, u32[]{:S(2)}, u32[]{:S(2)}) collective-permute-start(bf16[2,144,256]{2,1,0:T(8,128)(2,1)S(1)} %get-tuple-element.62), channel_id=1, source_target_pairs={{0,12},{1,13},{2,14},{3,15},{4,8},{5,9},{6,10},{7,11},{8,4},{9,5},... | collective-permute-start | bytes 442376 | tf_op jit(solution)/shard_map/ppermute | solution.py:736
  13.6 0.6 collective-permute-start.7
  14.2 8.7 %shard_map.65 = (f32[4,4,64,256]{3,2,1,0:T(8,128)S(1)}, f32[4,4,8,256]{3,2,1,0:T(8,128)S(1)}) custom-call(s32[1]{0:T(128)} %bitcast.index.refs_0_, s32[16]{0:T(128)S(1)} %copy-done.5, s32[16]{0:T(128)S(1)} %copy-done.6, bf16[4,144,512]{2,1,0:T(8,128)(2,1)S(1)} %copy-done.1, bf16[4,144,512]{2,1,0:T(8,128)(2,1)S(1)} %collective-permute-done.refs_1_.b_ref.refs_7_.refs_4_.refs_6_), custom_call_target="tpu_custom_call" | custom-call | tf_op jit(solution)/shard_map/pallas_call | solution.py:713
  23.1 3.8 %collective-permute-start.10 = (bf16[2,144,256]{2,1,0:T(8,128)(2,1)S(1)}, bf16[2,144,256]{2,1,0:T(8,128)(2,1)S(1)}, u32[]{:S(2)}, u32[]{:S(2)}) collective-permute-start(bf16[2,144,256]{2,1,0:T(8,128)(2,1)S(1)} %get-tuple-element.69), channel_id=1, source_target_pairs={{0,12},{1,13},{2,14},{3,15},{4,8},{5,9},{6,10},{7,11},{8,4},{9,5},... | collective-permute-start | bytes 442376 | tf_op jit(solution)/shard_map/ppermute | solution.py:736
  26.8 0.7 collective-permute-start.9
  27.5 0.6 collective-permute-start.3
  28.1 14.7 %shard_map.68 = (f32[4,4,64,256]{3,2,1,0:T(8,128)S(1)}, f32[4,4,8,256]{3,2,1,0:T(8,128)S(1)}, f32[4,2,64,256]{3,2,1,0:T(8,128)S(1)}, f32[4,2,8,256]{3,2,1,0:T(8,...) custom-call(s32[1]{0:T(128)} %bitcast.index.refs_0_, ...), custom_call_target="tpu_custom_call" | custom-call | tf_op jit(solution)/shard_map/pallas_call | solution.py:713
  42.8 11.4 %shard_map.69 = (bf16[48,1152]{1,0:T(8,128)(2,1)S(1)}, bf16[48,1152]{1,0:T(8,128)(2,1)S(1)}, bf16[48,1152]{1,0:T(8,128)(2,1)S(1)}, bf16[48,1152]{1,0:T(8,128)(2,1)S(1)}) custom-call(s32[1]{0:T(128)} %bitcast.index.refs_0_, s32[16]{0:T(128)S(1)} %copy-done.5, s32[16]{0:T(128)S(1)} %copy-done.6, ...), custom_call_target="tpu_custom_call" | custom-call | flops 8589934592 | tf_op jit(solution)/shard_map/pallas_call | solution.py:713
  54.2 1.3 %collective-permute-start.11 = (bf16[48,1152]{1,0:T(8,128)(2,1)S(1)}, bf16[48,1152]{1,0:T(8,128)(2,1)S(1)}, u32[]{:S(2)}, u32[]{:S(2)}) collective-permute-start(bf16[48,1152]{1,0:T(8,128)(2,1)S(1)} %get-tuple-element.79), channel_id=1, source_target_pairs={{0,4},{1,5},{2,6},{3,7},{4,0},{5,1},{6,2},{7,3},{8,12},{9,13},{10,... | collective-permute-start | bytes 331784 | tf_op jit(solution)/shard_map/ppermute | solution.py:736
  55.5 3.0 %collective-permute-start.14 = (bf16[48,1152]{1,0:T(8,128)(2,1)S(1)}, bf16[48,1152]{1,0:T(8,128)(2,1)S(1)}, u32[]{:S(2)}, u32[]{:S(2)}) collective-permute-start(bf16[48,1152]{1,0:T(8,128)(2,1)S(1)} %get-tuple-element.84), channel_id=1, source_target_pairs={{0,8},{1,9},{2,10},{3,11},{4,12},{5,13},{6,14},{7,15},{8,0},{9,1},... | collective-permute-start | bytes 331784 | tf_op jit(solution)/shard_map/ppermute | solution.py:736
  58.5 0.2 collective-permute-start.15
  58.7 5.4 %shard_map.70 = (f32[2,4,64,256]{3,2,1,0:T(8,128)S(1)}, f32[2,4,8,256]{3,2,1,0:T(8,128)S(1)}) custom-call(s32[1]{0:T(128)} %bitcast.index.refs_0_, s32[16]{0:T(128)S(1)} %copy-done.5, s32[16]{0:T(128)S(1)} %copy-done.6, bf16[4,144,512]{2,1,0:T(8,128)(2,1)S(1)} %copy-done.1, ...), custom_call_target="tpu_custom_call" | custom-call | tf_op jit(solution)/shard_map/pallas_call | solution.py:713
  64.1 0.1 shard_map.71
  64.2 0.1 collective-permute-start.12
  64.2 2.3 %collective-permute-start.13 = (bf16[2,48,512]{2,1,0:T(8,128)(2,1)S(1)}, bf16[2,48,512]{2,1,0:T(8,128)(2,1)S(1)}, u32[]{:S(2)}, u32[]{:S(2)}) collective-permute-start(bf16[2,48,512]{2,1,0:T(8,128)(2,1)S(1)} %get-tuple-element.81.refs_11_), channel_id=1, source_target_pairs={{0,3},{1,2},{2,1},{3,0},{4,7},{5,6},{6,5},{7,4},{8,11},{9,10},{10,... | collective-permute-start | bytes 294920 | tf_op jit(solution)/shard_map/ppermute | solution.py:736
  66.5 5.4 %shard_map.72 = (f32[2,4,64,256]{3,2,1,0:T(8,128)S(1)}, f32[2,4,8,256]{3,2,1,0:T(8,128)S(1)}) custom-call(s32[1]{0:T(128)} %bitcast.index.refs_0_, s32[16]{0:T(128)S(1)} %copy-done.5, s32[16]{0:T(128)S(1)} %copy-done.6, bf16[4,144,512]{2,1,0:T(8,128)(2,1)S(1)} %copy-done.1, ...), custom_call_target="tpu_custom_call" | custom-call | tf_op jit(solution)/shard_map/pallas_call | solution.py:713
  71.9 0.1 shard_map.74
  72.0 0.4 collective-permute-start.16
  72.4 0.9 %collective-permute-start.17 = (bf16[2,48,512]{2,1,0:T(8,128)(2,1)S(1)}, bf16[2,48,512]{2,1,0:T(8,128)(2,1)S(1)}, u32[]{:S(2)}, u32[]{:S(2)}) collective-permute-start(bf16[2,48,512]{2,1,0:T(8,128)(2,1)S(1)} %get-tuple-element.89.refs_13_), channel_id=1, source_target_pairs={{0,3},{1,2},{2,1},{3,0},{4,7},{5,6},{6,5},{7,4},{8,11},{9,10},{10,... | collective-permute-start | bytes 294920 | tf_op jit(solution)/shard_map/ppermute | solution.py:736
  73.3 6.1 %shard_map.76 = (bf16[4,48,512]{2,1,0:T(8,128)(2,1)S(1)}, bf16[4,48,512]{2,1,0:T(8,128)(2,1)S(1)}) custom-call(s32[1]{0:T(128)} %bitcast.index.refs_0_, s32[16]{0:T(128)S(1)} %copy-done.5, s32[16]{0:T(128)S(1)} %copy-done.6, bf16[4,144,256]{2,1,0:T(8,128)(2,1)S(1)} %collective-permute-done.3.refs_7_.refs_3_, ...), custom_call_target="tpu_custom_call" | custom-call | tf_op jit(solution)/shard_map/pallas_call | solution.py:713
  79.4 0.0 copy-start.2
  79.4 1.0 %collective-permute-start.18 = (bf16[4,48,512]{2,1,0:T(8,128)(2,1)S(1)}, bf16[4,48,512]{2,1,0:T(8,128)(2,1)S(1)}, u32[]{:S(2)}, u32[]{:S(2)}) collective-permute-start(bf16[4,48,512]{2,1,0:T(8,128)(2,1)S(1)} %get-tuple-element.98), channel_id=1, source_target_pairs={{0,1},{1,0},{2,3},{3,2},{4,5},{5,4},{6,7},{7,6},{8,9},{9,8},{10,11... | collective-permute-start | bytes 589832 | tf_op jit(solution)/shard_map/ppermute | solution.py:736
  80.4 1.1 %collective-permute-done.18.refs_5_ = bf16[4,48,512]{2,1,0:T(8,128)(2,1)S(1)} collective-permute-done((bf16[4,48,512]{2,1,0:T(8,128)(2,1)S(1)}, bf16[4,48,512]{2,1,0:T(8,128)(2,1)S(1)}, u32[]{:S(2)}, u32[]{:S(2)}) %collective-permute-start.18) | collective-permute-done | bytes 196640 | tf_op jit(solution)/shard_map/ppermute | solution.py:736
  81.5 3.0 %shard_map.77 = bf16[512,768]{1,0:T(8,128)(2,1)} custom-call(s32[1]{0:T(128)} %bitcast.index.refs_0_, s32[16]{0:T(128)S(1)} %copy-done.5, s32[16]{0:T(128)S(1)} %copy-done.6, bf16[2,48,512]{2,1,0:T(8,128)(2,1)S(1)} %get-tuple-element.90.refs_0_, bf16[2,48,512]{2,1,0:T(8,128)(2,1)S(1)} %get-tuple-element.91.refs_1_, ...), custom_call_target="tpu_custom_call" | custom-call | tf_op jit(solution)/shard_map/pallas_call | solution.py:713
  (34 shorter events, 0.1 us)
Async XLA Ops:
  5.0 9.2 %copy-start.5 = (s32[16]{0:T(128)S(1)}, s32[16]{0:T(128)}, u32[]{:S(2)}) copy-start(s32[16]{0:T(128)} %mid.9) | copy-start | bytes 196
  5.1 9.2 %copy-start.6 = (s32[16]{0:T(128)S(1)}, s32[16]{0:T(128)}, u32[]{:S(2)}) copy-start(s32[16]{0:T(128)} %top.9) | copy-start | bytes 196
  5.1 3.2 %collective-permute-start = (bf16[4,144,512]{2,1,0:T(8,128)(2,1)}, bf16[4,144,512]{2,1,0:T(8,128)(2,1)S(1)}, u32[]{:S(2)}, u32[]{:S(2)}) collective-permute-start(bf16[4,144,512]{2,1,0:T(8,128)(2,1)} %get-tuple-element.53), channel_id=1, source_target_pairs={{0,1},{1,0},{2,3},{3,2},{4,5},{5,4},{6,7},{7,6},{8,9},{9,8},{10,11... | collective-permute-start | bytes 1769480 | tf_op jit(solution)/shard_map/ppermute | solution.py:736
  5.6 17.4 %collective-permute-start.1 = (bf16[4,144,256]{2,1,0:T(8,128)(2,1)}, bf16[4,144,256]{2,1,0:T(8,128)(2,1)S(1)}, u32[]{:S(2)}, u32[]{:S(2)}) collective-permute-start(bf16[4,144,256]{2,1,0:T(8,128)(2,1)} %get-tuple-element.54), channel_id=1, source_target_pairs={{0,2},{1,3},{2,0},{3,1},{4,6},{5,7},{6,4},{7,5},{8,10},{9,11},{10,... | collective-permute-start | bytes 884744 | tf_op jit(solution)/shard_map/ppermute | solution.py:736
  8.2 14.8 %collective-permute-start.2 = (bf16[4,144,256]{2,1,0:T(8,128)(2,1)}, bf16[4,144,256]{2,1,0:T(8,128)(2,1)S(1)}, u32[]{:S(2)}, u32[]{:S(2)}) collective-permute-start(bf16[4,144,256]{2,1,0:T(8,128)(2,1)} %get-tuple-element.55), channel_id=1, source_target_pairs={{0,3},{1,2},{2,1},{3,0},{4,7},{5,6},{6,5},{7,4},{8,11},{9,10},{10,... | collective-permute-start | bytes 884744 | tf_op jit(solution)/shard_map/ppermute | solution.py:736
  8.2 1.1 %copy-start = (bf16[4,144,512]{2,1,0:T(8,128)(2,1)S(1)}, bf16[4,144,512]{2,1,0:T(8,128)(2,1)}, u32[]{:S(2)}) copy-start(bf16[4,144,512]{2,1,0:T(8,128)(2,1)} %get-tuple-element.52.refs_0_.a_ref.refs_6_.refs_3_.refs_5_) | copy-start | bytes 1769476
  9.3 4.9 %copy-start.1 = (bf16[4,144,512]{2,1,0:T(8,128)(2,1)S(1)}, bf16[4,144,512]{2,1,0:T(8,128)(2,1)}, u32[]{:S(2)}) copy-start(bf16[4,144,512]{2,1,0:T(8,128)(2,1)} %get-tuple-element.52.refs_0_.a_ref.refs_6_.refs_3_.refs_5_) | copy-start | bytes 1769476
  9.3 13.7 %copy-start.3 = (bf16[4,144,256]{2,1,0:T(8,128)(2,1)S(1)}, bf16[4,144,256]{2,1,0:T(8,128)(2,1)}, u32[]{:S(2)}) copy-start(bf16[4,144,256]{2,1,0:T(8,128)(2,1)} %get-tuple-element.57.refs_3_) | copy-start | bytes 884740
  9.3 13.7 %copy-start.4 = (bf16[4,144,256]{2,1,0:T(8,128)(2,1)S(1)}, bf16[4,144,256]{2,1,0:T(8,128)(2,1)}, u32[]{:S(2)}) copy-start(bf16[4,144,256]{2,1,0:T(8,128)(2,1)} %get-tuple-element.58.refs_4_) | copy-start | bytes 884740
  9.3 17.5 %collective-permute-start.5 = (bf16[2,144,256]{2,1,0:T(8,128)(2,1)S(1)}, bf16[2,144,256]{2,1,0:T(8,128)(2,1)S(1)}, u32[]{:S(2)}, u32[]{:S(2)}) collective-permute-start(bf16[2,144,256]{2,1,0:T(8,128)(2,1)S(1)} %get-tuple-element.62), channel_id=1, source_target_pairs={{0,12},{1,13},{2,14},{3,15},{4,8},{5,9},{6,10},{7,11},{8,4},{9,5},... | collective-permute-start | bytes 442376 | tf_op jit(solution)/shard_map/ppermute | solution.py:736
  13.6 13.9 %collective-permute-start.6 = (bf16[2,144,256]{2,1,0:T(8,128)(2,1)S(1)}, bf16[2,144,256]{2,1,0:T(8,128)(2,1)S(1)}, u32[]{:S(2)}, u32[]{:S(2)}) collective-permute-start(bf16[2,144,256]{2,1,0:T(8,128)(2,1)S(1)} %get-tuple-element.63), channel_id=1, source_target_pairs={{0,8},{1,9},{2,10},{3,11},{4,12},{5,13},{6,14},{7,15},{8,0},{9,1},... | collective-permute-start | bytes 442376 | tf_op jit(solution)/shard_map/ppermute | solution.py:736
  13.6 14.5 %collective-permute-start.7 = (bf16[2,144,256]{2,1,0:T(8,128)(2,1)S(1)}, bf16[2,144,256]{2,1,0:T(8,128)(2,1)S(1)}, u32[]{:S(2)}, u32[]{:S(2)}) collective-permute-start(bf16[2,144,256]{2,1,0:T(8,128)(2,1)S(1)} %get-tuple-element.64), channel_id=1, source_target_pairs={{0,4},{1,5},{2,6},{3,7},{4,0},{5,1},{6,2},{7,3},{8,12},{9,13},{10,... | collective-permute-start | bytes 442376 | tf_op jit(solution)/shard_map/ppermute | solution.py:736
  23.1 19.7 %collective-permute-start.10 = (bf16[2,144,256]{2,1,0:T(8,128)(2,1)S(1)}, bf16[2,144,256]{2,1,0:T(8,128)(2,1)S(1)}, u32[]{:S(2)}, u32[]{:S(2)}) collective-permute-start(bf16[2,144,256]{2,1,0:T(8,128)(2,1)S(1)} %get-tuple-element.69), channel_id=1, source_target_pairs={{0,12},{1,13},{2,14},{3,15},{4,8},{5,9},{6,10},{7,11},{8,4},{9,5},... | collective-permute-start | bytes 442376 | tf_op jit(solution)/shard_map/ppermute | solution.py:736
  26.8 15.9 %collective-permute-start.8 = (bf16[2,144,256]{2,1,0:T(8,128)(2,1)S(1)}, bf16[2,144,256]{2,1,0:T(8,128)(2,1)S(1)}, u32[]{:S(2)}, u32[]{:S(2)}) collective-permute-start(bf16[2,144,256]{2,1,0:T(8,128)(2,1)S(1)} %get-tuple-element.67), channel_id=1, source_target_pairs={{0,8},{1,9},{2,10},{3,11},{4,12},{5,13},{6,14},{7,15},{8,0},{9,1},... | collective-permute-start | bytes 442376 | tf_op jit(solution)/shard_map/ppermute | solution.py:736
  26.8 15.9 %collective-permute-start.9 = (bf16[2,144,256]{2,1,0:T(8,128)(2,1)S(1)}, bf16[2,144,256]{2,1,0:T(8,128)(2,1)S(1)}, u32[]{:S(2)}, u32[]{:S(2)}) collective-permute-start(bf16[2,144,256]{2,1,0:T(8,128)(2,1)S(1)} %get-tuple-element.68), channel_id=1, source_target_pairs={{0,4},{1,5},{2,6},{3,7},{4,0},{5,1},{6,2},{7,3},{8,12},{9,13},{10,... | collective-permute-start | bytes 442376 | tf_op jit(solution)/shard_map/ppermute | solution.py:736
  27.5 31.1 %collective-permute-start.3 = (bf16[4,144,256]{2,1,0:T(8,128)(2,1)S(1)}, bf16[4,144,256]{2,1,0:T(8,128)(2,1)S(1)}, u32[]{:S(2)}, u32[]{:S(2)}) collective-permute-start(bf16[4,144,256]{2,1,0:T(8,128)(2,1)S(1)} %get-tuple-element.59), channel_id=1, source_target_pairs={{0,2},{1,3},{2,0},{3,1},{4,6},{5,7},{6,4},{7,5},{8,10},{9,11},{10,... | collective-permute-start | bytes 884744 | tf_op jit(solution)/shard_map/ppermute | solution.py:736
  28.1 30.6 %collective-permute-start.4 = (bf16[4,144,256]{2,1,0:T(8,128)(2,1)S(1)}, bf16[4,144,256]{2,1,0:T(8,128)(2,1)S(1)}, u32[]{:S(2)}, u32[]{:S(2)}) collective-permute-start(bf16[4,144,256]{2,1,0:T(8,128)(2,1)S(1)} %get-tuple-element.60), channel_id=1, source_target_pairs={{0,3},{1,2},{2,1},{3,0},{4,7},{5,6},{6,5},{7,4},{8,11},{9,10},{10,... | collective-permute-start | bytes 884744 | tf_op jit(solution)/shard_map/ppermute | solution.py:736
  54.2 9.9 %collective-permute-start.11 = (bf16[48,1152]{1,0:T(8,128)(2,1)S(1)}, bf16[48,1152]{1,0:T(8,128)(2,1)S(1)}, u32[]{:S(2)}, u32[]{:S(2)}) collective-permute-start(bf16[48,1152]{1,0:T(8,128)(2,1)S(1)} %get-tuple-element.79), channel_id=1, source_target_pairs={{0,4},{1,5},{2,6},{3,7},{4,0},{5,1},{6,2},{7,3},{8,12},{9,13},{10,... | collective-permute-start | bytes 331784 | tf_op jit(solution)/shard_map/ppermute | solution.py:736
  55.5 16.4 %collective-permute-start.14 = (bf16[48,1152]{1,0:T(8,128)(2,1)S(1)}, bf16[48,1152]{1,0:T(8,128)(2,1)S(1)}, u32[]{:S(2)}, u32[]{:S(2)}) collective-permute-start(bf16[48,1152]{1,0:T(8,128)(2,1)S(1)} %get-tuple-element.84), channel_id=1, source_target_pairs={{0,8},{1,9},{2,10},{3,11},{4,12},{5,13},{6,14},{7,15},{8,0},{9,1},... | collective-permute-start | bytes 331784 | tf_op jit(solution)/shard_map/ppermute | solution.py:736
  58.5 13.4 %collective-permute-start.15 = (bf16[48,1152]{1,0:T(8,128)(2,1)S(1)}, bf16[48,1152]{1,0:T(8,128)(2,1)S(1)}, u32[]{:S(2)}, u32[]{:S(2)}) collective-permute-start(bf16[48,1152]{1,0:T(8,128)(2,1)S(1)} %get-tuple-element.85), channel_id=1, source_target_pairs={{0,12},{1,13},{2,14},{3,15},{4,8},{5,9},{6,10},{7,11},{8,4},{9,5},... | collective-permute-start | bytes 331784 | tf_op jit(solution)/shard_map/ppermute | solution.py:736
  64.2 9.2 %collective-permute-start.12 = (bf16[2,48,512]{2,1,0:T(8,128)(2,1)S(1)}, bf16[2,48,512]{2,1,0:T(8,128)(2,1)S(1)}, u32[]{:S(2)}, u32[]{:S(2)}) collective-permute-start(bf16[2,48,512]{2,1,0:T(8,128)(2,1)S(1)} %get-tuple-element.80), channel_id=1, source_target_pairs={{0,2},{1,3},{2,0},{3,1},{4,6},{5,7},{6,4},{7,5},{8,10},{9,11},{10,... | collective-permute-start | bytes 294920 | tf_op jit(solution)/shard_map/ppermute | solution.py:736
  64.2 9.1 %collective-permute-start.13 = (bf16[2,48,512]{2,1,0:T(8,128)(2,1)S(1)}, bf16[2,48,512]{2,1,0:T(8,128)(2,1)S(1)}, u32[]{:S(2)}, u32[]{:S(2)}) collective-permute-start(bf16[2,48,512]{2,1,0:T(8,128)(2,1)S(1)} %get-tuple-element.81.refs_11_), channel_id=1, source_target_pairs={{0,3},{1,2},{2,1},{3,0},{4,7},{5,6},{6,5},{7,4},{8,11},{9,10},{10,... | collective-permute-start | bytes 294920 | tf_op jit(solution)/shard_map/ppermute | solution.py:736
  72.0 8.4 %collective-permute-start.16 = (bf16[2,48,512]{2,1,0:T(8,128)(2,1)S(1)}, bf16[2,48,512]{2,1,0:T(8,128)(2,1)S(1)}, u32[]{:S(2)}, u32[]{:S(2)}) collective-permute-start(bf16[2,48,512]{2,1,0:T(8,128)(2,1)S(1)} %get-tuple-element.88), channel_id=1, source_target_pairs={{0,2},{1,3},{2,0},{3,1},{4,6},{5,7},{6,4},{7,5},{8,10},{9,11},{10,... | collective-permute-start | bytes 294920 | tf_op jit(solution)/shard_map/ppermute | solution.py:736
  72.4 8.0 %collective-permute-start.17 = (bf16[2,48,512]{2,1,0:T(8,128)(2,1)S(1)}, bf16[2,48,512]{2,1,0:T(8,128)(2,1)S(1)}, u32[]{:S(2)}, u32[]{:S(2)}) collective-permute-start(bf16[2,48,512]{2,1,0:T(8,128)(2,1)S(1)} %get-tuple-element.89.refs_13_), channel_id=1, source_target_pairs={{0,3},{1,2},{2,1},{3,0},{4,7},{5,6},{6,5},{7,4},{8,11},{9,10},{10,... | collective-permute-start | bytes 294920 | tf_op jit(solution)/shard_map/ppermute | solution.py:736
  79.4 2.1 %copy-start.2 = (bf16[768,768]{1,0:T(8,128)(2,1)S(1)}, bf16[768,768]{1,0:T(8,128)(2,1)}, u32[]{:S(2)}) copy-start(bf16[768,768]{1,0:T(8,128)(2,1)} %refs_6_.1) | copy-start | bytes 3538948
  79.4 2.0 %collective-permute-start.18 = (bf16[4,48,512]{2,1,0:T(8,128)(2,1)S(1)}, bf16[4,48,512]{2,1,0:T(8,128)(2,1)S(1)}, u32[]{:S(2)}, u32[]{:S(2)}) collective-permute-start(bf16[4,48,512]{2,1,0:T(8,128)(2,1)S(1)} %get-tuple-element.98), channel_id=1, source_target_pairs={{0,1},{1,0},{2,3},{3,2},{4,5},{5,4},{6,7},{7,6},{8,9},{9,8},{10,11... | collective-permute-start | bytes 589832 | tf_op jit(solution)/shard_map/ppermute | solution.py:736

commit v15 on v13

--- a/solution.py
+++ b/solution.py
@@ -796,7 +796,7 @@
     ours = regroup(own0, own1)
     ours = swap_segments(ours)
     held = {(0, 0): own0, (1, 0): own1}
-    state_own = near(held, own_sel + own_rest, [[(q, 0, None) for q in own]], [])
+    state_own = near(held, own_sel + own_rest, [[(q, 0, None) for q in own]], [], step=HG)
     *theirs, rest2, rest3 = regroup(sel2, sel3, after=state_own[1:], through=(rest2, rest3))
     theirs = swap_segments(theirs)
     rest2, rest3 = within(rest2, 2), within(rest3, 3)

time: 84.7 us -> 84.6 us (level)
  no operation moved by 1% of the time
where the time goes in v15:
time: 84.6 us; the launch traced here: 84.4 us
  Pallas kernels  59.8 us (71%)
  starting transfers between devices  22.1 us (26%)
  waiting for transfers between devices  1.11 us (1%)
  local copies, waits for them, and re-layouts  1.09 us (1%)
    pallas_call x14, Pallas kernels, call(): pl.pallas_call(body if extra else kernel, grid_spec=pltpu.PrefetchScalarG...  59.8 us
    ppermute x19, starting transfers between devices, within(): return lax.ppermute(array, 'seq', [(i, i ^ apart) for i in range(count)])  22.1 us
  transfers between devices with their start and end apart: 19, of which 1 were waited for; matrix products, arithmetic and copies ran while one was open for 0% of the time, Pallas kernels for 61%

profile of v15, /device:TPU:0, one launch (start us, length us, event | category | flops | bytes accessed | tf_op | source)
XLA Modules:
  0.0 84.4 jit_solution(12068464040801835350)
XLA Ops:
  0.0 5.0 %shard_map.64 = (bf16[4,144,512]{2,1,0:T(8,128)(2,1)}, bf16[4,144,512]{2,1,0:T(8,128)(2,1)}, bf16[4,144,256]{2,1,0:T(8,128)(2,1)}, bf16[4,144,256]{2,1,0:T(8,128...) custom-call(s32[1]{0:T(128)} %bitcast.index.refs_0_, s32[16]{0:T(128)} %mid.9, s32[16]{0:T(128)} %top.9, ...), custom_call_target="tpu_custom_call" | custom-call | tf_op jit(solution)/shard_map/pallas_call | solution.py:707
  5.0 0.0 copy-start.5
  5.1 0.0 copy-start.6
  5.1 0.5 collective-permute-start
  5.6 2.6 %collective-permute-start.1 = (bf16[4,144,256]{2,1,0:T(8,128)(2,1)}, bf16[4,144,256]{2,1,0:T(8,128)(2,1)S(1)}, u32[]{:S(2)}, u32[]{:S(2)}) collective-permute-start(bf16[4,144,256]{2,1,0:T(8,128)(2,1)} %get-tuple-element.54), channel_id=1, source_target_pairs={{0,2},{1,3},{2,0},{3,1},{4,6},{5,7},{6,4},{7,5},{8,10},{9,11},{10,... | collective-permute-start | bytes 884744 | tf_op jit(solution)/shard_map/ppermute | solution.py:730
  8.2 0.1 collective-permute-start.2
  8.2 0.0 collective-permute-done.refs_1_.b_ref.refs_7_.refs_4_.refs_6_
  8.2 1.1 %copy-done = bf16[4,144,512]{2,1,0:T(8,128)(2,1)S(1)} copy-done((bf16[4,144,512]{2,1,0:T(8,128)(2,1)S(1)}, bf16[4,144,512]{2,1,0:T(8,128)(2,1)}, u32[]{:S(2)}) %copy-start) | copy-done | bytes 589848
  9.3 4.2 %collective-permute-start.5 = (bf16[2,144,256]{2,1,0:T(8,128)(2,1)S(1)}, bf16[2,144,256]{2,1,0:T(8,128)(2,1)S(1)}, u32[]{:S(2)}, u32[]{:S(2)}) collective-permute-start(bf16[2,144,256]{2,1,0:T(8,128)(2,1)S(1)} %get-tuple-element.62), channel_id=1, source_target_pairs={{0,12},{1,13},{2,14},{3,15},{4,8},{5,9},{6,10},{7,11},{8,4},{9,5},... | collective-permute-start | bytes 442376 | tf_op jit(solution)/shard_map/ppermute | solution.py:730
  13.6 0.6 collective-permute-start.7
  14.2 8.6 %shard_map.65 = (f32[4,4,64,256]{3,2,1,0:T(8,128)S(1)}, f32[4,4,8,256]{3,2,1,0:T(8,128)S(1)}) custom-call(s32[1]{0:T(128)} %bitcast.index.refs_0_, s32[16]{0:T(128)S(1)} %copy-done.5, s32[16]{0:T(128)S(1)} %copy-done.6, bf16[4,144,512]{2,1,0:T(8,128)(2,1)S(1)} %copy-done.1, bf16[4,144,512]{2,1,0:T(8,128)(2,1)S(1)} %collective-permute-done.refs_1_.b_ref.refs_7_.refs_4_.refs_6_), custom_call_target="tpu_custom_call" | custom-call | tf_op jit(solution)/shard_map/pallas_call | solution.py:707
  22.9 3.8 %collective-permute-start.10 = (bf16[2,144,256]{2,1,0:T(8,128)(2,1)S(1)}, bf16[2,144,256]{2,1,0:T(8,128)(2,1)S(1)}, u32[]{:S(2)}, u32[]{:S(2)}) collective-permute-start(bf16[2,144,256]{2,1,0:T(8,128)(2,1)S(1)} %get-tuple-element.69), channel_id=1, source_target_pairs={{0,12},{1,13},{2,14},{3,15},{4,8},{5,9},{6,10},{7,11},{8,4},{9,5},... | collective-permute-start | bytes 442376 | tf_op jit(solution)/shard_map/ppermute | solution.py:730
  26.8 0.6 collective-permute-start.9
  27.4 0.7 collective-permute-start.3
  28.1 14.7 %shard_map.68 = (f32[4,4,64,256]{3,2,1,0:T(8,128)S(1)}, f32[4,4,8,256]{3,2,1,0:T(8,128)S(1)}, f32[4,2,64,256]{3,2,1,0:T(8,128)S(1)}, f32[4,2,8,256]{3,2,1,0:T(8,...) custom-call(s32[1]{0:T(128)} %bitcast.index.refs_0_, ...), custom_call_target="tpu_custom_call" | custom-call | tf_op jit(solution)/shard_map/pallas_call | solution.py:707
  42.8 11.4 %shard_map.69 = (bf16[48,1152]{1,0:T(8,128)(2,1)S(1)}, bf16[48,1152]{1,0:T(8,128)(2,1)S(1)}, bf16[48,1152]{1,0:T(8,128)(2,1)S(1)}, bf16[48,1152]{1,0:T(8,128)(2,1)S(1)}) custom-call(s32[1]{0:T(128)} %bitcast.index.refs_0_, s32[16]{0:T(128)S(1)} %copy-done.5, s32[16]{0:T(128)S(1)} %copy-done.6, ...), custom_call_target="tpu_custom_call" | custom-call | flops 8589934592 | tf_op jit(solution)/shard_map/pallas_call | solution.py:707
  54.2 1.3 %collective-permute-start.11 = (bf16[48,1152]{1,0:T(8,128)(2,1)S(1)}, bf16[48,1152]{1,0:T(8,128)(2,1)S(1)}, u32[]{:S(2)}, u32[]{:S(2)}) collective-permute-start(bf16[48,1152]{1,0:T(8,128)(2,1)S(1)} %get-tuple-element.79), channel_id=1, source_target_pairs={{0,4},{1,5},{2,6},{3,7},{4,0},{5,1},{6,2},{7,3},{8,12},{9,13},{10,... | collective-permute-start | bytes 331784 | tf_op jit(solution)/shard_map/ppermute | solution.py:730
  55.5 2.9 %collective-permute-start.14 = (bf16[48,1152]{1,0:T(8,128)(2,1)S(1)}, bf16[48,1152]{1,0:T(8,128)(2,1)S(1)}, u32[]{:S(2)}, u32[]{:S(2)}) collective-permute-start(bf16[48,1152]{1,0:T(8,128)(2,1)S(1)} %get-tuple-element.84), channel_id=1, source_target_pairs={{0,8},{1,9},{2,10},{3,11},{4,12},{5,13},{6,14},{7,15},{8,0},{9,1},... | collective-permute-start | bytes 331784 | tf_op jit(solution)/shard_map/ppermute | solution.py:730
  58.4 0.2 collective-permute-start.15
  58.7 5.4 %shard_map.70 = (f32[2,4,64,256]{3,2,1,0:T(8,128)S(1)}, f32[2,4,8,256]{3,2,1,0:T(8,128)S(1)}) custom-call(s32[1]{0:T(128)} %bitcast.index.refs_0_, s32[16]{0:T(128)S(1)} %copy-done.5, s32[16]{0:T(128)S(1)} %copy-done.6, bf16[4,144,512]{2,1,0:T(8,128)(2,1)S(1)} %copy-done.1, ...), custom_call_target="tpu_custom_call" | custom-call | tf_op jit(solution)/shard_map/pallas_call | solution.py:707
  64.1 0.1 shard_map.71
  64.2 0.1 collective-permute-start.12
  64.2 2.2 %collective-permute-start.13 = (bf16[2,48,512]{2,1,0:T(8,128)(2,1)S(1)}, bf16[2,48,512]{2,1,0:T(8,128)(2,1)S(1)}, u32[]{:S(2)}, u32[]{:S(2)}) collective-permute-start(bf16[2,48,512]{2,1,0:T(8,128)(2,1)S(1)} %get-tuple-element.81.refs_11_), channel_id=1, source_target_pairs={{0,3},{1,2},{2,1},{3,0},{4,7},{5,6},{6,5},{7,4},{8,11},{9,10},{10,... | collective-permute-start | bytes 294920 | tf_op jit(solution)/shard_map/ppermute | solution.py:730
  66.4 5.4 %shard_map.72 = (f32[2,4,64,256]{3,2,1,0:T(8,128)S(1)}, f32[2,4,8,256]{3,2,1,0:T(8,128)S(1)}) custom-call(s32[1]{0:T(128)} %bitcast.index.refs_0_, s32[16]{0:T(128)S(1)} %copy-done.5, s32[16]{0:T(128)S(1)} %copy-done.6, bf16[4,144,512]{2,1,0:T(8,128)(2,1)S(1)} %copy-done.1, ...), custom_call_target="tpu_custom_call" | custom-call | tf_op jit(solution)/shard_map/pallas_call | solution.py:707
  71.8 0.1 shard_map.74
  71.9 0.4 collective-permute-start.16
  72.3 1.0 %collective-permute-start.17 = (bf16[2,48,512]{2,1,0:T(8,128)(2,1)S(1)}, bf16[2,48,512]{2,1,0:T(8,128)(2,1)S(1)}, u32[]{:S(2)}, u32[]{:S(2)}) collective-permute-start(bf16[2,48,512]{2,1,0:T(8,128)(2,1)S(1)} %get-tuple-element.89.refs_13_), channel_id=1, source_target_pairs={{0,3},{1,2},{2,1},{3,0},{4,7},{5,6},{6,5},{7,4},{8,11},{9,10},{10,... | collective-permute-start | bytes 294920 | tf_op jit(solution)/shard_map/ppermute | solution.py:730
  73.3 6.1 %shard_map.76 = (bf16[4,48,512]{2,1,0:T(8,128)(2,1)S(1)}, bf16[4,48,512]{2,1,0:T(8,128)(2,1)S(1)}) custom-call(s32[1]{0:T(128)} %bitcast.index.refs_0_, s32[16]{0:T(128)S(1)} %copy-done.5, s32[16]{0:T(128)S(1)} %copy-done.6, bf16[4,144,256]{2,1,0:T(8,128)(2,1)S(1)} %collective-permute-done.3.refs_7_.refs_3_, ...), custom_call_target="tpu_custom_call" | custom-call | tf_op jit(solution)/shard_map/pallas_call | solution.py:707
  79.4 0.0 copy-start.2
  79.4 0.9 %collective-permute-start.18 = (bf16[4,48,512]{2,1,0:T(8,128)(2,1)S(1)}, bf16[4,48,512]{2,1,0:T(8,128)(2,1)S(1)}, u32[]{:S(2)}, u32[]{:S(2)}) collective-permute-start(bf16[4,48,512]{2,1,0:T(8,128)(2,1)S(1)} %get-tuple-element.98), channel_id=1, source_target_pairs={{0,1},{1,0},{2,3},{3,2},{4,5},{5,4},{6,7},{7,6},{8,9},{9,8},{10,11... | collective-permute-start | bytes 589832 | tf_op jit(solution)/shard_map/ppermute | solution.py:730
  80.3 1.1 %collective-permute-done.18.refs_5_ = bf16[4,48,512]{2,1,0:T(8,128)(2,1)S(1)} collective-permute-done((bf16[4,48,512]{2,1,0:T(8,128)(2,1)S(1)}, bf16[4,48,512]{2,1,0:T(8,128)(2,1)S(1)}, u32[]{:S(2)}, u32[]{:S(2)}) %collective-permute-start.18) | collective-permute-done | bytes 196640 | tf_op jit(solution)/shard_map/ppermute | solution.py:730
  81.4 3.0 %shard_map.77 = bf16[512,768]{1,0:T(8,128)(2,1)} custom-call(s32[1]{0:T(128)} %bitcast.index.refs_0_, s32[16]{0:T(128)S(1)} %copy-done.5, s32[16]{0:T(128)S(1)} %copy-done.6, bf16[2,48,512]{2,1,0:T(8,128)(2,1)S(1)} %get-tuple-element.90.refs_0_, bf16[2,48,512]{2,1,0:T(8,128)(2,1)S(1)} %get-tuple-element.91.refs_1_, ...), custom_call_target="tpu_custom_call" | custom-call | tf_op jit(solution)/shard_map/pallas_call | solution.py:707
  (34 shorter events, 0.1 us)
Async XLA Ops:
  5.0 9.2 %copy-start.5 = (s32[16]{0:T(128)S(1)}, s32[16]{0:T(128)}, u32[]{:S(2)}) copy-start(s32[16]{0:T(128)} %mid.9) | copy-start | bytes 196
  5.1 9.2 %copy-start.6 = (s32[16]{0:T(128)S(1)}, s32[16]{0:T(128)}, u32[]{:S(2)}) copy-start(s32[16]{0:T(128)} %top.9) | copy-start | bytes 196
  5.1 3.2 %collective-permute-start = (bf16[4,144,512]{2,1,0:T(8,128)(2,1)}, bf16[4,144,512]{2,1,0:T(8,128)(2,1)S(1)}, u32[]{:S(2)}, u32[]{:S(2)}) collective-permute-start(bf16[4,144,512]{2,1,0:T(8,128)(2,1)} %get-tuple-element.53), channel_id=1, source_target_pairs={{0,1},{1,0},{2,3},{3,2},{4,5},{5,4},{6,7},{7,6},{8,9},{9,8},{10,11... | collective-permute-start | bytes 1769480 | tf_op jit(solution)/shard_map/ppermute | solution.py:730
  5.6 17.3 %collective-permute-start.1 = (bf16[4,144,256]{2,1,0:T(8,128)(2,1)}, bf16[4,144,256]{2,1,0:T(8,128)(2,1)S(1)}, u32[]{:S(2)}, u32[]{:S(2)}) collective-permute-start(bf16[4,144,256]{2,1,0:T(8,128)(2,1)} %get-tuple-element.54), channel_id=1, source_target_pairs={{0,2},{1,3},{2,0},{3,1},{4,6},{5,7},{6,4},{7,5},{8,10},{9,11},{10,... | collective-permute-start | bytes 884744 | tf_op jit(solution)/shard_map/ppermute | solution.py:730
  8.2 14.7 %collective-permute-start.2 = (bf16[4,144,256]{2,1,0:T(8,128)(2,1)}, bf16[4,144,256]{2,1,0:T(8,128)(2,1)S(1)}, u32[]{:S(2)}, u32[]{:S(2)}) collective-permute-start(bf16[4,144,256]{2,1,0:T(8,128)(2,1)} %get-tuple-element.55), channel_id=1, source_target_pairs={{0,3},{1,2},{2,1},{3,0},{4,7},{5,6},{6,5},{7,4},{8,11},{9,10},{10,... | collective-permute-start | bytes 884744 | tf_op jit(solution)/shard_map/ppermute | solution.py:730
  8.2 1.1 %copy-start = (bf16[4,144,512]{2,1,0:T(8,128)(2,1)S(1)}, bf16[4,144,512]{2,1,0:T(8,128)(2,1)}, u32[]{:S(2)}) copy-start(bf16[4,144,512]{2,1,0:T(8,128)(2,1)} %get-tuple-element.52.refs_0_.a_ref.refs_6_.refs_3_.refs_5_) | copy-start | bytes 1769476
  9.3 4.9 %copy-start.1 = (bf16[4,144,512]{2,1,0:T(8,128)(2,1)S(1)}, bf16[4,144,512]{2,1,0:T(8,128)(2,1)}, u32[]{:S(2)}) copy-start(bf16[4,144,512]{2,1,0:T(8,128)(2,1)} %get-tuple-element.52.refs_0_.a_ref.refs_6_.refs_3_.refs_5_) | copy-start | bytes 1769476
  9.3 13.6 %copy-start.3 = (bf16[4,144,256]{2,1,0:T(8,128)(2,1)S(1)}, bf16[4,144,256]{2,1,0:T(8,128)(2,1)}, u32[]{:S(2)}) copy-start(bf16[4,144,256]{2,1,0:T(8,128)(2,1)} %get-tuple-element.57.refs_3_) | copy-start | bytes 884740
  9.3 13.6 %copy-start.4 = (bf16[4,144,256]{2,1,0:T(8,128)(2,1)S(1)}, bf16[4,144,256]{2,1,0:T(8,128)(2,1)}, u32[]{:S(2)}) copy-start(bf16[4,144,256]{2,1,0:T(8,128)(2,1)} %get-tuple-element.58.refs_4_) | copy-start | bytes 884740
  9.3 17.4 %collective-permute-start.5 = (bf16[2,144,256]{2,1,0:T(8,128)(2,1)S(1)}, bf16[2,144,256]{2,1,0:T(8,128)(2,1)S(1)}, u32[]{:S(2)}, u32[]{:S(2)}) collective-permute-start(bf16[2,144,256]{2,1,0:T(8,128)(2,1)S(1)} %get-tuple-element.62), channel_id=1, source_target_pairs={{0,12},{1,13},{2,14},{3,15},{4,8},{5,9},{6,10},{7,11},{8,4},{9,5},... | collective-permute-start | bytes 442376 | tf_op jit(solution)/shard_map/ppermute | solution.py:730
  13.6 13.8 %collective-permute-start.6 = (bf16[2,144,256]{2,1,0:T(8,128)(2,1)S(1)}, bf16[2,144,256]{2,1,0:T(8,128)(2,1)S(1)}, u32[]{:S(2)}, u32[]{:S(2)}) collective-permute-start(bf16[2,144,256]{2,1,0:T(8,128)(2,1)S(1)} %get-tuple-element.63), channel_id=1, source_target_pairs={{0,8},{1,9},{2,10},{3,11},{4,12},{5,13},{6,14},{7,15},{8,0},{9,1},... | collective-permute-start | bytes 442376 | tf_op jit(solution)/shard_map/ppermute | solution.py:730
  13.6 14.5 %collective-permute-start.7 = (bf16[2,144,256]{2,1,0:T(8,128)(2,1)S(1)}, bf16[2,144,256]{2,1,0:T(8,128)(2,1)S(1)}, u32[]{:S(2)}, u32[]{:S(2)}) collective-permute-start(bf16[2,144,256]{2,1,0:T(8,128)(2,1)S(1)} %get-tuple-element.64), channel_id=1, source_target_pairs={{0,4},{1,5},{2,6},{3,7},{4,0},{5,1},{6,2},{7,3},{8,12},{9,13},{10,... | collective-permute-start | bytes 442376 | tf_op jit(solution)/shard_map/ppermute | solution.py:730
  22.9 19.8 %collective-permute-start.10 = (bf16[2,144,256]{2,1,0:T(8,128)(2,1)S(1)}, bf16[2,144,256]{2,1,0:T(8,128)(2,1)S(1)}, u32[]{:S(2)}, u32[]{:S(2)}) collective-permute-start(bf16[2,144,256]{2,1,0:T(8,128)(2,1)S(1)} %get-tuple-element.69), channel_id=1, source_target_pairs={{0,12},{1,13},{2,14},{3,15},{4,8},{5,9},{6,10},{7,11},{8,4},{9,5},... | collective-permute-start | bytes 442376 | tf_op jit(solution)/shard_map/ppermute | solution.py:730
  26.7 16.0 %collective-permute-start.8 = (bf16[2,144,256]{2,1,0:T(8,128)(2,1)S(1)}, bf16[2,144,256]{2,1,0:T(8,128)(2,1)S(1)}, u32[]{:S(2)}, u32[]{:S(2)}) collective-permute-start(bf16[2,144,256]{2,1,0:T(8,128)(2,1)S(1)} %get-tuple-element.67), channel_id=1, source_target_pairs={{0,8},{1,9},{2,10},{3,11},{4,12},{5,13},{6,14},{7,15},{8,0},{9,1},... | collective-permute-start | bytes 442376 | tf_op jit(solution)/shard_map/ppermute | solution.py:730
  26.8 16.0 %collective-permute-start.9 = (bf16[2,144,256]{2,1,0:T(8,128)(2,1)S(1)}, bf16[2,144,256]{2,1,0:T(8,128)(2,1)S(1)}, u32[]{:S(2)}, u32[]{:S(2)}) collective-permute-start(bf16[2,144,256]{2,1,0:T(8,128)(2,1)S(1)} %get-tuple-element.68), channel_id=1, source_target_pairs={{0,4},{1,5},{2,6},{3,7},{4,0},{5,1},{6,2},{7,3},{8,12},{9,13},{10,... | collective-permute-start | bytes 442376 | tf_op jit(solution)/shard_map/ppermute | solution.py:730
  27.4 31.3 %collective-permute-start.3 = (bf16[4,144,256]{2,1,0:T(8,128)(2,1)S(1)}, bf16[4,144,256]{2,1,0:T(8,128)(2,1)S(1)}, u32[]{:S(2)}, u32[]{:S(2)}) collective-permute-start(bf16[4,144,256]{2,1,0:T(8,128)(2,1)S(1)} %get-tuple-element.59), channel_id=1, source_target_pairs={{0,2},{1,3},{2,0},{3,1},{4,6},{5,7},{6,4},{7,5},{8,10},{9,11},{10,... | collective-permute-start | bytes 884744 | tf_op jit(solution)/shard_map/ppermute | solution.py:730
  28.1 30.6 %collective-permute-start.4 = (bf16[4,144,256]{2,1,0:T(8,128)(2,1)S(1)}, bf16[4,144,256]{2,1,0:T(8,128)(2,1)S(1)}, u32[]{:S(2)}, u32[]{:S(2)}) collective-permute-start(bf16[4,144,256]{2,1,0:T(8,128)(2,1)S(1)} %get-tuple-element.60), channel_id=1, source_target_pairs={{0,3},{1,2},{2,1},{3,0},{4,7},{5,6},{6,5},{7,4},{8,11},{9,10},{10,... | collective-permute-start | bytes 884744 | tf_op jit(solution)/shard_map/ppermute | solution.py:730
  54.2 9.9 %collective-permute-start.11 = (bf16[48,1152]{1,0:T(8,128)(2,1)S(1)}, bf16[48,1152]{1,0:T(8,128)(2,1)S(1)}, u32[]{:S(2)}, u32[]{:S(2)}) collective-permute-start(bf16[48,1152]{1,0:T(8,128)(2,1)S(1)} %get-tuple-element.79), channel_id=1, source_target_pairs={{0,4},{1,5},{2,6},{3,7},{4,0},{5,1},{6,2},{7,3},{8,12},{9,13},{10,... | collective-permute-start | bytes 331784 | tf_op jit(solution)/shard_map/ppermute | solution.py:730
  55.5 16.3 %collective-permute-start.14 = (bf16[48,1152]{1,0:T(8,128)(2,1)S(1)}, bf16[48,1152]{1,0:T(8,128)(2,1)S(1)}, u32[]{:S(2)}, u32[]{:S(2)}) collective-permute-start(bf16[48,1152]{1,0:T(8,128)(2,1)S(1)} %get-tuple-element.84), channel_id=1, source_target_pairs={{0,8},{1,9},{2,10},{3,11},{4,12},{5,13},{6,14},{7,15},{8,0},{9,1},... | collective-permute-start | bytes 331784 | tf_op jit(solution)/shard_map/ppermute | solution.py:730
  58.4 13.4 %collective-permute-start.15 = (bf16[48,1152]{1,0:T(8,128)(2,1)S(1)}, bf16[48,1152]{1,0:T(8,128)(2,1)S(1)}, u32[]{:S(2)}, u32[]{:S(2)}) collective-permute-start(bf16[48,1152]{1,0:T(8,128)(2,1)S(1)} %get-tuple-element.85), channel_id=1, source_target_pairs={{0,12},{1,13},{2,14},{3,15},{4,8},{5,9},{6,10},{7,11},{8,4},{9,5},... | collective-permute-start | bytes 331784 | tf_op jit(solution)/shard_map/ppermute | solution.py:730
  64.2 9.2 %collective-permute-start.12 = (bf16[2,48,512]{2,1,0:T(8,128)(2,1)S(1)}, bf16[2,48,512]{2,1,0:T(8,128)(2,1)S(1)}, u32[]{:S(2)}, u32[]{:S(2)}) collective-permute-start(bf16[2,48,512]{2,1,0:T(8,128)(2,1)S(1)} %get-tuple-element.80), channel_id=1, source_target_pairs={{0,2},{1,3},{2,0},{3,1},{4,6},{5,7},{6,4},{7,5},{8,10},{9,11},{10,... | collective-permute-start | bytes 294920 | tf_op jit(solution)/shard_map/ppermute | solution.py:730
  64.2 9.1 %collective-permute-start.13 = (bf16[2,48,512]{2,1,0:T(8,128)(2,1)S(1)}, bf16[2,48,512]{2,1,0:T(8,128)(2,1)S(1)}, u32[]{:S(2)}, u32[]{:S(2)}) collective-permute-start(bf16[2,48,512]{2,1,0:T(8,128)(2,1)S(1)} %get-tuple-element.81.refs_11_), channel_id=1, source_target_pairs={{0,3},{1,2},{2,1},{3,0},{4,7},{5,6},{6,5},{7,4},{8,11},{9,10},{10,... | collective-permute-start | bytes 294920 | tf_op jit(solution)/shard_map/ppermute | solution.py:730
  71.9 8.4 %collective-permute-start.16 = (bf16[2,48,512]{2,1,0:T(8,128)(2,1)S(1)}, bf16[2,48,512]{2,1,0:T(8,128)(2,1)S(1)}, u32[]{:S(2)}, u32[]{:S(2)}) collective-permute-start(bf16[2,48,512]{2,1,0:T(8,128)(2,1)S(1)} %get-tuple-element.88), channel_id=1, source_target_pairs={{0,2},{1,3},{2,0},{3,1},{4,6},{5,7},{6,4},{7,5},{8,10},{9,11},{10,... | collective-permute-start | bytes 294920 | tf_op jit(solution)/shard_map/ppermute | solution.py:730
  72.3 8.0 %collective-permute-start.17 = (bf16[2,48,512]{2,1,0:T(8,128)(2,1)S(1)}, bf16[2,48,512]{2,1,0:T(8,128)(2,1)S(1)}, u32[]{:S(2)}, u32[]{:S(2)}) collective-permute-start(bf16[2,48,512]{2,1,0:T(8,128)(2,1)S(1)} %get-tuple-element.89.refs_13_), channel_id=1, source_target_pairs={{0,3},{1,2},{2,1},{3,0},{4,7},{5,6},{6,5},{7,4},{8,11},{9,10},{10,... | collective-permute-start | bytes 294920 | tf_op jit(solution)/shard_map/ppermute | solution.py:730
  79.4 2.0 %copy-start.2 = (bf16[768,768]{1,0:T(8,128)(2,1)S(1)}, bf16[768,768]{1,0:T(8,128)(2,1)}, u32[]{:S(2)}) copy-start(bf16[768,768]{1,0:T(8,128)(2,1)} %refs_6_.1) | copy-start | bytes 3538948
  79.4 1.9 %collective-permute-start.18 = (bf16[4,48,512]{2,1,0:T(8,128)(2,1)S(1)}, bf16[4,48,512]{2,1,0:T(8,128)(2,1)S(1)}, u32[]{:S(2)}, u32[]{:S(2)}) collective-permute-start(bf16[4,48,512]{2,1,0:T(8,128)(2,1)S(1)} %get-tuple-element.98), channel_id=1, source_target_pairs={{0,1},{1,0},{2,3},{3,2},{4,5},{5,4},{6,7},{7,6},{8,9},{9,8},{10,11... | collective-permute-start | bytes 589832 | tf_op jit(solution)/shard_map/ppermute | solution.py:730

commit v16 on v15

--- a/solution.py
+++ b/solution.py
@@ -152,7 +152,7 @@
 TOK = 512
 SCALE = DH**-0.5 * LOG2E
 BUSY = 1 << 33
-AHEAD = 6
+AHEAD = 8
 SAFE = 96.0
 CHUNKS = ((0, 2), (2, 2))
 DX = 64

time: 84.6 us -> 84.6 us (level)
  no operation moved by 1% of the time
where the time goes in v16:
time: 84.6 us; the launch traced here: 84.4 us
  Pallas kernels  59.9 us (71%)
  starting transfers between devices  22.1 us (26%)
  waiting for transfers between devices  1.11 us (1%)
  local copies, waits for them, and re-layouts  1.09 us (1%)
    pallas_call x14, Pallas kernels, call(): pl.pallas_call(body if extra else kernel, grid_spec=pltpu.PrefetchScalarG...  59.9 us
    ppermute x19, starting transfers between devices, within(): return lax.ppermute(array, 'seq', [(i, i ^ apart) for i in range(count)])  22.1 us
  transfers between devices with their start and end apart: 19, of which 1 were waited for; matrix products, arithmetic and copies ran while one was open for 0% of the time, Pallas kernels for 61%

profile of v16, /device:TPU:0, one launch (start us, length us, event | category | flops | bytes accessed | tf_op | source)
XLA Modules:
  0.0 84.4 jit_solution(14018317824999696431)
XLA Ops:
  0.0 5.0 %shard_map.64 = (bf16[4,144,512]{2,1,0:T(8,128)(2,1)}, bf16[4,144,512]{2,1,0:T(8,128)(2,1)}, bf16[4,144,256]{2,1,0:T(8,128)(2,1)}, bf16[4,144,256]{2,1,0:T(8,128...) custom-call(s32[1]{0:T(128)} %bitcast.index.refs_0_, s32[16]{0:T(128)} %mid.9, s32[16]{0:T(128)} %top.9, ...), custom_call_target="tpu_custom_call" | custom-call | tf_op jit(solution)/shard_map/pallas_call | solution.py:707
  5.0 0.0 copy-start.5
  5.1 0.0 copy-start.6
  5.1 0.5 collective-permute-start
  5.6 2.6 %collective-permute-start.1 = (bf16[4,144,256]{2,1,0:T(8,128)(2,1)}, bf16[4,144,256]{2,1,0:T(8,128)(2,1)S(1)}, u32[]{:S(2)}, u32[]{:S(2)}) collective-permute-start(bf16[4,144,256]{2,1,0:T(8,128)(2,1)} %get-tuple-element.54), channel_id=1, source_target_pairs={{0,2},{1,3},{2,0},{3,1},{4,6},{5,7},{6,4},{7,5},{8,10},{9,11},{10,... | collective-permute-start | bytes 884744 | tf_op jit(solution)/shard_map/ppermute | solution.py:730
  8.2 0.1 collective-permute-start.2
  8.2 1.1 %copy-done = bf16[4,144,512]{2,1,0:T(8,128)(2,1)S(1)} copy-done((bf16[4,144,512]{2,1,0:T(8,128)(2,1)S(1)}, bf16[4,144,512]{2,1,0:T(8,128)(2,1)}, u32[]{:S(2)}) %copy-start) | copy-done | bytes 589848
  9.3 4.2 %collective-permute-start.5 = (bf16[2,144,256]{2,1,0:T(8,128)(2,1)S(1)}, bf16[2,144,256]{2,1,0:T(8,128)(2,1)S(1)}, u32[]{:S(2)}, u32[]{:S(2)}) collective-permute-start(bf16[2,144,256]{2,1,0:T(8,128)(2,1)S(1)} %get-tuple-element.62), channel_id=1, source_target_pairs={{0,12},{1,13},{2,14},{3,15},{4,8},{5,9},{6,10},{7,11},{8,4},{9,5},... | collective-permute-start | bytes 442376 | tf_op jit(solution)/shard_map/ppermute | solution.py:730
  13.6 0.6 collective-permute-start.7
  14.2 8.6 %shard_map.65 = (f32[4,4,64,256]{3,2,1,0:T(8,128)S(1)}, f32[4,4,8,256]{3,2,1,0:T(8,128)S(1)}) custom-call(s32[1]{0:T(128)} %bitcast.index.refs_0_, s32[16]{0:T(128)S(1)} %copy-done.5, s32[16]{0:T(128)S(1)} %copy-done.6, bf16[4,144,512]{2,1,0:T(8,128)(2,1)S(1)} %copy-done.1, bf16[4,144,512]{2,1,0:T(8,128)(2,1)S(1)} %collective-permute-done.refs_1_.b_ref.refs_7_.refs_4_.refs_6_), custom_call_target="tpu_custom_call" | custom-call | tf_op jit(solution)/shard_map/pallas_call | solution.py:707
  22.9 0.0 collective-permute-done.1.refs_0_.refs_2_.refs_5_
  22.9 3.8 %collective-permute-start.10 = (bf16[2,144,256]{2,1,0:T(8,128)(2,1)S(1)}, bf16[2,144,256]{2,1,0:T(8,128)(2,1)S(1)}, u32[]{:S(2)}, u32[]{:S(2)}) collective-permute-start(bf16[2,144,256]{2,1,0:T(8,128)(2,1)S(1)} %get-tuple-element.69), channel_id=1, source_target_pairs={{0,12},{1,13},{2,14},{3,15},{4,8},{5,9},{6,10},{7,11},{8,4},{9,5},... | collective-permute-start | bytes 442376 | tf_op jit(solution)/shard_map/ppermute | solution.py:730
  26.8 0.6 collective-permute-start.9
  27.4 0.7 collective-permute-start.3
  28.1 14.7 %shard_map.68 = (f32[4,4,64,256]{3,2,1,0:T(8,128)S(1)}, f32[4,4,8,256]{3,2,1,0:T(8,128)S(1)}, f32[4,2,64,256]{3,2,1,0:T(8,128)S(1)}, f32[4,2,8,256]{3,2,1,0:T(8,...) custom-call(s32[1]{0:T(128)} %bitcast.index.refs_0_, ...), custom_call_target="tpu_custom_call" | custom-call | tf_op jit(solution)/shard_map/pallas_call | solution.py:707
  42.8 11.4 %shard_map.69 = (bf16[48,1152]{1,0:T(8,128)(2,1)S(1)}, bf16[48,1152]{1,0:T(8,128)(2,1)S(1)}, bf16[48,1152]{1,0:T(8,128)(2,1)S(1)}, bf16[48,1152]{1,0:T(8,128)(2,1)S(1)}) custom-call(s32[1]{0:T(128)} %bitcast.index.refs_0_, s32[16]{0:T(128)S(1)} %copy-done.5, s32[16]{0:T(128)S(1)} %copy-done.6, ...), custom_call_target="tpu_custom_call" | custom-call | flops 8589934592 | tf_op jit(solution)/shard_map/pallas_call | solution.py:707
  54.2 1.3 %collective-permute-start.11 = (bf16[48,1152]{1,0:T(8,128)(2,1)S(1)}, bf16[48,1152]{1,0:T(8,128)(2,1)S(1)}, u32[]{:S(2)}, u32[]{:S(2)}) collective-permute-start(bf16[48,1152]{1,0:T(8,128)(2,1)S(1)} %get-tuple-element.79), channel_id=1, source_target_pairs={{0,4},{1,5},{2,6},{3,7},{4,0},{5,1},{6,2},{7,3},{8,12},{9,13},{10,... | collective-permute-start | bytes 331784 | tf_op jit(solution)/shard_map/ppermute | solution.py:730
  55.6 2.9 %collective-permute-start.14 = (bf16[48,1152]{1,0:T(8,128)(2,1)S(1)}, bf16[48,1152]{1,0:T(8,128)(2,1)S(1)}, u32[]{:S(2)}, u32[]{:S(2)}) collective-permute-start(bf16[48,1152]{1,0:T(8,128)(2,1)S(1)} %get-tuple-element.84), channel_id=1, source_target_pairs={{0,8},{1,9},{2,10},{3,11},{4,12},{5,13},{6,14},{7,15},{8,0},{9,1},... | collective-permute-start | bytes 331784 | tf_op jit(solution)/shard_map/ppermute | solution.py:730
  58.5 0.2 collective-permute-start.15
  58.7 5.4 %shard_map.70 = (f32[2,4,64,256]{3,2,1,0:T(8,128)S(1)}, f32[2,4,8,256]{3,2,1,0:T(8,128)S(1)}) custom-call(s32[1]{0:T(128)} %bitcast.index.refs_0_, s32[16]{0:T(128)S(1)} %copy-done.5, s32[16]{0:T(128)S(1)} %copy-done.6, bf16[4,144,512]{2,1,0:T(8,128)(2,1)S(1)} %copy-done.1, ...), custom_call_target="tpu_custom_call" | custom-call | tf_op jit(solution)/shard_map/pallas_call | solution.py:707
  64.1 0.1 shard_map.71
  64.2 0.1 collective-permute-start.12
  64.3 2.2 %collective-permute-start.13 = (bf16[2,48,512]{2,1,0:T(8,128)(2,1)S(1)}, bf16[2,48,512]{2,1,0:T(8,128)(2,1)S(1)}, u32[]{:S(2)}, u32[]{:S(2)}) collective-permute-start(bf16[2,48,512]{2,1,0:T(8,128)(2,1)S(1)} %get-tuple-element.81.refs_11_), channel_id=1, source_target_pairs={{0,3},{1,2},{2,1},{3,0},{4,7},{5,6},{6,5},{7,4},{8,11},{9,10},{10,... | collective-permute-start | bytes 294920 | tf_op jit(solution)/shard_map/ppermute | solution.py:730
  66.4 5.4 %shard_map.72 = (f32[2,4,64,256]{3,2,1,0:T(8,128)S(1)}, f32[2,4,8,256]{3,2,1,0:T(8,128)S(1)}) custom-call(s32[1]{0:T(128)} %bitcast.index.refs_0_, s32[16]{0:T(128)S(1)} %copy-done.5, s32[16]{0:T(128)S(1)} %copy-done.6, bf16[4,144,512]{2,1,0:T(8,128)(2,1)S(1)} %copy-done.1, ...), custom_call_target="tpu_custom_call" | custom-call | tf_op jit(solution)/shard_map/pallas_call | solution.py:707
  71.9 0.1 shard_map.74
  72.0 0.4 collective-permute-start.16
  72.4 1.0 %collective-permute-start.17 = (bf16[2,48,512]{2,1,0:T(8,128)(2,1)S(1)}, bf16[2,48,512]{2,1,0:T(8,128)(2,1)S(1)}, u32[]{:S(2)}, u32[]{:S(2)}) collective-permute-start(bf16[2,48,512]{2,1,0:T(8,128)(2,1)S(1)} %get-tuple-element.89.refs_13_), channel_id=1, source_target_pairs={{0,3},{1,2},{2,1},{3,0},{4,7},{5,6},{6,5},{7,4},{8,11},{9,10},{10,... | collective-permute-start | bytes 294920 | tf_op jit(solution)/shard_map/ppermute | solution.py:730
  73.4 6.1 %shard_map.76 = (bf16[4,48,512]{2,1,0:T(8,128)(2,1)S(1)}, bf16[4,48,512]{2,1,0:T(8,128)(2,1)S(1)}) custom-call(s32[1]{0:T(128)} %bitcast.index.refs_0_, s32[16]{0:T(128)S(1)} %copy-done.5, s32[16]{0:T(128)S(1)} %copy-done.6, bf16[4,144,256]{2,1,0:T(8,128)(2,1)S(1)} %collective-permute-done.3.refs_7_.refs_3_, ...), custom_call_target="tpu_custom_call" | custom-call | tf_op jit(solution)/shard_map/pallas_call | solution.py:707
  79.5 0.0 copy-start.2
  79.5 0.9 %collective-permute-start.18 = (bf16[4,48,512]{2,1,0:T(8,128)(2,1)S(1)}, bf16[4,48,512]{2,1,0:T(8,128)(2,1)S(1)}, u32[]{:S(2)}, u32[]{:S(2)}) collective-permute-start(bf16[4,48,512]{2,1,0:T(8,128)(2,1)S(1)} %get-tuple-element.98), channel_id=1, source_target_pairs={{0,1},{1,0},{2,3},{3,2},{4,5},{5,4},{6,7},{7,6},{8,9},{9,8},{10,11... | collective-permute-start | bytes 589832 | tf_op jit(solution)/shard_map/ppermute | solution.py:730
  80.4 1.1 %collective-permute-done.18.refs_5_ = bf16[4,48,512]{2,1,0:T(8,128)(2,1)S(1)} collective-permute-done((bf16[4,48,512]{2,1,0:T(8,128)(2,1)S(1)}, bf16[4,48,512]{2,1,0:T(8,128)(2,1)S(1)}, u32[]{:S(2)}, u32[]{:S(2)}) %collective-permute-start.18) | collective-permute-done | bytes 196640 | tf_op jit(solution)/shard_map/ppermute | solution.py:730
  81.4 3.0 %shard_map.77 = bf16[512,768]{1,0:T(8,128)(2,1)} custom-call(s32[1]{0:T(128)} %bitcast.index.refs_0_, s32[16]{0:T(128)S(1)} %copy-done.5, s32[16]{0:T(128)S(1)} %copy-done.6, bf16[2,48,512]{2,1,0:T(8,128)(2,1)S(1)} %get-tuple-element.90.refs_0_, bf16[2,48,512]{2,1,0:T(8,128)(2,1)S(1)} %get-tuple-element.91.refs_1_, ...), custom_call_target="tpu_custom_call" | custom-call | tf_op jit(solution)/shard_map/pallas_call | solution.py:707
  (34 shorter events, 0.1 us)
Async XLA Ops:
  5.0 9.2 %copy-start.5 = (s32[16]{0:T(128)S(1)}, s32[16]{0:T(128)}, u32[]{:S(2)}) copy-start(s32[16]{0:T(128)} %mid.9) | copy-start | bytes 196
  5.1 9.2 %copy-start.6 = (s32[16]{0:T(128)S(1)}, s32[16]{0:T(128)}, u32[]{:S(2)}) copy-start(s32[16]{0:T(128)} %top.9) | copy-start | bytes 196
  5.1 3.2 %collective-permute-start = (bf16[4,144,512]{2,1,0:T(8,128)(2,1)}, bf16[4,144,512]{2,1,0:T(8,128)(2,1)S(1)}, u32[]{:S(2)}, u32[]{:S(2)}) collective-permute-start(bf16[4,144,512]{2,1,0:T(8,128)(2,1)} %get-tuple-element.53), channel_id=1, source_target_pairs={{0,1},{1,0},{2,3},{3,2},{4,5},{5,4},{6,7},{7,6},{8,9},{9,8},{10,11... | collective-permute-start | bytes 1769480 | tf_op jit(solution)/shard_map/ppermute | solution.py:730
  5.6 17.3 %collective-permute-start.1 = (bf16[4,144,256]{2,1,0:T(8,128)(2,1)}, bf16[4,144,256]{2,1,0:T(8,128)(2,1)S(1)}, u32[]{:S(2)}, u32[]{:S(2)}) collective-permute-start(bf16[4,144,256]{2,1,0:T(8,128)(2,1)} %get-tuple-element.54), channel_id=1, source_target_pairs={{0,2},{1,3},{2,0},{3,1},{4,6},{5,7},{6,4},{7,5},{8,10},{9,11},{10,... | collective-permute-start | bytes 884744 | tf_op jit(solution)/shard_map/ppermute | solution.py:730
  8.2 14.7 %collective-permute-start.2 = (bf16[4,144,256]{2,1,0:T(8,128)(2,1)}, bf16[4,144,256]{2,1,0:T(8,128)(2,1)S(1)}, u32[]{:S(2)}, u32[]{:S(2)}) collective-permute-start(bf16[4,144,256]{2,1,0:T(8,128)(2,1)} %get-tuple-element.55), channel_id=1, source_target_pairs={{0,3},{1,2},{2,1},{3,0},{4,7},{5,6},{6,5},{7,4},{8,11},{9,10},{10,... | collective-permute-start | bytes 884744 | tf_op jit(solution)/shard_map/ppermute | solution.py:730
  8.2 1.1 %copy-start = (bf16[4,144,512]{2,1,0:T(8,128)(2,1)S(1)}, bf16[4,144,512]{2,1,0:T(8,128)(2,1)}, u32[]{:S(2)}) copy-start(bf16[4,144,512]{2,1,0:T(8,128)(2,1)} %get-tuple-element.52.refs_0_.a_ref.refs_6_.refs_3_.refs_5_) | copy-start | bytes 1769476
  9.3 4.9 %copy-start.1 = (bf16[4,144,512]{2,1,0:T(8,128)(2,1)S(1)}, bf16[4,144,512]{2,1,0:T(8,128)(2,1)}, u32[]{:S(2)}) copy-start(bf16[4,144,512]{2,1,0:T(8,128)(2,1)} %get-tuple-element.52.refs_0_.a_ref.refs_6_.refs_3_.refs_5_) | copy-start | bytes 1769476
  9.3 13.6 %copy-start.3 = (bf16[4,144,256]{2,1,0:T(8,128)(2,1)S(1)}, bf16[4,144,256]{2,1,0:T(8,128)(2,1)}, u32[]{:S(2)}) copy-start(bf16[4,144,256]{2,1,0:T(8,128)(2,1)} %get-tuple-element.57.refs_3_) | copy-start | bytes 884740
  9.3 13.6 %copy-start.4 = (bf16[4,144,256]{2,1,0:T(8,128)(2,1)S(1)}, bf16[4,144,256]{2,1,0:T(8,128)(2,1)}, u32[]{:S(2)}) copy-start(bf16[4,144,256]{2,1,0:T(8,128)(2,1)} %get-tuple-element.58.refs_4_) | copy-start | bytes 884740
  9.3 17.4 %collective-permute-start.5 = (bf16[2,144,256]{2,1,0:T(8,128)(2,1)S(1)}, bf16[2,144,256]{2,1,0:T(8,128)(2,1)S(1)}, u32[]{:S(2)}, u32[]{:S(2)}) collective-permute-start(bf16[2,144,256]{2,1,0:T(8,128)(2,1)S(1)} %get-tuple-element.62), channel_id=1, source_target_pairs={{0,12},{1,13},{2,14},{3,15},{4,8},{5,9},{6,10},{7,11},{8,4},{9,5},... | collective-permute-start | bytes 442376 | tf_op jit(solution)/shard_map/ppermute | solution.py:730
  13.6 13.8 %collective-permute-start.6 = (bf16[2,144,256]{2,1,0:T(8,128)(2,1)S(1)}, bf16[2,144,256]{2,1,0:T(8,128)(2,1)S(1)}, u32[]{:S(2)}, u32[]{:S(2)}) collective-permute-start(bf16[2,144,256]{2,1,0:T(8,128)(2,1)S(1)} %get-tuple-element.63), channel_id=1, source_target_pairs={{0,8},{1,9},{2,10},{3,11},{4,12},{5,13},{6,14},{7,15},{8,0},{9,1},... | collective-permute-start | bytes 442376 | tf_op jit(solution)/shard_map/ppermute | solution.py:730
  13.6 14.5 %collective-permute-start.7 = (bf16[2,144,256]{2,1,0:T(8,128)(2,1)S(1)}, bf16[2,144,256]{2,1,0:T(8,128)(2,1)S(1)}, u32[]{:S(2)}, u32[]{:S(2)}) collective-permute-start(bf16[2,144,256]{2,1,0:T(8,128)(2,1)S(1)} %get-tuple-element.64), channel_id=1, source_target_pairs={{0,4},{1,5},{2,6},{3,7},{4,0},{5,1},{6,2},{7,3},{8,12},{9,13},{10,... | collective-permute-start | bytes 442376 | tf_op jit(solution)/shard_map/ppermute | solution.py:730
  22.9 19.8 %collective-permute-start.10 = (bf16[2,144,256]{2,1,0:T(8,128)(2,1)S(1)}, bf16[2,144,256]{2,1,0:T(8,128)(2,1)S(1)}, u32[]{:S(2)}, u32[]{:S(2)}) collective-permute-start(bf16[2,144,256]{2,1,0:T(8,128)(2,1)S(1)} %get-tuple-element.69), channel_id=1, source_target_pairs={{0,12},{1,13},{2,14},{3,15},{4,8},{5,9},{6,10},{7,11},{8,4},{9,5},... | collective-permute-start | bytes 442376 | tf_op jit(solution)/shard_map/ppermute | solution.py:730
  26.7 16.0 %collective-permute-start.8 = (bf16[2,144,256]{2,1,0:T(8,128)(2,1)S(1)}, bf16[2,144,256]{2,1,0:T(8,128)(2,1)S(1)}, u32[]{:S(2)}, u32[]{:S(2)}) collective-permute-start(bf16[2,144,256]{2,1,0:T(8,128)(2,1)S(1)} %get-tuple-element.67), channel_id=1, source_target_pairs={{0,8},{1,9},{2,10},{3,11},{4,12},{5,13},{6,14},{7,15},{8,0},{9,1},... | collective-permute-start | bytes 442376 | tf_op jit(solution)/shard_map/ppermute | solution.py:730
  26.8 16.1 %collective-permute-start.9 = (bf16[2,144,256]{2,1,0:T(8,128)(2,1)S(1)}, bf16[2,144,256]{2,1,0:T(8,128)(2,1)S(1)}, u32[]{:S(2)}, u32[]{:S(2)}) collective-permute-start(bf16[2,144,256]{2,1,0:T(8,128)(2,1)S(1)} %get-tuple-element.68), channel_id=1, source_target_pairs={{0,4},{1,5},{2,6},{3,7},{4,0},{5,1},{6,2},{7,3},{8,12},{9,13},{10,... | collective-permute-start | bytes 442376 | tf_op jit(solution)/shard_map/ppermute | solution.py:730
  27.4 31.3 %collective-permute-start.3 = (bf16[4,144,256]{2,1,0:T(8,128)(2,1)S(1)}, bf16[4,144,256]{2,1,0:T(8,128)(2,1)S(1)}, u32[]{:S(2)}, u32[]{:S(2)}) collective-permute-start(bf16[4,144,256]{2,1,0:T(8,128)(2,1)S(1)} %get-tuple-element.59), channel_id=1, source_target_pairs={{0,2},{1,3},{2,0},{3,1},{4,6},{5,7},{6,4},{7,5},{8,10},{9,11},{10,... | collective-permute-start | bytes 884744 | tf_op jit(solution)/shard_map/ppermute | solution.py:730
  28.1 30.6 %collective-permute-start.4 = (bf16[4,144,256]{2,1,0:T(8,128)(2,1)S(1)}, bf16[4,144,256]{2,1,0:T(8,128)(2,1)S(1)}, u32[]{:S(2)}, u32[]{:S(2)}) collective-permute-start(bf16[4,144,256]{2,1,0:T(8,128)(2,1)S(1)} %get-tuple-element.60), channel_id=1, source_target_pairs={{0,3},{1,2},{2,1},{3,0},{4,7},{5,6},{6,5},{7,4},{8,11},{9,10},{10,... | collective-permute-start | bytes 884744 | tf_op jit(solution)/shard_map/ppermute | solution.py:730
  54.2 9.9 %collective-permute-start.11 = (bf16[48,1152]{1,0:T(8,128)(2,1)S(1)}, bf16[48,1152]{1,0:T(8,128)(2,1)S(1)}, u32[]{:S(2)}, u32[]{:S(2)}) collective-permute-start(bf16[48,1152]{1,0:T(8,128)(2,1)S(1)} %get-tuple-element.79), channel_id=1, source_target_pairs={{0,4},{1,5},{2,6},{3,7},{4,0},{5,1},{6,2},{7,3},{8,12},{9,13},{10,... | collective-permute-start | bytes 331784 | tf_op jit(solution)/shard_map/ppermute | solution.py:730
  55.6 16.3 %collective-permute-start.14 = (bf16[48,1152]{1,0:T(8,128)(2,1)S(1)}, bf16[48,1152]{1,0:T(8,128)(2,1)S(1)}, u32[]{:S(2)}, u32[]{:S(2)}) collective-permute-start(bf16[48,1152]{1,0:T(8,128)(2,1)S(1)} %get-tuple-element.84), channel_id=1, source_target_pairs={{0,8},{1,9},{2,10},{3,11},{4,12},{5,13},{6,14},{7,15},{8,0},{9,1},... | collective-permute-start | bytes 331784 | tf_op jit(solution)/shard_map/ppermute | solution.py:730
  58.5 13.4 %collective-permute-start.15 = (bf16[48,1152]{1,0:T(8,128)(2,1)S(1)}, bf16[48,1152]{1,0:T(8,128)(2,1)S(1)}, u32[]{:S(2)}, u32[]{:S(2)}) collective-permute-start(bf16[48,1152]{1,0:T(8,128)(2,1)S(1)} %get-tuple-element.85), channel_id=1, source_target_pairs={{0,12},{1,13},{2,14},{3,15},{4,8},{5,9},{6,10},{7,11},{8,4},{9,5},... | collective-permute-start | bytes 331784 | tf_op jit(solution)/shard_map/ppermute | solution.py:730
  64.2 9.2 %collective-permute-start.12 = (bf16[2,48,512]{2,1,0:T(8,128)(2,1)S(1)}, bf16[2,48,512]{2,1,0:T(8,128)(2,1)S(1)}, u32[]{:S(2)}, u32[]{:S(2)}) collective-permute-start(bf16[2,48,512]{2,1,0:T(8,128)(2,1)S(1)} %get-tuple-element.80), channel_id=1, source_target_pairs={{0,2},{1,3},{2,0},{3,1},{4,6},{5,7},{6,4},{7,5},{8,10},{9,11},{10,... | collective-permute-start | bytes 294920 | tf_op jit(solution)/shard_map/ppermute | solution.py:730
  64.3 9.1 %collective-permute-start.13 = (bf16[2,48,512]{2,1,0:T(8,128)(2,1)S(1)}, bf16[2,48,512]{2,1,0:T(8,128)(2,1)S(1)}, u32[]{:S(2)}, u32[]{:S(2)}) collective-permute-start(bf16[2,48,512]{2,1,0:T(8,128)(2,1)S(1)} %get-tuple-element.81.refs_11_), channel_id=1, source_target_pairs={{0,3},{1,2},{2,1},{3,0},{4,7},{5,6},{6,5},{7,4},{8,11},{9,10},{10,... | collective-permute-start | bytes 294920 | tf_op jit(solution)/shard_map/ppermute | solution.py:730
  72.0 8.4 %collective-permute-start.16 = (bf16[2,48,512]{2,1,0:T(8,128)(2,1)S(1)}, bf16[2,48,512]{2,1,0:T(8,128)(2,1)S(1)}, u32[]{:S(2)}, u32[]{:S(2)}) collective-permute-start(bf16[2,48,512]{2,1,0:T(8,128)(2,1)S(1)} %get-tuple-element.88), channel_id=1, source_target_pairs={{0,2},{1,3},{2,0},{3,1},{4,6},{5,7},{6,4},{7,5},{8,10},{9,11},{10,... | collective-permute-start | bytes 294920 | tf_op jit(solution)/shard_map/ppermute | solution.py:730
  72.4 8.0 %collective-permute-start.17 = (bf16[2,48,512]{2,1,0:T(8,128)(2,1)S(1)}, bf16[2,48,512]{2,1,0:T(8,128)(2,1)S(1)}, u32[]{:S(2)}, u32[]{:S(2)}) collective-permute-start(bf16[2,48,512]{2,1,0:T(8,128)(2,1)S(1)} %get-tuple-element.89.refs_13_), channel_id=1, source_target_pairs={{0,3},{1,2},{2,1},{3,0},{4,7},{5,6},{6,5},{7,4},{8,11},{9,10},{10,... | collective-permute-start | bytes 294920 | tf_op jit(solution)/shard_map/ppermute | solution.py:730
  79.5 2.0 %copy-start.2 = (bf16[768,768]{1,0:T(8,128)(2,1)S(1)}, bf16[768,768]{1,0:T(8,128)(2,1)}, u32[]{:S(2)}) copy-start(bf16[768,768]{1,0:T(8,128)(2,1)} %refs_6_.1) | copy-start | bytes 3538948
  79.5 1.9 %collective-permute-start.18 = (bf16[4,48,512]{2,1,0:T(8,128)(2,1)S(1)}, bf16[4,48,512]{2,1,0:T(8,128)(2,1)S(1)}, u32[]{:S(2)}, u32[]{:S(2)}) collective-permute-start(bf16[4,48,512]{2,1,0:T(8,128)(2,1)S(1)} %get-tuple-element.98), channel_id=1, source_target_pairs={{0,1},{1,0},{2,3},{3,2},{4,5},{5,4},{6,7},{7,6},{8,9},{9,8},{10,11... | collective-permute-start | bytes 589832 | tf_op jit(solution)/shard_map/ppermute | solution.py:730
